TPU v7x, 32 devices: a whole 2x2x4 slice. The times are simulated.
32 devices in a mesh: ctx: 8 (over z, y), head: 4 (over x, core).
Axes of the slice: x: 2, y: 2, z: 4, core: 2. Of those that a mesh axis runs over, the one named last changes fastest.
Arguments:
- features: bfloat16 [2048, 1024], P('ctx', 'head'), may hold values from -30 to 30
- w_qkv: bfloat16 [1024, 3, 1024], P(None, None, 'head'), may hold values from -1 to 1
- block_links: int32 [16, 9], P('ctx'), may hold values from -1 to 15, as said below
- d_out: bfloat16 [2048, 1024], P('ctx', 'head'), may hold values from -6 to 6
Outputs:
- attended: bfloat16 [2048, 1024], P('ctx', 'head')
- grad_features: bfloat16 [2048, 1024], P('ctx', 'head')
Inputs may be any that keep to these rules, and one draw needn't show every extreme that they name: `block_links`: row q lists in order the key blocks q - 1 to q + 1; then p - 1 to p + 1, p being the block on the previous coil turn; then n - 1 to n + 1, n being the block on the next coil turn. q - p and n - q lie between 3 and 5, and a distance of 5 occurs in both directions in every draw. A coil neighbour may be absent; the entries of an absent neighbour and entries outside the sequence are -1. Live entries of a row are distinct.
All inputs are finite; a program needn't handle non-finite values.
Results may differ from a plain program's by a relative error of at most 0.025.
Values may be sent and summed in bfloat16 or wider, within the bound.
No kernel may reach another device: no remote copies, remote signals or barrier semaphores. Data moves between devices by JAX's collectives and lax.ppermute only.
A program may use at most 64 MiB of HBM per device.

v0:
```python
import jax
import jax.numpy as jnp
from jax import lax
from jax.sharding import PartitionSpec as P

HD = 128
BLK = 128
OMAX = 3


def shifted(value, axis, steps):
    count = lax.axis_size(axis)
    first, last = (max(0, -steps), min(count, count - steps))
    return lax.ppermute(value, axis, [(source, source + steps) for source in range(first, last)])


def rounded_terms(values):
    return lax.optimization_barrier(values.astype(jnp.bfloat16)).astype(jnp.float32)


def body(features, w_qkv, block_links, d_out):
    tok_rows = d_out.shape[0]
    local_width = w_qkv.shape[2]
    model_width = w_qkv.shape[0]
    resident_tiles = tok_rows // BLK
    heads_here = local_width // HD
    score_scale = HD ** (-0.5)
    w_flat = w_qkv.reshape(model_width, 3 * local_width)
    projected = jnp.dot(
        lax.all_gather(features, "head", axis=1, tiled=True),
        w_flat,
        preferred_element_type=jnp.float32,
    )
    projected = projected.astype(jnp.bfloat16)
    query_blocks = projected[:, :local_width].reshape(resident_tiles, BLK, heads_here, HD)
    pair_blocks = projected[:, local_width:].reshape(resident_tiles, BLK, 2 * local_width)
    lower_shards = []
    upper_shards = []
    for offset in range(1, OMAX + 1):
        for direction in (1, -1):
            arrived = shifted(pair_blocks, "ctx", direction * offset)
            if direction > 0:
                lower_shards.append(arrived)
            else:
                upper_shards.append(arrived)
    window_pairs = jnp.concatenate(
        list(reversed(lower_shards)) + [pair_blocks] + upper_shards, axis=0
    )
    extent = window_pairs.shape[0]
    own_start = OMAX * resident_tiles
    anchor = lax.axis_index("ctx") * resident_tiles - own_start
    live_slot = block_links >= 0
    slot_index = jnp.where(live_slot, block_links - anchor, own_start)
    drop_index = jnp.where(live_slot, block_links - anchor, extent)
    slots = block_links.shape[1]
    selected = window_pairs[slot_index].reshape(resident_tiles, slots * BLK, 2, heads_here, HD)
    lookup_rows = selected[:, :, 0]
    content_rows = selected[:, :, 1]
    key_mask = jnp.repeat(live_slot, BLK, axis=1)[:, None, None, :]
    grad_blocks = d_out.reshape(resident_tiles, BLK, heads_here, HD)
    scores = (
        jnp.einsum("iqhd,ikhd->ihqk", query_blocks, lookup_rows, preferred_element_type=jnp.float32)
        * score_scale
    )
    largest = jnp.max(jnp.where(key_mask, scores, -1e30), axis=-1, keepdims=True)
    exp_total = jnp.sum(jnp.where(key_mask, jnp.exp(scores - largest), 0.0), axis=-1, keepdims=True)
    normalized = jnp.where(key_mask, jnp.exp(scores - largest), 0.0) / exp_total
    softmax_share = normalized.astype(jnp.bfloat16)
    attended = jnp.einsum(
        "ihqk,ikhd->iqhd", softmax_share, content_rows, preferred_element_type=jnp.float32
    ).astype(jnp.bfloat16)
    row_dot = jnp.sum(grad_blocks.astype(jnp.float32) * attended.astype(jnp.float32), axis=-1)
    value_terms = jnp.einsum(
        "ihqk,iqhd->ikhd", softmax_share, grad_blocks, preferred_element_type=jnp.float32
    )
    probability_gradient = jnp.einsum(
        "iqhd,ikhd->ihqk", grad_blocks, content_rows, preferred_element_type=jnp.float32
    )
    recomputed = jnp.where(key_mask, jnp.exp(scores - largest), 0.0) / exp_total
    score_derivative = (
        recomputed * (probability_gradient - jnp.transpose(row_dot, (0, 2, 1))[:, :, :, None])
    ).astype(jnp.bfloat16)
    query_grad = (
        jnp.einsum(
            "ihqk,ikhd->iqhd", score_derivative, lookup_rows, preferred_element_type=jnp.float32
        )
        * score_scale
    )
    key_terms = (
        jnp.einsum(
            "ihqk,iqhd->ikhd", score_derivative, query_blocks, preferred_element_type=jnp.float32
        )
        * score_scale
    )
    flat_index = drop_index.reshape(-1)
    slot_owner = (flat_index[None, :] == jnp.arange(extent, dtype=jnp.int32)[:, None]).astype(
        jnp.float32
    )
    slot_terms = jnp.concatenate(
        [
            key_terms.reshape(resident_tiles * slots, BLK, local_width),
            value_terms.reshape(resident_tiles * slots, BLK, local_width),
        ],
        axis=2,
    )
    pair_grads = jnp.einsum(
        "es,sbc->ebc",
        slot_owner,
        slot_terms,
        precision=lax.Precision.HIGHEST,
        preferred_element_type=jnp.float32,
    )
    grad_total = rounded_terms(pair_grads[own_start : own_start + resident_tiles])
    for offset in range(1, OMAX + 1):
        for direction in (1, -1):
            domain_first_index = own_start + direction * offset * resident_tiles
            region = pair_grads[domain_first_index : domain_first_index + resident_tiles]
            arrived = shifted(region.astype(jnp.bfloat16), "ctx", direction * offset).astype(
                jnp.float32
            )
            grad_total = grad_total + arrived
    attended_all = attended.reshape(tok_rows, local_width)
    query_all = query_grad.reshape(tok_rows, local_width)
    grad_projected = jnp.concatenate(
        [query_all, grad_total.reshape(tok_rows, 2 * local_width)], axis=1
    ).astype(jnp.bfloat16)
    partial_sum = jnp.einsum(
        "tc,dc->td", grad_projected, w_flat, preferred_element_type=jnp.float32
    )
    grad_features = lax.psum_scatter(
        partial_sum.astype(jnp.bfloat16), "head", scatter_dimension=1, tiled=True
    )
    return (attended_all, grad_features)


def solution(mesh):
    return jax.shard_map(
        body,
        mesh=mesh,
        in_specs=(P("ctx", "head"), P(None, None, "head"), P("ctx", None), P("ctx", "head")),
        out_specs=(P("ctx", "head"), P("ctx", "head")),
        check_vma=False,
    )
```

profile of v0, /device:TPU:0, one launch (start us, length us, event | category | flops | bytes accessed | tf_op | source)
XLA Modules:
  0.0 171.9 jit_solution(625701603773314304)
XLA Ops:
  7.2 8.8 %all_gather.3 = bf16[256,1024]{1,0:T(8,128)(2,1)S(1)} all-gather(bf16[256,256]{1,0:T(8,128)(2,1)} %param.4), channel_id=1, replica_groups=mesh['ctx'=8,'head'=4] {'head'}, dimensions={1}, use_global_device_ids=true | all-gather | bytes 655360 | tf_op jit(solution)/shard_map/all_gather | solution.py:30
  16.0 1.7 copy.33
  18.4 1.3 collective-permute-start.5
  19.7 1.3 collective-permute-start.4
  21.0 3.4 %collective-permute-start.2 = (bf16[2,128,512]{2,1,0:T(8,128)(2,1)S(1)}, bf16[2,128,512]{2,1,0:T(8,128)(2,1)S(1)}, u32[]{:S(2)}, u32[]{:S(2)}) collective-permute-start(bf16[2,128,512]{2,1,0:T(8,128)(2,1)S(1)} %bitcast.64), channel_id=1, source_target_pairs={{0,4},{4,8},{8,12},{12,16},{16,20},{20,24},{24,28},{1,5},{5,9},{9,... | collective-permute-start | bytes 786440 | tf_op jit(solution)/shard_map/ppermute | solution.py:14
  24.5 5.8 %collective-permute-start.1 = (bf16[2,128,512]{2,1,0:T(8,128)(2,1)S(1)}, bf16[2,128,512]{2,1,0:T(8,128)(2,1)}, u32[]{:S(2)}, u32[]{:S(2)}) collective-permute-start(bf16[2,128,512]{2,1,0:T(8,128)(2,1)S(1)} %bitcast.65), channel_id=1, source_target_pairs={{0,8},{4,12},{8,16},{12,20},{16,24},{20,28},{1,9},{5,13},{9,17},{1... | collective-permute-start | bytes 786440 | tf_op jit(solution)/shard_map/ppermute | solution.py:14
  30.3 5.8 %collective-permute-start = (bf16[2,128,512]{2,1,0:T(8,128)(2,1)S(1)}, bf16[2,128,512]{2,1,0:T(8,128)(2,1)}, u32[]{:S(2)}, u32[]{:S(2)}) collective-permute-start(bf16[2,128,512]{2,1,0:T(8,128)(2,1)S(1)} %bitcast.66), channel_id=1, source_target_pairs={{0,12},{4,16},{8,20},{12,24},{16,28},{1,13},{5,17},{9,21},{13,25},... | collective-permute-start | bytes 786440 | tf_op jit(solution)/shard_map/ppermute | solution.py:14
  36.8 4.0 %collective-permute-done = bf16[2,128,512]{2,1,0:T(8,128)(2,1)} collective-permute-done((bf16[2,128,512]{2,1,0:T(8,128)(2,1)S(1)}, bf16[2,128,512]{2,1,0:T(8,128)(2,1)}, u32[]{:S(2)}, u32[]{:S(2)}) %collective-permute-start) | collective-permute-done | bytes 262176 | tf_op jit(solution)/shard_map/ppermute | solution.py:14
  42.1 1.7 constant_dynamic-update-slice_fusion.6
  43.7 1.7 constant_dynamic-update-slice_fusion.5
  46.8 7.0 %collective-permute-done.3 = bf16[2,128,512]{2,1,0:T(8,128)(2,1)S(1)} collective-permute-done((bf16[2,128,512]{2,1,0:T(8,128)(2,1)S(1)}, bf16[2,128,512]{2,1,0:T(8,128)(2,1)S(1)}, u32[]{:S(2)}, u32[]{:S(2)}) %collective-permute-start.3) | collective-permute-done | bytes 262176 | tf_op jit(solution)/shard_map/ppermute | solution.py:14
  56.0 2.2 %gather_fusion = bf16[18,128,512]{2,1,0:T(8,128)(2,1)S(1)} fusion(bf16[14,128,512]{2,1,0:T(8,128)(2,1)} %constant_dynamic-update-slice_fusion, s32[1024]{0:T(1024)S(1)} %pad_clamp_fusion), kind=kCustom, calls=%fused_computation | custom fusion | bytes 4718664 | tf_op jit(solution)/shard_map/gather | solution.py:56
  58.2 2.3 %reshape.43 = bf16[2,1152,2,2,128]{4,3,2,1,0:T(2,128)(2,1)} reshape(bf16[18,128,512]{2,1,0:T(8,128)(2,1)S(1)} %gather_fusion) | data formatting | bytes 4718592 | tf_op jit(solution)/shard_map/reshape | solution.py:56
  60.6 2.9 %fusion.42 = (bf16[2,1152,1,2,128]{4,3,2,1,0:T(2,128)(2,1)S(1)}, bf16[2,1152,1,2,128]{4,3,2,1,0:T(2,128)(2,1)S(1)}) fusion(bf16[2,1152,2,2,128]{4,3,2,1,0:T(2,128)(2,1)} %reshape.43), kind=kLoop, calls=%fused_computation.61 | loop fusion | bytes 4718592 | tf_op jit(solution)/shard_map/slice | solution.py:57
  63.5 2.8 %copy.56 = bf16[2,1152,1,2,128]{1,4,3,0,2:T(8,128)(2,1)} copy(bf16[2,1152,1,2,128]{4,3,2,1,0:T(2,128)(2,1)S(1)} %get-tuple-element.3) | data formatting | bytes 2359296
  70.3 1.6 fusion.16
  71.9 8.9 %copy.48 = f32[2,1152,2,128]{3,2,1,0:T(2,128)S(1)} copy(f32[2,1152,2,128]{3,1,2,0:T(8,128)S(1)} %convolution_bitcast_fusion) | data formatting | bytes 4718592 | tf_op jit(solution)/shard_map/ihqk,iqhd->ikhd/transpose | solution.py:73
  80.8 2.9 %reshape.49 = f32[18,128,256]{2,1,0:T(8,128)} reshape(f32[2,1152,2,128]{3,2,1,0:T(2,128)S(1)} %copy.48) | data formatting | bytes 4718592 | tf_op jit(solution)/shard_map/reshape | solution.py:102
  83.7 3.2 %copy.50 = f32[18,128,256]{2,0,1:T(8,128)S(1)} copy(f32[18,128,256]{2,1,0:T(8,128)} %reshape.49) | data formatting | bytes 4718592 | tf_op jit(solution)/shard_map/reshape | solution.py:102
  86.9 1.9 %fusion.13 = f32[2,1152,2,128]{1,3,2,0:T(8,128)} fusion(bf16[2,128,2,128]{1,3,2,0:T(8,128)(2,1)S(1)} %copy.44, bf16[2,2,128,1152]{3,2,1,0:T(8,128)(2,1)S(1)} %copy-done.4), kind=kOutput, calls=%fused_computation.15 | convolution fusion | flops 151584768 | bytes 3670016 | tf_op jit(solution)/shard_map/ihqk,iqhd->ikhd/dot_general | solution.py:90
  88.8 5.0 %copy.45 = f32[2,1152,2,128]{3,2,1,0:T(2,128)} copy(f32[2,1152,2,128]{1,3,2,0:T(8,128)} %fusion.13) | data formatting | bytes 4718592 | tf_op jit(solution)/shard_map/mul | solution.py:90
  93.8 4.1 %reshape.48 = f32[18,128,256]{2,1,0:T(8,128)} reshape(f32[2,1152,2,128]{3,2,1,0:T(2,128)} %copy.45) | data formatting | bytes 4718592 | tf_op jit(solution)/shard_map/reshape | solution.py:101
  97.9 3.1 %copy.49 = f32[18,128,256]{2,0,1:T(8,128)S(1)} copy(f32[18,128,256]{2,1,0:T(8,128)} %reshape.48) | data formatting | bytes 4718592 | tf_op jit(solution)/shard_map/reshape | solution.py:101
  101.0 3.7 %fusion.1 = bf16[14,128,512]{2,0,1:T(8,128)(2,1)S(1)} fusion(f32[18,128,256]{2,0,1:T(8,128)S(1)} %copy.50, f32[18,128,256]{2,0,1:T(8,128)S(1)} %copy.49, s32[18]{0:T(128)S(1)} %eq.15), kind=kOutput, calls=%fused_computation.2 | convolution fusion | flops 199360768 | bytes 6553672 | tf_op jit(solution)/shard_map/es,sbc->ebc/dot_general | solution.py:106
  106.0 1.4 collective-permute-start.11
  107.4 12.5 %collective-permute-start.10 = (bf16[2,128,512]{2,1,0:T(8,128)(2,1)S(1)}, bf16[2,128,512]{2,1,0:T(8,128)(2,1)}, u32[]{:S(2)}, u32[]{:S(2)}) collective-permute-start(bf16[2,128,512]{2,1,0:T(8,128)(2,1)S(1)} %get-tuple-element.6), channel_id=1, source_target_pairs={{0,12},{4,16},{8,20},{12,24},{16,28},{1,13},{5,17},{9,21},{13,25},... | collective-permute-start | bytes 786440 | tf_op jit(solution)/shard_map/ppermute | solution.py:14
  121.1 5.3 %collective-permute-start.8 = (bf16[2,128,512]{2,1,0:T(8,128)(2,1)S(1)}, bf16[2,128,512]{2,1,0:T(8,128)(2,1)}, u32[]{:S(2)}, u32[]{:S(2)}) collective-permute-start(bf16[2,128,512]{2,1,0:T(8,128)(2,1)S(1)} %get-tuple-element.8), channel_id=1, source_target_pairs={{0,8},{4,12},{8,16},{12,20},{16,24},{20,28},{1,9},{5,13},{9,17},{1... | collective-permute-start | bytes 786440 | tf_op jit(solution)/shard_map/ppermute | solution.py:14
  127.7 5.3 %collective-permute-start.6 = (bf16[2,128,512]{2,1,0:T(8,128)(2,1)S(1)}, bf16[2,128,512]{2,1,0:T(8,128)(2,1)}, u32[]{:S(2)}, u32[]{:S(2)}) collective-permute-start(bf16[2,128,512]{2,1,0:T(8,128)(2,1)S(1)} %get-tuple-element.10), channel_id=1, source_target_pairs={{0,4},{4,8},{8,12},{12,16},{16,20},{20,24},{24,28},{1,5},{5,9},{9,... | collective-permute-start | bytes 786440 | tf_op jit(solution)/shard_map/ppermute | solution.py:14
  135.4 4.2 %collective-permute-done.6 = bf16[2,128,512]{2,1,0:T(8,128)(2,1)} collective-permute-done((bf16[2,128,512]{2,1,0:T(8,128)(2,1)S(1)}, bf16[2,128,512]{2,1,0:T(8,128)(2,1)}, u32[]{:S(2)}, u32[]{:S(2)}) %collective-permute-start.6) | collective-permute-done | bytes 262176 | tf_op jit(solution)/shard_map/ppermute | solution.py:14
  139.7 1.5 add_convert_fusion
  141.2 1.4 convolution_convert_fusion
  143.4 21.6 %reduce-scatter.2.cloned.1.call-done = bf16[256,256]{1,0:T(8,128)(2,1)} async-done(((bf16[256,1024]{1,0:T(8,128)(2,1)}), bf16[256,256]{1,0:T(8,128)(2,1)}) %reduce-scatter.2.cloned.1.call-update) | async-done | bytes 131088 | tf_op jit(solution)/shard_map/reduce_scatter | solution.py:130
  (64 shorter events, 17.1 us)
Async XLA Ops:
  7.2 157.9 %reduce-scatter.2.cloned.1.call-start = ((), (), s32[]{:S(2)}) async-start(), calls=%async_computation.1 | async-start | bytes 655360 | tf_op jit(solution)/shard_map/reduce_scatter | solution.py:130
  17.8 18.7 %copy-start.2 = (bf16[1024,3,256]{0,2,1:T(8,128)(2,1)}, bf16[1024,3,256]{0,2,1:T(8,128)(2,1)S(1)}, u32[]{:S(2)}) copy-start(bf16[1024,3,256]{0,2,1:T(8,128)(2,1)S(1)} %copy.33) | copy-start | bytes 4718596
  17.8 18.3 %copy-start.9 = (s32[2,9]{1,0:T(2,128)S(1)}, s32[2,9]{1,0:T(2,128)}, u32[]{:S(2)}) copy-start(s32[2,9]{1,0:T(2,128)} %param.6) | copy-start | bytes 220
  17.8 18.6 %copy-start.7 = (bf16[256,256]{1,0:T(8,128)(2,1)S(1)}, bf16[256,256]{1,0:T(8,128)(2,1)}, u32[]{:S(2)}) copy-start(bf16[256,256]{1,0:T(8,128)(2,1)} %param.7) | copy-start | bytes 393220
  18.4 36.9 %collective-permute-start.5 = (bf16[2,128,512]{2,1,0:T(8,128)(2,1)S(1)}, bf16[2,128,512]{2,1,0:T(8,128)(2,1)S(1)}, u32[]{:S(2)}, u32[]{:S(2)}) collective-permute-start(bf16[2,128,512]{2,1,0:T(8,128)(2,1)S(1)} %bitcast.62), channel_id=1, source_target_pairs={{12,0},{16,4},{20,8},{24,12},{28,16},{13,1},{17,5},{21,9},{25,13},... | collective-permute-start | bytes 786440 | tf_op jit(solution)/shard_map/ppermute | solution.py:14
  19.7 34.9 %collective-permute-start.4 = (bf16[2,128,512]{2,1,0:T(8,128)(2,1)S(1)}, bf16[2,128,512]{2,1,0:T(8,128)(2,1)S(1)}, u32[]{:S(2)}, u32[]{:S(2)}) collective-permute-start(bf16[2,128,512]{2,1,0:T(8,128)(2,1)S(1)} %bitcast.63), channel_id=1, source_target_pairs={{8,0},{12,4},{16,8},{20,12},{24,16},{28,20},{9,1},{13,5},{17,9},{2... | collective-permute-start | bytes 786440 | tf_op jit(solution)/shard_map/ppermute | solution.py:14
  21.0 24.4 %collective-permute-start.2 = (bf16[2,128,512]{2,1,0:T(8,128)(2,1)S(1)}, bf16[2,128,512]{2,1,0:T(8,128)(2,1)S(1)}, u32[]{:S(2)}, u32[]{:S(2)}) collective-permute-start(bf16[2,128,512]{2,1,0:T(8,128)(2,1)S(1)} %bitcast.64), channel_id=1, source_target_pairs={{0,4},{4,8},{8,12},{12,16},{16,20},{20,24},{24,28},{1,5},{5,9},{9,... | collective-permute-start | bytes 786440 | tf_op jit(solution)/shard_map/ppermute | solution.py:14
  24.5 19.2 %collective-permute-start.1 = (bf16[2,128,512]{2,1,0:T(8,128)(2,1)S(1)}, bf16[2,128,512]{2,1,0:T(8,128)(2,1)}, u32[]{:S(2)}, u32[]{:S(2)}) collective-permute-start(bf16[2,128,512]{2,1,0:T(8,128)(2,1)S(1)} %bitcast.65), channel_id=1, source_target_pairs={{0,8},{4,12},{8,16},{12,20},{16,24},{20,28},{1,9},{5,13},{9,17},{1... | collective-permute-start | bytes 786440 | tf_op jit(solution)/shard_map/ppermute | solution.py:14
  30.3 10.4 %collective-permute-start = (bf16[2,128,512]{2,1,0:T(8,128)(2,1)S(1)}, bf16[2,128,512]{2,1,0:T(8,128)(2,1)}, u32[]{:S(2)}, u32[]{:S(2)}) collective-permute-start(bf16[2,128,512]{2,1,0:T(8,128)(2,1)S(1)} %bitcast.66), channel_id=1, source_target_pairs={{0,12},{4,16},{8,20},{12,24},{16,28},{1,13},{5,17},{9,21},{13,25},... | collective-permute-start | bytes 786440 | tf_op jit(solution)/shard_map/ppermute | solution.py:14
  40.8 13.1 %collective-permute-start.3 = (bf16[2,128,512]{2,1,0:T(8,128)(2,1)S(1)}, bf16[2,128,512]{2,1,0:T(8,128)(2,1)S(1)}, u32[]{:S(2)}, u32[]{:S(2)}) collective-permute-start(bf16[2,128,512]{2,1,0:T(8,128)(2,1)S(1)} %bitcast.67), channel_id=1, source_target_pairs={{4,0},{8,4},{12,8},{16,12},{20,16},{24,20},{28,24},{5,1},{9,5},{13... | collective-permute-start | bytes 786440 | tf_op jit(solution)/shard_map/ppermute | solution.py:14
  63.5 3.4 %copy-start = (bf16[2,1152,1,2,128]{4,3,2,1,0:T(2,128)(2,1)}, bf16[2,1152,1,2,128]{4,3,2,1,0:T(2,128)(2,1)S(1)}, u32[]{:S(2)}) copy-start(bf16[2,1152,1,2,128]{4,3,2,1,0:T(2,128)(2,1)S(1)} %get-tuple-element.2) | copy-start | bytes 3538948
  67.7 1.3 copy-start.6
  83.7 3.2 %copy-start.4 = (bf16[2,2,128,1152]{3,2,1,0:T(8,128)(2,1)S(1)}, bf16[2,2,128,1152]{3,2,1,0:T(8,128)(2,1)}, u32[]{:S(2)}) copy-start(bf16[2,2,128,1152]{3,2,1,0:T(8,128)(2,1)} %fusion.16) | copy-start | bytes 3538948
  105.8 27.2 %copy-start.1 = (bf16[2,1152,1,2,128]{4,3,2,1,0:T(2,128)(2,1)S(1)}, bf16[2,1152,1,2,128]{4,3,2,1,0:T(2,128)(2,1)}, u32[]{:S(2)}) copy-start(bf16[2,1152,1,2,128]{4,3,2,1,0:T(2,128)(2,1)} %copy-done) | copy-start | bytes 3538948
  105.8 27.2 %copy-start.5 = (bf16[2,2,128,1152]{3,2,1,0:T(8,128)(2,1)S(1)}, bf16[2,2,128,1152]{3,2,1,0:T(8,128)(2,1)}, u32[]{:S(2)}) copy-start(bf16[2,2,128,1152]{3,2,1,0:T(8,128)(2,1)} %fusion.16) | copy-start | bytes 3538948
  106.0 21.7 %collective-permute-start.11 = (bf16[2,128,512]{2,1,0:T(8,128)(2,1)S(1)}, bf16[2,128,512]{2,1,0:T(8,128)(2,1)S(1)}, u32[]{:S(2)}, u32[]{:S(2)}) collective-permute-start(bf16[2,128,512]{2,1,0:T(8,128)(2,1)S(1)} %get-tuple-element.5), channel_id=1, source_target_pairs={{12,0},{16,4},{20,8},{24,12},{28,16},{13,1},{17,5},{21,9},{25,13},... | collective-permute-start | bytes 786440 | tf_op jit(solution)/shard_map/ppermute | solution.py:14
  107.4 28.0 %collective-permute-start.10 = (bf16[2,128,512]{2,1,0:T(8,128)(2,1)S(1)}, bf16[2,128,512]{2,1,0:T(8,128)(2,1)}, u32[]{:S(2)}, u32[]{:S(2)}) collective-permute-start(bf16[2,128,512]{2,1,0:T(8,128)(2,1)S(1)} %get-tuple-element.6), channel_id=1, source_target_pairs={{0,12},{4,16},{8,20},{12,24},{16,28},{1,13},{5,17},{9,21},{13,25},... | collective-permute-start | bytes 786440 | tf_op jit(solution)/shard_map/ppermute | solution.py:14
  119.9 15.6 %collective-permute-start.9 = (bf16[2,128,512]{2,1,0:T(8,128)(2,1)S(1)}, bf16[2,128,512]{2,1,0:T(8,128)(2,1)}, u32[]{:S(2)}, u32[]{:S(2)}) collective-permute-start(bf16[2,128,512]{2,1,0:T(8,128)(2,1)S(1)} %get-tuple-element.7), channel_id=1, source_target_pairs={{8,0},{12,4},{16,8},{20,12},{24,16},{28,20},{9,1},{13,5},{17,9},{2... | collective-permute-start | bytes 786440 | tf_op jit(solution)/shard_map/ppermute | solution.py:14
  121.1 14.3 %collective-permute-start.8 = (bf16[2,128,512]{2,1,0:T(8,128)(2,1)S(1)}, bf16[2,128,512]{2,1,0:T(8,128)(2,1)}, u32[]{:S(2)}, u32[]{:S(2)}) collective-permute-start(bf16[2,128,512]{2,1,0:T(8,128)(2,1)S(1)} %get-tuple-element.8), channel_id=1, source_target_pairs={{0,8},{4,12},{8,16},{12,20},{16,24},{20,28},{1,9},{5,13},{9,17},{1... | collective-permute-start | bytes 786440 | tf_op jit(solution)/shard_map/ppermute | solution.py:14
  126.4 9.0 %collective-permute-start.7 = (bf16[2,128,512]{2,1,0:T(8,128)(2,1)S(1)}, bf16[2,128,512]{2,1,0:T(8,128)(2,1)}, u32[]{:S(2)}, u32[]{:S(2)}) collective-permute-start(bf16[2,128,512]{2,1,0:T(8,128)(2,1)S(1)} %get-tuple-element.9), channel_id=1, source_target_pairs={{4,0},{8,4},{12,8},{16,12},{20,16},{24,20},{28,24},{5,1},{9,5},{13... | collective-permute-start | bytes 786440 | tf_op jit(solution)/shard_map/ppermute | solution.py:14
  127.7 12.0 %collective-permute-start.6 = (bf16[2,128,512]{2,1,0:T(8,128)(2,1)S(1)}, bf16[2,128,512]{2,1,0:T(8,128)(2,1)}, u32[]{:S(2)}, u32[]{:S(2)}) collective-permute-start(bf16[2,128,512]{2,1,0:T(8,128)(2,1)S(1)} %get-tuple-element.10), channel_id=1, source_target_pairs={{0,4},{4,8},{8,12},{12,16},{16,20},{20,24},{24,28},{1,5},{5,9},{9,... | collective-permute-start | bytes 786440 | tf_op jit(solution)/shard_map/ppermute | solution.py:14
  134.2 7.0 %copy-start.3 = (bf16[1024,3,256]{0,2,1:T(8,128)(2,1)S(1)}, bf16[1024,3,256]{0,2,1:T(8,128)(2,1)}, u32[]{:S(2)}) copy-start(bf16[1024,3,256]{0,2,1:T(8,128)(2,1)} %copy-done.2) | copy-start | bytes 4718596
  141.2 1.4 copy-start.8
Sparse Core Ops, SparseCore 0:
  142.7 22.2 reduce-scatter.1
where the time goes:
time: 173 us; the launch traced here: 172 us
  local copies, waits for them, and re-layouts  50.5 us (29%)
  starting transfers between devices  45.9 us (27%)
  waiting for transfers between devices  36.9 us (21%)
  between operations  14.4 us (8%)
  matrix products  13 us (8%)
  blocking collectives  8.83 us (5%)
  other arithmetic  2.32 us (1%)
    ppermute x12, starting transfers between devices, shifted(): lax.ppermute(value, axis, [(source, source + steps) for source in range(f...  45.9 us
    reduce_scatter x1, waiting for transfers between devices, body(): lax.psum_scatter(partial_sum.astype(jnp.bfloat16), 'head', scatter_dimens...  21.6 us
    ppermute x12, waiting for transfers between devices, shifted(): lax.ppermute(value, axis, [(source, source + steps) for source in range(f...  15.3 us
    unnamed x32, local copies, waits for them, and re-layouts  12.1 us
    transpose x1, local copies, waits for them, and re-layouts, body(): jnp.einsum('ihqk,iqhd->ikhd', softmax_share, grad_blocks, preferred_eleme...  8.88 us
    all_gather x1, blocking collectives, body(): lax.all_gather(features, 'head', axis=1, tiled=True)  8.83 us
    reshape x2, local copies, waits for them, and re-layouts, body(): key_terms.reshape(resident_tiles * slots, BLK, local_width)  7.22 us
    reshape x2, local copies, waits for them, and re-layouts, body(): value_terms.reshape(resident_tiles * slots, BLK, local_width)  6.11 us
  transfers between devices with their start and end apart: 13, of which 4 were waited for; matrix products, arithmetic and copies ran while one was open for 6% of the time, Pallas kernels for 0%

commit v1 on v0

v1 whole, which is shorter than its diff:
```python
import functools

import jax
import jax.numpy as jnp
from jax import lax
from jax.experimental import pallas as pl
from jax.experimental.pallas import tpu as pltpu
from jax.sharding import PartitionSpec as P

HD = 128
BLK = 128
REACH = 6
SPAN = 3
LOG2E = 1.4426950408889634
DEAD = -1e30
BF = jnp.bfloat16
F32 = jnp.float32

GROUP = 4
ROWS = GROUP * BLK
HALF = ROWS // 2
WINDOW = GROUP + 2 * REACH
NEAR_LEFT = (REACH - GROUP) * BLK
OWN = REACH * BLK
NEAR_RIGHT = OWN + ROWS
FAR_RIGHT = NEAR_RIGHT + ROWS


def params(flops, moved):
    return dict(
        compiler_params=pltpu.CompilerParams(vmem_limit_bytes=48 * 1024 * 1024),
        cost_estimate=pl.CostEstimate(flops=flops, bytes_accessed=moved, transcendentals=0),
    )


VMEM = pl.BlockSpec(memory_space=pltpu.VMEM)
SMEM = pl.BlockSpec(memory_space=pltpu.SMEM)


def dot(a, b, dims):
    return lax.dot_general(a, b, (dims, ((), ())), preferred_element_type=F32)


def project_kernel(place, f, sx, sy, sd, other, w, q_out, kv_out):
    side, head = place[0], place[3]
    width = f.shape[1]
    for group, near, far in ((0, f, sx), (1, sy, sd)):
        total = None
        pieces = (
            (head, near[...]),
            (head ^ 2, far[...]),
            (head ^ 1, other[2 * group * HALF : (2 * group + 1) * HALF]),
            (head ^ 3, other[(2 * group + 1) * HALF : (2 * group + 2) * HALF]),
        )
        for source, piece in pieces:
            term = dot(piece, w[pl.ds(pl.multiple_of(source * width, width), width), :], ((1,), (0,)))
            total = term if total is None else total + term
        rows = pl.ds(pl.multiple_of((side ^ group) * HALF, HALF), HALF)
        q_out[rows, :] = total[:, :HD].astype(BF)
        kv_out[rows, :] = total[:, HD:].astype(BF)


def attend_kernel(
    place, links, q, kv, near_a, near_b, far_a, far_b, d_own, d_other,
    att_own, att_other, dq_out, own_out, a_out, b_out, far_a_out, far_b_out,
    win, acc, att,
):
    side, odd, first = place[0], place[1], place[2]
    scale = HD ** -0.5
    even = 1 - odd
    at_a = pl.multiple_of(even * NEAR_RIGHT + odd * NEAR_LEFT, BLK)
    at_b = pl.multiple_of(odd * NEAR_RIGHT + even * NEAR_LEFT, BLK)
    at_far_a = pl.multiple_of(even * FAR_RIGHT, BLK)
    at_far_b = pl.multiple_of(odd * FAR_RIGHT, BLK)
    win[OWN : OWN + ROWS, :] = kv[...]
    win[pl.ds(at_a, ROWS), :] = near_a[...]
    win[pl.ds(at_b, ROWS), :] = near_b[...]
    win[pl.ds(at_far_a, HALF), :] = far_a[...]
    win[pl.ds(at_far_b, HALF), :] = far_b[...]
    acc[...] = jnp.zeros_like(acc)
    zeros = jnp.zeros((BLK, HD), BF)
    own_cols = pl.ds(pl.multiple_of(side * HD, HD), HD)
    for i in range(GROUP):
        rows = slice(i * BLK, (i + 1) * BLK)
        here = slice((i % 2) * BLK, (i % 2 + 1) * BLK)
        d_blk = jnp.where(side == i // 2, d_own[here, own_cols], d_other[here, :])
        pair = jnp.concatenate(
            [
                jnp.concatenate([q[rows, :], zeros], axis=1),
                jnp.concatenate([zeros, d_blk], axis=1),
            ],
            axis=0,
        )
        starts, both, scores = [], [], []
        for t in range(3):
            if t == 0:
                start = (REACH + i - 1) * BLK
            else:
                base = jnp.int32(-(1 << 20))
                for j in range(SPAN):
                    entry = links[i, SPAN * t + j]
                    base = jnp.maximum(base, jnp.where(entry >= 0, entry - j, -(1 << 20)))
                base = jnp.where(base > -(1 << 19), base - first + REACH, REACH + i)
                base = jnp.clip(base, 0, WINDOW - SPAN)
                start = pl.multiple_of(base * BLK, BLK)
            starts.append(start)
            product = dot(win[pl.ds(start, SPAN * BLK), :], pair, ((1,), (1,)))
            both.append(product[:, BLK:])
            for j in range(SPAN):
                bias = jnp.where(links[i, SPAN * t + j] >= 0, 0.0, DEAD).astype(F32)
                scores.append(product[j * BLK : (j + 1) * BLK, :BLK] + bias)
        scores = jnp.concatenate(scores, axis=0)
        largest = jnp.max(scores, axis=0, keepdims=True)
        terms = jnp.exp2((scores - largest) * (scale * LOG2E))
        share = terms * (1.0 / jnp.sum(terms, axis=0, keepdims=True))
        prob_grad = jnp.concatenate(both, axis=0)
        row_dot = jnp.sum(share * prob_grad, axis=0, keepdims=True)
        score_grad = share * (prob_grad - row_dot)
        mixed = jnp.concatenate([score_grad.astype(BF), share.astype(BF)], axis=1)
        out = None
        for t in range(3):
            part = mixed[t * SPAN * BLK : (t + 1) * SPAN * BLK, :]
            keys = win[pl.ds(starts[t], SPAN * BLK), :]
            term = dot(part, keys, ((0,), (0,)))
            out = term if out is None else out + term
            acc[pl.ds(starts[t], SPAN * BLK), :] += dot(part, pair, ((1,), (0,)))
        att[rows, :] = out[BLK:, HD:].astype(BF)
        dq_out[rows, :] = (out[:BLK, :HD] * scale).astype(BF)
    att_own[...] = att[pl.ds(pl.multiple_of(side * HALF, HALF), HALF), :]
    att_other[...] = att[pl.ds(pl.multiple_of((1 - side) * HALF, HALF), HALF), :]
    factor = jnp.where(lax.broadcasted_iota(jnp.int32, (1, 2 * HD), 1) < HD, scale, 1.0).astype(F32)
    own_out[...] = acc[OWN : OWN + ROWS, :] * factor
    a_out[...] = (acc[pl.ds(at_a, ROWS), :] * factor).astype(BF)
    b_out[...] = (acc[pl.ds(at_b, ROWS), :] * factor).astype(BF)
    far_a_out[...] = (acc[pl.ds(at_far_a, HALF), :] * factor).astype(BF)
    far_b_out[...] = (acc[pl.ds(at_far_b, HALF), :] * factor).astype(BF)


def spread_kernel(place, own, from_a, from_b, dq, w, keep, send):
    side, head = place[0], place[3]
    width = 2 * HD
    dkv = (own[...] + from_a[...].astype(F32) + from_b[...].astype(F32)).astype(BF)
    grads = jnp.concatenate([dq[...], dkv], axis=1)
    for step in range(4):
        dest = head ^ step
        out = dot(grads, w[pl.ds(pl.multiple_of(dest * width, width), width), :], ((1,), (1,))).astype(BF)
        target = keep if step % 2 == 0 else send
        for group in range(2):
            index = 2 * group + step // 2
            part = jnp.where(side == group, out[:HALF], out[HALF:])
            target[index * HALF : (index + 1) * HALF, :] = part


def body(features, w_qkv, block_links, d_out, n_ctx, n_head):
    ctx, head = lax.axis_index("ctx"), lax.axis_index("head")
    side = ctx % 2
    group = ctx // 2
    odd = group % 2
    n_group = n_ctx // 2
    place = jnp.stack([side, odd, group * GROUP, head]).astype(jnp.int32)

    def across(value, flip_ctx, flip_head):
        pairs = [
            (c * n_head + h, (c ^ flip_ctx) * n_head + (h ^ flip_head))
            for c in range(n_ctx)
            for h in range(n_head)
        ]
        return lax.ppermute(value, ("ctx", "head"), pairs)

    def group_swap(value, offset):
        pairs = []
        for low in range(offset, n_group - 1, 2):
            for s in range(2):
                pairs.append((2 * low + s, 2 * low + 2 + s))
                pairs.append((2 * low + 2 + s, 2 * low + s))
        return lax.ppermute(value, "ctx", pairs)

    f = features
    sx = across(f, 0, 2)
    sy = across(f, 1, 0)
    sd = across(f, 1, 2)
    w_sel = lax.dynamic_slice_in_dim(w_qkv, side * HD, HD, axis=2).reshape(w_qkv.shape[0], 3 * HD)
    other = across(jnp.concatenate([f, sx, sy, sd], axis=0), 0, 1)

    q, kv = pl.pallas_call(
        project_kernel,
        name="project",
        out_shape=[
            jax.ShapeDtypeStruct((ROWS, HD), BF),
            jax.ShapeDtypeStruct((ROWS, 2 * HD), BF),
        ],
        in_specs=[SMEM] + [VMEM] * 6,
        out_specs=[VMEM] * 2,
        **params(2 * ROWS * 1024 * 3 * HD, 4 << 20),
    )(place, f, sx, sy, sd, other, w_sel)

    near_a = group_swap(kv, 0)
    near_b = group_swap(kv, 1)
    far_b = group_swap(lax.dynamic_slice_in_dim(near_a, odd * HALF, HALF, axis=0), 1)
    far_a = group_swap(lax.dynamic_slice_in_dim(near_b, (1 - odd) * HALF, HALF, axis=0), 0)

    link_rows = jnp.zeros((16, HD), BF).at[: block_links.shape[0], : block_links.shape[1]].set(
        block_links.astype(BF)
    )
    d_payload = jnp.concatenate(
        [lax.dynamic_slice_in_dim(d_out, (1 - side) * HD, HD, axis=1), link_rows], axis=0
    )
    d_other = across(d_payload, 1, 0)
    other_links = d_other[HALF : HALF + block_links.shape[0], : block_links.shape[1]].astype(jnp.int32)
    links = jnp.where(
        side == 0,
        jnp.concatenate([block_links, other_links], axis=0),
        jnp.concatenate([other_links, block_links], axis=0),
    )

    att_own, att_other, dq, own, near_a_grad, near_b_grad, far_a_grad, far_b_grad = pl.pallas_call(
        attend_kernel,
        name="attend",
        out_shape=[
            jax.ShapeDtypeStruct((HALF, HD), BF),
            jax.ShapeDtypeStruct((HALF, HD), BF),
            jax.ShapeDtypeStruct((ROWS, HD), BF),
            jax.ShapeDtypeStruct((ROWS, 2 * HD), F32),
            jax.ShapeDtypeStruct((ROWS, 2 * HD), BF),
            jax.ShapeDtypeStruct((ROWS, 2 * HD), BF),
            jax.ShapeDtypeStruct((HALF, 2 * HD), BF),
            jax.ShapeDtypeStruct((HALF, 2 * HD), BF),
        ],
        in_specs=[SMEM] * 2 + [VMEM] * 8,
        out_specs=[VMEM] * 8,
        scratch_shapes=[
            pltpu.VMEM((WINDOW * BLK, 2 * HD), BF),
            pltpu.VMEM((WINDOW * BLK, 2 * HD), F32),
            pltpu.VMEM((ROWS, HD), BF),
        ],
        **params(6 * 2 * GROUP * 9 * BLK * BLK * 2 * HD, 4 << 20),
    )(place, links, q, kv, near_a, near_b, far_a, far_b, d_out, d_other[:HALF])

    back_a = group_swap(far_a_grad, 0)
    back_b = group_swap(far_b_grad, 1)

    def add_half(whole, part, start):
        old = lax.dynamic_slice_in_dim(whole, start, HALF, axis=0)
        new = (old.astype(F32) + part.astype(F32)).astype(BF)
        return lax.dynamic_update_slice_in_dim(whole, new, start, axis=0)

    from_b = group_swap(add_half(near_b_grad, back_a, (1 - odd) * HALF), 1)
    from_a = group_swap(add_half(near_a_grad, back_b, odd * HALF), 0)
    att_back = across(att_other, 1, 0)
    attended = jnp.where(
        side == 0,
        jnp.concatenate([att_own, att_back], axis=1),
        jnp.concatenate([att_back, att_own], axis=1),
    )

    keep, send = pl.pallas_call(
        spread_kernel,
        name="spread",
        out_shape=[jax.ShapeDtypeStruct((4 * HALF, 2 * HD), BF)] * 2,
        in_specs=[SMEM] + [VMEM] * 5,
        out_specs=[VMEM] * 2,
        **params(2 * ROWS * 1024 * 3 * HD, 4 << 20),
    )(place, own, from_a, from_b, dq, w_sel)

    arrived = across(send, 0, 1)
    chip = (keep.astype(F32) + arrived.astype(F32)).astype(BF)
    gx = across(chip[HALF : 2 * HALF], 0, 2)
    gy = across(chip[2 * HALF : 3 * HALF], 1, 0)
    gd = across(chip[3 * HALF :], 1, 2)
    grad_features = (
        chip[:HALF].astype(F32) + gx.astype(F32) + gy.astype(F32) + gd.astype(F32)
    ).astype(BF)
    return attended, grad_features


def solution(mesh):
    sizes = dict(mesh.shape)
    return jax.shard_map(
        functools.partial(body, n_ctx=sizes["ctx"], n_head=sizes["head"]),
        mesh=mesh,
        in_specs=(P("ctx", "head"), P(None, None, "head"), P("ctx", None), P("ctx", "head")),
        out_specs=(P("ctx", "head"), P("ctx", "head")),
        check_vma=False,
    )
```

time: 173 us -> 73.1 us (0.42)
  local copies, waits for them, and re-layouts: 50.5 us -> 4.47 us
  waiting for transfers between devices: 36.9 us -> 22.3 us
  between operations: 14.4 us -> 0.84 us
  starting transfers between devices: 45.9 us -> 32.8 us
  matrix products: 13 us -> 0 us
  Pallas kernels: 0 us -> 8.91 us
  blocking collectives: 8.83 us -> 0 us
    reduce_scatter x1 -> x0, waiting for transfers between devices: 21.6 us -> none  [body(): lax.psum_scatter(partial_sum.astype(jnp.bfloat16), 'head', scatter_dimens...]
    reshape x9 -> x1, local copies, waits for them, and re-layouts: 16 us -> 1.52 us  [body(): lax.dynamic_slice_in_dim(w_qkv, side * HD, HD, axis=2)]
    ppermute x12 -> x18, starting transfers between devices: 45.9 us -> 32.8 us  [the longest x8 21.5 us: group_swap(): return lax.ppermute(value, 'ctx', pairs)]
    dot_general x9 -> x0, matrix products: 13 us -> none  [the longest x1 3.72 us: body(): jnp.einsum('es,sbc->ebc', slot_owner, slot_terms, precision=lax.Precision...]
    unnamed x32 -> x13, local copies, waits for them, and re-layouts: 12.1 us -> 2.75 us
    pallas_call x0 -> x3, Pallas kernels: none -> 8.91 us  [the longest x1 5.66 us: body(): pl.pallas_call(attend_kernel, name='attend', out_shape=[jax.ShapeDtypeStr...]
    transpose x1 -> x0, local copies, waits for them, and re-layouts: 8.88 us -> none  [body(): jnp.einsum('ihqk,iqhd->ikhd', softmax_share, grad_blocks, preferred_eleme...]
    all_gather x1 -> x0, blocking collectives: 8.83 us -> none  [body(): lax.all_gather(features, 'head', axis=1, tiled=True)]
  transfers between devices with their start and end apart: 13 -> 18, of which waited for: 4 -> 10; matrix products, arithmetic and copies ran while one was open for 6% -> 5% of each run, Pallas kernels for 0% -> 0%
where the time goes in v1:
time: 73.1 us; the launch traced here: 72.8 us
  starting transfers between devices  32.8 us (45%)
  waiting for transfers between devices  22.3 us (31%)
  Pallas kernels  8.91 us (12%)
  local copies, waits for them, and re-layouts  4.47 us (6%)
  other arithmetic  3.49 us (5%)
  between operations  0.84 us (1%)
    ppermute x8, starting transfers between devices, group_swap(): return lax.ppermute(value, 'ctx', pairs)  21.5 us
    ppermute x10, waiting for transfers between devices, across(): return lax.ppermute(value, ('ctx', 'head'), pairs)  13 us
    ppermute x10, starting transfers between devices, across(): return lax.ppermute(value, ('ctx', 'head'), pairs)  11.3 us
    ppermute x8, waiting for transfers between devices, group_swap(): return lax.ppermute(value, 'ctx', pairs)  9.29 us
    pallas_call x1, Pallas kernels, body(): pl.pallas_call(attend_kernel, name='attend', out_shape=[jax.ShapeDtypeStr...  5.66 us
    unnamed x13, local copies, waits for them, and re-layouts  2.75 us
    pallas_call x1, Pallas kernels, body(): pl.pallas_call(project_kernel, name='project', out_shape=[jax.ShapeDtypeS...  1.95 us
    concatenate x1, other arithmetic, body(): other = across(jnp.concatenate([f, sx, sy, sd], axis=0), 0, 1)  1.76 us
  transfers between devices with their start and end apart: 18, of which 10 were waited for; matrix products, arithmetic and copies ran while one was open for 5% of the time, Pallas kernels for 0%

profile of v1, /device:TPU:0, one launch (start us, length us, event | category | flops | bytes accessed | tf_op | source)
XLA Modules:
  0.0 72.8 jit_solution(17676002138047979510)
XLA Ops:
  0.6 4.0 %collective-permute-start.3 = (bf16[256,256]{1,0:T(8,128)(2,1)}, bf16[256,256]{1,0:T(8,128)(2,1)S(1)}, u32[]{:S(2)}, u32[]{:S(2)}) collective-permute-start(bf16[256,256]{1,0:T(8,128)(2,1)} %f.1), channel_id=1, source_target_pairs={{0,6},{1,7},{2,4},{3,5},{4,2},{5,3},{6,0},{7,1},{8,14},{9,15},{10,... | collective-permute-start | bytes 393224 | tf_op jit(solution)/shard_map/ppermute | solution.py:168
  5.2 3.6 %collective-permute-done.3.sd = bf16[256,256]{1,0:T(8,128)(2,1)S(1)} collective-permute-done((bf16[256,256]{1,0:T(8,128)(2,1)}, bf16[256,256]{1,0:T(8,128)(2,1)S(1)}, u32[]{:S(2)}, u32[]{:S(2)}) %collective-permute-start.3) | collective-permute-done | bytes 131104 | tf_op jit(solution)/shard_map/ppermute | solution.py:168
  8.8 2.3 %collective-permute-done.2.sy = bf16[256,256]{1,0:T(8,128)(2,1)S(1)} collective-permute-done((bf16[256,256]{1,0:T(8,128)(2,1)}, bf16[256,256]{1,0:T(8,128)(2,1)S(1)}, u32[]{:S(2)}, u32[]{:S(2)}) %collective-permute-start.2) | collective-permute-done | bytes 131104 | tf_op jit(solution)/shard_map/ppermute | solution.py:168
  11.4 1.8 %pad_maximum_fusion = bf16[1024,256]{1,0:T(8,128)(2,1)} fusion(bf16[256,256]{1,0:T(8,128)(2,1)S(1)} %collective-permute-done.3.sd, bf16[256,256]{1,0:T(8,128)(2,1)S(1)} %collective-permute-done.2.sy, bf16[256,256]{1,0:T(8,128)(2,1)S(1)} %collective-permute-done.1.sx, bf16[256,256]{1,0:T(8,128)(2,1)} %f.1), kind=kLoop, calls=%fused_computation.1 | loop fusion | flops 2097152 | bytes 1048576 | tf_op jit(solution)/shard_map/concatenate | solution.py:183
  13.3 1.2 %copy.10 = bf16[1024,3,128]{0,2,1:T(8,128)(2,1)} copy(bf16[1024,3,128]{2,0,1:T(8,128)(2,1)S(1)} %constant_dynamic-slice_fusion.2) | data formatting | bytes 1572864
  14.5 1.5 %copy.8.w = bf16[1024,384]{1,0:T(8,128)(2,1)S(1)} copy(bf16[1024,384]{0,1:T(8,128)(2,1)} %bitcast.5) | data formatting | bytes 1572864 | tf_op jit(solution)/shard_map/reshape | solution.py:182
  16.1 1.9 %project.1 = (bf16[512,128]{1,0:T(8,128)(2,1)S(1)}, bf16[512,256]{1,0:T(8,128)(2,1)}) custom-call(s32[4]{0:T(128)S(1)} %pad_add_fusion.place, bf16[256,256]{1,0:T(8,128)(2,1)S(1)} %copy-done.1, bf16[256,256]{1,0:T(8,128)(2,1)S(1)} %collective-permute-done.1.sx, bf16[256,256]{1,0:T(8,128)(2,1)S(1)} %collective-permute-done.2.sy, ...), custom_call_target="tpu_custom_call" | custom-call | flops 402653184 | bytes 4194304 | tf_op jit(solution)/shard_map/project/pallas_call | solution.py:185
  18.0 0.7 copy-done.3
  18.7 0.7 collective-permute-start.6
  19.4 4.5 %collective-permute-start.5 = (bf16[512,256]{1,0:T(8,128)(2,1)}, bf16[512,256]{1,0:T(8,128)(2,1)S(1)}, u32[]{:S(2)}, u32[]{:S(2)}) collective-permute-start(bf16[512,256]{1,0:T(8,128)(2,1)} %get-tuple-element.27.kv), channel_id=1, source_target_pairs={{0,8},{8,0},{4,12},{12,4},{16,24},{24,16},{20,28},{28,20},{1,9},{9... | collective-permute-start | bytes 786440 | tf_op jit(solution)/shard_map/ppermute | solution.py:176
  23.9 1.5 %collective-permute-start = (bf16[272,128]{1,0:T(8,128)(2,1)S(1)}, bf16[272,128]{1,0:T(8,128)(2,1)S(1)}, u32[]{:S(2)}, u32[]{:S(2)}) collective-permute-start(bf16[272,128]{1,0:T(8,128)(2,1)S(1)} %fusion.3), channel_id=1, source_target_pairs={{0,4},{1,5},{2,6},{3,7},{4,0},{5,1},{6,2},{7,3},{8,12},{9,13},{10,... | collective-permute-start | bytes 208904 | tf_op jit(solution)/shard_map/ppermute | solution.py:168
  25.4 5.7 %collective-permute-start.7 = (bf16[256,256]{1,0:T(8,128)(2,1)S(1)}, bf16[256,256]{1,0:T(8,128)(2,1)S(1)}, u32[]{:S(2)}, u32[]{:S(2)}) collective-permute-start(bf16[256,256]{1,0:T(8,128)(2,1)S(1)} %constant_dynamic-slice_fusion.1), channel_id=1, source_target_pairs={{0,8},{8,0},{4,12},{12,4},{16,24},{24,16},{20,28},{28,20},{1,9},{9... | collective-permute-start | bytes 393224 | tf_op jit(solution)/shard_map/ppermute | solution.py:176
  31.2 0.7 collective-permute-start.8
  31.9 2.6 %collective-permute-done.7.far_a = bf16[256,256]{1,0:T(8,128)(2,1)S(1)} collective-permute-done((bf16[256,256]{1,0:T(8,128)(2,1)S(1)}, bf16[256,256]{1,0:T(8,128)(2,1)S(1)}, u32[]{:S(2)}, u32[]{:S(2)}) %collective-permute-start.7) | collective-permute-done | bytes 131104 | tf_op jit(solution)/shard_map/ppermute | solution.py:176
  34.5 0.9 %copy-done.4 = bf16[512,128]{1,0:T(8,128)(2,1)S(1)} copy-done((bf16[512,128]{1,0:T(8,128)(2,1)S(1)}, bf16[512,128]{1,0:T(8,128)(2,1)}, u32[]{:S(2)}) %copy-start.4) | copy-done | bytes 131096
  35.5 5.7 %attend.1 = (bf16[256,128]{1,0:T(8,128)(2,1)S(1)}, bf16[256,128]{1,0:T(8,128)(2,1)S(1)}, bf16[512,128]{1,0:T(8,128)(2,1)S(1)}, f32[512,256]{1,0:T(8,128)S(1)}, b...) custom-call(s32[4]{0:T(128)S(1)} %pad_add_fusion.place, ...), custom_call_target="tpu_custom_call" | custom-call | flops 1811939328 | bytes 4194304 | tf_op jit(solution)/shard_map/attend/pallas_call | solution.py:216
  41.1 4.9 %collective-permute-start.12 = (bf16[256,256]{1,0:T(8,128)(2,1)S(1)}, bf16[256,256]{1,0:T(8,128)(2,1)S(1)}, u32[]{:S(2)}, u32[]{:S(2)}) collective-permute-start(bf16[256,256]{1,0:T(8,128)(2,1)S(1)} %get-tuple-element.34), channel_id=1, source_target_pairs={{0,8},{8,0},{4,12},{12,4},{16,24},{24,16},{20,28},{28,20},{1,9},{9... | collective-permute-start | bytes 393224 | tf_op jit(solution)/shard_map/ppermute | solution.py:176
  46.0 0.7 collective-permute-start.10
  46.6 2.3 %collective-permute-done.12 = bf16[256,256]{1,0:T(8,128)(2,1)S(1)} collective-permute-done((bf16[256,256]{1,0:T(8,128)(2,1)S(1)}, bf16[256,256]{1,0:T(8,128)(2,1)S(1)}, u32[]{:S(2)}, u32[]{:S(2)}) %collective-permute-start.12) | collective-permute-done | bytes 131104 | tf_op jit(solution)/shard_map/ppermute | solution.py:176
  49.0 0.7 collective-permute-start.13
  49.7 3.8 %collective-permute-start.11 = (bf16[512,256]{1,0:T(8,128)(2,1)S(1)}, bf16[512,256]{1,0:T(8,128)(2,1)S(1)}, u32[]{:S(2)}, u32[]{:S(2)}) collective-permute-start(bf16[512,256]{1,0:T(8,128)(2,1)S(1)} %fusion.1), channel_id=1, source_target_pairs={{0,8},{8,0},{4,12},{12,4},{16,24},{24,16},{20,28},{28,20},{1,9},{9... | collective-permute-start | bytes 786440 | tf_op jit(solution)/shard_map/ppermute | solution.py:176
  53.5 4.3 %collective-permute-done.11.from_a = bf16[512,256]{1,0:T(8,128)(2,1)S(1)} collective-permute-done((bf16[512,256]{1,0:T(8,128)(2,1)S(1)}, bf16[512,256]{1,0:T(8,128)(2,1)S(1)}, u32[]{:S(2)}, u32[]{:S(2)}) %collective-permute-start.11) | collective-permute-done | bytes 262176 | tf_op jit(solution)/shard_map/ppermute | solution.py:176
  57.8 1.3 %spread.1 = (bf16[1024,256]{1,0:T(8,128)(2,1)S(1)}, bf16[1024,256]{1,0:T(8,128)(2,1)S(1)}) custom-call(s32[4]{0:T(128)S(1)} %pad_add_fusion.place, f32[512,256]{1,0:T(8,128)S(1)} %get-tuple-element.30.own, bf16[512,256]{1,0:T(8,128)(2,1)S(1)} %collective-permute-done.11.from_a, bf16[512,256]{1,0:T(8,128)(2,1)S(1)} %collective-permute-done.13.from_b, ...), custom_call_target="tpu_custom_call" | custom-call | flops 402653184 | bytes 4194304 | tf_op jit(solution)/shard_map/spread/pallas_call | solution.py:256
  59.2 1.5 %collective-permute-start.9 = (bf16[256,128]{1,0:T(8,128)(2,1)S(1)}, bf16[256,128]{1,0:T(8,128)(2,1)S(1)}, u32[]{:S(2)}, u32[]{:S(2)}) collective-permute-start(bf16[256,128]{1,0:T(8,128)(2,1)S(1)} %get-tuple-element.29), channel_id=1, source_target_pairs={{0,4},{1,5},{2,6},{3,7},{4,0},{5,1},{6,2},{7,3},{8,12},{9,13},{10,... | collective-permute-start | bytes 196616 | tf_op jit(solution)/shard_map/ppermute | solution.py:168
  61.3 1.6 %collective-permute-start.15 = (bf16[256,256]{1,0:T(8,128)(2,1)S(1)}, bf16[256,256]{1,0:T(8,128)(2,1)S(1)}, u32[]{:S(2)}, u32[]{:S(2)}) collective-permute-start(bf16[256,256]{1,0:T(8,128)(2,1)S(1)} %get-tuple-element.38), channel_id=1, source_target_pairs={{0,2},{1,3},{2,0},{3,1},{4,6},{5,7},{6,4},{7,5},{8,10},{9,11},{10,... | collective-permute-start | bytes 393224 | tf_op jit(solution)/shard_map/ppermute | solution.py:168
  62.9 1.4 %collective-permute-start.17 = (bf16[256,256]{1,0:T(8,128)(2,1)S(1)}, bf16[256,256]{1,0:T(8,128)(2,1)S(1)}, u32[]{:S(2)}, u32[]{:S(2)}) collective-permute-start(bf16[256,256]{1,0:T(8,128)(2,1)S(1)} %get-tuple-element.39), channel_id=1, source_target_pairs={{0,6},{1,7},{2,4},{3,5},{4,2},{5,3},{6,0},{7,1},{8,14},{9,15},{10,... | collective-permute-start | bytes 393224 | tf_op jit(solution)/shard_map/ppermute | solution.py:168
  64.3 0.6 collective-permute-start.16
  64.9 0.7 maximum_select_fusion
  65.6 2.2 %collective-permute-done.15 = bf16[256,256]{1,0:T(8,128)(2,1)S(1)} collective-permute-done((bf16[256,256]{1,0:T(8,128)(2,1)S(1)}, bf16[256,256]{1,0:T(8,128)(2,1)S(1)}, u32[]{:S(2)}, u32[]{:S(2)}) %collective-permute-start.15) | collective-permute-done | bytes 131104 | tf_op jit(solution)/shard_map/ppermute | solution.py:168
  67.7 3.0 %collective-permute-done.17 = bf16[256,256]{1,0:T(8,128)(2,1)S(1)} collective-permute-done((bf16[256,256]{1,0:T(8,128)(2,1)S(1)}, bf16[256,256]{1,0:T(8,128)(2,1)S(1)}, u32[]{:S(2)}, u32[]{:S(2)}) %collective-permute-start.17) | collective-permute-done | bytes 131104 | tf_op jit(solution)/shard_map/ppermute | solution.py:168
  70.7 1.4 %collective-permute-done.16 = bf16[256,256]{1,0:T(8,128)(2,1)S(1)} collective-permute-done((bf16[256,256]{1,0:T(8,128)(2,1)S(1)}, bf16[256,256]{1,0:T(8,128)(2,1)S(1)}, u32[]{:S(2)}, u32[]{:S(2)}) %collective-permute-start.16) | collective-permute-done | bytes 131104 | tf_op jit(solution)/shard_map/ppermute | solution.py:168
  72.1 0.7 add_convert_fusion.1
  (38 shorter events, 1.9 us)
Async XLA Ops:
  0.6 12.5 %copy-start = (bf16[1024,3,256]{2,0,1:T(8,128)(2,1)S(1)}, bf16[1024,3,256]{2,0,1:T(8,128)(2,1)}, u32[]{:S(2)}) copy-start(bf16[1024,3,256]{2,0,1:T(8,128)(2,1)} %param.7) | copy-start | bytes 4718596
  0.6 8.2 %collective-permute-start.3 = (bf16[256,256]{1,0:T(8,128)(2,1)}, bf16[256,256]{1,0:T(8,128)(2,1)S(1)}, u32[]{:S(2)}, u32[]{:S(2)}) collective-permute-start(bf16[256,256]{1,0:T(8,128)(2,1)} %f.1), channel_id=1, source_target_pairs={{0,6},{1,7},{2,4},{3,5},{4,2},{5,3},{6,0},{7,1},{8,14},{9,15},{10,... | collective-permute-start | bytes 393224 | tf_op jit(solution)/shard_map/ppermute | solution.py:168
  4.6 6.5 %collective-permute-start.2 = (bf16[256,256]{1,0:T(8,128)(2,1)}, bf16[256,256]{1,0:T(8,128)(2,1)S(1)}, u32[]{:S(2)}, u32[]{:S(2)}) collective-permute-start(bf16[256,256]{1,0:T(8,128)(2,1)} %f.1), channel_id=1, source_target_pairs={{0,4},{1,5},{2,6},{3,7},{4,0},{5,1},{6,2},{7,3},{8,12},{9,13},{10,... | collective-permute-start | bytes 393224 | tf_op jit(solution)/shard_map/ppermute | solution.py:168
  5.1 6.3 %collective-permute-start.1 = (bf16[256,256]{1,0:T(8,128)(2,1)}, bf16[256,256]{1,0:T(8,128)(2,1)S(1)}, u32[]{:S(2)}, u32[]{:S(2)}) collective-permute-start(bf16[256,256]{1,0:T(8,128)(2,1)} %f.1), channel_id=1, source_target_pairs={{0,2},{1,3},{2,0},{3,1},{4,6},{5,7},{6,4},{7,5},{8,10},{9,11},{10,... | collective-permute-start | bytes 393224 | tf_op jit(solution)/shard_map/ppermute | solution.py:168
  13.1 3.0 %collective-permute-start.4 = (bf16[1024,256]{1,0:T(8,128)(2,1)}, bf16[1024,256]{1,0:T(8,128)(2,1)S(1)}, u32[]{:S(2)}, u32[]{:S(2)}) collective-permute-start(bf16[1024,256]{1,0:T(8,128)(2,1)} %pad_maximum_fusion), channel_id=1, source_target_pairs={{0,1},{1,0},{2,3},{3,2},{4,5},{5,4},{6,7},{7,6},{8,9},{9,8},{10,11... | collective-permute-start | bytes 1572872 | tf_op jit(solution)/shard_map/ppermute | solution.py:168
  13.3 2.8 %copy-start.1 = (bf16[256,256]{1,0:T(8,128)(2,1)S(1)}, bf16[256,256]{1,0:T(8,128)(2,1)}, u32[]{:S(2)}) copy-start(bf16[256,256]{1,0:T(8,128)(2,1)} %f.1) | copy-start | bytes 393220
  14.5 9.4 %copy-start.2 = (bf16[256,256]{1,0:T(8,128)(2,1)S(1)}, bf16[256,256]{1,0:T(8,128)(2,1)}, u32[]{:S(2)}) copy-start(bf16[256,256]{1,0:T(8,128)(2,1)} %d_own.1) | copy-start | bytes 393220
  14.5 9.4 %copy-start.5 = (s32[2,9]{1,0:T(2,128)S(1)}, s32[2,9]{1,0:T(2,128)}, u32[]{:S(2)}) copy-start(s32[2,9]{1,0:T(2,128)} %param.8) | copy-start | bytes 220
  18.0 0.7 copy-start.3
  18.7 6.7 %collective-permute-start.6 = (bf16[512,256]{1,0:T(8,128)(2,1)}, bf16[512,256]{1,0:T(8,128)(2,1)S(1)}, u32[]{:S(2)}, u32[]{:S(2)}) collective-permute-start(bf16[512,256]{1,0:T(8,128)(2,1)} %get-tuple-element.27.kv), channel_id=1, source_target_pairs={{8,16},{16,8},{12,20},{20,12},{9,17},{17,9},{13,21},{21,13},{10,18... | collective-permute-start | bytes 786440 | tf_op jit(solution)/shard_map/ppermute | solution.py:176
  19.4 11.8 %collective-permute-start.5 = (bf16[512,256]{1,0:T(8,128)(2,1)}, bf16[512,256]{1,0:T(8,128)(2,1)S(1)}, u32[]{:S(2)}, u32[]{:S(2)}) collective-permute-start(bf16[512,256]{1,0:T(8,128)(2,1)} %get-tuple-element.27.kv), channel_id=1, source_target_pairs={{0,8},{8,0},{4,12},{12,4},{16,24},{24,16},{20,28},{28,20},{1,9},{9... | collective-permute-start | bytes 786440 | tf_op jit(solution)/shard_map/ppermute | solution.py:176
  23.9 8.0 %collective-permute-start = (bf16[272,128]{1,0:T(8,128)(2,1)S(1)}, bf16[272,128]{1,0:T(8,128)(2,1)S(1)}, u32[]{:S(2)}, u32[]{:S(2)}) collective-permute-start(bf16[272,128]{1,0:T(8,128)(2,1)S(1)} %fusion.3), channel_id=1, source_target_pairs={{0,4},{1,5},{2,6},{3,7},{4,0},{5,1},{6,2},{7,3},{8,12},{9,13},{10,... | collective-permute-start | bytes 208904 | tf_op jit(solution)/shard_map/ppermute | solution.py:168
  25.4 9.1 %collective-permute-start.7 = (bf16[256,256]{1,0:T(8,128)(2,1)S(1)}, bf16[256,256]{1,0:T(8,128)(2,1)S(1)}, u32[]{:S(2)}, u32[]{:S(2)}) collective-permute-start(bf16[256,256]{1,0:T(8,128)(2,1)S(1)} %constant_dynamic-slice_fusion.1), channel_id=1, source_target_pairs={{0,8},{8,0},{4,12},{12,4},{16,24},{24,16},{20,28},{28,20},{1,9},{9... | collective-permute-start | bytes 393224 | tf_op jit(solution)/shard_map/ppermute | solution.py:176
  31.2 3.4 %collective-permute-start.8 = (bf16[256,256]{1,0:T(8,128)(2,1)S(1)}, bf16[256,256]{1,0:T(8,128)(2,1)S(1)}, u32[]{:S(2)}, u32[]{:S(2)}) collective-permute-start(bf16[256,256]{1,0:T(8,128)(2,1)S(1)} %constant_dynamic-slice_fusion), channel_id=1, source_target_pairs={{8,16},{16,8},{12,20},{20,12},{9,17},{17,9},{13,21},{21,13},{10,18... | collective-permute-start | bytes 393224 | tf_op jit(solution)/shard_map/ppermute | solution.py:176
  34.5 0.9 %copy-start.4 = (bf16[512,128]{1,0:T(8,128)(2,1)S(1)}, bf16[512,128]{1,0:T(8,128)(2,1)}, u32[]{:S(2)}) copy-start(bf16[512,128]{1,0:T(8,128)(2,1)} %copy-done.3) | copy-start | bytes 393220
  41.1 7.8 %collective-permute-start.12 = (bf16[256,256]{1,0:T(8,128)(2,1)S(1)}, bf16[256,256]{1,0:T(8,128)(2,1)S(1)}, u32[]{:S(2)}, u32[]{:S(2)}) collective-permute-start(bf16[256,256]{1,0:T(8,128)(2,1)S(1)} %get-tuple-element.34), channel_id=1, source_target_pairs={{0,8},{8,0},{4,12},{12,4},{16,24},{24,16},{20,28},{28,20},{1,9},{9... | collective-permute-start | bytes 393224 | tf_op jit(solution)/shard_map/ppermute | solution.py:176
  46.0 3.7 %collective-permute-start.10 = (bf16[256,256]{1,0:T(8,128)(2,1)S(1)}, bf16[256,256]{1,0:T(8,128)(2,1)S(1)}, u32[]{:S(2)}, u32[]{:S(2)}) collective-permute-start(bf16[256,256]{1,0:T(8,128)(2,1)S(1)} %get-tuple-element.32), channel_id=1, source_target_pairs={{8,16},{16,8},{12,20},{20,12},{9,17},{17,9},{13,21},{21,13},{10,18... | collective-permute-start | bytes 393224 | tf_op jit(solution)/shard_map/ppermute | solution.py:176
  49.0 4.5 %collective-permute-start.13 = (bf16[512,256]{1,0:T(8,128)(2,1)S(1)}, bf16[512,256]{1,0:T(8,128)(2,1)S(1)}, u32[]{:S(2)}, u32[]{:S(2)}) collective-permute-start(bf16[512,256]{1,0:T(8,128)(2,1)S(1)} %fusion.2), channel_id=1, source_target_pairs={{8,16},{16,8},{12,20},{20,12},{9,17},{17,9},{13,21},{21,13},{10,18... | collective-permute-start | bytes 786440 | tf_op jit(solution)/shard_map/ppermute | solution.py:176
  49.7 8.1 %collective-permute-start.11 = (bf16[512,256]{1,0:T(8,128)(2,1)S(1)}, bf16[512,256]{1,0:T(8,128)(2,1)S(1)}, u32[]{:S(2)}, u32[]{:S(2)}) collective-permute-start(bf16[512,256]{1,0:T(8,128)(2,1)S(1)} %fusion.1), channel_id=1, source_target_pairs={{0,8},{8,0},{4,12},{12,4},{16,24},{24,16},{20,28},{28,20},{1,9},{9... | collective-permute-start | bytes 786440 | tf_op jit(solution)/shard_map/ppermute | solution.py:176
  59.2 2.0 %collective-permute-start.14 = (bf16[1024,256]{1,0:T(8,128)(2,1)S(1)}, bf16[1024,256]{1,0:T(8,128)(2,1)S(1)}, u32[]{:S(2)}, u32[]{:S(2)}) collective-permute-start(bf16[1024,256]{1,0:T(8,128)(2,1)S(1)} %get-tuple-element.37), channel_id=1, source_target_pairs={{0,1},{1,0},{2,3},{3,2},{4,5},{5,4},{6,7},{7,6},{8,9},{9,8},{10,11... | collective-permute-start | bytes 1572872 | tf_op jit(solution)/shard_map/ppermute | solution.py:168
  59.2 5.6 %collective-permute-start.9 = (bf16[256,128]{1,0:T(8,128)(2,1)S(1)}, bf16[256,128]{1,0:T(8,128)(2,1)S(1)}, u32[]{:S(2)}, u32[]{:S(2)}) collective-permute-start(bf16[256,128]{1,0:T(8,128)(2,1)S(1)} %get-tuple-element.29), channel_id=1, source_target_pairs={{0,4},{1,5},{2,6},{3,7},{4,0},{5,1},{6,2},{7,3},{8,12},{9,13},{10,... | collective-permute-start | bytes 196616 | tf_op jit(solution)/shard_map/ppermute | solution.py:168
  61.3 6.4 %collective-permute-start.15 = (bf16[256,256]{1,0:T(8,128)(2,1)S(1)}, bf16[256,256]{1,0:T(8,128)(2,1)S(1)}, u32[]{:S(2)}, u32[]{:S(2)}) collective-permute-start(bf16[256,256]{1,0:T(8,128)(2,1)S(1)} %get-tuple-element.38), channel_id=1, source_target_pairs={{0,2},{1,3},{2,0},{3,1},{4,6},{5,7},{6,4},{7,5},{8,10},{9,11},{10,... | collective-permute-start | bytes 393224 | tf_op jit(solution)/shard_map/ppermute | solution.py:168
  62.9 7.8 %collective-permute-start.17 = (bf16[256,256]{1,0:T(8,128)(2,1)S(1)}, bf16[256,256]{1,0:T(8,128)(2,1)S(1)}, u32[]{:S(2)}, u32[]{:S(2)}) collective-permute-start(bf16[256,256]{1,0:T(8,128)(2,1)S(1)} %get-tuple-element.39), channel_id=1, source_target_pairs={{0,6},{1,7},{2,4},{3,5},{4,2},{5,3},{6,0},{7,1},{8,14},{9,15},{10,... | collective-permute-start | bytes 393224 | tf_op jit(solution)/shard_map/ppermute | solution.py:168
  64.3 7.8 %collective-permute-start.16 = (bf16[256,256]{1,0:T(8,128)(2,1)S(1)}, bf16[256,256]{1,0:T(8,128)(2,1)S(1)}, u32[]{:S(2)}, u32[]{:S(2)}) collective-permute-start(bf16[256,256]{1,0:T(8,128)(2,1)S(1)} %get-tuple-element.40), channel_id=1, source_target_pairs={{0,4},{1,5},{2,6},{3,7},{4,0},{5,1},{6,2},{7,3},{8,12},{9,13},{10,... | collective-permute-start | bytes 393224 | tf_op jit(solution)/shard_map/ppermute | solution.py:168

commit v2 on v1

--- a/solution.py
+++ b/solution.py
@@ -26,9 +26,9 @@
 FAR_RIGHT = NEAR_RIGHT + ROWS
 
 
-def params(flops, moved):
+def params(flops, moved, mebibytes):
     return dict(
-        compiler_params=pltpu.CompilerParams(vmem_limit_bytes=48 * 1024 * 1024),
+        compiler_params=pltpu.CompilerParams(vmem_limit_bytes=mebibytes * 1024 * 1024),
         cost_estimate=pl.CostEstimate(flops=flops, bytes_accessed=moved, transcendentals=0),
     )
 
@@ -41,23 +41,30 @@
     return lax.dot_general(a, b, (dims, ((), ())), preferred_element_type=F32)
 
 
-def project_kernel(place, f, sx, sy, sd, other, w, q_out, kv_out):
+def pack_kernel(f, sx, sy, sd, out):
+    for index, piece in enumerate((f, sx, sy, sd)):
+        out[index * HALF : (index + 1) * HALF, :] = piece[...]
+
+
+def weight_rows(w, source, side, groups):
+    width = w.shape[2]
+    rows = pl.ds(pl.multiple_of(source * width, width), width)
+    cols = pl.ds(pl.multiple_of(side * HD, HD), HD)
+    return jnp.concatenate([w[g, rows, cols] for g in groups], axis=1)
+
+
+def project_kernel(place, pack, other, w, q_out, kv_out):
     side, head = place[0], place[3]
-    width = f.shape[1]
-    for group, near, far in ((0, f, sx), (1, sy, sd)):
-        total = None
-        pieces = (
-            (head, near[...]),
-            (head ^ 2, far[...]),
-            (head ^ 1, other[2 * group * HALF : (2 * group + 1) * HALF]),
-            (head ^ 3, other[(2 * group + 1) * HALF : (2 * group + 2) * HALF]),
-        )
-        for source, piece in pieces:
-            term = dot(piece, w[pl.ds(pl.multiple_of(source * width, width), width), :], ((1,), (0,)))
-            total = term if total is None else total + term
+    total = None
+    for source, store, index in ((head, pack, 0), (head ^ 2, pack, 1), (head ^ 1, other, 0), (head ^ 3, other, 1)):
+        rows = [store[(2 * group + index) * HALF : (2 * group + index + 1) * HALF, :] for group in range(2)]
+        term = dot(jnp.concatenate(rows, axis=0), weight_rows(w, source, side, (0, 1, 2)), ((1,), (0,)))
+        total = term if total is None else total + term
+    for group in range(2):
         rows = pl.ds(pl.multiple_of((side ^ group) * HALF, HALF), HALF)
-        q_out[rows, :] = total[:, :HD].astype(BF)
-        kv_out[rows, :] = total[:, HD:].astype(BF)
+        part = total[group * HALF : (group + 1) * HALF]
+        q_out[rows, :] = part[:, :HD].astype(BF)
+        kv_out[rows, :] = part[:, HD:].astype(BF)
 
 
 def attend_kernel(
@@ -91,7 +98,7 @@
             ],
             axis=0,
         )
-        starts, both, scores = [], [], []
+        starts, scores, prob_grads, peaks, biases = [], [], [], [], []
         for t in range(3):
             if t == 0:
                 start = (REACH + i - 1) * BLK
@@ -105,21 +112,35 @@
                 start = pl.multiple_of(base * BLK, BLK)
             starts.append(start)
             product = dot(win[pl.ds(start, SPAN * BLK), :], pair, ((1,), (1,)))
-            both.append(product[:, BLK:])
             for j in range(SPAN):
+                block = product[j * BLK : (j + 1) * BLK]
                 bias = jnp.where(links[i, SPAN * t + j] >= 0, 0.0, DEAD).astype(F32)
-                scores.append(product[j * BLK : (j + 1) * BLK, :BLK] + bias)
-        scores = jnp.concatenate(scores, axis=0)
-        largest = jnp.max(scores, axis=0, keepdims=True)
-        terms = jnp.exp2((scores - largest) * (scale * LOG2E))
-        share = terms * (1.0 / jnp.sum(terms, axis=0, keepdims=True))
-        prob_grad = jnp.concatenate(both, axis=0)
-        row_dot = jnp.sum(share * prob_grad, axis=0, keepdims=True)
-        score_grad = share * (prob_grad - row_dot)
-        mixed = jnp.concatenate([score_grad.astype(BF), share.astype(BF)], axis=1)
+                scores.append(block[:, :BLK])
+                prob_grads.append(block[:, BLK:])
+                biases.append(bias)
+                peaks.append(jnp.max(block[:, :BLK].reshape(BLK // 8, 8, BLK), axis=0) + bias)
+        largest = peaks[0]
+        for peak in peaks[1:]:
+            largest = jnp.maximum(largest, peak)
+        largest = jnp.max(largest, axis=0, keepdims=True)
+        terms = []
+        total = jnp.zeros((8, BLK), F32)
+        weighted = jnp.zeros((8, BLK), F32)
+        for n in range(3 * SPAN):
+            term = jnp.exp2((scores[n] - (largest - biases[n])) * (scale * LOG2E))
+            terms.append(term)
+            total = total + jnp.sum(term.reshape(BLK // 8, 8, BLK), axis=0)
+            weighted = weighted + jnp.sum((term * prob_grads[n]).reshape(BLK // 8, 8, BLK), axis=0)
+        inverse = 1.0 / jnp.sum(total, axis=0, keepdims=True)
+        row_dot = jnp.sum(weighted, axis=0, keepdims=True) * inverse
         out = None
         for t in range(3):
-            part = mixed[t * SPAN * BLK : (t + 1) * SPAN * BLK, :]
+            parts = []
+            for n in range(SPAN * t, SPAN * t + SPAN):
+                share = terms[n] * inverse
+                grad = share * (prob_grads[n] - row_dot)
+                parts.append(jnp.concatenate([grad.astype(BF), share.astype(BF)], axis=1))
+            part = jnp.concatenate(parts, axis=0)
             keys = win[pl.ds(starts[t], SPAN * BLK), :]
             term = dot(part, keys, ((0,), (0,)))
             out = term if out is None else out + term
@@ -138,12 +159,11 @@
 
 def spread_kernel(place, own, from_a, from_b, dq, w, keep, send):
     side, head = place[0], place[3]
-    width = 2 * HD
     dkv = (own[...] + from_a[...].astype(F32) + from_b[...].astype(F32)).astype(BF)
     grads = jnp.concatenate([dq[...], dkv], axis=1)
     for step in range(4):
         dest = head ^ step
-        out = dot(grads, w[pl.ds(pl.multiple_of(dest * width, width), width), :], ((1,), (1,))).astype(BF)
+        out = dot(grads, weight_rows(w, dest, side, (0, 1, 2)), ((1,), (1,))).astype(BF)
         target = keep if step % 2 == 0 else send
         for group in range(2):
             index = 2 * group + step // 2
@@ -179,8 +199,16 @@
     sx = across(f, 0, 2)
     sy = across(f, 1, 0)
     sd = across(f, 1, 2)
-    w_sel = lax.dynamic_slice_in_dim(w_qkv, side * HD, HD, axis=2).reshape(w_qkv.shape[0], 3 * HD)
-    other = across(jnp.concatenate([f, sx, sy, sd], axis=0), 0, 1)
+    w = jnp.transpose(w_qkv, (1, 0, 2))
+    pack = pl.pallas_call(
+        pack_kernel,
+        name="pack",
+        out_shape=jax.ShapeDtypeStruct((4 * f.shape[0], f.shape[1]), BF),
+        in_specs=[VMEM] * 4,
+        out_specs=VMEM,
+        **params(0, 1 << 20, 4),
+    )(f, sx, sy, sd)
+    other = across(pack, 0, 1)
 
     q, kv = pl.pallas_call(
         project_kernel,
@@ -189,10 +217,10 @@
             jax.ShapeDtypeStruct((ROWS, HD), BF),
             jax.ShapeDtypeStruct((ROWS, 2 * HD), BF),
         ],
-        in_specs=[SMEM] + [VMEM] * 6,
+        in_specs=[SMEM] + [VMEM] * 3,
         out_specs=[VMEM] * 2,
-        **params(2 * ROWS * 1024 * 3 * HD, 4 << 20),
-    )(place, f, sx, sy, sd, other, w_sel)
+        **params(2 * ROWS * 1024 * 3 * HD, 4 << 20, 8),
+    )(place, pack, other, w)
 
     near_a = group_swap(kv, 0)
     near_b = group_swap(kv, 1)
@@ -233,7 +261,7 @@
             pltpu.VMEM((WINDOW * BLK, 2 * HD), F32),
             pltpu.VMEM((ROWS, HD), BF),
         ],
-        **params(6 * 2 * GROUP * 9 * BLK * BLK * 2 * HD, 4 << 20),
+        **params(6 * 2 * GROUP * 9 * BLK * BLK * 2 * HD, 4 << 20, 16),
     )(place, links, q, kv, near_a, near_b, far_a, far_b, d_out, d_other[:HALF])
 
     back_a = group_swap(far_a_grad, 0)
@@ -259,8 +287,8 @@
         out_shape=[jax.ShapeDtypeStruct((4 * HALF, 2 * HD), BF)] * 2,
         in_specs=[SMEM] + [VMEM] * 5,
         out_specs=[VMEM] * 2,
-        **params(2 * ROWS * 1024 * 3 * HD, 4 << 20),
-    )(place, own, from_a, from_b, dq, w_sel)
+        **params(2 * ROWS * 1024 * 3 * HD, 4 << 20, 8),
+    )(place, own, from_a, from_b, dq, w)
 
     arrived = across(send, 0, 1)
     chip = (keep.astype(F32) + arrived.astype(F32)).astype(BF)

time: 73.1 us -> 69.2 us (0.947)
  local copies, waits for them, and re-layouts: 4.47 us -> 2.38 us
  Pallas kernels: 8.91 us -> 7.11 us
  other arithmetic: 3.49 us -> 1.75 us
  waiting for transfers between devices: 22.3 us -> 23.8 us
    ppermute x10, waiting for transfers between devices: 13 us -> 14.9 us  [across(): return lax.ppermute(value, ('ctx', 'head'), pairs)]
    concatenate x1 -> x0, other arithmetic: 1.76 us -> none  [body(): other = across(jnp.concatenate([f, sx, sy, sd], axis=0), 0, 1)]
    reshape x1 -> x0, local copies, waits for them, and re-layouts: 1.52 us -> none  [body(): lax.dynamic_slice_in_dim(w_qkv, side * HD, HD, axis=2)]
    pallas_call x1, Pallas kernels: 5.66 us -> 4.52 us  [body(): pl.pallas_call(attend_kernel, name='attend', out_shape=[jax.ShapeDtypeStr...]
    unnamed x13 -> x10, local copies, waits for them, and re-layouts: 2.75 us -> 2.33 us
  transfers between devices with their start and end apart: 18 -> 18, of which waited for: 10 -> 11; matrix products, arithmetic and copies ran while one was open for 5% -> 2% of each run, Pallas kernels for 0% -> 0%
where the time goes in v2:
time: 69.2 us; the launch traced here: 69 us
  starting transfers between devices  33.1 us (48%)
  waiting for transfers between devices  23.8 us (34%)
  Pallas kernels  7.11 us (10%)
  local copies, waits for them, and re-layouts  2.38 us (3%)
  other arithmetic  1.75 us (3%)
  between operations  0.86 us (1%)
    ppermute x8, starting transfers between devices, group_swap(): return lax.ppermute(value, 'ctx', pairs)  21.7 us
    ppermute x10, waiting for transfers between devices, across(): return lax.ppermute(value, ('ctx', 'head'), pairs)  14.9 us
    ppermute x10, starting transfers between devices, across(): return lax.ppermute(value, ('ctx', 'head'), pairs)  11.4 us
    ppermute x8, waiting for transfers between devices, group_swap(): return lax.ppermute(value, 'ctx', pairs)  8.86 us
    pallas_call x1, Pallas kernels, body(): pl.pallas_call(attend_kernel, name='attend', out_shape=[jax.ShapeDtypeStr...  4.52 us
    unnamed x10, local copies, waits for them, and re-layouts  2.33 us
  transfers between devices with their start and end apart: 18, of which 11 were waited for; matrix products, arithmetic and copies ran while one was open for 2% of the time, Pallas kernels for 0%

profile of v2, /device:TPU:0, one launch (start us, length us, event | category | flops | bytes accessed | tf_op | source)
XLA Modules:
  0.0 69.0 jit_solution(18196991856725530292)
XLA Ops:
  0.6 3.0 %collective-permute-start.2 = (bf16[256,256]{1,0:T(8,128)(2,1)}, bf16[256,256]{1,0:T(8,128)(2,1)S(1)}, u32[]{:S(2)}, u32[]{:S(2)}) collective-permute-start(bf16[256,256]{1,0:T(8,128)(2,1)} %f.1), channel_id=1, source_target_pairs={{0,4},{1,5},{2,6},{3,7},{4,0},{5,1},{6,2},{7,3},{8,12},{9,13},{10,... | collective-permute-start | bytes 393224 | tf_op jit(solution)/shard_map/ppermute | solution.py:188
  3.7 1.5 %collective-permute-start.1 = (bf16[256,256]{1,0:T(8,128)(2,1)}, bf16[256,256]{1,0:T(8,128)(2,1)S(1)}, u32[]{:S(2)}, u32[]{:S(2)}) collective-permute-start(bf16[256,256]{1,0:T(8,128)(2,1)} %f.1), channel_id=1, source_target_pairs={{0,2},{1,3},{2,0},{3,1},{4,6},{5,7},{6,4},{7,5},{8,10},{9,11},{10,... | collective-permute-start | bytes 393224 | tf_op jit(solution)/shard_map/ppermute | solution.py:188
  5.2 2.2 %collective-permute-done.2.sy = bf16[256,256]{1,0:T(8,128)(2,1)S(1)} collective-permute-done((bf16[256,256]{1,0:T(8,128)(2,1)}, bf16[256,256]{1,0:T(8,128)(2,1)S(1)}, u32[]{:S(2)}, u32[]{:S(2)}) %collective-permute-start.2) | collective-permute-done | bytes 131104 | tf_op jit(solution)/shard_map/ppermute | solution.py:188
  7.4 2.9 %collective-permute-done.1.sx = bf16[256,256]{1,0:T(8,128)(2,1)S(1)} collective-permute-done((bf16[256,256]{1,0:T(8,128)(2,1)}, bf16[256,256]{1,0:T(8,128)(2,1)S(1)}, u32[]{:S(2)}, u32[]{:S(2)}) %collective-permute-start.1) | collective-permute-done | bytes 131104 | tf_op jit(solution)/shard_map/ppermute | solution.py:188
  10.2 1.2 %collective-permute-done.3.sd = bf16[256,256]{1,0:T(8,128)(2,1)S(1)} collective-permute-done((bf16[256,256]{1,0:T(8,128)(2,1)}, bf16[256,256]{1,0:T(8,128)(2,1)S(1)}, u32[]{:S(2)}, u32[]{:S(2)}) %collective-permute-start.3) | collective-permute-done | bytes 131104 | tf_op jit(solution)/shard_map/ppermute | solution.py:188
  11.4 0.9 %copy-done.2 = bf16[256,256]{1,0:T(8,128)(2,1)S(1)} copy-done((bf16[256,256]{1,0:T(8,128)(2,1)S(1)}, bf16[256,256]{1,0:T(8,128)(2,1)}, u32[]{:S(2)}) %copy-start.2) | copy-done | bytes 131096
  12.6 1.8 %collective-permute-done.4.other = bf16[1024,256]{1,0:T(8,128)(2,1)S(1)} collective-permute-done((bf16[1024,256]{1,0:T(8,128)(2,1)S(1)}, bf16[1024,256]{1,0:T(8,128)(2,1)S(1)}, u32[]{:S(2)}, u32[]{:S(2)}) %collective-permute-start.4) | collective-permute-done | bytes 524320 | tf_op jit(solution)/shard_map/ppermute | solution.py:188
  14.4 1.4 %copy-done = bf16[1024,3,256]{2,0,1:T(8,128)(2,1)S(1)} copy-done((bf16[1024,3,256]{2,0,1:T(8,128)(2,1)S(1)}, bf16[1024,3,256]{2,0,1:T(8,128)(2,1)}, u32[]{:S(2)}) %copy-start) | copy-done | bytes 1572888
  15.8 1.3 %project.1 = (bf16[512,128]{1,0:T(8,128)(2,1)S(1)}, bf16[512,256]{1,0:T(8,128)(2,1)S(1)}) custom-call(s32[4]{0:T(128)S(1)} %pad_add_fusion.place, bf16[1024,256]{1,0:T(8,128)(2,1)S(1)} %pack.1, bf16[1024,256]{1,0:T(8,128)(2,1)S(1)} %collective-permute-done.4.other, bf16[3,1024,256]{2,1,0:T(8,128)(2,1)S(1)} %bitcast.5), custom_call_target="tpu_custom_call" | custom-call | flops 402653184 | bytes 4194304 | tf_op jit(solution)/shard_map/project/pallas_call | solution.py:213
  17.0 0.7 collective-permute-start.6
  17.7 4.6 %collective-permute-start.5 = (bf16[512,256]{1,0:T(8,128)(2,1)S(1)}, bf16[512,256]{1,0:T(8,128)(2,1)S(1)}, u32[]{:S(2)}, u32[]{:S(2)}) collective-permute-start(bf16[512,256]{1,0:T(8,128)(2,1)S(1)} %get-tuple-element.27.kv), channel_id=1, source_target_pairs={{0,8},{8,0},{4,12},{12,4},{16,24},{24,16},{20,28},{28,20},{1,9},{9... | collective-permute-start | bytes 786440 | tf_op jit(solution)/shard_map/ppermute | solution.py:196
  22.4 1.6 %collective-permute-start = (bf16[272,128]{1,0:T(8,128)(2,1)S(1)}, bf16[272,128]{1,0:T(8,128)(2,1)S(1)}, u32[]{:S(2)}, u32[]{:S(2)}) collective-permute-start(bf16[272,128]{1,0:T(8,128)(2,1)S(1)} %fusion.3), channel_id=1, source_target_pairs={{0,4},{1,5},{2,6},{3,7},{4,0},{5,1},{6,2},{7,3},{8,12},{9,13},{10,... | collective-permute-start | bytes 208904 | tf_op jit(solution)/shard_map/ppermute | solution.py:188
  24.0 5.1 %collective-permute-start.7 = (bf16[256,256]{1,0:T(8,128)(2,1)S(1)}, bf16[256,256]{1,0:T(8,128)(2,1)S(1)}, u32[]{:S(2)}, u32[]{:S(2)}) collective-permute-start(bf16[256,256]{1,0:T(8,128)(2,1)S(1)} %constant_dynamic-slice_fusion.1), channel_id=1, source_target_pairs={{0,8},{8,0},{4,12},{12,4},{16,24},{24,16},{20,28},{28,20},{1,9},{9... | collective-permute-start | bytes 393224 | tf_op jit(solution)/shard_map/ppermute | solution.py:196
  29.1 0.7 collective-permute-start.8
  29.8 2.2 %collective-permute-done.7.far_a = bf16[256,256]{1,0:T(8,128)(2,1)S(1)} collective-permute-done((bf16[256,256]{1,0:T(8,128)(2,1)S(1)}, bf16[256,256]{1,0:T(8,128)(2,1)S(1)}, u32[]{:S(2)}, u32[]{:S(2)}) %collective-permute-start.7) | collective-permute-done | bytes 131104 | tf_op jit(solution)/shard_map/ppermute | solution.py:196
  32.1 4.5 %attend.1 = (bf16[256,128]{1,0:T(8,128)(2,1)S(1)}, bf16[256,128]{1,0:T(8,128)(2,1)S(1)}, bf16[512,128]{1,0:T(8,128)(2,1)S(1)}, f32[512,256]{1,0:T(8,128)S(1)}, b...) custom-call(s32[4]{0:T(128)S(1)} %pad_add_fusion.place, ...), custom_call_target="tpu_custom_call" | custom-call | flops 1811939328 | bytes 4194304 | tf_op jit(solution)/shard_map/attend/pallas_call | solution.py:244
  36.6 5.3 %collective-permute-start.12 = (bf16[256,256]{1,0:T(8,128)(2,1)S(1)}, bf16[256,256]{1,0:T(8,128)(2,1)S(1)}, u32[]{:S(2)}, u32[]{:S(2)}) collective-permute-start(bf16[256,256]{1,0:T(8,128)(2,1)S(1)} %get-tuple-element.34), channel_id=1, source_target_pairs={{0,8},{8,0},{4,12},{12,4},{16,24},{24,16},{20,28},{28,20},{1,9},{9... | collective-permute-start | bytes 393224 | tf_op jit(solution)/shard_map/ppermute | solution.py:196
  41.9 0.7 collective-permute-start.10
  42.5 2.3 %collective-permute-done.12 = bf16[256,256]{1,0:T(8,128)(2,1)S(1)} collective-permute-done((bf16[256,256]{1,0:T(8,128)(2,1)S(1)}, bf16[256,256]{1,0:T(8,128)(2,1)S(1)}, u32[]{:S(2)}, u32[]{:S(2)}) %collective-permute-start.12) | collective-permute-done | bytes 131104 | tf_op jit(solution)/shard_map/ppermute | solution.py:196
  44.9 0.7 collective-permute-start.13
  45.6 4.0 %collective-permute-start.11 = (bf16[512,256]{1,0:T(8,128)(2,1)S(1)}, bf16[512,256]{1,0:T(8,128)(2,1)S(1)}, u32[]{:S(2)}, u32[]{:S(2)}) collective-permute-start(bf16[512,256]{1,0:T(8,128)(2,1)S(1)} %fusion.1), channel_id=1, source_target_pairs={{0,8},{8,0},{4,12},{12,4},{16,24},{24,16},{20,28},{28,20},{1,9},{9... | collective-permute-start | bytes 786440 | tf_op jit(solution)/shard_map/ppermute | solution.py:196
  49.6 4.3 %collective-permute-done.11.from_a = bf16[512,256]{1,0:T(8,128)(2,1)S(1)} collective-permute-done((bf16[512,256]{1,0:T(8,128)(2,1)S(1)}, bf16[512,256]{1,0:T(8,128)(2,1)S(1)}, u32[]{:S(2)}, u32[]{:S(2)}) %collective-permute-start.11) | collective-permute-done | bytes 262176 | tf_op jit(solution)/shard_map/ppermute | solution.py:196
  54.0 1.3 %spread.1 = (bf16[1024,256]{1,0:T(8,128)(2,1)S(1)}, bf16[1024,256]{1,0:T(8,128)(2,1)S(1)}) custom-call(s32[4]{0:T(128)S(1)} %pad_add_fusion.place, f32[512,256]{1,0:T(8,128)S(1)} %get-tuple-element.30.own, bf16[512,256]{1,0:T(8,128)(2,1)S(1)} %collective-permute-done.11.from_a, bf16[512,256]{1,0:T(8,128)(2,1)S(1)} %collective-permute-done.13.from_b, ...), custom_call_target="tpu_custom_call" | custom-call | flops 402653184 | bytes 4194304 | tf_op jit(solution)/shard_map/spread/pallas_call | solution.py:284
  55.3 1.6 %collective-permute-start.9 = (bf16[256,128]{1,0:T(8,128)(2,1)S(1)}, bf16[256,128]{1,0:T(8,128)(2,1)S(1)}, u32[]{:S(2)}, u32[]{:S(2)}) collective-permute-start(bf16[256,128]{1,0:T(8,128)(2,1)S(1)} %get-tuple-element.29), channel_id=1, source_target_pairs={{0,4},{1,5},{2,6},{3,7},{4,0},{5,1},{6,2},{7,3},{8,12},{9,13},{10,... | collective-permute-start | bytes 196616 | tf_op jit(solution)/shard_map/ppermute | solution.py:188
  57.4 1.5 %collective-permute-start.15 = (bf16[256,256]{1,0:T(8,128)(2,1)S(1)}, bf16[256,256]{1,0:T(8,128)(2,1)S(1)}, u32[]{:S(2)}, u32[]{:S(2)}) collective-permute-start(bf16[256,256]{1,0:T(8,128)(2,1)S(1)} %get-tuple-element.38), channel_id=1, source_target_pairs={{0,2},{1,3},{2,0},{3,1},{4,6},{5,7},{6,4},{7,5},{8,10},{9,11},{10,... | collective-permute-start | bytes 393224 | tf_op jit(solution)/shard_map/ppermute | solution.py:188
  59.0 1.5 %collective-permute-start.17 = (bf16[256,256]{1,0:T(8,128)(2,1)S(1)}, bf16[256,256]{1,0:T(8,128)(2,1)S(1)}, u32[]{:S(2)}, u32[]{:S(2)}) collective-permute-start(bf16[256,256]{1,0:T(8,128)(2,1)S(1)} %get-tuple-element.39), channel_id=1, source_target_pairs={{0,6},{1,7},{2,4},{3,5},{4,2},{5,3},{6,0},{7,1},{8,14},{9,15},{10,... | collective-permute-start | bytes 393224 | tf_op jit(solution)/shard_map/ppermute | solution.py:188
  60.5 0.5 collective-permute-start.16
  61.0 0.7 %maximum_select_fusion = bf16[256,256]{1,0:T(8,128)(2,1)} fusion(bf16[256,128]{1,0:T(8,128)(2,1)S(1)} %collective-permute-done.9, bf16[256,128]{1,0:T(8,128)(2,1)S(1)} %get-tuple-element.28, pred[]{:T(512)S(6)} %eq.7), kind=kLoop, calls=%fused_computation.8 | loop fusion | flops 589824 | bytes 262145 | tf_op jit(solution)/shard_map/jit(_where)/select_n | solution.py:278
  61.7 2.0 %collective-permute-done.15 = bf16[256,256]{1,0:T(8,128)(2,1)S(1)} collective-permute-done((bf16[256,256]{1,0:T(8,128)(2,1)S(1)}, bf16[256,256]{1,0:T(8,128)(2,1)S(1)}, u32[]{:S(2)}, u32[]{:S(2)}) %collective-permute-start.15) | collective-permute-done | bytes 131104 | tf_op jit(solution)/shard_map/ppermute | solution.py:188
  63.6 3.3 %collective-permute-done.17 = bf16[256,256]{1,0:T(8,128)(2,1)S(1)} collective-permute-done((bf16[256,256]{1,0:T(8,128)(2,1)S(1)}, bf16[256,256]{1,0:T(8,128)(2,1)S(1)}, u32[]{:S(2)}, u32[]{:S(2)}) %collective-permute-start.17) | collective-permute-done | bytes 131104 | tf_op jit(solution)/shard_map/ppermute | solution.py:188
  66.9 1.4 %collective-permute-done.16 = bf16[256,256]{1,0:T(8,128)(2,1)S(1)} collective-permute-done((bf16[256,256]{1,0:T(8,128)(2,1)S(1)}, bf16[256,256]{1,0:T(8,128)(2,1)S(1)}, u32[]{:S(2)}, u32[]{:S(2)}) %collective-permute-start.16) | collective-permute-done | bytes 131104 | tf_op jit(solution)/shard_map/ppermute | solution.py:188
  68.3 0.7 %add_convert_fusion.1 = bf16[256,256]{1,0:T(8,128)(2,1)} fusion(bf16[256,256]{1,0:T(8,128)(2,1)S(1)} %collective-permute-done.17, bf16[256,256]{1,0:T(8,128)(2,1)S(1)} %collective-permute-done.16, bf16[256,256]{1,0:T(8,128)(2,1)S(1)} %collective-permute-done.15, bf16[1024,256]{1,0:T(8,128)(2,1)S(1)} %add_convert_fusion), kind=kLoop, calls=%fused_computation.1 | loop fusion | flops 524288 | bytes 655360 | tf_op jit(solution)/shard_map/convert_element_type | solution.py:300
  (33 shorter events, 1.0 us)
Async XLA Ops:
  0.6 6.7 %collective-permute-start.2 = (bf16[256,256]{1,0:T(8,128)(2,1)}, bf16[256,256]{1,0:T(8,128)(2,1)S(1)}, u32[]{:S(2)}, u32[]{:S(2)}) collective-permute-start(bf16[256,256]{1,0:T(8,128)(2,1)} %f.1), channel_id=1, source_target_pairs={{0,4},{1,5},{2,6},{3,7},{4,0},{5,1},{6,2},{7,3},{8,12},{9,13},{10,... | collective-permute-start | bytes 393224 | tf_op jit(solution)/shard_map/ppermute | solution.py:188
  3.7 6.6 %collective-permute-start.1 = (bf16[256,256]{1,0:T(8,128)(2,1)}, bf16[256,256]{1,0:T(8,128)(2,1)S(1)}, u32[]{:S(2)}, u32[]{:S(2)}) collective-permute-start(bf16[256,256]{1,0:T(8,128)(2,1)} %f.1), channel_id=1, source_target_pairs={{0,2},{1,3},{2,0},{3,1},{4,6},{5,7},{6,4},{7,5},{8,10},{9,11},{10,... | collective-permute-start | bytes 393224 | tf_op jit(solution)/shard_map/ppermute | solution.py:188
  5.2 6.3 %collective-permute-start.3 = (bf16[256,256]{1,0:T(8,128)(2,1)}, bf16[256,256]{1,0:T(8,128)(2,1)S(1)}, u32[]{:S(2)}, u32[]{:S(2)}) collective-permute-start(bf16[256,256]{1,0:T(8,128)(2,1)} %f.1), channel_id=1, source_target_pairs={{0,6},{1,7},{2,4},{3,5},{4,2},{5,3},{6,0},{7,1},{8,14},{9,15},{10,... | collective-permute-start | bytes 393224 | tf_op jit(solution)/shard_map/ppermute | solution.py:188
  11.4 0.9 %copy-start.2 = (bf16[256,256]{1,0:T(8,128)(2,1)S(1)}, bf16[256,256]{1,0:T(8,128)(2,1)}, u32[]{:S(2)}) copy-start(bf16[256,256]{1,0:T(8,128)(2,1)} %f.1) | copy-start | bytes 393220
  12.3 10.0 %copy-start.3 = (bf16[256,256]{1,0:T(8,128)(2,1)S(1)}, bf16[256,256]{1,0:T(8,128)(2,1)}, u32[]{:S(2)}) copy-start(bf16[256,256]{1,0:T(8,128)(2,1)} %d_own.1) | copy-start | bytes 393220
  12.4 10.0 %copy-start.4 = (s32[2,9]{1,0:T(2,128)S(1)}, s32[2,9]{1,0:T(2,128)}, u32[]{:S(2)}) copy-start(s32[2,9]{1,0:T(2,128)} %param.8) | copy-start | bytes 220
  12.4 2.0 %collective-permute-start.4 = (bf16[1024,256]{1,0:T(8,128)(2,1)S(1)}, bf16[1024,256]{1,0:T(8,128)(2,1)S(1)}, u32[]{:S(2)}, u32[]{:S(2)}) collective-permute-start(bf16[1024,256]{1,0:T(8,128)(2,1)S(1)} %pack.1), channel_id=1, source_target_pairs={{0,1},{1,0},{2,3},{3,2},{4,5},{5,4},{6,7},{7,6},{8,9},{9,8},{10,11... | collective-permute-start | bytes 1572872 | tf_op jit(solution)/shard_map/ppermute | solution.py:188
  14.4 1.4 %copy-start = (bf16[1024,3,256]{2,0,1:T(8,128)(2,1)S(1)}, bf16[1024,3,256]{2,0,1:T(8,128)(2,1)}, u32[]{:S(2)}) copy-start(bf16[1024,3,256]{2,0,1:T(8,128)(2,1)} %param.7) | copy-start | bytes 4718596
  17.0 6.9 %collective-permute-start.6 = (bf16[512,256]{1,0:T(8,128)(2,1)S(1)}, bf16[512,256]{1,0:T(8,128)(2,1)S(1)}, u32[]{:S(2)}, u32[]{:S(2)}) collective-permute-start(bf16[512,256]{1,0:T(8,128)(2,1)S(1)} %get-tuple-element.27.kv), channel_id=1, source_target_pairs={{8,16},{16,8},{12,20},{20,12},{9,17},{17,9},{13,21},{21,13},{10,18... | collective-permute-start | bytes 786440 | tf_op jit(solution)/shard_map/ppermute | solution.py:196
  17.7 11.4 %collective-permute-start.5 = (bf16[512,256]{1,0:T(8,128)(2,1)S(1)}, bf16[512,256]{1,0:T(8,128)(2,1)S(1)}, u32[]{:S(2)}, u32[]{:S(2)}) collective-permute-start(bf16[512,256]{1,0:T(8,128)(2,1)S(1)} %get-tuple-element.27.kv), channel_id=1, source_target_pairs={{0,8},{8,0},{4,12},{12,4},{16,24},{24,16},{20,28},{28,20},{1,9},{9... | collective-permute-start | bytes 786440 | tf_op jit(solution)/shard_map/ppermute | solution.py:196
  22.4 7.4 %collective-permute-start = (bf16[272,128]{1,0:T(8,128)(2,1)S(1)}, bf16[272,128]{1,0:T(8,128)(2,1)S(1)}, u32[]{:S(2)}, u32[]{:S(2)}) collective-permute-start(bf16[272,128]{1,0:T(8,128)(2,1)S(1)} %fusion.3), channel_id=1, source_target_pairs={{0,4},{1,5},{2,6},{3,7},{4,0},{5,1},{6,2},{7,3},{8,12},{9,13},{10,... | collective-permute-start | bytes 208904 | tf_op jit(solution)/shard_map/ppermute | solution.py:188
  24.0 8.1 %collective-permute-start.7 = (bf16[256,256]{1,0:T(8,128)(2,1)S(1)}, bf16[256,256]{1,0:T(8,128)(2,1)S(1)}, u32[]{:S(2)}, u32[]{:S(2)}) collective-permute-start(bf16[256,256]{1,0:T(8,128)(2,1)S(1)} %constant_dynamic-slice_fusion.1), channel_id=1, source_target_pairs={{0,8},{8,0},{4,12},{12,4},{16,24},{24,16},{20,28},{28,20},{1,9},{9... | collective-permute-start | bytes 393224 | tf_op jit(solution)/shard_map/ppermute | solution.py:196
  29.1 3.0 %collective-permute-start.8 = (bf16[256,256]{1,0:T(8,128)(2,1)S(1)}, bf16[256,256]{1,0:T(8,128)(2,1)S(1)}, u32[]{:S(2)}, u32[]{:S(2)}) collective-permute-start(bf16[256,256]{1,0:T(8,128)(2,1)S(1)} %constant_dynamic-slice_fusion), channel_id=1, source_target_pairs={{8,16},{16,8},{12,20},{20,12},{9,17},{17,9},{13,21},{21,13},{10,18... | collective-permute-start | bytes 393224 | tf_op jit(solution)/shard_map/ppermute | solution.py:196
  32.1 21.9 %copy-start.1 = (bf16[1024,3,256]{2,0,1:T(8,128)(2,1)S(1)}, bf16[1024,3,256]{2,0,1:T(8,128)(2,1)}, u32[]{:S(2)}) copy-start(bf16[1024,3,256]{2,0,1:T(8,128)(2,1)} %param.7) | copy-start | bytes 4718596
  36.6 8.2 %collective-permute-start.12 = (bf16[256,256]{1,0:T(8,128)(2,1)S(1)}, bf16[256,256]{1,0:T(8,128)(2,1)S(1)}, u32[]{:S(2)}, u32[]{:S(2)}) collective-permute-start(bf16[256,256]{1,0:T(8,128)(2,1)S(1)} %get-tuple-element.34), channel_id=1, source_target_pairs={{0,8},{8,0},{4,12},{12,4},{16,24},{24,16},{20,28},{28,20},{1,9},{9... | collective-permute-start | bytes 393224 | tf_op jit(solution)/shard_map/ppermute | solution.py:196
  41.9 3.7 %collective-permute-start.10 = (bf16[256,256]{1,0:T(8,128)(2,1)S(1)}, bf16[256,256]{1,0:T(8,128)(2,1)S(1)}, u32[]{:S(2)}, u32[]{:S(2)}) collective-permute-start(bf16[256,256]{1,0:T(8,128)(2,1)S(1)} %get-tuple-element.32), channel_id=1, source_target_pairs={{8,16},{16,8},{12,20},{20,12},{9,17},{17,9},{13,21},{21,13},{10,18... | collective-permute-start | bytes 393224 | tf_op jit(solution)/shard_map/ppermute | solution.py:196
  44.9 4.7 %collective-permute-start.13 = (bf16[512,256]{1,0:T(8,128)(2,1)S(1)}, bf16[512,256]{1,0:T(8,128)(2,1)S(1)}, u32[]{:S(2)}, u32[]{:S(2)}) collective-permute-start(bf16[512,256]{1,0:T(8,128)(2,1)S(1)} %fusion.2), channel_id=1, source_target_pairs={{8,16},{16,8},{12,20},{20,12},{9,17},{17,9},{13,21},{21,13},{10,18... | collective-permute-start | bytes 786440 | tf_op jit(solution)/shard_map/ppermute | solution.py:196
  45.6 8.3 %collective-permute-start.11 = (bf16[512,256]{1,0:T(8,128)(2,1)S(1)}, bf16[512,256]{1,0:T(8,128)(2,1)S(1)}, u32[]{:S(2)}, u32[]{:S(2)}) collective-permute-start(bf16[512,256]{1,0:T(8,128)(2,1)S(1)} %fusion.1), channel_id=1, source_target_pairs={{0,8},{8,0},{4,12},{12,4},{16,24},{24,16},{20,28},{28,20},{1,9},{9... | collective-permute-start | bytes 786440 | tf_op jit(solution)/shard_map/ppermute | solution.py:196
  55.3 2.0 %collective-permute-start.14 = (bf16[1024,256]{1,0:T(8,128)(2,1)S(1)}, bf16[1024,256]{1,0:T(8,128)(2,1)S(1)}, u32[]{:S(2)}, u32[]{:S(2)}) collective-permute-start(bf16[1024,256]{1,0:T(8,128)(2,1)S(1)} %get-tuple-element.37), channel_id=1, source_target_pairs={{0,1},{1,0},{2,3},{3,2},{4,5},{5,4},{6,7},{7,6},{8,9},{9,8},{10,11... | collective-permute-start | bytes 1572872 | tf_op jit(solution)/shard_map/ppermute | solution.py:188
  55.3 5.6 %collective-permute-start.9 = (bf16[256,128]{1,0:T(8,128)(2,1)S(1)}, bf16[256,128]{1,0:T(8,128)(2,1)S(1)}, u32[]{:S(2)}, u32[]{:S(2)}) collective-permute-start(bf16[256,128]{1,0:T(8,128)(2,1)S(1)} %get-tuple-element.29), channel_id=1, source_target_pairs={{0,4},{1,5},{2,6},{3,7},{4,0},{5,1},{6,2},{7,3},{8,12},{9,13},{10,... | collective-permute-start | bytes 196616 | tf_op jit(solution)/shard_map/ppermute | solution.py:188
  57.4 6.2 %collective-permute-start.15 = (bf16[256,256]{1,0:T(8,128)(2,1)S(1)}, bf16[256,256]{1,0:T(8,128)(2,1)S(1)}, u32[]{:S(2)}, u32[]{:S(2)}) collective-permute-start(bf16[256,256]{1,0:T(8,128)(2,1)S(1)} %get-tuple-element.38), channel_id=1, source_target_pairs={{0,2},{1,3},{2,0},{3,1},{4,6},{5,7},{6,4},{7,5},{8,10},{9,11},{10,... | collective-permute-start | bytes 393224 | tf_op jit(solution)/shard_map/ppermute | solution.py:188
  59.0 7.9 %collective-permute-start.17 = (bf16[256,256]{1,0:T(8,128)(2,1)S(1)}, bf16[256,256]{1,0:T(8,128)(2,1)S(1)}, u32[]{:S(2)}, u32[]{:S(2)}) collective-permute-start(bf16[256,256]{1,0:T(8,128)(2,1)S(1)} %get-tuple-element.39), channel_id=1, source_target_pairs={{0,6},{1,7},{2,4},{3,5},{4,2},{5,3},{6,0},{7,1},{8,14},{9,15},{10,... | collective-permute-start | bytes 393224 | tf_op jit(solution)/shard_map/ppermute | solution.py:188
  60.5 7.8 %collective-permute-start.16 = (bf16[256,256]{1,0:T(8,128)(2,1)S(1)}, bf16[256,256]{1,0:T(8,128)(2,1)S(1)}, u32[]{:S(2)}, u32[]{:S(2)}) collective-permute-start(bf16[256,256]{1,0:T(8,128)(2,1)S(1)} %get-tuple-element.40), channel_id=1, source_target_pairs={{0,4},{1,5},{2,6},{3,7},{4,0},{5,1},{6,2},{7,3},{8,12},{9,13},{10,... | collective-permute-start | bytes 393224 | tf_op jit(solution)/shard_map/ppermute | solution.py:188

commit v3 on v2

--- a/solution.py
+++ b/solution.py
@@ -41,9 +41,11 @@
     return lax.dot_general(a, b, (dims, ((), ())), preferred_element_type=F32)
 
 
-def pack_kernel(f, sx, sy, sd, out):
-    for index, piece in enumerate((f, sx, sy, sd)):
-        out[index * HALF : (index + 1) * HALF, :] = piece[...]
+def pack_kernel(near, far, begun, out):
+    out[:HALF, :] = begun[:HALF, :]
+    out[HALF : 2 * HALF, :] = near[...]
+    out[2 * HALF : 3 * HALF, :] = begun[HALF:, :]
+    out[3 * HALF :, :] = far[...]
 
 
 def weight_rows(w, source, side, groups):
@@ -53,37 +55,68 @@
     return jnp.concatenate([w[g, rows, cols] for g in groups], axis=1)
 
 
-def project_kernel(place, pack, other, w, q_out, kv_out):
-    side, head = place[0], place[3]
+def project_near_kernel(place, near, far, w, total, pack):
+    rows = jnp.concatenate([near[...], far[...]], axis=0)
+    pack[...] = rows
+    total[...] = dot(rows, weight_rows(w, place[3], place[0], (0, 1, 2)), ((1,), (0,)))
+
+
+def project_across_kernel(place, near, far, before, w, total):
+    rows = jnp.concatenate([near[...], far[...]], axis=0)
+    total[...] = before[...] + dot(rows, weight_rows(w, place[3] ^ 2, place[0], (0, 1, 2)), ((1,), (0,)))
+
+
+def sibling_product(place, other, w, groups):
     total = None
-    for source, store, index in ((head, pack, 0), (head ^ 2, pack, 1), (head ^ 1, other, 0), (head ^ 3, other, 1)):
-        rows = [store[(2 * group + index) * HALF : (2 * group + index + 1) * HALF, :] for group in range(2)]
-        term = dot(jnp.concatenate(rows, axis=0), weight_rows(w, source, side, (0, 1, 2)), ((1,), (0,)))
+    for index in range(2):
+        rows = [other[(2 * group + index) * HALF : (2 * group + index + 1) * HALF, :] for group in range(2)]
+        source = place[3] ^ (1 + 2 * index)
+        term = dot(jnp.concatenate(rows, axis=0), weight_rows(w, source, place[0], groups), ((1,), (0,)))
         total = term if total is None else total + term
+    return total
+
+
+def project_kv_kernel(place, other, before, w, first_out, second_out, kv):
+    kv[...] = (before[:, HD:] + sibling_product(place, other, w, (1, 2))).astype(BF)
+    start = (place[0] ^ (1 - place[1])) * HALF
+    first_out[...] = kv[pl.ds(pl.multiple_of(start, HALF), HALF), :]
+    second_out[...] = kv[pl.ds(pl.multiple_of(HALF - start, HALF), HALF), :]
+
+
+def project_q_kernel(place, other, before, w, q_out):
+    total = (before[:, :HD] + sibling_product(place, other, w, (0,))).astype(BF)
     for group in range(2):
-        rows = pl.ds(pl.multiple_of((side ^ group) * HALF, HALF), HALF)
-        part = total[group * HALF : (group + 1) * HALF]
-        q_out[rows, :] = part[:, :HD].astype(BF)
-        kv_out[rows, :] = part[:, HD:].astype(BF)
+        rows = pl.ds(pl.multiple_of((place[0] ^ group) * HALF, HALF), HALF)
+        q_out[rows, :] = total[group * HALF : (group + 1) * HALF]
+
+
+def regions(odd):
+    even = 1 - odd
+    left_lo, left_hi = NEAR_LEFT, NEAR_LEFT + HALF
+    right_lo, right_hi = NEAR_RIGHT, NEAR_RIGHT + HALF
+    pick = lambda at_even, at_odd: pl.multiple_of(even * at_even + odd * at_odd, HALF)
+    return (
+        pick(OWN + HALF, OWN),
+        pick(OWN, OWN + HALF),
+        pick(right_lo, left_hi),
+        pick(right_hi, left_lo),
+        pick(left_hi, right_lo),
+        pick(left_lo, right_hi),
+        pick(FAR_RIGHT, 0),
+        pick(0, FAR_RIGHT),
+    )
 
 
 def attend_kernel(
-    place, links, q, kv, near_a, near_b, far_a, far_b, d_own, d_other,
-    att_own, att_other, dq_out, own_out, a_out, b_out, far_a_out, far_b_out,
+    place, links, q, first_kv, second_kv, a1, a2, b1, b2, far_a, far_b, d_own, d_other,
+    att_own, att_other, dq_out, first_out, second_out, a1_out, a2_out, b1_out, b2_out, far_a_out, far_b_out,
     win, acc, att,
 ):
     side, odd, first = place[0], place[1], place[2]
     scale = HD ** -0.5
-    even = 1 - odd
-    at_a = pl.multiple_of(even * NEAR_RIGHT + odd * NEAR_LEFT, BLK)
-    at_b = pl.multiple_of(odd * NEAR_RIGHT + even * NEAR_LEFT, BLK)
-    at_far_a = pl.multiple_of(even * FAR_RIGHT, BLK)
-    at_far_b = pl.multiple_of(odd * FAR_RIGHT, BLK)
-    win[OWN : OWN + ROWS, :] = kv[...]
-    win[pl.ds(at_a, ROWS), :] = near_a[...]
-    win[pl.ds(at_b, ROWS), :] = near_b[...]
-    win[pl.ds(at_far_a, HALF), :] = far_a[...]
-    win[pl.ds(at_far_b, HALF), :] = far_b[...]
+    places = regions(odd)
+    for at, source in zip(places, (first_kv, second_kv, a1, a2, b1, b2, far_a, far_b)):
+        win[pl.ds(at, HALF), :] = source[...]
     acc[...] = jnp.zeros_like(acc)
     zeros = jnp.zeros((BLK, HD), BF)
     own_cols = pl.ds(pl.multiple_of(side * HD, HD), HD)
@@ -150,25 +183,32 @@
     att_own[...] = att[pl.ds(pl.multiple_of(side * HALF, HALF), HALF), :]
     att_other[...] = att[pl.ds(pl.multiple_of((1 - side) * HALF, HALF), HALF), :]
     factor = jnp.where(lax.broadcasted_iota(jnp.int32, (1, 2 * HD), 1) < HD, scale, 1.0).astype(F32)
-    own_out[...] = acc[OWN : OWN + ROWS, :] * factor
-    a_out[...] = (acc[pl.ds(at_a, ROWS), :] * factor).astype(BF)
-    b_out[...] = (acc[pl.ds(at_b, ROWS), :] * factor).astype(BF)
-    far_a_out[...] = (acc[pl.ds(at_far_a, HALF), :] * factor).astype(BF)
-    far_b_out[...] = (acc[pl.ds(at_far_b, HALF), :] * factor).astype(BF)
-
-
-def spread_kernel(place, own, from_a, from_b, dq, w, keep, send):
-    side, head = place[0], place[3]
-    dkv = (own[...] + from_a[...].astype(F32) + from_b[...].astype(F32)).astype(BF)
-    grads = jnp.concatenate([dq[...], dkv], axis=1)
-    for step in range(4):
-        dest = head ^ step
-        out = dot(grads, weight_rows(w, dest, side, (0, 1, 2)), ((1,), (1,))).astype(BF)
-        target = keep if step % 2 == 0 else send
+    targets = (first_out, second_out, a1_out, a2_out, b1_out, b2_out, far_a_out, far_b_out)
+    for at, target in zip(places, targets):
+        target[...] = (acc[pl.ds(at, HALF), :] * factor).astype(target.dtype)
+
+
+def spread_send_kernel(place, first_own, second_own, a1, b2, b1, a2, dq, w, send, grads):
+    side, odd, head = place[0], place[1], place[3]
+    grads[:, :HD] = dq[...]
+    first = first_own[...] + a1[...].astype(F32) + b2[...].astype(F32)
+    second = second_own[...] + b1[...].astype(F32) + a2[...].astype(F32)
+    grads[pl.ds(pl.multiple_of((1 - odd) * HALF, HALF), HALF), HD:] = first.astype(BF)
+    grads[pl.ds(pl.multiple_of(odd * HALF, HALF), HALF), HD:] = second.astype(BF)
+    spread(grads, w, side, head ^ 1, send)
+
+
+def spread(grads, w, side, head, target):
+    for step in range(2):
+        out = dot(grads[...], weight_rows(w, head ^ (2 * step), side, (0, 1, 2)), ((1,), (1,))).astype(BF)
         for group in range(2):
-            index = 2 * group + step // 2
+            index = 2 * group + step
             part = jnp.where(side == group, out[:HALF], out[HALF:])
             target[index * HALF : (index + 1) * HALF, :] = part
+
+
+def spread_keep_kernel(place, grads, w, keep):
+    spread(grads, w, place[0], place[3], keep)
 
 
 def body(features, w_qkv, block_links, d_out, n_ctx, n_head):
@@ -200,32 +240,46 @@
     sy = across(f, 1, 0)
     sd = across(f, 1, 2)
     w = jnp.transpose(w_qkv, (1, 0, 2))
-    pack = pl.pallas_call(
-        pack_kernel,
-        name="pack",
-        out_shape=jax.ShapeDtypeStruct((4 * f.shape[0], f.shape[1]), BF),
-        in_specs=[VMEM] * 4,
-        out_specs=VMEM,
-        **params(0, 1 << 20, 4),
-    )(f, sx, sy, sd)
+    def call(kernel, name, outs, ins, moved, mebibytes, flops, scratch=()):
+        return pl.pallas_call(
+            kernel,
+            name=name,
+            out_shape=outs,
+            in_specs=[SMEM if v.dtype == jnp.int32 else VMEM for v in ins],
+            out_specs=jax.tree.map(lambda _: VMEM, outs),
+            scratch_shapes=list(scratch),
+            **params(flops, moved, mebibytes),
+        )(*ins)
+
+    def out(rows, cols, kind=BF):
+        return jax.ShapeDtypeStruct((rows, cols), kind)
+
+    product = 2 * ROWS * f.shape[1] * 3 * HD
+    total, begun = call(
+        project_near_kernel,
+        "project_near",
+        [out(ROWS, 3 * HD, F32), out(ROWS, f.shape[1])],
+        (place, f, sy, w),
+        2 << 20,
+        8,
+        product,
+    )
+    pack = call(pack_kernel, "pack", out(4 * HALF, f.shape[1]), (sx, sd, begun), 1 << 20, 4, 0)
     other = across(pack, 0, 1)
-
-    q, kv = pl.pallas_call(
-        project_kernel,
-        name="project",
-        out_shape=[
-            jax.ShapeDtypeStruct((ROWS, HD), BF),
-            jax.ShapeDtypeStruct((ROWS, 2 * HD), BF),
-        ],
-        in_specs=[SMEM] + [VMEM] * 3,
-        out_specs=[VMEM] * 2,
-        **params(2 * ROWS * 1024 * 3 * HD, 4 << 20, 8),
-    )(place, pack, other, w)
-
-    near_a = group_swap(kv, 0)
-    near_b = group_swap(kv, 1)
-    far_b = group_swap(lax.dynamic_slice_in_dim(near_a, odd * HALF, HALF, axis=0), 1)
-    far_a = group_swap(lax.dynamic_slice_in_dim(near_b, (1 - odd) * HALF, HALF, axis=0), 0)
+    total = call(
+        project_across_kernel, "project_across", out(ROWS, 3 * HD, F32), (place, sx, sd, total, w), 2 << 20, 8, product
+    )
+    first, second = call(
+        project_kv_kernel, "project_kv", [out(HALF, 2 * HD)] * 2, (place, other, total, w), 2 << 20, 8, product,
+        [pltpu.VMEM((ROWS, 2 * HD), BF)],
+    )
+    a1 = group_swap(first, 0)
+    b1 = group_swap(second, 1)
+    a2 = group_swap(second, 0)
+    b2 = group_swap(first, 1)
+    q = call(project_q_kernel, "project_q", out(ROWS, HD), (place, other, total, w), 2 << 20, 8, product)
+    far_b = group_swap(a1, 1)
+    far_a = group_swap(b1, 0)
 
     link_rows = jnp.zeros((16, HD), BF).at[: block_links.shape[0], : block_links.shape[1]].set(
         block_links.astype(BF)
@@ -241,39 +295,30 @@
         jnp.concatenate([other_links, block_links], axis=0),
     )
 
-    att_own, att_other, dq, own, near_a_grad, near_b_grad, far_a_grad, far_b_grad = pl.pallas_call(
+    (
+        att_own, att_other, dq, first_own, second_own,
+        a1_grad, a2_grad, b1_grad, b2_grad, far_a_grad, far_b_grad,
+    ) = call(
         attend_kernel,
-        name="attend",
-        out_shape=[
-            jax.ShapeDtypeStruct((HALF, HD), BF),
-            jax.ShapeDtypeStruct((HALF, HD), BF),
-            jax.ShapeDtypeStruct((ROWS, HD), BF),
-            jax.ShapeDtypeStruct((ROWS, 2 * HD), F32),
-            jax.ShapeDtypeStruct((ROWS, 2 * HD), BF),
-            jax.ShapeDtypeStruct((ROWS, 2 * HD), BF),
-            jax.ShapeDtypeStruct((HALF, 2 * HD), BF),
-            jax.ShapeDtypeStruct((HALF, 2 * HD), BF),
-        ],
-        in_specs=[SMEM] * 2 + [VMEM] * 8,
-        out_specs=[VMEM] * 8,
-        scratch_shapes=[
+        "attend",
+        [out(HALF, HD)] * 2 + [out(ROWS, HD)] + [out(HALF, 2 * HD, F32)] * 2 + [out(HALF, 2 * HD)] * 6,
+        (place, links, q, first, second, a1, a2, b1, b2, far_a, far_b, d_out, d_other[:HALF]),
+        4 << 20,
+        16,
+        6 * 2 * GROUP * 9 * BLK * BLK * 2 * HD,
+        [
             pltpu.VMEM((WINDOW * BLK, 2 * HD), BF),
             pltpu.VMEM((WINDOW * BLK, 2 * HD), F32),
             pltpu.VMEM((ROWS, HD), BF),
         ],
-        **params(6 * 2 * GROUP * 9 * BLK * BLK * 2 * HD, 4 << 20, 16),
-    )(place, links, q, kv, near_a, near_b, far_a, far_b, d_out, d_other[:HALF])
+    )
 
     back_a = group_swap(far_a_grad, 0)
     back_b = group_swap(far_b_grad, 1)
-
-    def add_half(whole, part, start):
-        old = lax.dynamic_slice_in_dim(whole, start, HALF, axis=0)
-        new = (old.astype(F32) + part.astype(F32)).astype(BF)
-        return lax.dynamic_update_slice_in_dim(whole, new, start, axis=0)
-
-    from_b = group_swap(add_half(near_b_grad, back_a, (1 - odd) * HALF), 1)
-    from_a = group_swap(add_half(near_a_grad, back_b, odd * HALF), 0)
+    a2_back = group_swap(a2_grad, 0)
+    b2_back = group_swap(b2_grad, 1)
+    b1_back = group_swap((b1_grad.astype(F32) + back_a.astype(F32)).astype(BF), 1)
+    a1_back = group_swap((a1_grad.astype(F32) + back_b.astype(F32)).astype(BF), 0)
     att_back = across(att_other, 1, 0)
     attended = jnp.where(
         side == 0,
@@ -281,15 +326,16 @@
         jnp.concatenate([att_back, att_own], axis=1),
     )
 
-    keep, send = pl.pallas_call(
-        spread_kernel,
-        name="spread",
-        out_shape=[jax.ShapeDtypeStruct((4 * HALF, 2 * HD), BF)] * 2,
-        in_specs=[SMEM] + [VMEM] * 5,
-        out_specs=[VMEM] * 2,
-        **params(2 * ROWS * 1024 * 3 * HD, 4 << 20, 8),
-    )(place, own, from_a, from_b, dq, w)
-
+    send, grads = call(
+        spread_send_kernel,
+        "spread_send",
+        [out(4 * HALF, 2 * HD), out(ROWS, 3 * HD)],
+        (place, first_own, second_own, a1_back, b2_back, b1_back, a2_back, dq, w),
+        4 << 20,
+        8,
+        product,
+    )
+    keep = call(spread_keep_kernel, "spread_keep", out(4 * HALF, 2 * HD), (place, grads, w), 4 << 20, 8, product)
     arrived = across(send, 0, 1)
     chip = (keep.astype(F32) + arrived.astype(F32)).astype(BF)
     gx = across(chip[HALF : 2 * HALF], 0, 2)

time: 69.2 us -> 73.5 us (1.062)
  the two profiles are of different devices: /device:TPU:0 before, /device:TPU:16 now
where the time goes in v3:
time: 73.5 us; the launch traced here: 73.2 us
  starting transfers between devices  30.4 us (41%)
  waiting for transfers between devices  22.1 us (30%)
  Pallas kernels  10.1 us (14%)
  local copies, waits for them, and re-layouts  6.63 us (9%)
  other arithmetic  3.02 us (4%)
  between operations  0.92 us (1%)
    ppermute x12, starting transfers between devices, group_swap(): return lax.ppermute(value, 'ctx', pairs)  20.6 us
    ppermute x12, waiting for transfers between devices, group_swap(): return lax.ppermute(value, 'ctx', pairs)  11.2 us
    ppermute x10, waiting for transfers between devices, across(): return lax.ppermute(value, ('ctx', 'head'), pairs)  10.9 us
    pallas_call x8, Pallas kernels, call(): pl.pallas_call(kernel, name=name, out_shape=outs, in_specs=[SMEM if v.dty...  10.1 us
    ppermute x10, starting transfers between devices, across(): return lax.ppermute(value, ('ctx', 'head'), pairs)  9.82 us
    unnamed x20, local copies, waits for them, and re-layouts  5.71 us
  transfers between devices with their start and end apart: 22, of which 11 were waited for; matrix products, arithmetic and copies ran while one was open for 4% of the time, Pallas kernels for 5%

profile of v3, /device:TPU:16, one launch (start us, length us, event | category | flops | bytes accessed | tf_op | source)
XLA Modules:
  0.0 73.2 jit_solution(17501083345443479731)
XLA Ops:
  0.6 1.6 %collective-permute-start.3 = (bf16[256,256]{1,0:T(8,128)(2,1)}, bf16[256,256]{1,0:T(8,128)(2,1)S(1)}, u32[]{:S(2)}, u32[]{:S(2)}) collective-permute-start(bf16[256,256]{1,0:T(8,128)(2,1)} %near.1), channel_id=1, source_target_pairs={{0,4},{1,5},{2,6},{3,7},{4,0},{5,1},{6,2},{7,3},{8,12},{9,13},{10,... | collective-permute-start | bytes 393224 | tf_op jit(solution)/shard_map/ppermute | solution.py:228
  2.2 1.4 %collective-permute-start.2 = (bf16[256,256]{1,0:T(8,128)(2,1)}, bf16[256,256]{1,0:T(8,128)(2,1)S(1)}, u32[]{:S(2)}, u32[]{:S(2)}) collective-permute-start(bf16[256,256]{1,0:T(8,128)(2,1)} %near.1), channel_id=1, source_target_pairs={{0,6},{1,7},{2,4},{3,5},{4,2},{5,3},{6,0},{7,1},{8,14},{9,15},{10,... | collective-permute-start | bytes 393224 | tf_op jit(solution)/shard_map/ppermute | solution.py:228
  4.3 3.9 %collective-permute-done.3.far = bf16[256,256]{1,0:T(8,128)(2,1)S(1)} collective-permute-done((bf16[256,256]{1,0:T(8,128)(2,1)}, bf16[256,256]{1,0:T(8,128)(2,1)S(1)}, u32[]{:S(2)}, u32[]{:S(2)}) %collective-permute-start.3) | collective-permute-done | bytes 131104 | tf_op jit(solution)/shard_map/ppermute | solution.py:228
  8.2 1.4 %copy-done = bf16[1024,3,256]{2,0,1:T(8,128)(2,1)S(1)} copy-done((bf16[1024,3,256]{2,0,1:T(8,128)(2,1)S(1)}, bf16[1024,3,256]{2,0,1:T(8,128)(2,1)}, u32[]{:S(2)}) %copy-start) | copy-done | bytes 1572888
  9.6 0.9 %copy-done.6 = bf16[256,256]{1,0:T(8,128)(2,1)S(1)} copy-done((bf16[256,256]{1,0:T(8,128)(2,1)S(1)}, bf16[256,256]{1,0:T(8,128)(2,1)}, u32[]{:S(2)}) %copy-start.6) | copy-done | bytes 131096
  11.3 0.9 %copy-done.2 = f32[512,384]{1,0:T(8,128)} copy-done((f32[512,384]{1,0:T(8,128)}, f32[512,384]{1,0:T(8,128)S(1)}, u32[]{:S(2)}) %copy-start.2) | copy-done | bytes 786456
  12.9 1.1 %copy-done.3 = f32[512,384]{1,0:T(8,128)S(1)} copy-done((f32[512,384]{1,0:T(8,128)S(1)}, f32[512,384]{1,0:T(8,128)}, u32[]{:S(2)}) %copy-start.3) | copy-done | bytes 786456
  14.0 0.9 %copy-done.5 = bf16[256,256]{1,0:T(8,128)(2,1)S(1)} copy-done((bf16[256,256]{1,0:T(8,128)(2,1)S(1)}, bf16[256,256]{1,0:T(8,128)(2,1)}, u32[]{:S(2)}) %copy-start.5) | copy-done | bytes 131096
  15.8 0.9 %project_kv.1 = (bf16[256,256]{1,0:T(8,128)(2,1)S(1)}, bf16[256,256]{1,0:T(8,128)(2,1)S(1)}) custom-call(s32[4]{0:T(128)S(1)} %pad_add_fusion.place, bf16[1024,256]{1,0:T(8,128)(2,1)S(1)} %collective-permute-done.4.other, f32[512,384]{1,0:T(8,128)S(1)} %project_across.1.before, bf16[3,1024,256]{2,1,0:T(8,128)(2,1)S(1)} %bitcast.7), custom_call_target="tpu_custom_call" | custom-call | flops 100663296 | bytes 2097152 | tf_op jit(solution)/shard_map/project_kv/pallas_call | solution.py:244
  16.6 1.6 %collective-permute-start.5 = (bf16[256,256]{1,0:T(8,128)(2,1)S(1)}, bf16[256,256]{1,0:T(8,128)(2,1)S(1)}, u32[]{:S(2)}, u32[]{:S(2)}) collective-permute-start(bf16[256,256]{1,0:T(8,128)(2,1)S(1)} %get-tuple-element.33.first_kv), channel_id=1, source_target_pairs={{0,8},{8,0},{4,12},{12,4},{16,24},{24,16},{20,28},{28,20},{1,9},{9... | collective-permute-start | bytes 393224 | tf_op jit(solution)/shard_map/ppermute | solution.py:236
  18.3 1.9 %collective-permute-start.7 = (bf16[256,256]{1,0:T(8,128)(2,1)S(1)}, bf16[256,256]{1,0:T(8,128)(2,1)S(1)}, u32[]{:S(2)}, u32[]{:S(2)}) collective-permute-start(bf16[256,256]{1,0:T(8,128)(2,1)S(1)} %get-tuple-element.34.second_kv), channel_id=1, source_target_pairs={{8,16},{16,8},{12,20},{20,12},{9,17},{17,9},{13,21},{21,13},{10,18... | collective-permute-start | bytes 393224 | tf_op jit(solution)/shard_map/ppermute | solution.py:236
  20.8 2.3 %collective-permute-start = (bf16[272,128]{1,0:T(8,128)(2,1)}, bf16[272,128]{1,0:T(8,128)(2,1)}, u32[]{:S(2)}, u32[]{:S(2)}) collective-permute-start(bf16[272,128]{1,0:T(8,128)(2,1)} %fusion.1), channel_id=1, source_target_pairs={{0,4},{1,5},{2,6},{3,7},{4,0},{5,1},{6,2},{7,3},{8,12},{9,13},{10,... | collective-permute-start | bytes 208904 | tf_op jit(solution)/shard_map/ppermute | solution.py:228
  23.2 3.9 %collective-permute-start.8 = (bf16[256,256]{1,0:T(8,128)(2,1)S(1)}, bf16[256,256]{1,0:T(8,128)(2,1)S(1)}, u32[]{:S(2)}, u32[]{:S(2)}) collective-permute-start(bf16[256,256]{1,0:T(8,128)(2,1)S(1)} %get-tuple-element.33.first_kv), channel_id=1, source_target_pairs={{8,16},{16,8},{12,20},{20,12},{9,17},{17,9},{13,21},{21,13},{10,18... | collective-permute-start | bytes 393224 | tf_op jit(solution)/shard_map/ppermute | solution.py:236
  27.2 1.9 %collective-permute-start.10 = (bf16[256,256]{1,0:T(8,128)(2,1)S(1)}, bf16[256,256]{1,0:T(8,128)(2,1)S(1)}, u32[]{:S(2)}, u32[]{:S(2)}) collective-permute-start(bf16[256,256]{1,0:T(8,128)(2,1)S(1)} %collective-permute-done.5.a1), channel_id=1, source_target_pairs={{8,16},{16,8},{12,20},{20,12},{9,17},{17,9},{13,21},{21,13},{10,18... | collective-permute-start | bytes 393224 | tf_op jit(solution)/shard_map/ppermute | solution.py:236
  30.6 0.9 %slice.45.d_other = bf16[256,128]{1,0:T(8,128)(2,1)S(1)} slice(bf16[272,128]{1,0:T(8,128)(2,1)} %collective-permute-done), slice={[0:256], [0:128]} | slice | bytes 131072 | tf_op jit(solution)/shard_map/slice | solution.py:305
  31.5 0.8 %project_q.1.q = bf16[512,128]{1,0:T(8,128)(2,1)S(1)} custom-call(s32[4]{0:T(128)S(1)} %pad_add_fusion.place, bf16[1024,256]{1,0:T(8,128)(2,1)S(1)} %collective-permute-done.4.other, f32[512,384]{1,0:T(8,128)S(1)} %project_across.1.before, bf16[3,1024,256]{2,1,0:T(8,128)(2,1)S(1)} %bitcast.8), custom_call_target="tpu_custom_call" | custom-call | flops 100663296 | bytes 2097152 | tf_op jit(solution)/shard_map/project_q/pallas_call | solution.py:244
  32.4 1.1 %collective-permute-done.6.a2 = bf16[256,256]{1,0:T(8,128)(2,1)S(1)} collective-permute-done((bf16[256,256]{1,0:T(8,128)(2,1)S(1)}, bf16[256,256]{1,0:T(8,128)(2,1)S(1)}, u32[]{:S(2)}, u32[]{:S(2)}) %collective-permute-start.6) | collective-permute-done | bytes 131104 | tf_op jit(solution)/shard_map/ppermute | solution.py:236
  34.0 0.8 %collective-permute-done.9.far_a = bf16[256,256]{1,0:T(8,128)(2,1)S(1)} collective-permute-done((bf16[256,256]{1,0:T(8,128)(2,1)S(1)}, bf16[256,256]{1,0:T(8,128)(2,1)S(1)}, u32[]{:S(2)}, u32[]{:S(2)}) %collective-permute-start.9) | collective-permute-done | bytes 131104 | tf_op jit(solution)/shard_map/ppermute | solution.py:236
  34.9 4.5 %attend.1 = (bf16[256,128]{1,0:T(8,128)(2,1)S(1)}, bf16[256,128]{1,0:T(8,128)(2,1)S(1)}, bf16[512,128]{1,0:T(8,128)(2,1)S(1)}, f32[256,256]{1,0:T(8,128)S(1)}, f...) custom-call(s32[4]{0:T(128)S(1)} %pad_add_fusion.place, ...), custom_call_target="tpu_custom_call" | custom-call | flops 1811939328 | bytes 4194304 | tf_op jit(solution)/shard_map/attend/pallas_call | solution.py:244
  39.4 3.2 %collective-permute-start.12 = (bf16[256,256]{1,0:T(8,128)(2,1)S(1)}, bf16[256,256]{1,0:T(8,128)(2,1)S(1)}, u32[]{:S(2)}, u32[]{:S(2)}) collective-permute-start(bf16[256,256]{1,0:T(8,128)(2,1)S(1)} %get-tuple-element.40), channel_id=1, source_target_pairs={{8,16},{16,8},{12,20},{20,12},{9,17},{17,9},{13,21},{21,13},{10,18... | collective-permute-start | bytes 393224 | tf_op jit(solution)/shard_map/ppermute | solution.py:236
  42.6 2.7 %collective-permute-start.14 = (bf16[256,256]{1,0:T(8,128)(2,1)S(1)}, bf16[256,256]{1,0:T(8,128)(2,1)S(1)}, u32[]{:S(2)}, u32[]{:S(2)}) collective-permute-start(bf16[256,256]{1,0:T(8,128)(2,1)S(1)} %get-tuple-element.41), channel_id=1, source_target_pairs={{8,16},{16,8},{12,20},{20,12},{9,17},{17,9},{13,21},{21,13},{10,18... | collective-permute-start | bytes 393224 | tf_op jit(solution)/shard_map/ppermute | solution.py:236
  45.4 2.0 %collective-permute-start.17 = (bf16[256,256]{1,0:T(8,128)(2,1)S(1)}, bf16[256,256]{1,0:T(8,128)(2,1)S(1)}, u32[]{:S(2)}, u32[]{:S(2)}) collective-permute-start(bf16[256,256]{1,0:T(8,128)(2,1)S(1)} %get-tuple-element.44), channel_id=1, source_target_pairs={{0,8},{8,0},{4,12},{12,4},{16,24},{24,16},{20,28},{28,20},{1,9},{9... | collective-permute-start | bytes 393224 | tf_op jit(solution)/shard_map/ppermute | solution.py:236
  47.6 4.1 %collective-permute-done.15 = bf16[256,256]{1,0:T(8,128)(2,1)S(1)} collective-permute-done((bf16[256,256]{1,0:T(8,128)(2,1)S(1)}, bf16[256,256]{1,0:T(8,128)(2,1)S(1)}, u32[]{:S(2)}, u32[]{:S(2)}) %collective-permute-start.15) | collective-permute-done | bytes 131104 | tf_op jit(solution)/shard_map/ppermute | solution.py:236
  51.7 2.3 %collective-permute-start.16 = (bf16[256,256]{1,0:T(8,128)(2,1)S(1)}, bf16[256,256]{1,0:T(8,128)(2,1)S(1)}, u32[]{:S(2)}, u32[]{:S(2)}) collective-permute-start(bf16[256,256]{1,0:T(8,128)(2,1)S(1)} %add_convert_fusion.2), channel_id=1, source_target_pairs={{8,16},{16,8},{12,20},{20,12},{9,17},{17,9},{13,21},{21,13},{10,18... | collective-permute-start | bytes 393224 | tf_op jit(solution)/shard_map/ppermute | solution.py:236
  54.5 4.1 %collective-permute-done.16.b1 = bf16[256,256]{1,0:T(8,128)(2,1)S(1)} collective-permute-done((bf16[256,256]{1,0:T(8,128)(2,1)S(1)}, bf16[256,256]{1,0:T(8,128)(2,1)S(1)}, u32[]{:S(2)}, u32[]{:S(2)}) %collective-permute-start.16) | collective-permute-done | bytes 131104 | tf_op jit(solution)/shard_map/ppermute | solution.py:236
  58.6 1.1 %spread_send.1 = (bf16[1024,256]{1,0:T(8,128)(2,1)S(1)}, bf16[512,384]{1,0:T(8,128)(2,1)S(1)}) custom-call(s32[4]{0:T(128)S(1)} %pad_add_fusion.place, f32[256,256]{1,0:T(8,128)S(1)} %get-tuple-element.37.first_own, f32[256,256]{1,0:T(8,128)S(1)} %get-tuple-element.38.second_own, bf16[256,256]{1,0:T(8,128)(2,1)S(1)} %collective-permute-done.13.a1, ...), custom_call_target="tpu_custom_call" | custom-call | flops 100663296 | bytes 4194304 | tf_op jit(solution)/shard_map/spread_send/pallas_call | solution.py:244
  60.0 1.0 %spread_keep.1 = bf16[1024,256]{1,0:T(8,128)(2,1)S(1)} custom-call(s32[4]{0:T(128)S(1)} %pad_add_fusion.place, bf16[512,384]{1,0:T(8,128)(2,1)S(1)} %get-tuple-element.46.grads, bf16[3,1024,256]{2,1,0:T(8,128)(2,1)S(1)} %bitcast.10), custom_call_target="tpu_custom_call" | custom-call | flops 100663296 | bytes 4194304 | tf_op jit(solution)/shard_map/spread_keep/pallas_call | solution.py:244
  61.9 1.5 %collective-permute-start.19 = (bf16[256,256]{1,0:T(8,128)(2,1)S(1)}, bf16[256,256]{1,0:T(8,128)(2,1)S(1)}, u32[]{:S(2)}, u32[]{:S(2)}) collective-permute-start(bf16[256,256]{1,0:T(8,128)(2,1)S(1)} %get-tuple-element.48), channel_id=1, source_target_pairs={{0,2},{1,3},{2,0},{3,1},{4,6},{5,7},{6,4},{7,5},{8,10},{9,11},{10,... | collective-permute-start | bytes 393224 | tf_op jit(solution)/shard_map/ppermute | solution.py:228
  63.4 1.2 %collective-permute-start.21 = (bf16[256,256]{1,0:T(8,128)(2,1)S(1)}, bf16[256,256]{1,0:T(8,128)(2,1)S(1)}, u32[]{:S(2)}, u32[]{:S(2)}) collective-permute-start(bf16[256,256]{1,0:T(8,128)(2,1)S(1)} %get-tuple-element.49), channel_id=1, source_target_pairs={{0,6},{1,7},{2,4},{3,5},{4,2},{5,3},{6,0},{7,1},{8,14},{9,15},{10,... | collective-permute-start | bytes 393224 | tf_op jit(solution)/shard_map/ppermute | solution.py:228
  66.1 2.1 %collective-permute-done.19 = bf16[256,256]{1,0:T(8,128)(2,1)S(1)} collective-permute-done((bf16[256,256]{1,0:T(8,128)(2,1)S(1)}, bf16[256,256]{1,0:T(8,128)(2,1)S(1)}, u32[]{:S(2)}, u32[]{:S(2)}) %collective-permute-start.19) | collective-permute-done | bytes 131104 | tf_op jit(solution)/shard_map/ppermute | solution.py:228
  68.3 2.8 %collective-permute-done.21 = bf16[256,256]{1,0:T(8,128)(2,1)S(1)} collective-permute-done((bf16[256,256]{1,0:T(8,128)(2,1)S(1)}, bf16[256,256]{1,0:T(8,128)(2,1)S(1)}, u32[]{:S(2)}, u32[]{:S(2)}) %collective-permute-start.21) | collective-permute-done | bytes 131104 | tf_op jit(solution)/shard_map/ppermute | solution.py:228
  71.1 1.4 %collective-permute-done.20 = bf16[256,256]{1,0:T(8,128)(2,1)S(1)} collective-permute-done((bf16[256,256]{1,0:T(8,128)(2,1)S(1)}, bf16[256,256]{1,0:T(8,128)(2,1)S(1)}, u32[]{:S(2)}, u32[]{:S(2)}) %collective-permute-start.20) | collective-permute-done | bytes 131104 | tf_op jit(solution)/shard_map/ppermute | solution.py:228
  (53 shorter events, 9.8 us)
Async XLA Ops:
  0.6 11.7 %copy-start.9 = (s32[2,9]{1,0:T(2,128)S(1)}, s32[2,9]{1,0:T(2,128)}, u32[]{:S(2)}) copy-start(s32[2,9]{1,0:T(2,128)} %param.8) | copy-start | bytes 220
  0.6 7.5 %collective-permute-start.3 = (bf16[256,256]{1,0:T(8,128)(2,1)}, bf16[256,256]{1,0:T(8,128)(2,1)S(1)}, u32[]{:S(2)}, u32[]{:S(2)}) collective-permute-start(bf16[256,256]{1,0:T(8,128)(2,1)} %near.1), channel_id=1, source_target_pairs={{0,4},{1,5},{2,6},{3,7},{4,0},{5,1},{6,2},{7,3},{8,12},{9,13},{10,... | collective-permute-start | bytes 393224 | tf_op jit(solution)/shard_map/ppermute | solution.py:228
  2.2 10.0 %collective-permute-start.2 = (bf16[256,256]{1,0:T(8,128)(2,1)}, bf16[256,256]{1,0:T(8,128)(2,1)S(1)}, u32[]{:S(2)}, u32[]{:S(2)}) collective-permute-start(bf16[256,256]{1,0:T(8,128)(2,1)} %near.1), channel_id=1, source_target_pairs={{0,6},{1,7},{2,4},{3,5},{4,2},{5,3},{6,0},{7,1},{8,14},{9,15},{10,... | collective-permute-start | bytes 393224 | tf_op jit(solution)/shard_map/ppermute | solution.py:228
  3.7 8.6 %collective-permute-start.1 = (bf16[256,256]{1,0:T(8,128)(2,1)}, bf16[256,256]{1,0:T(8,128)(2,1)S(1)}, u32[]{:S(2)}, u32[]{:S(2)}) collective-permute-start(bf16[256,256]{1,0:T(8,128)(2,1)} %near.1), channel_id=1, source_target_pairs={{0,2},{1,3},{2,0},{3,1},{4,6},{5,7},{6,4},{7,5},{8,10},{9,11},{10,... | collective-permute-start | bytes 393224 | tf_op jit(solution)/shard_map/ppermute | solution.py:228
  8.2 1.4 %copy-start = (bf16[1024,3,256]{2,0,1:T(8,128)(2,1)S(1)}, bf16[1024,3,256]{2,0,1:T(8,128)(2,1)}, u32[]{:S(2)}) copy-start(bf16[1024,3,256]{2,0,1:T(8,128)(2,1)} %param.7) | copy-start | bytes 4718596
  9.6 0.9 %copy-start.6 = (bf16[256,256]{1,0:T(8,128)(2,1)S(1)}, bf16[256,256]{1,0:T(8,128)(2,1)}, u32[]{:S(2)}) copy-start(bf16[256,256]{1,0:T(8,128)(2,1)} %near.1) | copy-start | bytes 393220
  10.5 1.9 %copy-start.7 = (bf16[256,256]{1,0:T(8,128)(2,1)S(1)}, bf16[256,256]{1,0:T(8,128)(2,1)}, u32[]{:S(2)}) copy-start(bf16[256,256]{1,0:T(8,128)(2,1)} %d_own.1) | copy-start | bytes 393220
  10.5 2.4 %copy-start.1 = (bf16[1024,3,256]{2,0,1:T(8,128)(2,1)S(1)}, bf16[1024,3,256]{2,0,1:T(8,128)(2,1)}, u32[]{:S(2)}) copy-start(bf16[1024,3,256]{2,0,1:T(8,128)(2,1)} %param.7) | copy-start | bytes 4718596
  11.3 0.9 %copy-start.2 = (f32[512,384]{1,0:T(8,128)}, f32[512,384]{1,0:T(8,128)S(1)}, u32[]{:S(2)}) copy-start(f32[512,384]{1,0:T(8,128)S(1)} %get-tuple-element.32.before) | copy-start | bytes 2359300
  12.2 0.7 copy-start.4
  12.3 3.5 %collective-permute-start.4 = (bf16[1024,256]{1,0:T(8,128)(2,1)S(1)}, bf16[1024,256]{1,0:T(8,128)(2,1)S(1)}, u32[]{:S(2)}, u32[]{:S(2)}) collective-permute-start(bf16[1024,256]{1,0:T(8,128)(2,1)S(1)} %pack.1), channel_id=1, source_target_pairs={{0,1},{1,0},{2,3},{3,2},{4,5},{5,4},{6,7},{7,6},{8,9},{9,8},{10,11... | collective-permute-start | bytes 1572872 | tf_op jit(solution)/shard_map/ppermute | solution.py:228
  12.9 1.1 %copy-start.3 = (f32[512,384]{1,0:T(8,128)S(1)}, f32[512,384]{1,0:T(8,128)}, u32[]{:S(2)}) copy-start(f32[512,384]{1,0:T(8,128)} %copy-done.2) | copy-start | bytes 2359300
  14.0 0.9 %copy-start.5 = (bf16[256,256]{1,0:T(8,128)(2,1)S(1)}, bf16[256,256]{1,0:T(8,128)(2,1)}, u32[]{:S(2)}) copy-start(bf16[256,256]{1,0:T(8,128)(2,1)} %copy-done.4) | copy-start | bytes 393220
  16.6 10.5 %collective-permute-start.5 = (bf16[256,256]{1,0:T(8,128)(2,1)S(1)}, bf16[256,256]{1,0:T(8,128)(2,1)S(1)}, u32[]{:S(2)}, u32[]{:S(2)}) collective-permute-start(bf16[256,256]{1,0:T(8,128)(2,1)S(1)} %get-tuple-element.33.first_kv), channel_id=1, source_target_pairs={{0,8},{8,0},{4,12},{12,4},{16,24},{24,16},{20,28},{28,20},{1,9},{9... | collective-permute-start | bytes 393224 | tf_op jit(solution)/shard_map/ppermute | solution.py:236
  18.3 10.8 %collective-permute-start.7 = (bf16[256,256]{1,0:T(8,128)(2,1)S(1)}, bf16[256,256]{1,0:T(8,128)(2,1)S(1)}, u32[]{:S(2)}, u32[]{:S(2)}) collective-permute-start(bf16[256,256]{1,0:T(8,128)(2,1)S(1)} %get-tuple-element.34.second_kv), channel_id=1, source_target_pairs={{8,16},{16,8},{12,20},{20,12},{9,17},{17,9},{13,21},{21,13},{10,18... | collective-permute-start | bytes 393224 | tf_op jit(solution)/shard_map/ppermute | solution.py:236
  20.8 9.1 %collective-permute-start = (bf16[272,128]{1,0:T(8,128)(2,1)}, bf16[272,128]{1,0:T(8,128)(2,1)}, u32[]{:S(2)}, u32[]{:S(2)}) collective-permute-start(bf16[272,128]{1,0:T(8,128)(2,1)} %fusion.1), channel_id=1, source_target_pairs={{0,4},{1,5},{2,6},{3,7},{4,0},{5,1},{6,2},{7,3},{8,12},{9,13},{10,... | collective-permute-start | bytes 208904 | tf_op jit(solution)/shard_map/ppermute | solution.py:228
  23.2 9.2 %collective-permute-start.8 = (bf16[256,256]{1,0:T(8,128)(2,1)S(1)}, bf16[256,256]{1,0:T(8,128)(2,1)S(1)}, u32[]{:S(2)}, u32[]{:S(2)}) collective-permute-start(bf16[256,256]{1,0:T(8,128)(2,1)S(1)} %get-tuple-element.33.first_kv), channel_id=1, source_target_pairs={{8,16},{16,8},{12,20},{20,12},{9,17},{17,9},{13,21},{21,13},{10,18... | collective-permute-start | bytes 393224 | tf_op jit(solution)/shard_map/ppermute | solution.py:236
  27.1 6.4 %collective-permute-start.6 = (bf16[256,256]{1,0:T(8,128)(2,1)S(1)}, bf16[256,256]{1,0:T(8,128)(2,1)S(1)}, u32[]{:S(2)}, u32[]{:S(2)}) collective-permute-start(bf16[256,256]{1,0:T(8,128)(2,1)S(1)} %get-tuple-element.34.second_kv), channel_id=1, source_target_pairs={{0,8},{8,0},{4,12},{12,4},{16,24},{24,16},{20,28},{28,20},{1,9},{9... | collective-permute-start | bytes 393224 | tf_op jit(solution)/shard_map/ppermute | solution.py:236
  27.2 6.9 %collective-permute-start.10 = (bf16[256,256]{1,0:T(8,128)(2,1)S(1)}, bf16[256,256]{1,0:T(8,128)(2,1)S(1)}, u32[]{:S(2)}, u32[]{:S(2)}) collective-permute-start(bf16[256,256]{1,0:T(8,128)(2,1)S(1)} %collective-permute-done.5.a1), channel_id=1, source_target_pairs={{8,16},{16,8},{12,20},{20,12},{9,17},{17,9},{13,21},{21,13},{10,18... | collective-permute-start | bytes 393224 | tf_op jit(solution)/shard_map/ppermute | solution.py:236
  29.1 5.8 %collective-permute-start.9 = (bf16[256,256]{1,0:T(8,128)(2,1)S(1)}, bf16[256,256]{1,0:T(8,128)(2,1)S(1)}, u32[]{:S(2)}, u32[]{:S(2)}) collective-permute-start(bf16[256,256]{1,0:T(8,128)(2,1)S(1)} %collective-permute-done.7.b1), channel_id=1, source_target_pairs={{0,8},{8,0},{4,12},{12,4},{16,24},{24,16},{20,28},{28,20},{1,9},{9... | collective-permute-start | bytes 393224 | tf_op jit(solution)/shard_map/ppermute | solution.py:236
  30.6 4.3 %copy-start.8 = (bf16[256,256]{1,0:T(8,128)(2,1)S(1)}, bf16[256,256]{1,0:T(8,128)(2,1)}, u32[]{:S(2)}) copy-start(bf16[256,256]{1,0:T(8,128)(2,1)} %d_own.1) | copy-start | bytes 393220
  39.4 8.0 %collective-permute-start.12 = (bf16[256,256]{1,0:T(8,128)(2,1)S(1)}, bf16[256,256]{1,0:T(8,128)(2,1)S(1)}, u32[]{:S(2)}, u32[]{:S(2)}) collective-permute-start(bf16[256,256]{1,0:T(8,128)(2,1)S(1)} %get-tuple-element.40), channel_id=1, source_target_pairs={{8,16},{16,8},{12,20},{20,12},{9,17},{17,9},{13,21},{21,13},{10,18... | collective-permute-start | bytes 393224 | tf_op jit(solution)/shard_map/ppermute | solution.py:236
  42.6 11.4 %collective-permute-start.14 = (bf16[256,256]{1,0:T(8,128)(2,1)S(1)}, bf16[256,256]{1,0:T(8,128)(2,1)S(1)}, u32[]{:S(2)}, u32[]{:S(2)}) collective-permute-start(bf16[256,256]{1,0:T(8,128)(2,1)S(1)} %get-tuple-element.41), channel_id=1, source_target_pairs={{8,16},{16,8},{12,20},{20,12},{9,17},{17,9},{13,21},{21,13},{10,18... | collective-permute-start | bytes 393224 | tf_op jit(solution)/shard_map/ppermute | solution.py:236
  45.3 6.4 %collective-permute-start.15 = (bf16[256,256]{1,0:T(8,128)(2,1)S(1)}, bf16[256,256]{1,0:T(8,128)(2,1)S(1)}, u32[]{:S(2)}, u32[]{:S(2)}) collective-permute-start(bf16[256,256]{1,0:T(8,128)(2,1)S(1)} %get-tuple-element.43), channel_id=1, source_target_pairs={{0,8},{8,0},{4,12},{12,4},{16,24},{24,16},{20,28},{28,20},{1,9},{9... | collective-permute-start | bytes 393224 | tf_op jit(solution)/shard_map/ppermute | solution.py:236
  45.4 8.6 %collective-permute-start.17 = (bf16[256,256]{1,0:T(8,128)(2,1)S(1)}, bf16[256,256]{1,0:T(8,128)(2,1)S(1)}, u32[]{:S(2)}, u32[]{:S(2)}) collective-permute-start(bf16[256,256]{1,0:T(8,128)(2,1)S(1)} %get-tuple-element.44), channel_id=1, source_target_pairs={{0,8},{8,0},{4,12},{12,4},{16,24},{24,16},{20,28},{28,20},{1,9},{9... | collective-permute-start | bytes 393224 | tf_op jit(solution)/shard_map/ppermute | solution.py:236
  47.4 7.0 %collective-permute-start.13 = (bf16[256,256]{1,0:T(8,128)(2,1)S(1)}, bf16[256,256]{1,0:T(8,128)(2,1)S(1)}, u32[]{:S(2)}, u32[]{:S(2)}) collective-permute-start(bf16[256,256]{1,0:T(8,128)(2,1)S(1)} %add_convert_fusion.3), channel_id=1, source_target_pairs={{0,8},{8,0},{4,12},{12,4},{16,24},{24,16},{20,28},{28,20},{1,9},{9... | collective-permute-start | bytes 393224 | tf_op jit(solution)/shard_map/ppermute | solution.py:236
  51.7 6.9 %collective-permute-start.16 = (bf16[256,256]{1,0:T(8,128)(2,1)S(1)}, bf16[256,256]{1,0:T(8,128)(2,1)S(1)}, u32[]{:S(2)}, u32[]{:S(2)}) collective-permute-start(bf16[256,256]{1,0:T(8,128)(2,1)S(1)} %add_convert_fusion.2), channel_id=1, source_target_pairs={{8,16},{16,8},{12,20},{20,12},{9,17},{17,9},{13,21},{21,13},{10,18... | collective-permute-start | bytes 393224 | tf_op jit(solution)/shard_map/ppermute | solution.py:236
  59.7 2.0 %collective-permute-start.18 = (bf16[1024,256]{1,0:T(8,128)(2,1)S(1)}, bf16[1024,256]{1,0:T(8,128)(2,1)S(1)}, u32[]{:S(2)}, u32[]{:S(2)}) collective-permute-start(bf16[1024,256]{1,0:T(8,128)(2,1)S(1)} %get-tuple-element.47), channel_id=1, source_target_pairs={{0,1},{1,0},{2,3},{3,2},{4,5},{5,4},{6,7},{7,6},{8,9},{9,8},{10,11... | collective-permute-start | bytes 1572872 | tf_op jit(solution)/shard_map/ppermute | solution.py:228
  59.8 5.6 %collective-permute-start.11 = (bf16[256,128]{1,0:T(8,128)(2,1)S(1)}, bf16[256,128]{1,0:T(8,128)(2,1)S(1)}, u32[]{:S(2)}, u32[]{:S(2)}) collective-permute-start(bf16[256,128]{1,0:T(8,128)(2,1)S(1)} %get-tuple-element.36), channel_id=1, source_target_pairs={{0,4},{1,5},{2,6},{3,7},{4,0},{5,1},{6,2},{7,3},{8,12},{9,13},{10,... | collective-permute-start | bytes 196616 | tf_op jit(solution)/shard_map/ppermute | solution.py:228
  61.9 6.4 %collective-permute-start.19 = (bf16[256,256]{1,0:T(8,128)(2,1)S(1)}, bf16[256,256]{1,0:T(8,128)(2,1)S(1)}, u32[]{:S(2)}, u32[]{:S(2)}) collective-permute-start(bf16[256,256]{1,0:T(8,128)(2,1)S(1)} %get-tuple-element.48), channel_id=1, source_target_pairs={{0,2},{1,3},{2,0},{3,1},{4,6},{5,7},{6,4},{7,5},{8,10},{9,11},{10,... | collective-permute-start | bytes 393224 | tf_op jit(solution)/shard_map/ppermute | solution.py:228
  63.4 7.7 %collective-permute-start.21 = (bf16[256,256]{1,0:T(8,128)(2,1)S(1)}, bf16[256,256]{1,0:T(8,128)(2,1)S(1)}, u32[]{:S(2)}, u32[]{:S(2)}) collective-permute-start(bf16[256,256]{1,0:T(8,128)(2,1)S(1)} %get-tuple-element.49), channel_id=1, source_target_pairs={{0,6},{1,7},{2,4},{3,5},{4,2},{5,3},{6,0},{7,1},{8,14},{9,15},{10,... | collective-permute-start | bytes 393224 | tf_op jit(solution)/shard_map/ppermute | solution.py:228
  64.6 7.8 %collective-permute-start.20 = (bf16[256,256]{1,0:T(8,128)(2,1)S(1)}, bf16[256,256]{1,0:T(8,128)(2,1)S(1)}, u32[]{:S(2)}, u32[]{:S(2)}) collective-permute-start(bf16[256,256]{1,0:T(8,128)(2,1)S(1)} %get-tuple-element.50), channel_id=1, source_target_pairs={{0,4},{1,5},{2,6},{3,7},{4,0},{5,1},{6,2},{7,3},{8,12},{9,13},{10,... | collective-permute-start | bytes 393224 | tf_op jit(solution)/shard_map/ppermute | solution.py:228

commit v4 on v2

v4 whole, which is shorter than its diff:
```python
import functools

import jax
import jax.numpy as jnp
from jax import lax
from jax.experimental import pallas as pl
from jax.experimental.pallas import tpu as pltpu
from jax.sharding import PartitionSpec as P

HD = 128
BLK = 128
REACH = 6
SPAN = 3
LOG2E = 1.4426950408889634
DEAD = -1e30
BF = jnp.bfloat16
F32 = jnp.float32

GROUP = 4
ROWS = GROUP * BLK
HALF = ROWS // 2
WINDOW = GROUP + 2 * REACH
NEAR_LEFT = (REACH - GROUP) * BLK
OWN = REACH * BLK
NEAR_RIGHT = OWN + ROWS
FAR_RIGHT = NEAR_RIGHT + ROWS


def params(flops, moved, mebibytes):
    return dict(
        compiler_params=pltpu.CompilerParams(vmem_limit_bytes=mebibytes * 1024 * 1024),
        cost_estimate=pl.CostEstimate(flops=flops, bytes_accessed=moved, transcendentals=0),
    )


VMEM = pl.BlockSpec(memory_space=pltpu.VMEM)
SMEM = pl.BlockSpec(memory_space=pltpu.SMEM)


def dot(a, b, dims):
    return lax.dot_general(a, b, (dims, ((), ())), preferred_element_type=F32)


def begin_kernel(place, sy, f, w, w_mine, fy, total, sems):
    side, head = place[0], place[3]
    copies = [pltpu.make_async_copy(f, fy.at[pl.ds(0, HALF), :], sems.at[3])]
    for g in range(3):
        cols = pl.ds(pl.multiple_of(side * HD, HD), HD)
        copies.append(pltpu.make_async_copy(w.at[g, :, cols], w_mine.at[:, pl.ds(g * HD, HD)], sems.at[g]))
    for copy in copies:
        copy.start()
    fy[HALF:, :] = sy[...]
    for copy in copies:
        copy.wait()
    total[...] = dot(fy[...], weight_rows(w_mine, head, fy.shape[1]), ((1,), (0,)))


def weight_rows(w_mine, source, width):
    return w_mine[pl.ds(pl.multiple_of(source * width, width), width), :]


def pack_kernel(sd, sx, fy, out):
    out[:HALF, :] = fy[:HALF, :]
    out[HALF : 2 * HALF, :] = fy[HALF:, :]
    out[2 * HALF : 3 * HALF, :] = sx[...]
    out[3 * HALF :, :] = sd[...]


def project_across_kernel(place, pack, before, w_mine, total):
    width = pack.shape[1]
    total[...] = before[...] + dot(pack[2 * HALF :, :], weight_rows(w_mine, place[3] ^ 2, width), ((1,), (0,)))


def sibling_product(place, other, w_mine, cols):
    width = other.shape[1]
    total = None
    for index in range(2):
        rows = pl.ds(pl.multiple_of((place[3] ^ (1 + 2 * index)) * width, width), width)
        term = dot(other[2 * index * HALF : 2 * (index + 1) * HALF, :], w_mine[rows, cols], ((1,), (0,)))
        total = term if total is None else total + term
    return total


def store_groups(side, total, target):
    for group in range(2):
        rows = pl.ds(pl.multiple_of((side ^ group) * HALF, HALF), HALF)
        target[rows, :] = total[group * HALF : (group + 1) * HALF]


def project_kv_kernel(place, other, before, w_mine, kv_out):
    total = before[:, HD:] + sibling_product(place, other, w_mine, slice(HD, 3 * HD))
    store_groups(place[0], total.astype(BF), kv_out)


def project_q_kernel(place, other, before, w_mine, q_out):
    total = before[:, :HD] + sibling_product(place, other, w_mine, slice(0, HD))
    store_groups(place[0], total.astype(BF), q_out)


def regions(odd):
    even = 1 - odd
    pick = lambda at_even, at_odd: pl.multiple_of(even * at_even + odd * at_odd, HALF)
    return (
        pick(NEAR_RIGHT, NEAR_LEFT),
        pick(NEAR_LEFT, NEAR_RIGHT),
        pick(FAR_RIGHT, 0),
        pick(0, FAR_RIGHT),
    )


def start_of(links, first, i, t):
    if t == 0:
        return (REACH + i - 1) * BLK
    base = jnp.int32(-(1 << 20))
    for j in range(SPAN):
        entry = links[i, SPAN * t + j]
        base = jnp.maximum(base, jnp.where(entry >= 0, entry - j, -(1 << 20)))
    base = jnp.where(base > -(1 << 19), base - first + REACH, REACH + i)
    base = jnp.clip(base, 0, WINDOW - SPAN)
    return pl.multiple_of(base * BLK, BLK)


def is_far(i, t):
    return t == (1 if i < GROUP // 2 else 2)


def run_rows(i, t):
    return slice((i * 3 + t) * SPAN * BLK, (i * 3 + t + 1) * SPAN * BLK)


def side_factor():
    scale = HD ** -0.5
    return jnp.where(lax.broadcasted_iota(jnp.int32, (1, 2 * HD), 1) < HD, scale, 1.0).astype(F32)


def attend_kernel(
    place, links, q, kv, near_a, near_b, far_a, far_b, d_own, d_other,
    mixed, pairs, win, acc, far_a_out, far_b_out,
):
    side, odd, first = place[0], place[1], place[2]
    scale = HD ** -0.5
    at_a, at_b, at_far_a, at_far_b = regions(odd)
    win[OWN : OWN + ROWS, :] = kv[...]
    win[pl.ds(at_a, ROWS), :] = near_a[...]
    win[pl.ds(at_b, ROWS), :] = near_b[...]
    win[pl.ds(at_far_a, HALF), :] = far_a[...]
    win[pl.ds(at_far_b, HALF), :] = far_b[...]
    acc[...] = jnp.zeros_like(acc)
    zeros = jnp.zeros((BLK, HD), BF)
    own_cols = pl.ds(pl.multiple_of(side * HD, HD), HD)
    for i in range(GROUP):
        rows = slice(i * BLK, (i + 1) * BLK)
        here = slice((i % 2) * BLK, (i % 2 + 1) * BLK)
        d_blk = jnp.where(side == i // 2, d_own[here, own_cols], d_other[here, :])
        pair = jnp.concatenate(
            [
                jnp.concatenate([q[rows, :], zeros], axis=1),
                jnp.concatenate([zeros, d_blk], axis=1),
            ],
            axis=0,
        )
        pairs[2 * i * BLK : 2 * (i + 1) * BLK, :] = pair
        scores, prob_grads, peaks, biases = [], [], [], []
        for t in range(3):
            product = dot(win[pl.ds(start_of(links, first, i, t), SPAN * BLK), :], pair, ((1,), (1,)))
            for j in range(SPAN):
                block = product[j * BLK : (j + 1) * BLK]
                bias = jnp.where(links[i, SPAN * t + j] >= 0, 0.0, DEAD).astype(F32)
                scores.append(block[:, :BLK])
                prob_grads.append(block[:, BLK:])
                biases.append(bias)
                peaks.append(jnp.max(block[:, :BLK].reshape(BLK // 8, 8, BLK), axis=0) + bias)
        largest = peaks[0]
        for peak in peaks[1:]:
            largest = jnp.maximum(largest, peak)
        largest = jnp.max(largest, axis=0, keepdims=True)
        terms = []
        total = jnp.zeros((8, BLK), F32)
        weighted = jnp.zeros((8, BLK), F32)
        for n in range(3 * SPAN):
            term = jnp.exp2((scores[n] - (largest - biases[n])) * (scale * LOG2E))
            terms.append(term)
            total = total + jnp.sum(term.reshape(BLK // 8, 8, BLK), axis=0)
            weighted = weighted + jnp.sum((term * prob_grads[n]).reshape(BLK // 8, 8, BLK), axis=0)
        inverse = 1.0 / jnp.sum(total, axis=0, keepdims=True)
        row_dot = jnp.sum(weighted, axis=0, keepdims=True) * inverse
        for t in range(3):
            parts = []
            for n in range(SPAN * t, SPAN * t + SPAN):
                share = terms[n] * inverse
                grad = share * (prob_grads[n] - row_dot)
                parts.append(jnp.concatenate([grad.astype(BF), share.astype(BF)], axis=1))
            part = jnp.concatenate(parts, axis=0)
            mixed[run_rows(i, t), :] = part
            if is_far(i, t):
                acc[pl.ds(start_of(links, first, i, t), SPAN * BLK), :] += dot(part, pair, ((1,), (0,)))
    factor = side_factor()
    far_a_out[...] = (acc[pl.ds(at_far_a, HALF), :] * factor).astype(BF)
    far_b_out[...] = (acc[pl.ds(at_far_b, HALF), :] * factor).astype(BF)


def near_grads_kernel(place, links, mixed, pairs, far_acc, own_out, a_out, b_out, acc):
    odd, first = place[1], place[2]
    acc[...] = far_acc[...]
    for i in range(GROUP):
        pair = pairs[2 * i * BLK : 2 * (i + 1) * BLK, :]
        for t in range(3):
            if not is_far(i, t):
                at = pl.ds(start_of(links, first, i, t), SPAN * BLK)
                acc[at, :] += dot(mixed[run_rows(i, t), :], pair, ((1,), (0,)))
    factor = side_factor()
    at_a, at_b, _, _ = regions(odd)
    own_out[...] = acc[OWN : OWN + ROWS, :] * factor
    a_out[...] = (acc[pl.ds(at_a, ROWS), :] * factor).astype(BF)
    b_out[...] = (acc[pl.ds(at_b, ROWS), :] * factor).astype(BF)


def outputs_kernel(place, links, mixed, win, att_own, att_other, dq_out, att):
    side, first = place[0], place[2]
    for i in range(GROUP):
        rows = slice(i * BLK, (i + 1) * BLK)
        out = None
        for t in range(3):
            keys = win[pl.ds(start_of(links, first, i, t), SPAN * BLK), :]
            term = dot(mixed[run_rows(i, t), :], keys, ((0,), (0,)))
            out = term if out is None else out + term
        att[rows, :] = out[BLK:, HD:].astype(BF)
        dq_out[rows, :] = (out[:BLK, :HD] * (HD ** -0.5)).astype(BF)
    att_own[...] = att[pl.ds(pl.multiple_of(side * HALF, HALF), HALF), :]
    att_other[...] = att[pl.ds(pl.multiple_of((1 - side) * HALF, HALF), HALF), :]


def spread(grads, w_mine, side, head, target):
    for step in range(2):
        out = dot(grads, weight_rows(w_mine, head ^ (2 * step), 2 * HD), ((1,), (1,))).astype(BF)
        for group in range(2):
            index = 2 * group + step
            part = jnp.where(side == group, out[:HALF], out[HALF:])
            target[index * HALF : (index + 1) * HALF, :] = part


def spread_send_kernel(place, own, from_a, from_b, dq, w_mine, send, grads):
    dkv = (own[...] + from_a[...].astype(F32) + from_b[...].astype(F32)).astype(BF)
    grads[:, :HD] = dq[...]
    grads[:, HD:] = dkv
    spread(grads[...], w_mine, place[0], place[3] ^ 1, send)


def spread_keep_kernel(place, grads, w_mine, keep):
    spread(grads[...], w_mine, place[0], place[3], keep)


def body(features, w_qkv, block_links, d_out, n_ctx, n_head):
    ctx, head = lax.axis_index("ctx"), lax.axis_index("head")
    side = ctx % 2
    group = ctx // 2
    odd = group % 2
    n_group = n_ctx // 2
    place = jnp.stack([side, odd, group * GROUP, head]).astype(jnp.int32)

    def across(value, flip_ctx, flip_head):
        pairs = [
            (c * n_head + h, (c ^ flip_ctx) * n_head + (h ^ flip_head))
            for c in range(n_ctx)
            for h in range(n_head)
        ]
        return lax.ppermute(value, ("ctx", "head"), pairs)

    def group_swap(value, offset):
        pairs = []
        for low in range(offset, n_group - 1, 2):
            for s in range(2):
                pairs.append((2 * low + s, 2 * low + 2 + s))
                pairs.append((2 * low + 2 + s, 2 * low + s))
        return lax.ppermute(value, "ctx", pairs)

    f = features
    sx = across(f, 0, 2)
    sy = across(f, 1, 0)
    sd = across(f, 1, 2)
    w = jnp.transpose(w_qkv, (1, 0, 2))

    def call(kernel, name, outs, ins, mebibytes, flops, scratch=()):
        specs = [SMEM if v.dtype == jnp.int32 else VMEM for v in ins]
        if kernel is begin_kernel:
            specs[2:] = [pl.BlockSpec(memory_space=pltpu.HBM)] * 2
            ins = ins[:2] + tuple(pltpu.with_memory_space_constraint(v, pltpu.HBM) for v in ins[2:])
        return pl.pallas_call(
            kernel,
            name=name,
            out_shape=outs,
            in_specs=specs,
            out_specs=[VMEM] * len(outs),
            scratch_shapes=list(scratch),
            **params(flops, 2 << 20, mebibytes),
        )(*ins)

    def out(rows, cols, kind=BF):
        return jax.ShapeDtypeStruct((rows, cols), kind)

    def held(rows, cols, kind=BF):
        return pltpu.VMEM((rows, cols), kind)

    product = 2 * ROWS * f.shape[1] * 3 * HD
    attention = 2 * GROUP * 9 * BLK * BLK * 2 * HD
    w_mine, fy, total = call(
        begin_kernel,
        "begin",
        [held(w.shape[1], 3 * HD), held(ROWS, f.shape[1]), held(ROWS, 3 * HD, F32)],
        (place, sy, f, w),
        4,
        product,
        [pltpu.SemaphoreType.DMA((4,))],
    )
    (pack,) = call(pack_kernel, "pack", [out(4 * HALF, f.shape[1])], (sd, sx, fy), 4, 0)
    other = across(pack, 0, 1)
    (total,) = call(
        project_across_kernel, "project_across", [held(ROWS, 3 * HD, F32)], (place, pack, total, w_mine), 4, product
    )
    (kv,) = call(project_kv_kernel, "project_kv", [out(ROWS, 2 * HD)], (place, other, total, w_mine), 4, product)

    near_a = group_swap(kv, 0)
    near_b = group_swap(kv, 1)
    (q,) = call(project_q_kernel, "project_q", [held(ROWS, HD)], (place, other, total, w_mine), 4, product)
    far_b = group_swap(lax.dynamic_slice_in_dim(near_a, odd * HALF, HALF, axis=0), 1)
    far_a = group_swap(lax.dynamic_slice_in_dim(near_b, (1 - odd) * HALF, HALF, axis=0), 0)

    link_rows = jnp.zeros((16, HD), BF).at[: block_links.shape[0], : block_links.shape[1]].set(
        block_links.astype(BF)
    )
    d_payload = jnp.concatenate(
        [lax.dynamic_slice_in_dim(d_out, (1 - side) * HD, HD, axis=1), link_rows], axis=0
    )
    d_other = across(d_payload, 1, 0)
    other_links = d_other[HALF : HALF + block_links.shape[0], : block_links.shape[1]].astype(jnp.int32)
    links = jnp.where(
        side == 0,
        jnp.concatenate([block_links, other_links], axis=0),
        jnp.concatenate([other_links, block_links], axis=0),
    )

    mixed, pairs, win, acc, far_a_grad, far_b_grad = call(
        attend_kernel,
        "attend",
        [
            held(GROUP * 9 * BLK, 2 * HD),
            held(GROUP * 2 * BLK, 2 * HD),
            held(WINDOW * BLK, 2 * HD),
            held(WINDOW * BLK, 2 * HD, F32),
            out(HALF, 2 * HD),
            out(HALF, 2 * HD),
        ],
        (place, links, q, kv, near_a, near_b, far_a, far_b, d_out, d_other[:HALF]),
        16,
        2 * attention,
    )
    own, near_a_grad, near_b_grad = call(
        near_grads_kernel,
        "near_grads",
        [held(ROWS, 2 * HD, F32), out(ROWS, 2 * HD), out(ROWS, 2 * HD)],
        (place, links, mixed, pairs, acc),
        8,
        attention,
        [pltpu.VMEM((WINDOW * BLK, 2 * HD), F32)],
    )
    att_own, att_other, dq = call(
        outputs_kernel,
        "outputs",
        [out(HALF, HD), out(HALF, HD), held(ROWS, HD)],
        (place, links, mixed, win),
        8,
        attention,
        [pltpu.VMEM((ROWS, HD), BF)],
    )

    back_a = group_swap(far_a_grad, 0)
    back_b = group_swap(far_b_grad, 1)

    def add_half(whole, part, start):
        old = lax.dynamic_slice_in_dim(whole, start, HALF, axis=0)
        new = (old.astype(F32) + part.astype(F32)).astype(BF)
        return lax.dynamic_update_slice_in_dim(whole, new, start, axis=0)

    from_b = group_swap(add_half(near_b_grad, back_a, (1 - odd) * HALF), 1)
    from_a = group_swap(add_half(near_a_grad, back_b, odd * HALF), 0)
    att_back = across(att_other, 1, 0)
    from_a, from_b, att_back = lax.optimization_barrier((from_a, from_b, att_back))
    attended = jnp.where(
        side == 0,
        jnp.concatenate([att_own, att_back], axis=1),
        jnp.concatenate([att_back, att_own], axis=1),
    )

    send, grads = call(
        spread_send_kernel,
        "spread_send",
        [out(4 * HALF, 2 * HD), held(ROWS, 3 * HD)],
        (place, own, from_a, from_b, dq, w_mine),
        4,
        product,
    )
    (keep,) = call(spread_keep_kernel, "spread_keep", [held(4 * HALF, 2 * HD)], (place, grads, w_mine), 4, product)
    arrived = across(send, 0, 1)
    chip = (keep.astype(F32) + arrived.astype(F32)).astype(BF)
    gd = across(chip[3 * HALF :], 1, 2)
    gy = across(chip[2 * HALF : 3 * HALF], 1, 0)
    gx = across(chip[HALF : 2 * HALF], 0, 2)
    grad_features = (
        chip[:HALF].astype(F32) + gd.astype(F32) + gy.astype(F32) + gx.astype(F32)
    ).astype(BF)
    return attended, grad_features


def solution(mesh):
    sizes = dict(mesh.shape)
    return jax.shard_map(
        functools.partial(body, n_ctx=sizes["ctx"], n_head=sizes["head"]),
        mesh=mesh,
        in_specs=(P("ctx", "head"), P(None, None, "head"), P("ctx", None), P("ctx", "head")),
        out_specs=(P("ctx", "head"), P("ctx", "head")),
        check_vma=False,
    )
```

time: 69.2 us -> 65.2 us (0.942)
  waiting for transfers between devices: 23.8 us -> 16.1 us
  Pallas kernels: 7.11 us -> 13.1 us
  local copies, waits for them, and re-layouts: 2.38 us -> 0.07 us
    ppermute x8, waiting for transfers between devices: 8.86 us -> 2.21 us  [group_swap(): return lax.ppermute(value, 'ctx', pairs)]
    pallas_call x4 -> x10, Pallas kernels: 7.11 us -> 13.1 us  [call(): pl.pallas_call(kernel, name=name, out_shape=outs, in_specs=specs, out_spe...]
    unnamed x10 -> x4, local copies, waits for them, and re-layouts: 2.33 us -> 0.01 us
    ppermute x10, waiting for transfers between devices: 14.9 us -> 13.9 us  [across(): return lax.ppermute(value, ('ctx', 'head'), pairs)]
  transfers between devices with their start and end apart: 18 -> 18, of which waited for: 11 -> 10; matrix products, arithmetic and copies ran while one was open for 2% -> 1% of each run, Pallas kernels for 0% -> 12%
where the time goes in v4:
time: 65.2 us; the launch traced here: 65 us
  starting transfers between devices  33.1 us (51%)
  waiting for transfers between devices  16.1 us (25%)
  Pallas kernels  13.1 us (20%)
  other arithmetic  1.74 us (3%)
  between operations  0.88 us (1%)
    ppermute x8, starting transfers between devices, group_swap(): return lax.ppermute(value, 'ctx', pairs)  21.7 us
    ppermute x10, waiting for transfers between devices, across(): return lax.ppermute(value, ('ctx', 'head'), pairs)  13.9 us
    pallas_call x10, Pallas kernels, call(): pl.pallas_call(kernel, name=name, out_shape=outs, in_specs=specs, out_spe...  13.1 us
    ppermute x10, starting transfers between devices, across(): return lax.ppermute(value, ('ctx', 'head'), pairs)  11.4 us
    ppermute x8, waiting for transfers between devices, group_swap(): return lax.ppermute(value, 'ctx', pairs)  2.21 us
  transfers between devices with their start and end apart: 18, of which 10 were waited for; matrix products, arithmetic and copies ran while one was open for 1% of the time, Pallas kernels for 12%

profile of v4, /device:TPU:0, one launch (start us, length us, event | category | flops | bytes accessed | tf_op | source)
XLA Modules:
  0.0 65.0 jit_solution(6039980888860922788)
XLA Ops:
  0.6 3.0 %collective-permute-start.3 = (bf16[256,256]{1,0:T(8,128)(2,1)}, bf16[256,256]{1,0:T(8,128)(2,1)S(1)}, u32[]{:S(2)}, u32[]{:S(2)}) collective-permute-start(bf16[256,256]{1,0:T(8,128)(2,1)} %f.1), channel_id=1, source_target_pairs={{0,4},{1,5},{2,6},{3,7},{4,0},{5,1},{6,2},{7,3},{8,12},{9,13},{10,... | collective-permute-start | bytes 393224 | tf_op jit(solution)/shard_map/ppermute | solution.py:267
  3.7 1.5 %collective-permute-start.2 = (bf16[256,256]{1,0:T(8,128)(2,1)}, bf16[256,256]{1,0:T(8,128)(2,1)S(1)}, u32[]{:S(2)}, u32[]{:S(2)}) collective-permute-start(bf16[256,256]{1,0:T(8,128)(2,1)} %f.1), channel_id=1, source_target_pairs={{0,2},{1,3},{2,0},{3,1},{4,6},{5,7},{6,4},{7,5},{8,10},{9,11},{10,... | collective-permute-start | bytes 393224 | tf_op jit(solution)/shard_map/ppermute | solution.py:267
  5.3 2.1 %collective-permute-done.3.sy = bf16[256,256]{1,0:T(8,128)(2,1)S(1)} collective-permute-done((bf16[256,256]{1,0:T(8,128)(2,1)}, bf16[256,256]{1,0:T(8,128)(2,1)S(1)}, u32[]{:S(2)}, u32[]{:S(2)}) %collective-permute-start.3) | collective-permute-done | bytes 131104 | tf_op jit(solution)/shard_map/ppermute | solution.py:267
  7.4 2.0 %begin.1 = (bf16[1024,384]{1,0:T(8,128)(2,1)S(1)}, bf16[512,256]{1,0:T(8,128)(2,1)S(1)}, f32[512,384]{1,0:T(8,128)S(1)}) custom-call(s32[4]{0:T(128)S(1)} %pad_add_fusion.place, bf16[256,256]{1,0:T(8,128)(2,1)S(1)} %collective-permute-done.3.sy, bf16[256,256]{1,0:T(8,128)(2,1)} %f.1, bf16[3,1024,256]{2,1,0:T(8,128)(2,1)} %bitcast.5), custom_call_target="tpu_custom_call" | custom-call | flops 100663296 | bytes 2097152 | tf_op jit(solution)/shard_map/begin/pallas_call | solution.py:288
  9.4 0.8 %collective-permute-done.2.sx = bf16[256,256]{1,0:T(8,128)(2,1)S(1)} collective-permute-done((bf16[256,256]{1,0:T(8,128)(2,1)}, bf16[256,256]{1,0:T(8,128)(2,1)S(1)}, u32[]{:S(2)}, u32[]{:S(2)}) %collective-permute-start.2) | collective-permute-done | bytes 131104 | tf_op jit(solution)/shard_map/ppermute | solution.py:267
  10.2 1.2 %collective-permute-done.1.sd = bf16[256,256]{1,0:T(8,128)(2,1)S(1)} collective-permute-done((bf16[256,256]{1,0:T(8,128)(2,1)}, bf16[256,256]{1,0:T(8,128)(2,1)S(1)}, u32[]{:S(2)}, u32[]{:S(2)}) %collective-permute-start.1) | collective-permute-done | bytes 131104 | tf_op jit(solution)/shard_map/ppermute | solution.py:267
  11.6 0.8 %project_across.1.before = f32[512,384]{1,0:T(8,128)S(1)} custom-call(s32[4]{0:T(128)S(1)} %pad_add_fusion.place, bf16[1024,256]{1,0:T(8,128)(2,1)S(1)} %pack.1, f32[512,384]{1,0:T(8,128)S(1)} %get-tuple-element.35.before, bf16[1024,384]{1,0:T(8,128)(2,1)S(1)} %get-tuple-element.36.w_mine), custom_call_target="tpu_custom_call" | custom-call | flops 100663296 | bytes 2097152 | tf_op jit(solution)/shard_map/project_across/pallas_call | solution.py:288
  12.4 1.0 %collective-permute-done.4.other = bf16[1024,256]{1,0:T(8,128)(2,1)S(1)} collective-permute-done((bf16[1024,256]{1,0:T(8,128)(2,1)S(1)}, bf16[1024,256]{1,0:T(8,128)(2,1)S(1)}, u32[]{:S(2)}, u32[]{:S(2)}) %collective-permute-start.4) | collective-permute-done | bytes 524320 | tf_op jit(solution)/shard_map/ppermute | solution.py:267
  13.4 0.8 %project_kv.1.kv = bf16[512,256]{1,0:T(8,128)(2,1)S(1)} custom-call(s32[4]{0:T(128)S(1)} %pad_add_fusion.place, bf16[1024,256]{1,0:T(8,128)(2,1)S(1)} %collective-permute-done.4.other, f32[512,384]{1,0:T(8,128)S(1)} %project_across.1.before, bf16[1024,384]{1,0:T(8,128)(2,1)S(1)} %get-tuple-element.36.w_mine), custom_call_target="tpu_custom_call" | custom-call | flops 100663296 | bytes 2097152 | tf_op jit(solution)/shard_map/project_kv/pallas_call | solution.py:288
  14.3 0.7 %collective-permute-start.6 = (bf16[512,256]{1,0:T(8,128)(2,1)S(1)}, bf16[512,256]{1,0:T(8,128)(2,1)S(1)}, u32[]{:S(2)}, u32[]{:S(2)}) collective-permute-start(bf16[512,256]{1,0:T(8,128)(2,1)S(1)} %project_kv.1.kv), channel_id=1, source_target_pairs={{8,16},{16,8},{12,20},{20,12},{9,17},{17,9},{13,21},{21,13},{10,18... | collective-permute-start | bytes 786440 | tf_op jit(solution)/shard_map/ppermute | solution.py:275
  15.0 4.6 %collective-permute-start.5 = (bf16[512,256]{1,0:T(8,128)(2,1)S(1)}, bf16[512,256]{1,0:T(8,128)(2,1)S(1)}, u32[]{:S(2)}, u32[]{:S(2)}) collective-permute-start(bf16[512,256]{1,0:T(8,128)(2,1)S(1)} %project_kv.1.kv), channel_id=1, source_target_pairs={{0,8},{8,0},{4,12},{12,4},{16,24},{24,16},{20,28},{28,20},{1,9},{9... | collective-permute-start | bytes 786440 | tf_op jit(solution)/shard_map/ppermute | solution.py:275
  19.6 1.6 %collective-permute-start = (bf16[272,128]{1,0:T(8,128)(2,1)S(1)}, bf16[272,128]{1,0:T(8,128)(2,1)S(1)}, u32[]{:S(2)}, u32[]{:S(2)}) collective-permute-start(bf16[272,128]{1,0:T(8,128)(2,1)S(1)} %fusion.3), channel_id=1, source_target_pairs={{0,4},{1,5},{2,6},{3,7},{4,0},{5,1},{6,2},{7,3},{8,12},{9,13},{10,... | collective-permute-start | bytes 208904 | tf_op jit(solution)/shard_map/ppermute | solution.py:267
  21.2 5.1 %collective-permute-start.7 = (bf16[256,256]{1,0:T(8,128)(2,1)S(1)}, bf16[256,256]{1,0:T(8,128)(2,1)S(1)}, u32[]{:S(2)}, u32[]{:S(2)}) collective-permute-start(bf16[256,256]{1,0:T(8,128)(2,1)S(1)} %constant_dynamic-slice_fusion.1), channel_id=1, source_target_pairs={{0,8},{8,0},{4,12},{12,4},{16,24},{24,16},{20,28},{28,20},{1,9},{9... | collective-permute-start | bytes 393224 | tf_op jit(solution)/shard_map/ppermute | solution.py:275
  27.1 0.8 %project_q.1.q = bf16[512,128]{1,0:T(8,128)(2,1)S(1)} custom-call(s32[4]{0:T(128)S(1)} %pad_add_fusion.place, bf16[1024,256]{1,0:T(8,128)(2,1)S(1)} %collective-permute-done.4.other, f32[512,384]{1,0:T(8,128)S(1)} %project_across.1.before, bf16[1024,384]{1,0:T(8,128)(2,1)S(1)} %get-tuple-element.36.w_mine), custom_call_target="tpu_custom_call" | custom-call | flops 100663296 | bytes 2097152 | tf_op jit(solution)/shard_map/project_q/pallas_call | solution.py:288
  27.9 1.4 %collective-permute-done.7.far_a = bf16[256,256]{1,0:T(8,128)(2,1)S(1)} collective-permute-done((bf16[256,256]{1,0:T(8,128)(2,1)S(1)}, bf16[256,256]{1,0:T(8,128)(2,1)S(1)}, u32[]{:S(2)}, u32[]{:S(2)}) %collective-permute-start.7) | collective-permute-done | bytes 131104 | tf_op jit(solution)/shard_map/ppermute | solution.py:275
  29.3 3.4 %attend.1 = (bf16[4608,256]{1,0:T(8,128)(2,1)S(1)}, bf16[1024,256]{1,0:T(8,128)(2,1)S(1)}, bf16[2048,256]{1,0:T(8,128)(2,1)S(1)}, f32[2048,256]{1,0:T(8,128)S(1)...) custom-call(s32[4]{0:T(128)S(1)} %pad_add_fusion.place, s32[4,9]{1,0:T(4,128)S(1)} %add_select_fusion.links, ...), custom_call_target="tpu_custom_call" | custom-call | flops 603979776 | bytes 2097152 | tf_op jit(solution)/shard_map/attend/pallas_call | solution.py:288
  32.7 5.3 %collective-permute-start.11 = (bf16[256,256]{1,0:T(8,128)(2,1)S(1)}, bf16[256,256]{1,0:T(8,128)(2,1)S(1)}, u32[]{:S(2)}, u32[]{:S(2)}) collective-permute-start(bf16[256,256]{1,0:T(8,128)(2,1)S(1)} %get-tuple-element.45), channel_id=1, source_target_pairs={{0,8},{8,0},{4,12},{12,4},{16,24},{24,16},{20,28},{28,20},{1,9},{9... | collective-permute-start | bytes 393224 | tf_op jit(solution)/shard_map/ppermute | solution.py:275
  38.7 1.5 %near_grads.1 = (f32[512,256]{1,0:T(8,128)S(1)}, bf16[512,256]{1,0:T(8,128)(2,1)S(1)}, bf16[512,256]{1,0:T(8,128)(2,1)S(1)}) custom-call(s32[4]{0:T(128)S(1)} %pad_add_fusion.place, s32[4,9]{1,0:T(4,128)S(1)} %add_select_fusion.links, bf16[4608,256]{1,0:T(8,128)(2,1)S(1)} %get-tuple-element.37.mixed, bf16[1024,256]{1,0:T(8,128)(2,1)S(1)} %get-tuple-element.40.pairs, ...), custom_call_target="tpu_custom_call" | custom-call | flops 301989888 | bytes 2097152 | tf_op jit(solution)/shard_map/near_grads/pallas_call | solution.py:288
  40.1 0.8 %collective-permute-done.11 = bf16[256,256]{1,0:T(8,128)(2,1)S(1)} collective-permute-done((bf16[256,256]{1,0:T(8,128)(2,1)S(1)}, bf16[256,256]{1,0:T(8,128)(2,1)S(1)}, u32[]{:S(2)}, u32[]{:S(2)}) %collective-permute-start.11) | collective-permute-done | bytes 131104 | tf_op jit(solution)/shard_map/ppermute | solution.py:275
  41.0 0.7 %collective-permute-start.12 = (bf16[512,256]{1,0:T(8,128)(2,1)S(1)}, bf16[512,256]{1,0:T(8,128)(2,1)S(1)}, u32[]{:S(2)}, u32[]{:S(2)}) collective-permute-start(bf16[512,256]{1,0:T(8,128)(2,1)S(1)} %fusion.2), channel_id=1, source_target_pairs={{8,16},{16,8},{12,20},{20,12},{9,17},{17,9},{13,21},{21,13},{10,18... | collective-permute-start | bytes 786440 | tf_op jit(solution)/shard_map/ppermute | solution.py:275
  41.7 4.0 %collective-permute-start.10 = (bf16[512,256]{1,0:T(8,128)(2,1)S(1)}, bf16[512,256]{1,0:T(8,128)(2,1)S(1)}, u32[]{:S(2)}, u32[]{:S(2)}) collective-permute-start(bf16[512,256]{1,0:T(8,128)(2,1)S(1)} %fusion.1), channel_id=1, source_target_pairs={{0,8},{8,0},{4,12},{12,4},{16,24},{24,16},{20,28},{28,20},{1,9},{9... | collective-permute-start | bytes 786440 | tf_op jit(solution)/shard_map/ppermute | solution.py:275
  45.7 1.6 %outputs.1 = (bf16[256,128]{1,0:T(8,128)(2,1)S(1)}, bf16[256,128]{1,0:T(8,128)(2,1)S(1)}, bf16[512,128]{1,0:T(8,128)(2,1)S(1)}) custom-call(s32[4]{0:T(128)S(1)} %pad_add_fusion.place, s32[4,9]{1,0:T(4,128)S(1)} %add_select_fusion.links, bf16[4608,256]{1,0:T(8,128)(2,1)S(1)} %get-tuple-element.37.mixed, bf16[2048,256]{1,0:T(8,128)(2,1)S(1)} %get-tuple-element.38.win), custom_call_target="tpu_custom_call" | custom-call | flops 301989888 | bytes 2097152 | tf_op jit(solution)/shard_map/outputs/pallas_call | solution.py:288
  47.3 1.6 %collective-permute-start.13 = (bf16[256,128]{1,0:T(8,128)(2,1)S(1)}, bf16[256,128]{1,0:T(8,128)(2,1)S(1)}, u32[]{:S(2)}, u32[]{:S(2)}) collective-permute-start(bf16[256,128]{1,0:T(8,128)(2,1)S(1)} %get-tuple-element.46), channel_id=1, source_target_pairs={{0,4},{1,5},{2,6},{3,7},{4,0},{5,1},{6,2},{7,3},{8,12},{9,13},{10,... | collective-permute-start | bytes 196616 | tf_op jit(solution)/shard_map/ppermute | solution.py:267
  48.9 2.7 %collective-permute-done.13 = bf16[256,128]{1,0:T(8,128)(2,1)S(1)} collective-permute-done((bf16[256,128]{1,0:T(8,128)(2,1)S(1)}, bf16[256,128]{1,0:T(8,128)(2,1)S(1)}, u32[]{:S(2)}, u32[]{:S(2)}) %collective-permute-start.13) | collective-permute-done | bytes 65568 | tf_op jit(solution)/shard_map/ppermute | solution.py:267
  51.6 1.0 %spread_send.1 = (bf16[1024,256]{1,0:T(8,128)(2,1)S(1)}, bf16[512,384]{1,0:T(8,128)(2,1)S(1)}) custom-call(s32[4]{0:T(128)S(1)} %pad_add_fusion.place, f32[512,256]{1,0:T(8,128)S(1)} %get-tuple-element.48.own, bf16[512,256]{1,0:T(8,128)(2,1)S(1)} %collective-permute-done.10.from_a, bf16[512,256]{1,0:T(8,128)(2,1)S(1)} %collective-permute-done.12.from_b, ...), custom_call_target="tpu_custom_call" | custom-call | flops 100663296 | bytes 2097152 | tf_op jit(solution)/shard_map/spread_send/pallas_call | solution.py:288
  52.8 1.0 %spread_keep.1 = bf16[1024,256]{1,0:T(8,128)(2,1)S(1)} custom-call(s32[4]{0:T(128)S(1)} %pad_add_fusion.place, bf16[512,384]{1,0:T(8,128)(2,1)S(1)} %get-tuple-element.52.grads, bf16[1024,384]{1,0:T(8,128)(2,1)S(1)} %get-tuple-element.36.w_mine), custom_call_target="tpu_custom_call" | custom-call | flops 100663296 | bytes 2097152 | tf_op jit(solution)/shard_map/spread_keep/pallas_call | solution.py:288
  53.8 0.9 %collective-permute-done.14 = bf16[1024,256]{1,0:T(8,128)(2,1)S(1)} collective-permute-done((bf16[1024,256]{1,0:T(8,128)(2,1)S(1)}, bf16[1024,256]{1,0:T(8,128)(2,1)S(1)}, u32[]{:S(2)}, u32[]{:S(2)}) %collective-permute-start.14) | collective-permute-done | bytes 524320 | tf_op jit(solution)/shard_map/ppermute | solution.py:267
  54.8 2.5 %collective-permute-start.15 = (bf16[256,256]{1,0:T(8,128)(2,1)S(1)}, bf16[256,256]{1,0:T(8,128)(2,1)S(1)}, u32[]{:S(2)}, u32[]{:S(2)}) collective-permute-start(bf16[256,256]{1,0:T(8,128)(2,1)S(1)} %get-tuple-element.54), channel_id=1, source_target_pairs={{0,6},{1,7},{2,4},{3,5},{4,2},{5,3},{6,0},{7,1},{8,14},{9,15},{10,... | collective-permute-start | bytes 393224 | tf_op jit(solution)/shard_map/ppermute | solution.py:267
  58.4 0.7 %maximum_select_fusion = bf16[256,256]{1,0:T(8,128)(2,1)} fusion(bf16[256,128]{1,0:T(8,128)(2,1)S(1)} %collective-permute-done.13, bf16[256,128]{1,0:T(8,128)(2,1)S(1)} %get-tuple-element.39, pred[]{:T(512)S(6)} %eq.7), kind=kLoop, calls=%fused_computation.8 | loop fusion | flops 589824 | bytes 262145 | tf_op jit(solution)/shard_map/jit(_where)/select_n | solution.py:388
  59.1 3.1 %collective-permute-done.15 = bf16[256,256]{1,0:T(8,128)(2,1)S(1)} collective-permute-done((bf16[256,256]{1,0:T(8,128)(2,1)S(1)}, bf16[256,256]{1,0:T(8,128)(2,1)S(1)}, u32[]{:S(2)}, u32[]{:S(2)}) %collective-permute-start.15) | collective-permute-done | bytes 131104 | tf_op jit(solution)/shard_map/ppermute | solution.py:267
  62.1 2.1 %collective-permute-done.17 = bf16[256,256]{1,0:T(8,128)(2,1)S(1)} collective-permute-done((bf16[256,256]{1,0:T(8,128)(2,1)S(1)}, bf16[256,256]{1,0:T(8,128)(2,1)S(1)}, u32[]{:S(2)}, u32[]{:S(2)}) %collective-permute-start.17) | collective-permute-done | bytes 131104 | tf_op jit(solution)/shard_map/ppermute | solution.py:267
  64.2 0.7 %add_convert_fusion.1 = bf16[256,256]{1,0:T(8,128)(2,1)} fusion(bf16[256,256]{1,0:T(8,128)(2,1)S(1)} %collective-permute-done.17, bf16[256,256]{1,0:T(8,128)(2,1)S(1)} %collective-permute-done.16, bf16[256,256]{1,0:T(8,128)(2,1)S(1)} %collective-permute-done.15, bf16[1024,256]{1,0:T(8,128)(2,1)S(1)} %add_convert_fusion), kind=kLoop, calls=%fused_computation.1 | loop fusion | flops 524288 | bytes 655360 | tf_op jit(solution)/shard_map/convert_element_type | solution.py:410
  (33 shorter events, 3.0 us)
Async XLA Ops:
  0.6 6.7 %collective-permute-start.3 = (bf16[256,256]{1,0:T(8,128)(2,1)}, bf16[256,256]{1,0:T(8,128)(2,1)S(1)}, u32[]{:S(2)}, u32[]{:S(2)}) collective-permute-start(bf16[256,256]{1,0:T(8,128)(2,1)} %f.1), channel_id=1, source_target_pairs={{0,4},{1,5},{2,6},{3,7},{4,0},{5,1},{6,2},{7,3},{8,12},{9,13},{10,... | collective-permute-start | bytes 393224 | tf_op jit(solution)/shard_map/ppermute | solution.py:267
  3.7 6.6 %collective-permute-start.2 = (bf16[256,256]{1,0:T(8,128)(2,1)}, bf16[256,256]{1,0:T(8,128)(2,1)S(1)}, u32[]{:S(2)}, u32[]{:S(2)}) collective-permute-start(bf16[256,256]{1,0:T(8,128)(2,1)} %f.1), channel_id=1, source_target_pairs={{0,2},{1,3},{2,0},{3,1},{4,6},{5,7},{6,4},{7,5},{8,10},{9,11},{10,... | collective-permute-start | bytes 393224 | tf_op jit(solution)/shard_map/ppermute | solution.py:267
  5.2 6.3 %collective-permute-start.1 = (bf16[256,256]{1,0:T(8,128)(2,1)}, bf16[256,256]{1,0:T(8,128)(2,1)S(1)}, u32[]{:S(2)}, u32[]{:S(2)}) collective-permute-start(bf16[256,256]{1,0:T(8,128)(2,1)} %f.1), channel_id=1, source_target_pairs={{0,6},{1,7},{2,4},{3,5},{4,2},{5,3},{6,0},{7,1},{8,14},{9,15},{10,... | collective-permute-start | bytes 393224 | tf_op jit(solution)/shard_map/ppermute | solution.py:267
  11.5 2.0 %collective-permute-start.4 = (bf16[1024,256]{1,0:T(8,128)(2,1)S(1)}, bf16[1024,256]{1,0:T(8,128)(2,1)S(1)}, u32[]{:S(2)}, u32[]{:S(2)}) collective-permute-start(bf16[1024,256]{1,0:T(8,128)(2,1)S(1)} %pack.1), channel_id=1, source_target_pairs={{0,1},{1,0},{2,3},{3,2},{4,5},{5,4},{6,7},{7,6},{8,9},{9,8},{10,11... | collective-permute-start | bytes 1572872 | tf_op jit(solution)/shard_map/ppermute | solution.py:267
  11.6 8.0 %copy-start = (bf16[256,256]{1,0:T(8,128)(2,1)S(1)}, bf16[256,256]{1,0:T(8,128)(2,1)}, u32[]{:S(2)}) copy-start(bf16[256,256]{1,0:T(8,128)(2,1)} %d_own.1) | copy-start | bytes 393220
  11.6 8.0 %copy-start.1 = (s32[2,9]{1,0:T(2,128)S(1)}, s32[2,9]{1,0:T(2,128)}, u32[]{:S(2)}) copy-start(s32[2,9]{1,0:T(2,128)} %param.8) | copy-start | bytes 220
  14.3 6.9 %collective-permute-start.6 = (bf16[512,256]{1,0:T(8,128)(2,1)S(1)}, bf16[512,256]{1,0:T(8,128)(2,1)S(1)}, u32[]{:S(2)}, u32[]{:S(2)}) collective-permute-start(bf16[512,256]{1,0:T(8,128)(2,1)S(1)} %project_kv.1.kv), channel_id=1, source_target_pairs={{8,16},{16,8},{12,20},{20,12},{9,17},{17,9},{13,21},{21,13},{10,18... | collective-permute-start | bytes 786440 | tf_op jit(solution)/shard_map/ppermute | solution.py:275
  15.0 11.4 %collective-permute-start.5 = (bf16[512,256]{1,0:T(8,128)(2,1)S(1)}, bf16[512,256]{1,0:T(8,128)(2,1)S(1)}, u32[]{:S(2)}, u32[]{:S(2)}) collective-permute-start(bf16[512,256]{1,0:T(8,128)(2,1)S(1)} %project_kv.1.kv), channel_id=1, source_target_pairs={{0,8},{8,0},{4,12},{12,4},{16,24},{24,16},{20,28},{28,20},{1,9},{9... | collective-permute-start | bytes 786440 | tf_op jit(solution)/shard_map/ppermute | solution.py:275
  19.6 7.4 %collective-permute-start = (bf16[272,128]{1,0:T(8,128)(2,1)S(1)}, bf16[272,128]{1,0:T(8,128)(2,1)S(1)}, u32[]{:S(2)}, u32[]{:S(2)}) collective-permute-start(bf16[272,128]{1,0:T(8,128)(2,1)S(1)} %fusion.3), channel_id=1, source_target_pairs={{0,4},{1,5},{2,6},{3,7},{4,0},{5,1},{6,2},{7,3},{8,12},{9,13},{10,... | collective-permute-start | bytes 208904 | tf_op jit(solution)/shard_map/ppermute | solution.py:267
  21.2 8.1 %collective-permute-start.7 = (bf16[256,256]{1,0:T(8,128)(2,1)S(1)}, bf16[256,256]{1,0:T(8,128)(2,1)S(1)}, u32[]{:S(2)}, u32[]{:S(2)}) collective-permute-start(bf16[256,256]{1,0:T(8,128)(2,1)S(1)} %constant_dynamic-slice_fusion.1), channel_id=1, source_target_pairs={{0,8},{8,0},{4,12},{12,4},{16,24},{24,16},{20,28},{28,20},{1,9},{9... | collective-permute-start | bytes 393224 | tf_op jit(solution)/shard_map/ppermute | solution.py:275
  26.4 3.0 %collective-permute-start.8 = (bf16[256,256]{1,0:T(8,128)(2,1)S(1)}, bf16[256,256]{1,0:T(8,128)(2,1)S(1)}, u32[]{:S(2)}, u32[]{:S(2)}) collective-permute-start(bf16[256,256]{1,0:T(8,128)(2,1)S(1)} %constant_dynamic-slice_fusion), channel_id=1, source_target_pairs={{8,16},{16,8},{12,20},{20,12},{9,17},{17,9},{13,21},{21,13},{10,18... | collective-permute-start | bytes 393224 | tf_op jit(solution)/shard_map/ppermute | solution.py:275
  32.7 8.2 %collective-permute-start.11 = (bf16[256,256]{1,0:T(8,128)(2,1)S(1)}, bf16[256,256]{1,0:T(8,128)(2,1)S(1)}, u32[]{:S(2)}, u32[]{:S(2)}) collective-permute-start(bf16[256,256]{1,0:T(8,128)(2,1)S(1)} %get-tuple-element.45), channel_id=1, source_target_pairs={{0,8},{8,0},{4,12},{12,4},{16,24},{24,16},{20,28},{28,20},{1,9},{9... | collective-permute-start | bytes 393224 | tf_op jit(solution)/shard_map/ppermute | solution.py:275
  38.0 3.7 %collective-permute-start.9 = (bf16[256,256]{1,0:T(8,128)(2,1)S(1)}, bf16[256,256]{1,0:T(8,128)(2,1)S(1)}, u32[]{:S(2)}, u32[]{:S(2)}) collective-permute-start(bf16[256,256]{1,0:T(8,128)(2,1)S(1)} %get-tuple-element.43), channel_id=1, source_target_pairs={{8,16},{16,8},{12,20},{20,12},{9,17},{17,9},{13,21},{21,13},{10,18... | collective-permute-start | bytes 393224 | tf_op jit(solution)/shard_map/ppermute | solution.py:275
  41.0 10.7 %collective-permute-start.12 = (bf16[512,256]{1,0:T(8,128)(2,1)S(1)}, bf16[512,256]{1,0:T(8,128)(2,1)S(1)}, u32[]{:S(2)}, u32[]{:S(2)}) collective-permute-start(bf16[512,256]{1,0:T(8,128)(2,1)S(1)} %fusion.2), channel_id=1, source_target_pairs={{8,16},{16,8},{12,20},{20,12},{9,17},{17,9},{13,21},{21,13},{10,18... | collective-permute-start | bytes 786440 | tf_op jit(solution)/shard_map/ppermute | solution.py:275
  41.7 9.9 %collective-permute-start.10 = (bf16[512,256]{1,0:T(8,128)(2,1)S(1)}, bf16[512,256]{1,0:T(8,128)(2,1)S(1)}, u32[]{:S(2)}, u32[]{:S(2)}) collective-permute-start(bf16[512,256]{1,0:T(8,128)(2,1)S(1)} %fusion.1), channel_id=1, source_target_pairs={{0,8},{8,0},{4,12},{12,4},{16,24},{24,16},{20,28},{28,20},{1,9},{9... | collective-permute-start | bytes 786440 | tf_op jit(solution)/shard_map/ppermute | solution.py:275
  47.3 4.3 %collective-permute-start.13 = (bf16[256,128]{1,0:T(8,128)(2,1)S(1)}, bf16[256,128]{1,0:T(8,128)(2,1)S(1)}, u32[]{:S(2)}, u32[]{:S(2)}) collective-permute-start(bf16[256,128]{1,0:T(8,128)(2,1)S(1)} %get-tuple-element.46), channel_id=1, source_target_pairs={{0,4},{1,5},{2,6},{3,7},{4,0},{5,1},{6,2},{7,3},{8,12},{9,13},{10,... | collective-permute-start | bytes 196616 | tf_op jit(solution)/shard_map/ppermute | solution.py:267
  52.7 2.0 %collective-permute-start.14 = (bf16[1024,256]{1,0:T(8,128)(2,1)S(1)}, bf16[1024,256]{1,0:T(8,128)(2,1)S(1)}, u32[]{:S(2)}, u32[]{:S(2)}) collective-permute-start(bf16[1024,256]{1,0:T(8,128)(2,1)S(1)} %get-tuple-element.53), channel_id=1, source_target_pairs={{0,1},{1,0},{2,3},{3,2},{4,5},{5,4},{6,7},{7,6},{8,9},{9,8},{10,11... | collective-permute-start | bytes 1572872 | tf_op jit(solution)/shard_map/ppermute | solution.py:267
  54.8 7.3 %collective-permute-start.15 = (bf16[256,256]{1,0:T(8,128)(2,1)S(1)}, bf16[256,256]{1,0:T(8,128)(2,1)S(1)}, u32[]{:S(2)}, u32[]{:S(2)}) collective-permute-start(bf16[256,256]{1,0:T(8,128)(2,1)S(1)} %get-tuple-element.54), channel_id=1, source_target_pairs={{0,6},{1,7},{2,4},{3,5},{4,2},{5,3},{6,0},{7,1},{8,14},{9,15},{10,... | collective-permute-start | bytes 393224 | tf_op jit(solution)/shard_map/ppermute | solution.py:267
  57.3 6.9 %collective-permute-start.17 = (bf16[256,256]{1,0:T(8,128)(2,1)S(1)}, bf16[256,256]{1,0:T(8,128)(2,1)S(1)}, u32[]{:S(2)}, u32[]{:S(2)}) collective-permute-start(bf16[256,256]{1,0:T(8,128)(2,1)S(1)} %get-tuple-element.55), channel_id=1, source_target_pairs={{0,2},{1,3},{2,0},{3,1},{4,6},{5,7},{6,4},{7,5},{8,10},{9,11},{10,... | collective-permute-start | bytes 393224 | tf_op jit(solution)/shard_map/ppermute | solution.py:267
  57.9 6.3 %collective-permute-start.16 = (bf16[256,256]{1,0:T(8,128)(2,1)S(1)}, bf16[256,256]{1,0:T(8,128)(2,1)S(1)}, u32[]{:S(2)}, u32[]{:S(2)}) collective-permute-start(bf16[256,256]{1,0:T(8,128)(2,1)S(1)} %get-tuple-element.56), channel_id=1, source_target_pairs={{0,4},{1,5},{2,6},{3,7},{4,0},{5,1},{6,2},{7,3},{8,12},{9,13},{10,... | collective-permute-start | bytes 393224 | tf_op jit(solution)/shard_map/ppermute | solution.py:267

commit v5 on v4

v5 whole, which is shorter than its diff:
```python
import functools

import jax
import jax.numpy as jnp
from jax import lax
from jax.experimental import pallas as pl
from jax.experimental.pallas import tpu as pltpu
from jax.sharding import PartitionSpec as P

HD = 128
BLK = 128
REACH = 6
SPAN = 3
LOG2E = 1.4426950408889634
DEAD = -1e30
BF = jnp.bfloat16
F32 = jnp.float32

GROUP = 4
ROWS = GROUP * BLK
HALF = ROWS // 2
WINDOW = GROUP + 2 * REACH
NEAR_LEFT = (REACH - GROUP) * BLK
OWN = REACH * BLK
NEAR_RIGHT = OWN + ROWS
FAR_RIGHT = NEAR_RIGHT + ROWS


def params(flops, moved, mebibytes):
    return dict(
        compiler_params=pltpu.CompilerParams(vmem_limit_bytes=mebibytes * 1024 * 1024),
        cost_estimate=pl.CostEstimate(flops=flops, bytes_accessed=moved, transcendentals=0),
    )


VMEM = pl.BlockSpec(memory_space=pltpu.VMEM)
SMEM = pl.BlockSpec(memory_space=pltpu.SMEM)


def dot(a, b, dims):
    return lax.dot_general(a, b, (dims, ((), ())), preferred_element_type=F32)


def position():
    ctx = lax.axis_index("ctx")
    group = ctx // 2
    return ctx % 2, group % 2, group * GROUP, lax.axis_index("head")


def begin_kernel(f, w, w_mine, fm, total, sems):
    side, _, _, head = position()
    copies = [pltpu.make_async_copy(f, fm, sems.at[3])]
    for g in range(3):
        cols = pl.ds(pl.multiple_of(side * HD, HD), HD)
        copies.append(pltpu.make_async_copy(w.at[g, :, cols], w_mine.at[:, pl.ds(g * HD, HD)], sems.at[g]))
    for copy in copies:
        copy.start()
    for copy in copies:
        copy.wait()
    total[...] = dot(fm[...], weight_rows(w_mine, head, fm.shape[1]), ((1,), (0,)))


def weight_rows(w_mine, source, width):
    return w_mine[pl.ds(pl.multiple_of(source * width, width), width), :]


def pack_kernel(fm, sy, sx, sd, out):
    for index, piece in enumerate((fm, sy, sx, sd)):
        out[index * HALF : (index + 1) * HALF, :] = piece[...]


def project_across_kernel(pack, before, w_mine, total):
    head = position()[3]
    width = pack.shape[1]
    far = dot(pack[2 * HALF :, :], weight_rows(w_mine, head ^ 2, width), ((1,), (0,)))
    total[:HALF, :] = before[...] + far[:HALF]
    total[HALF:, :] = far[HALF:] + dot(pack[HALF : 2 * HALF, :], weight_rows(w_mine, head, width), ((1,), (0,)))


def sibling_product(head, other, w_mine, cols):
    width = other.shape[1]
    total = None
    for index in range(2):
        rows = pl.ds(pl.multiple_of((head ^ (1 + 2 * index)) * width, width), width)
        term = dot(other[2 * index * HALF : 2 * (index + 1) * HALF, :], w_mine[rows, cols], ((1,), (0,)))
        total = term if total is None else total + term
    return total


def store_groups(side, total, target):
    for group in range(2):
        rows = pl.ds(pl.multiple_of((side ^ group) * HALF, HALF), HALF)
        target[rows, :] = total[group * HALF : (group + 1) * HALF]


def project_kv_kernel(other, before, w_mine, first_out, second_out):
    side, odd, _, head = position()
    total = (before[:, HD:] + sibling_product(head, other, w_mine, slice(HD, 3 * HD))).astype(BF)
    near_first = side ^ (1 - odd) == 0
    first_out[...] = jnp.where(near_first, total[:HALF], total[HALF:])
    second_out[...] = jnp.where(near_first, total[HALF:], total[:HALF])


def merge_kernel(whole, part, out, which):
    at = pl.ds(pl.multiple_of((position()[1] ^ which) * HALF, HALF), HALF)
    out[...] = whole[...]
    out[at, :] = (whole[at, :].astype(F32) + part[...].astype(F32)).astype(BF)


def lay_out_kernel(own, other, out):
    side = position()[0]
    for half in range(2):
        cols = slice(half * HD, (half + 1) * HD)
        out[:, cols] = jnp.where(side == half, own[...], other[...])


def join_kernel(own_half, arrived, out):
    out[:HALF, :] = own_half[...]
    out[HALF:, :] = arrived[...]


def project_q_kernel(other, before, w_mine, to_a, to_b, q_out):
    del to_a, to_b
    side, _, _, head = position()
    total = before[:, :HD] + sibling_product(head, other, w_mine, slice(0, HD))
    store_groups(side, total.astype(BF), q_out)


def payload_kernel(d_own, link_rows, pack, payload):
    del pack
    side = position()[0]
    payload[:HALF, :] = jnp.where(side == 0, d_own[:, HD:], d_own[:, :HD])
    payload[HALF:, :] = link_rows[...]


def links_kernel(own, other, q, links):
    del q
    side, _, first, _ = position()
    for i in range(GROUP):
        for k in range(3 * SPAN):
            links[i, k] = jnp.where(side == i // 2, own[i % 2, k], other[i % 2, k])
        for t in (1, 2):
            base = jnp.int32(-(1 << 20))
            for j in range(SPAN):
                entry = links[i, SPAN * t + j]
                base = jnp.maximum(base, jnp.where(entry >= 0, entry - j, -(1 << 20)))
            base = jnp.where(base > -(1 << 19), base - first + REACH, REACH + i)
            links[GROUP, 2 * i + t - 1] = jnp.clip(base, 0, WINDOW - SPAN) * BLK


def regions(odd):
    even = 1 - odd
    left_lo, left_hi = NEAR_LEFT, NEAR_LEFT + HALF
    right_lo, right_hi = NEAR_RIGHT, NEAR_RIGHT + HALF
    pick = lambda at_even, at_odd: pl.multiple_of(even * at_even + odd * at_odd, HALF)
    return (
        pick(OWN + HALF, OWN),
        pick(OWN, OWN + HALF),
        pick(right_lo, left_hi),
        pick(left_hi, right_lo),
        pick(right_hi, left_lo),
        pick(FAR_RIGHT, 0),
        pick(left_lo, right_hi),
        pick(0, FAR_RIGHT),
    )


def near_regions(odd):
    even = 1 - odd
    pick = lambda at_even, at_odd: pl.multiple_of(even * at_even + odd * at_odd, HALF)
    return pick(NEAR_RIGHT, NEAR_LEFT), pick(NEAR_LEFT, NEAR_RIGHT)


def start_of(links, i, t):
    if t == 0:
        return (REACH + i - 1) * BLK
    return pl.multiple_of(links[GROUP, 2 * i + t - 1], BLK)


def is_far(i, t):
    return t == (1 if i < GROUP // 2 else 2)


def run_rows(i, t):
    return slice((i * 3 + t) * SPAN * BLK, (i * 3 + t + 1) * SPAN * BLK)


def side_factor():
    scale = HD ** -0.5
    return jnp.where(lax.broadcasted_iota(jnp.int32, (1, 2 * HD), 1) < HD, scale, 1.0).astype(F32)


def attend_kernel(
    links, q, first_kv, second_kv, a1, b1, a2, b2, d_own, d_other,
    mixed, pairs, win, near_acc, far_a_out, far_b_out, acc,
):
    side, odd, _, _ = position()
    scale = HD ** -0.5
    places = regions(odd)
    halves = (
        first_kv[...], second_kv[...], a1[...], b1[...], a2[:HALF, :], a2[HALF:, :], b2[:HALF, :], b2[HALF:, :],
    )
    for at, half in zip(places, halves):
        win[pl.ds(at, HALF), :] = half
    at_far_a, at_far_b = places[5], places[7]
    acc[...] = jnp.zeros_like(acc)
    zeros = jnp.zeros((BLK, HD), BF)
    own_cols = pl.ds(pl.multiple_of(side * HD, HD), HD)
    for i in range(GROUP):
        rows = slice(i * BLK, (i + 1) * BLK)
        here = slice((i % 2) * BLK, (i % 2 + 1) * BLK)
        d_blk = jnp.where(side == i // 2, d_own[here, own_cols], d_other[here, :])
        pair = jnp.concatenate(
            [
                jnp.concatenate([q[rows, :], zeros], axis=1),
                jnp.concatenate([zeros, d_blk], axis=1),
            ],
            axis=0,
        )
        pairs[2 * i * BLK : 2 * (i + 1) * BLK, :] = pair
        scores, prob_grads, peaks, biases = [], [], [], []
        for t in range(3):
            product = dot(win[pl.ds(start_of(links, i, t), SPAN * BLK), :], pair, ((1,), (1,)))
            for j in range(SPAN):
                block = product[j * BLK : (j + 1) * BLK]
                bias = jnp.where(links[i, SPAN * t + j] >= 0, 0.0, DEAD).astype(F32)
                scores.append(block[:, :BLK])
                prob_grads.append(block[:, BLK:])
                biases.append(bias)
                peaks.append(jnp.max(block[:, :BLK].reshape(BLK // 8, 8, BLK), axis=0) + bias)
        largest = peaks[0]
        for peak in peaks[1:]:
            largest = jnp.maximum(largest, peak)
        largest = jnp.max(largest, axis=0, keepdims=True)
        terms = []
        total = jnp.zeros((8, BLK), F32)
        weighted = jnp.zeros((8, BLK), F32)
        for n in range(3 * SPAN):
            term = jnp.exp2((scores[n] - (largest - biases[n])) * (scale * LOG2E))
            terms.append(term)
            total = total + jnp.sum(term.reshape(BLK // 8, 8, BLK), axis=0)
            weighted = weighted + jnp.sum((term * prob_grads[n]).reshape(BLK // 8, 8, BLK), axis=0)
        inverse = 1.0 / jnp.sum(total, axis=0, keepdims=True)
        row_dot = jnp.sum(weighted, axis=0, keepdims=True) * inverse
        for t in range(3):
            parts = []
            for n in range(SPAN * t, SPAN * t + SPAN):
                share = terms[n] * inverse
                grad = share * (prob_grads[n] - row_dot)
                parts.append(jnp.concatenate([grad.astype(BF), share.astype(BF)], axis=1))
            part = jnp.concatenate(parts, axis=0)
            mixed[run_rows(i, t), :] = part
            if is_far(i, t):
                acc[pl.ds(start_of(links, i, t), SPAN * BLK), :] += dot(part, pair, ((1,), (0,)))
    factor = side_factor()
    far_a_out[...] = (acc[pl.ds(at_far_a, HALF), :] * factor).astype(BF)
    far_b_out[...] = (acc[pl.ds(at_far_b, HALF), :] * factor).astype(BF)
    near_acc[:ROWS, :] = acc[NEAR_LEFT:OWN, :]
    near_acc[ROWS:, :] = acc[NEAR_RIGHT:FAR_RIGHT, :]


def near_grads_kernel(links, mixed, pairs, near_acc, own_out, a_out, b_out, acc):
    odd = position()[1]
    acc[NEAR_LEFT:OWN, :] = near_acc[:ROWS, :]
    acc[OWN:NEAR_RIGHT, :] = jnp.zeros((ROWS, 2 * HD), F32)
    acc[NEAR_RIGHT:FAR_RIGHT, :] = near_acc[ROWS:, :]
    for i in range(GROUP):
        pair = pairs[2 * i * BLK : 2 * (i + 1) * BLK, :]
        for t in range(3):
            if not is_far(i, t):
                at = pl.ds(start_of(links, i, t), SPAN * BLK)
                acc[at, :] += dot(mixed[run_rows(i, t), :], pair, ((1,), (0,)))
    factor = side_factor()
    at_a, at_b = near_regions(odd)
    own_out[...] = acc[OWN : OWN + ROWS, :] * factor
    a_out[...] = (acc[pl.ds(at_a, ROWS), :] * factor).astype(BF)
    b_out[...] = (acc[pl.ds(at_b, ROWS), :] * factor).astype(BF)


def outputs_kernel(links, mixed, win, att_own, att_other, dq_out, att):
    side = position()[0]
    for i in range(GROUP):
        rows = slice(i * BLK, (i + 1) * BLK)
        out = None
        for t in range(3):
            keys = win[pl.ds(start_of(links, i, t), SPAN * BLK), :]
            term = dot(mixed[run_rows(i, t), :], keys, ((0,), (0,)))
            out = term if out is None else out + term
        att[rows, :] = out[BLK:, HD:].astype(BF)
        dq_out[rows, :] = (out[:BLK, :HD] * (HD ** -0.5)).astype(BF)
    att_own[...] = att[pl.ds(pl.multiple_of(side * HALF, HALF), HALF), :]
    att_other[...] = att[pl.ds(pl.multiple_of((1 - side) * HALF, HALF), HALF), :]


def spread(grads, w_mine, side, head, target):
    for step in range(2):
        out = dot(grads, weight_rows(w_mine, head ^ (2 * step), 2 * HD), ((1,), (1,))).astype(BF)
        for group in range(2):
            index = 2 * group + step
            part = jnp.where(side == group, out[:HALF], out[HALF:])
            target[index * HALF : (index + 1) * HALF, :] = part


def spread_send_kernel(own, from_a, from_b, dq, w_mine, send, grads):
    dkv = (own[...] + from_a[...].astype(F32) + from_b[...].astype(F32)).astype(BF)
    grads[:, :HD] = dq[...]
    grads[:, HD:] = dkv
    side, _, _, head = position()
    spread(grads[...], w_mine, side, head ^ 1, send)


def spread_keep_kernel(grads, w_mine, keep):
    side, _, _, head = position()
    spread(grads[...], w_mine, side, head, keep)


def body(features, w_qkv, block_links, d_out, n_ctx, n_head):
    n_group = n_ctx // 2

    def across(value, flip_ctx, flip_head):
        pairs = [
            (c * n_head + h, (c ^ flip_ctx) * n_head + (h ^ flip_head))
            for c in range(n_ctx)
            for h in range(n_head)
        ]
        return lax.ppermute(value, ("ctx", "head"), pairs)

    def group_swap(value, offset):
        pairs = []
        for low in range(offset, n_group - 1, 2):
            for s in range(2):
                pairs.append((2 * low + s, 2 * low + 2 + s))
                pairs.append((2 * low + 2 + s, 2 * low + s))
        return lax.ppermute(value, "ctx", pairs)

    f = features
    sx = across(f, 0, 2)
    sy = across(f, 1, 0)
    sd = across(f, 1, 2)
    w = jnp.transpose(w_qkv, (1, 0, 2))

    def call(kernel, name, outs, ins, mebibytes, flops, scratch=()):
        specs = [SMEM if v.dtype == jnp.int32 else VMEM for v in ins]
        if kernel is begin_kernel:
            specs = [pl.BlockSpec(memory_space=pltpu.HBM)] * 2
            ins = [pltpu.with_memory_space_constraint(v, pltpu.HBM) for v in ins]
        return pl.pallas_call(
            kernel,
            name=name,
            out_shape=outs,
            in_specs=specs,
            out_specs=[SMEM if v.dtype == jnp.int32 else VMEM for v in outs],
            scratch_shapes=list(scratch),
            **params(flops, 2 << 20, mebibytes),
        )(*ins)

    def out(rows, cols, kind=BF):
        return jax.ShapeDtypeStruct((rows, cols), kind)

    def held(rows, cols, kind=BF):
        return pltpu.VMEM((rows, cols), kind)

    product = 2 * ROWS * f.shape[1] * 3 * HD
    attention = 2 * GROUP * 9 * BLK * BLK * 2 * HD
    w_mine, fm, total = call(
        begin_kernel,
        "begin",
        [held(w.shape[1], 3 * HD), held(*f.shape), held(HALF, 3 * HD, F32)],
        (f, w),
        4,
        product,
        [pltpu.SemaphoreType.DMA((4,))],
    )
    (pack,) = call(pack_kernel, "pack", [out(4 * HALF, f.shape[1])], (fm, sy, sx, sd), 4, 0)
    other = across(pack, 0, 1)
    (total,) = call(
        project_across_kernel, "project_across", [held(ROWS, 3 * HD, F32)], (pack, total, w_mine), 4, product
    )
    first, second = call(
        project_kv_kernel, "project_kv", [out(HALF, 2 * HD)] * 2, (other, total, w_mine), 4, product
    )

    a1 = group_swap(first, 0)
    b1 = group_swap(second, 1)
    (to_b,) = call(join_kernel, "join_b", [out(ROWS, 2 * HD)], (first, a1), 4, 0)
    (to_a,) = call(join_kernel, "join_a", [out(ROWS, 2 * HD)], (second, b1), 4, 0)
    b2 = group_swap(to_b, 1)
    a2 = group_swap(to_a, 0)
    rows, slots = block_links.shape
    link_rows = jnp.pad(block_links.astype(BF), ((0, 16 - rows), (0, HD - slots)))
    (payload,) = call(payload_kernel, "payload", [out(HALF + 16, HD)], (d_out, link_rows, pack), 4, 0)
    d_other = across(payload, 1, 0)
    (q,) = call(project_q_kernel, "project_q", [held(ROWS, HD)], (other, total, w_mine, to_a, to_b), 4, product)
    other_links = d_other[HALF : HALF + rows, :slots].astype(jnp.int32)
    (links,) = call(
        links_kernel, "links", [pltpu.SMEM((GROUP + 1, slots), jnp.int32)], (block_links, other_links, q), 4, 0
    )
    links = pltpu.with_memory_space_constraint(links, pltpu.SMEM)
    mixed, pairs, win, near_acc, far_a_grad, far_b_grad = call(
        attend_kernel,
        "attend",
        [
            held(GROUP * 9 * BLK, 2 * HD),
            held(GROUP * 2 * BLK, 2 * HD),
            held(WINDOW * BLK, 2 * HD),
            held(2 * ROWS, 2 * HD, F32),
            out(HALF, 2 * HD),
            out(HALF, 2 * HD),
        ],
        (links, q, first, second, a1, b1, a2, b2, d_out, d_other),
        8,
        2 * attention,
        [pltpu.VMEM((WINDOW * BLK, 2 * HD), F32)],
    )
    own, near_a_grad, near_b_grad = call(
        near_grads_kernel,
        "near_grads",
        [held(ROWS, 2 * HD, F32), out(ROWS, 2 * HD), out(ROWS, 2 * HD)],
        (links, mixed, pairs, near_acc),
        4,
        attention,
        [pltpu.VMEM((WINDOW * BLK, 2 * HD), F32)],
    )
    att_own, att_other, dq = call(
        outputs_kernel,
        "outputs",
        [out(HALF, HD), out(HALF, HD), held(ROWS, HD)],
        (links, mixed, win),
        4,
        attention,
        [pltpu.VMEM((ROWS, HD), BF)],
    )

    back_a = group_swap(far_a_grad, 0)
    back_b = group_swap(far_b_grad, 1)

    def merge(whole, part, which, name):
        kernel = functools.partial(merge_kernel, which=which)
        return call(kernel, name, [out(ROWS, 2 * HD)], (whole, part), 4, 0)[0]

    from_b = group_swap(merge(near_b_grad, back_a, 1, "merge_b"), 1)
    from_a = group_swap(merge(near_a_grad, back_b, 0, "merge_a"), 0)
    att_back = across(att_other, 1, 0)
    from_a, from_b, att_back = lax.optimization_barrier((from_a, from_b, att_back))
    (attended,) = call(lay_out_kernel, "lay_out", [out(HALF, 2 * HD)], (att_own, att_back), 4, 0)
    send, grads = call(
        spread_send_kernel,
        "spread_send",
        [out(4 * HALF, 2 * HD), held(ROWS, 3 * HD)],
        (own, from_a, from_b, dq, w_mine),
        4,
        product,
    )
    (keep,) = call(spread_keep_kernel, "spread_keep", [held(4 * HALF, 2 * HD)], (grads, w_mine), 4, product)
    arrived = across(send, 0, 1)
    chip = (keep.astype(F32) + arrived.astype(F32)).astype(BF)
    gd = across(chip[3 * HALF :], 1, 2)
    gy = across(chip[2 * HALF : 3 * HALF], 1, 0)
    gx = across(chip[HALF : 2 * HALF], 0, 2)
    grad_features = (
        chip[:HALF].astype(F32) + gd.astype(F32) + gy.astype(F32) + gx.astype(F32)
    ).astype(BF)
    return attended, grad_features


def solution(mesh):
    sizes = dict(mesh.shape)
    return jax.shard_map(
        functools.partial(body, n_ctx=sizes["ctx"], n_head=sizes["head"]),
        mesh=mesh,
        in_specs=(P("ctx", "head"), P(None, None, "head"), P("ctx", None), P("ctx", "head")),
        out_specs=(P("ctx", "head"), P("ctx", "head")),
        check_vma=False,
    )
```

time: 65.2 us -> 62.5 us (0.959)
  waiting for transfers between devices: 16.1 us -> 21.2 us
  starting transfers between devices: 33.1 us -> 29.6 us
  Pallas kernels: 13.1 us -> 9.74 us
  other arithmetic: 1.74 us -> 0.89 us
    ppermute x8, starting transfers between devices: 21.7 us -> 18.2 us  [group_swap(): return lax.ppermute(value, 'ctx', pairs)]
    pallas_call x10 -> x17, Pallas kernels: 13.1 us -> 9.74 us  [call(): pl.pallas_call(kernel, name=name, out_shape=outs, in_specs=specs, out_spe...]
    ppermute x8, waiting for transfers between devices: 2.21 us -> 5.5 us  [group_swap(): return lax.ppermute(value, 'ctx', pairs)]
    ppermute x10, waiting for transfers between devices: 13.9 us -> 15.7 us  [across(): return lax.ppermute(value, ('ctx', 'head'), pairs)]
    select_n x2 -> x0, other arithmetic: 0.7 us -> none  [the longest x1 0.69 us: body(): jnp.where(side == 0, jnp.concatenate([att_own, att_back], axis=1), jnp.co...]
  transfers between devices with their start and end apart: 18 -> 18, of which waited for: 10 -> 10; matrix products, arithmetic and copies ran while one was open for 1% -> 0% of each run, Pallas kernels for 12% -> 10%
where the time goes in v5:
time: 62.5 us; the launch traced here: 62.3 us
  starting transfers between devices  29.6 us (47%)
  waiting for transfers between devices  21.2 us (34%)
  Pallas kernels  9.74 us (16%)
  other arithmetic  0.89 us (1%)
  between operations  0.84 us (1%)
    ppermute x8, starting transfers between devices, group_swap(): return lax.ppermute(value, 'ctx', pairs)  18.2 us
    ppermute x10, waiting for transfers between devices, across(): return lax.ppermute(value, ('ctx', 'head'), pairs)  15.7 us
    ppermute x10, starting transfers between devices, across(): return lax.ppermute(value, ('ctx', 'head'), pairs)  11.4 us
    pallas_call x17, Pallas kernels, call(): pl.pallas_call(kernel, name=name, out_shape=outs, in_specs=specs, out_spe...  9.74 us
    ppermute x8, waiting for transfers between devices, group_swap(): return lax.ppermute(value, 'ctx', pairs)  5.5 us
  transfers between devices with their start and end apart: 18, of which 10 were waited for; matrix products, arithmetic and copies ran while one was open for 0% of the time, Pallas kernels for 10%

profile of v5, /device:TPU:0, one launch (start us, length us, event | category | flops | bytes accessed | tf_op | source)
XLA Modules:
  0.0 62.3 jit_solution(2260226319038641885)
XLA Ops:
  0.6 3.0 %collective-permute-start = (bf16[256,256]{1,0:T(8,128)(2,1)}, bf16[256,256]{1,0:T(8,128)(2,1)S(1)}, u32[]{:S(2)}, u32[]{:S(2)}) collective-permute-start(bf16[256,256]{1,0:T(8,128)(2,1)} %f.1), channel_id=1, source_target_pairs={{0,4},{1,5},{2,6},{3,7},{4,0},{5,1},{6,2},{7,3},{8,12},{9,13},{10,... | collective-permute-start | bytes 393224 | tf_op jit(solution)/shard_map/ppermute | solution.py:326
  3.7 1.4 %collective-permute-start.2 = (bf16[256,256]{1,0:T(8,128)(2,1)}, bf16[256,256]{1,0:T(8,128)(2,1)S(1)}, u32[]{:S(2)}, u32[]{:S(2)}) collective-permute-start(bf16[256,256]{1,0:T(8,128)(2,1)} %f.1), channel_id=1, source_target_pairs={{0,6},{1,7},{2,4},{3,5},{4,2},{5,3},{6,0},{7,1},{8,14},{9,15},{10,... | collective-permute-start | bytes 393224 | tf_op jit(solution)/shard_map/ppermute | solution.py:326
  5.2 1.4 %begin.1 = (bf16[1024,384]{1,0:T(8,128)(2,1)S(1)}, bf16[256,256]{1,0:T(8,128)(2,1)S(1)}, f32[256,384]{1,0:T(8,128)S(1)}) custom-call(bf16[256,256]{1,0:T(8,128)(2,1)} %f.1, bf16[3,1024,256]{2,1,0:T(8,128)(2,1)} %bitcast.1), custom_call_target="tpu_custom_call" | custom-call | flops 100663296 | bytes 2097152 | tf_op jit(solution)/shard_map/begin/pallas_call | solution.py:347
  6.6 2.9 %collective-permute-done.sy = bf16[256,256]{1,0:T(8,128)(2,1)S(1)} collective-permute-done((bf16[256,256]{1,0:T(8,128)(2,1)}, bf16[256,256]{1,0:T(8,128)(2,1)S(1)}, u32[]{:S(2)}, u32[]{:S(2)}) %collective-permute-start) | collective-permute-done | bytes 131104 | tf_op jit(solution)/shard_map/ppermute | solution.py:326
  9.5 1.6 %collective-permute-done.2.sd = bf16[256,256]{1,0:T(8,128)(2,1)S(1)} collective-permute-done((bf16[256,256]{1,0:T(8,128)(2,1)}, bf16[256,256]{1,0:T(8,128)(2,1)S(1)}, u32[]{:S(2)}, u32[]{:S(2)}) %collective-permute-start.2) | collective-permute-done | bytes 131104 | tf_op jit(solution)/shard_map/ppermute | solution.py:326
  12.0 1.5 %collective-permute-done.4.other = bf16[1024,256]{1,0:T(8,128)(2,1)S(1)} collective-permute-done((bf16[1024,256]{1,0:T(8,128)(2,1)S(1)}, bf16[1024,256]{1,0:T(8,128)(2,1)S(1)}, u32[]{:S(2)}, u32[]{:S(2)}) %collective-permute-start.4) | collective-permute-done | bytes 524320 | tf_op jit(solution)/shard_map/ppermute | solution.py:326
  13.8 0.7 %collective-permute-start.5 = (bf16[256,256]{1,0:T(8,128)(2,1)S(1)}, bf16[256,256]{1,0:T(8,128)(2,1)S(1)}, u32[]{:S(2)}, u32[]{:S(2)}) collective-permute-start(bf16[256,256]{1,0:T(8,128)(2,1)S(1)} %get-tuple-element.27.own_half.second_kv), channel_id=1, source_target_pairs={{8,16},{16,8},{12,20},{20,12},{9,17},{17,9},{13,21},{21,13},{10,18... | collective-permute-start | bytes 393224 | tf_op jit(solution)/shard_map/ppermute | solution.py:334
  14.5 4.6 %collective-permute-start.6 = (bf16[256,256]{1,0:T(8,128)(2,1)S(1)}, bf16[256,256]{1,0:T(8,128)(2,1)S(1)}, u32[]{:S(2)}, u32[]{:S(2)}) collective-permute-start(bf16[256,256]{1,0:T(8,128)(2,1)S(1)} %get-tuple-element.28.own_half.first_kv), channel_id=1, source_target_pairs={{0,8},{8,0},{4,12},{12,4},{16,24},{24,16},{20,28},{28,20},{1,9},{9... | collective-permute-start | bytes 393224 | tf_op jit(solution)/shard_map/ppermute | solution.py:334
  19.2 1.6 %collective-permute-start.3 = (bf16[272,128]{1,0:T(8,128)(2,1)S(1)}, bf16[272,128]{1,0:T(8,128)(2,1)S(1)}, u32[]{:S(2)}, u32[]{:S(2)}) collective-permute-start(bf16[272,128]{1,0:T(8,128)(2,1)S(1)} %payload.1), channel_id=1, source_target_pairs={{0,4},{1,5},{2,6},{3,7},{4,0},{5,1},{6,2},{7,3},{8,12},{9,13},{10,... | collective-permute-start | bytes 208904 | tf_op jit(solution)/shard_map/ppermute | solution.py:326
  20.8 2.3 %collective-permute-start.7 = (bf16[512,256]{1,0:T(8,128)(2,1)S(1)}, bf16[512,256]{1,0:T(8,128)(2,1)S(1)}, u32[]{:S(2)}, u32[]{:S(2)}) collective-permute-start(bf16[512,256]{1,0:T(8,128)(2,1)S(1)} %join_a.1.to_a), channel_id=1, source_target_pairs={{0,8},{8,0},{4,12},{12,4},{16,24},{24,16},{20,28},{28,20},{1,9},{9... | collective-permute-start | bytes 786440 | tf_op jit(solution)/shard_map/ppermute | solution.py:334
  23.1 0.7 %collective-permute-start.8 = (bf16[512,256]{1,0:T(8,128)(2,1)S(1)}, bf16[512,256]{1,0:T(8,128)(2,1)S(1)}, u32[]{:S(2)}, u32[]{:S(2)}) collective-permute-start(bf16[512,256]{1,0:T(8,128)(2,1)S(1)} %join_b.1.to_b), channel_id=1, source_target_pairs={{8,16},{16,8},{12,20},{20,12},{9,17},{17,9},{13,21},{21,13},{10,18... | collective-permute-start | bytes 786440 | tf_op jit(solution)/shard_map/ppermute | solution.py:334
  24.1 0.7 %links.1 = s32[5,9]{1,0:T(8,128)S(4)} custom-call(s32[2,9]{1,0:T(2,128)S(1)} %copy-done.1, s32[2,9]{1,0:T(2,128)S(1)} %slice_convert_fusion.other, bf16[512,128]{1,0:T(8,128)(2,1)S(1)} %project_q.1.q), custom_call_target="tpu_custom_call" | custom-call | bytes 2097152 | tf_op jit(solution)/shard_map/links/pallas_call | solution.py:347
  24.8 4.0 %collective-permute-done.7.a2 = bf16[512,256]{1,0:T(8,128)(2,1)S(1)} collective-permute-done((bf16[512,256]{1,0:T(8,128)(2,1)S(1)}, bf16[512,256]{1,0:T(8,128)(2,1)S(1)}, u32[]{:S(2)}, u32[]{:S(2)}) %collective-permute-start.7) | collective-permute-done | bytes 262176 | tf_op jit(solution)/shard_map/ppermute | solution.py:334
  28.9 2.9 %attend.1 = (bf16[4608,256]{1,0:T(8,128)(2,1)S(1)}, bf16[1024,256]{1,0:T(8,128)(2,1)S(1)}, bf16[2048,256]{1,0:T(8,128)(2,1)S(1)}, f32[1024,256]{1,0:T(8,128)S(1)...) custom-call(s32[5,9]{1,0:T(8,128)S(4)} %links.1, bf16[512,128]{1,0:T(8,128)(2,1)S(1)} %project_q.1.q, ...), custom_call_target="tpu_custom_call" | custom-call | flops 603979776 | bytes 2097152 | tf_op jit(solution)/shard_map/attend/pallas_call | solution.py:347
  31.8 4.7 %collective-permute-start.11 = (bf16[256,256]{1,0:T(8,128)(2,1)S(1)}, bf16[256,256]{1,0:T(8,128)(2,1)S(1)}, u32[]{:S(2)}, u32[]{:S(2)}) collective-permute-start(bf16[256,256]{1,0:T(8,128)(2,1)S(1)} %get-tuple-element.37), channel_id=1, source_target_pairs={{0,8},{8,0},{4,12},{12,4},{16,24},{24,16},{20,28},{28,20},{1,9},{9... | collective-permute-start | bytes 393224 | tf_op jit(solution)/shard_map/ppermute | solution.py:334
  36.5 0.7 %collective-permute-start.9 = (bf16[256,256]{1,0:T(8,128)(2,1)S(1)}, bf16[256,256]{1,0:T(8,128)(2,1)S(1)}, u32[]{:S(2)}, u32[]{:S(2)}) collective-permute-start(bf16[256,256]{1,0:T(8,128)(2,1)S(1)} %get-tuple-element.35), channel_id=1, source_target_pairs={{8,16},{16,8},{12,20},{20,12},{9,17},{17,9},{13,21},{21,13},{10,18... | collective-permute-start | bytes 393224 | tf_op jit(solution)/shard_map/ppermute | solution.py:334
  37.1 0.8 %near_grads.1 = (f32[512,256]{1,0:T(8,128)S(1)}, bf16[512,256]{1,0:T(8,128)(2,1)S(1)}, bf16[512,256]{1,0:T(8,128)(2,1)S(1)}) custom-call(s32[5,9]{1,0:T(8,128)S(4)} %links.1, bf16[4608,256]{1,0:T(8,128)(2,1)S(1)} %get-tuple-element.29.mixed, bf16[1024,256]{1,0:T(8,128)(2,1)S(1)} %get-tuple-element.32.pairs, f32[1024,256]{1,0:T(8,128)S(1)} %get-tuple-element.33.near_acc), custom_call_target="tpu_custom_call" | custom-call | flops 301989888 | bytes 2097152 | tf_op jit(solution)/shard_map/near_grads/pallas_call | solution.py:347
  37.9 1.5 %collective-permute-done.11.part = bf16[256,256]{1,0:T(8,128)(2,1)S(1)} collective-permute-done((bf16[256,256]{1,0:T(8,128)(2,1)S(1)}, bf16[256,256]{1,0:T(8,128)(2,1)S(1)}, u32[]{:S(2)}, u32[]{:S(2)}) %collective-permute-start.11) | collective-permute-done | bytes 131104 | tf_op jit(solution)/shard_map/ppermute | solution.py:334
  39.5 0.7 %collective-permute-start.12 = (bf16[512,256]{1,0:T(8,128)(2,1)S(1)}, bf16[512,256]{1,0:T(8,128)(2,1)S(1)}, u32[]{:S(2)}, u32[]{:S(2)}) collective-permute-start(bf16[512,256]{1,0:T(8,128)(2,1)S(1)} %merge_b.1), channel_id=1, source_target_pairs={{8,16},{16,8},{12,20},{20,12},{9,17},{17,9},{13,21},{21,13},{10,18... | collective-permute-start | bytes 786440 | tf_op jit(solution)/shard_map/ppermute | solution.py:334
  40.2 4.0 %collective-permute-start.10 = (bf16[512,256]{1,0:T(8,128)(2,1)S(1)}, bf16[512,256]{1,0:T(8,128)(2,1)S(1)}, u32[]{:S(2)}, u32[]{:S(2)}) collective-permute-start(bf16[512,256]{1,0:T(8,128)(2,1)S(1)} %merge_a.1), channel_id=1, source_target_pairs={{0,8},{8,0},{4,12},{12,4},{16,24},{24,16},{20,28},{28,20},{1,9},{9... | collective-permute-start | bytes 786440 | tf_op jit(solution)/shard_map/ppermute | solution.py:334
  44.2 1.0 %outputs.1 = (bf16[256,128]{1,0:T(8,128)(2,1)S(1)}, bf16[256,128]{1,0:T(8,128)(2,1)S(1)}, bf16[512,128]{1,0:T(8,128)(2,1)S(1)}) custom-call(s32[5,9]{1,0:T(8,128)S(4)} %links.1, bf16[4608,256]{1,0:T(8,128)(2,1)S(1)} %get-tuple-element.29.mixed, bf16[2048,256]{1,0:T(8,128)(2,1)S(1)} %get-tuple-element.30.win), custom_call_target="tpu_custom_call" | custom-call | flops 301989888 | bytes 2097152 | tf_op jit(solution)/shard_map/outputs/pallas_call | solution.py:347
  45.2 1.6 %collective-permute-start.13 = (bf16[256,128]{1,0:T(8,128)(2,1)S(1)}, bf16[256,128]{1,0:T(8,128)(2,1)S(1)}, u32[]{:S(2)}, u32[]{:S(2)}) collective-permute-start(bf16[256,128]{1,0:T(8,128)(2,1)S(1)} %get-tuple-element.38), channel_id=1, source_target_pairs={{0,4},{1,5},{2,6},{3,7},{4,0},{5,1},{6,2},{7,3},{8,12},{9,13},{10,... | collective-permute-start | bytes 196616 | tf_op jit(solution)/shard_map/ppermute | solution.py:326
  46.8 2.7 %collective-permute-done.13.other = bf16[256,128]{1,0:T(8,128)(2,1)S(1)} collective-permute-done((bf16[256,128]{1,0:T(8,128)(2,1)S(1)}, bf16[256,128]{1,0:T(8,128)(2,1)S(1)}, u32[]{:S(2)}, u32[]{:S(2)}) %collective-permute-start.13) | collective-permute-done | bytes 65568 | tf_op jit(solution)/shard_map/ppermute | solution.py:326
  49.5 0.5 spread_send.1
  50.6 1.4 %collective-permute-done.14 = bf16[1024,256]{1,0:T(8,128)(2,1)S(1)} collective-permute-done((bf16[1024,256]{1,0:T(8,128)(2,1)S(1)}, bf16[1024,256]{1,0:T(8,128)(2,1)S(1)}, u32[]{:S(2)}, u32[]{:S(2)}) %collective-permute-start.14) | collective-permute-done | bytes 524320 | tf_op jit(solution)/shard_map/ppermute | solution.py:326
  52.2 2.5 %collective-permute-start.15 = (bf16[256,256]{1,0:T(8,128)(2,1)S(1)}, bf16[256,256]{1,0:T(8,128)(2,1)S(1)}, u32[]{:S(2)}, u32[]{:S(2)}) collective-permute-start(bf16[256,256]{1,0:T(8,128)(2,1)S(1)} %get-tuple-element.46), channel_id=1, source_target_pairs={{0,6},{1,7},{2,4},{3,5},{4,2},{5,3},{6,0},{7,1},{8,14},{9,15},{10,... | collective-permute-start | bytes 393224 | tf_op jit(solution)/shard_map/ppermute | solution.py:326
  54.7 0.5 collective-permute-start.17
  55.3 0.5 collective-permute-start.16
  55.8 0.7 %lay_out.1 = bf16[256,256]{1,0:T(8,128)(2,1)} custom-call(bf16[256,128]{1,0:T(8,128)(2,1)S(1)} %get-tuple-element.31.own, bf16[256,128]{1,0:T(8,128)(2,1)S(1)} %collective-permute-done.13.other), custom_call_target="tpu_custom_call" | custom-call | bytes 2097152 | tf_op jit(solution)/shard_map/lay_out/pallas_call | solution.py:347
  56.5 3.1 %collective-permute-done.15 = bf16[256,256]{1,0:T(8,128)(2,1)S(1)} collective-permute-done((bf16[256,256]{1,0:T(8,128)(2,1)S(1)}, bf16[256,256]{1,0:T(8,128)(2,1)S(1)}, u32[]{:S(2)}, u32[]{:S(2)}) %collective-permute-start.15) | collective-permute-done | bytes 131104 | tf_op jit(solution)/shard_map/ppermute | solution.py:326
  59.5 2.1 %collective-permute-done.17 = bf16[256,256]{1,0:T(8,128)(2,1)S(1)} collective-permute-done((bf16[256,256]{1,0:T(8,128)(2,1)S(1)}, bf16[256,256]{1,0:T(8,128)(2,1)S(1)}, u32[]{:S(2)}, u32[]{:S(2)}) %collective-permute-start.17) | collective-permute-done | bytes 131104 | tf_op jit(solution)/shard_map/ppermute | solution.py:326
  61.6 0.7 %add_convert_fusion.1 = bf16[256,256]{1,0:T(8,128)(2,1)} fusion(bf16[256,256]{1,0:T(8,128)(2,1)S(1)} %collective-permute-done.17, bf16[256,256]{1,0:T(8,128)(2,1)S(1)} %collective-permute-done.16, bf16[256,256]{1,0:T(8,128)(2,1)S(1)} %collective-permute-done.15, bf16[1024,256]{1,0:T(8,128)(2,1)S(1)} %add_convert_fusion), kind=kLoop, calls=%fused_computation.1 | loop fusion | flops 524288 | bytes 655360 | tf_op jit(solution)/shard_map/convert_element_type | solution.py:462
  (31 shorter events, 2.5 us)
Async XLA Ops:
  0.6 8.9 %collective-permute-start = (bf16[256,256]{1,0:T(8,128)(2,1)}, bf16[256,256]{1,0:T(8,128)(2,1)S(1)}, u32[]{:S(2)}, u32[]{:S(2)}) collective-permute-start(bf16[256,256]{1,0:T(8,128)(2,1)} %f.1), channel_id=1, source_target_pairs={{0,4},{1,5},{2,6},{3,7},{4,0},{5,1},{6,2},{7,3},{8,12},{9,13},{10,... | collective-permute-start | bytes 393224 | tf_op jit(solution)/shard_map/ppermute | solution.py:326
  3.7 7.5 %collective-permute-start.2 = (bf16[256,256]{1,0:T(8,128)(2,1)}, bf16[256,256]{1,0:T(8,128)(2,1)S(1)}, u32[]{:S(2)}, u32[]{:S(2)}) collective-permute-start(bf16[256,256]{1,0:T(8,128)(2,1)} %f.1), channel_id=1, source_target_pairs={{0,6},{1,7},{2,4},{3,5},{4,2},{5,3},{6,0},{7,1},{8,14},{9,15},{10,... | collective-permute-start | bytes 393224 | tf_op jit(solution)/shard_map/ppermute | solution.py:326
  5.1 6.4 %collective-permute-start.1 = (bf16[256,256]{1,0:T(8,128)(2,1)}, bf16[256,256]{1,0:T(8,128)(2,1)S(1)}, u32[]{:S(2)}, u32[]{:S(2)}) collective-permute-start(bf16[256,256]{1,0:T(8,128)(2,1)} %f.1), channel_id=1, source_target_pairs={{0,2},{1,3},{2,0},{3,1},{4,6},{5,7},{6,4},{7,5},{8,10},{9,11},{10,... | collective-permute-start | bytes 393224 | tf_op jit(solution)/shard_map/ppermute | solution.py:326
  11.5 7.6 %copy-start.1 = (s32[2,9]{1,0:T(2,128)S(1)}, s32[2,9]{1,0:T(2,128)}, u32[]{:S(2)}) copy-start(s32[2,9]{1,0:T(2,128)} %own.1) | copy-start | bytes 220
  11.6 7.6 %copy-start = (bf16[256,256]{1,0:T(8,128)(2,1)S(1)}, bf16[256,256]{1,0:T(8,128)(2,1)}, u32[]{:S(2)}) copy-start(bf16[256,256]{1,0:T(8,128)(2,1)} %d_own.3) | copy-start | bytes 393220
  11.6 2.0 %collective-permute-start.4 = (bf16[1024,256]{1,0:T(8,128)(2,1)S(1)}, bf16[1024,256]{1,0:T(8,128)(2,1)S(1)}, u32[]{:S(2)}, u32[]{:S(2)}) collective-permute-start(bf16[1024,256]{1,0:T(8,128)(2,1)S(1)} %pack.1), channel_id=1, source_target_pairs={{0,1},{1,0},{2,3},{3,2},{4,5},{5,4},{6,7},{7,6},{8,9},{9,8},{10,11... | collective-permute-start | bytes 1572872 | tf_op jit(solution)/shard_map/ppermute | solution.py:326
  13.8 6.9 %collective-permute-start.5 = (bf16[256,256]{1,0:T(8,128)(2,1)S(1)}, bf16[256,256]{1,0:T(8,128)(2,1)S(1)}, u32[]{:S(2)}, u32[]{:S(2)}) collective-permute-start(bf16[256,256]{1,0:T(8,128)(2,1)S(1)} %get-tuple-element.27.own_half.second_kv), channel_id=1, source_target_pairs={{8,16},{16,8},{12,20},{20,12},{9,17},{17,9},{13,21},{21,13},{10,18... | collective-permute-start | bytes 393224 | tf_op jit(solution)/shard_map/ppermute | solution.py:334
  14.5 8.6 %collective-permute-start.6 = (bf16[256,256]{1,0:T(8,128)(2,1)S(1)}, bf16[256,256]{1,0:T(8,128)(2,1)S(1)}, u32[]{:S(2)}, u32[]{:S(2)}) collective-permute-start(bf16[256,256]{1,0:T(8,128)(2,1)S(1)} %get-tuple-element.28.own_half.first_kv), channel_id=1, source_target_pairs={{0,8},{8,0},{4,12},{12,4},{16,24},{24,16},{20,28},{28,20},{1,9},{9... | collective-permute-start | bytes 393224 | tf_op jit(solution)/shard_map/ppermute | solution.py:334
  19.2 4.6 %collective-permute-start.3 = (bf16[272,128]{1,0:T(8,128)(2,1)S(1)}, bf16[272,128]{1,0:T(8,128)(2,1)S(1)}, u32[]{:S(2)}, u32[]{:S(2)}) collective-permute-start(bf16[272,128]{1,0:T(8,128)(2,1)S(1)} %payload.1), channel_id=1, source_target_pairs={{0,4},{1,5},{2,6},{3,7},{4,0},{5,1},{6,2},{7,3},{8,12},{9,13},{10,... | collective-permute-start | bytes 208904 | tf_op jit(solution)/shard_map/ppermute | solution.py:326
  20.8 8.1 %collective-permute-start.7 = (bf16[512,256]{1,0:T(8,128)(2,1)S(1)}, bf16[512,256]{1,0:T(8,128)(2,1)S(1)}, u32[]{:S(2)}, u32[]{:S(2)}) collective-permute-start(bf16[512,256]{1,0:T(8,128)(2,1)S(1)} %join_a.1.to_a), channel_id=1, source_target_pairs={{0,8},{8,0},{4,12},{12,4},{16,24},{24,16},{20,28},{28,20},{1,9},{9... | collective-permute-start | bytes 786440 | tf_op jit(solution)/shard_map/ppermute | solution.py:334
  23.1 5.8 %collective-permute-start.8 = (bf16[512,256]{1,0:T(8,128)(2,1)S(1)}, bf16[512,256]{1,0:T(8,128)(2,1)S(1)}, u32[]{:S(2)}, u32[]{:S(2)}) collective-permute-start(bf16[512,256]{1,0:T(8,128)(2,1)S(1)} %join_b.1.to_b), channel_id=1, source_target_pairs={{8,16},{16,8},{12,20},{20,12},{9,17},{17,9},{13,21},{21,13},{10,18... | collective-permute-start | bytes 786440 | tf_op jit(solution)/shard_map/ppermute | solution.py:334
  31.8 7.6 %collective-permute-start.11 = (bf16[256,256]{1,0:T(8,128)(2,1)S(1)}, bf16[256,256]{1,0:T(8,128)(2,1)S(1)}, u32[]{:S(2)}, u32[]{:S(2)}) collective-permute-start(bf16[256,256]{1,0:T(8,128)(2,1)S(1)} %get-tuple-element.37), channel_id=1, source_target_pairs={{0,8},{8,0},{4,12},{12,4},{16,24},{24,16},{20,28},{28,20},{1,9},{9... | collective-permute-start | bytes 393224 | tf_op jit(solution)/shard_map/ppermute | solution.py:334
  36.5 3.7 %collective-permute-start.9 = (bf16[256,256]{1,0:T(8,128)(2,1)S(1)}, bf16[256,256]{1,0:T(8,128)(2,1)S(1)}, u32[]{:S(2)}, u32[]{:S(2)}) collective-permute-start(bf16[256,256]{1,0:T(8,128)(2,1)S(1)} %get-tuple-element.35), channel_id=1, source_target_pairs={{8,16},{16,8},{12,20},{20,12},{9,17},{17,9},{13,21},{21,13},{10,18... | collective-permute-start | bytes 393224 | tf_op jit(solution)/shard_map/ppermute | solution.py:334
  39.5 10.1 %collective-permute-start.12 = (bf16[512,256]{1,0:T(8,128)(2,1)S(1)}, bf16[512,256]{1,0:T(8,128)(2,1)S(1)}, u32[]{:S(2)}, u32[]{:S(2)}) collective-permute-start(bf16[512,256]{1,0:T(8,128)(2,1)S(1)} %merge_b.1), channel_id=1, source_target_pairs={{8,16},{16,8},{12,20},{20,12},{9,17},{17,9},{13,21},{21,13},{10,18... | collective-permute-start | bytes 786440 | tf_op jit(solution)/shard_map/ppermute | solution.py:334
  40.2 9.3 %collective-permute-start.10 = (bf16[512,256]{1,0:T(8,128)(2,1)S(1)}, bf16[512,256]{1,0:T(8,128)(2,1)S(1)}, u32[]{:S(2)}, u32[]{:S(2)}) collective-permute-start(bf16[512,256]{1,0:T(8,128)(2,1)S(1)} %merge_a.1), channel_id=1, source_target_pairs={{0,8},{8,0},{4,12},{12,4},{16,24},{24,16},{20,28},{28,20},{1,9},{9... | collective-permute-start | bytes 786440 | tf_op jit(solution)/shard_map/ppermute | solution.py:334
  45.2 4.3 %collective-permute-start.13 = (bf16[256,128]{1,0:T(8,128)(2,1)S(1)}, bf16[256,128]{1,0:T(8,128)(2,1)S(1)}, u32[]{:S(2)}, u32[]{:S(2)}) collective-permute-start(bf16[256,128]{1,0:T(8,128)(2,1)S(1)} %get-tuple-element.38), channel_id=1, source_target_pairs={{0,4},{1,5},{2,6},{3,7},{4,0},{5,1},{6,2},{7,3},{8,12},{9,13},{10,... | collective-permute-start | bytes 196616 | tf_op jit(solution)/shard_map/ppermute | solution.py:326
  50.1 2.0 %collective-permute-start.14 = (bf16[1024,256]{1,0:T(8,128)(2,1)S(1)}, bf16[1024,256]{1,0:T(8,128)(2,1)S(1)}, u32[]{:S(2)}, u32[]{:S(2)}) collective-permute-start(bf16[1024,256]{1,0:T(8,128)(2,1)S(1)} %get-tuple-element.45), channel_id=1, source_target_pairs={{0,1},{1,0},{2,3},{3,2},{4,5},{5,4},{6,7},{7,6},{8,9},{9,8},{10,11... | collective-permute-start | bytes 1572872 | tf_op jit(solution)/shard_map/ppermute | solution.py:326
  52.2 7.3 %collective-permute-start.15 = (bf16[256,256]{1,0:T(8,128)(2,1)S(1)}, bf16[256,256]{1,0:T(8,128)(2,1)S(1)}, u32[]{:S(2)}, u32[]{:S(2)}) collective-permute-start(bf16[256,256]{1,0:T(8,128)(2,1)S(1)} %get-tuple-element.46), channel_id=1, source_target_pairs={{0,6},{1,7},{2,4},{3,5},{4,2},{5,3},{6,0},{7,1},{8,14},{9,15},{10,... | collective-permute-start | bytes 393224 | tf_op jit(solution)/shard_map/ppermute | solution.py:326
  54.7 6.9 %collective-permute-start.17 = (bf16[256,256]{1,0:T(8,128)(2,1)S(1)}, bf16[256,256]{1,0:T(8,128)(2,1)S(1)}, u32[]{:S(2)}, u32[]{:S(2)}) collective-permute-start(bf16[256,256]{1,0:T(8,128)(2,1)S(1)} %get-tuple-element.47), channel_id=1, source_target_pairs={{0,2},{1,3},{2,0},{3,1},{4,6},{5,7},{6,4},{7,5},{8,10},{9,11},{10,... | collective-permute-start | bytes 393224 | tf_op jit(solution)/shard_map/ppermute | solution.py:326
  55.3 6.3 %collective-permute-start.16 = (bf16[256,256]{1,0:T(8,128)(2,1)S(1)}, bf16[256,256]{1,0:T(8,128)(2,1)S(1)}, u32[]{:S(2)}, u32[]{:S(2)}) collective-permute-start(bf16[256,256]{1,0:T(8,128)(2,1)S(1)} %get-tuple-element.48), channel_id=1, source_target_pairs={{0,4},{1,5},{2,6},{3,7},{4,0},{5,1},{6,2},{7,3},{8,12},{9,13},{10,... | collective-permute-start | bytes 393224 | tf_op jit(solution)/shard_map/ppermute | solution.py:326

commit v6 on v5

--- a/solution.py
+++ b/solution.py
@@ -326,12 +326,16 @@
         return lax.ppermute(value, ("ctx", "head"), pairs)
 
     def group_swap(value, offset):
+        partner = list(range(n_group))
+        for low in range(offset, n_group - 1, 2):
+            partner[low], partner[low + 1] = low + 1, low
         pairs = []
-        for low in range(offset, n_group - 1, 2):
-            for s in range(2):
-                pairs.append((2 * low + s, 2 * low + 2 + s))
-                pairs.append((2 * low + 2 + s, 2 * low + s))
-        return lax.ppermute(value, "ctx", pairs)
+        for ctx in range(n_ctx):
+            group, side = divmod(ctx, 2)
+            for h in range(n_head):
+                alone = 1 if partner[group] == group else 0
+                pairs.append((ctx * n_head + h, (2 * partner[group] + side) * n_head + (h ^ alone)))
+        return lax.ppermute(value, ("ctx", "head"), pairs)
 
     f = features
     sx = across(f, 0, 2)

time: 62.5 us -> 57.6 us (0.922)
  starting transfers between devices: 29.6 us -> 22.8 us
  waiting for transfers between devices: 21.2 us -> 23.1 us
    ppermute x8, starting transfers between devices: 18.2 us -> 11.4 us  [group_swap(): return lax.ppermute(value, ('ctx', 'head'), pairs)]
    ppermute x8, waiting for transfers between devices: 5.5 us -> 7.12 us  [group_swap(): return lax.ppermute(value, ('ctx', 'head'), pairs)]
  transfers between devices with their start and end apart: 18 -> 18, of which waited for: 10 -> 12; matrix products, arithmetic and copies ran while one was open for 0% -> 0% of each run, Pallas kernels for 10% -> 10%
where the time goes in v6:
time: 57.6 us; the launch traced here: 57.4 us
  waiting for transfers between devices  23.1 us (40%)
  starting transfers between devices  22.8 us (40%)
  Pallas kernels  9.74 us (17%)
  other arithmetic  0.89 us (2%)
  between operations  0.82 us (1%)
    ppermute x10, waiting for transfers between devices, across(): return lax.ppermute(value, ('ctx', 'head'), pairs)  15.9 us
    ppermute x10, starting transfers between devices, across(): return lax.ppermute(value, ('ctx', 'head'), pairs)  11.4 us
    ppermute x8, starting transfers between devices, group_swap(): return lax.ppermute(value, ('ctx', 'head'), pairs)  11.4 us
    pallas_call x17, Pallas kernels, call(): pl.pallas_call(kernel, name=name, out_shape=outs, in_specs=specs, out_spe...  9.74 us
    ppermute x8, waiting for transfers between devices, group_swap(): return lax.ppermute(value, ('ctx', 'head'), pairs)  7.12 us
  transfers between devices with their start and end apart: 18, of which 12 were waited for; matrix products, arithmetic and copies ran while one was open for 0% of the time, Pallas kernels for 10%

profile of v6, /device:TPU:0, one launch (start us, length us, event | category | flops | bytes accessed | tf_op | source)
XLA Modules:
  0.0 57.4 jit_solution(10740033816404776783)
XLA Ops:
  0.6 3.0 %collective-permute-start = (bf16[256,256]{1,0:T(8,128)(2,1)}, bf16[256,256]{1,0:T(8,128)(2,1)S(1)}, u32[]{:S(2)}, u32[]{:S(2)}) collective-permute-start(bf16[256,256]{1,0:T(8,128)(2,1)} %f.1), channel_id=1, source_target_pairs={{0,4},{1,5},{2,6},{3,7},{4,0},{5,1},{6,2},{7,3},{8,12},{9,13},{10,... | collective-permute-start | bytes 393224 | tf_op jit(solution)/shard_map/ppermute | solution.py:326
  3.7 1.4 %collective-permute-start.2 = (bf16[256,256]{1,0:T(8,128)(2,1)}, bf16[256,256]{1,0:T(8,128)(2,1)S(1)}, u32[]{:S(2)}, u32[]{:S(2)}) collective-permute-start(bf16[256,256]{1,0:T(8,128)(2,1)} %f.1), channel_id=1, source_target_pairs={{0,6},{1,7},{2,4},{3,5},{4,2},{5,3},{6,0},{7,1},{8,14},{9,15},{10,... | collective-permute-start | bytes 393224 | tf_op jit(solution)/shard_map/ppermute | solution.py:326
  5.2 1.4 %begin.1 = (bf16[1024,384]{1,0:T(8,128)(2,1)S(1)}, bf16[256,256]{1,0:T(8,128)(2,1)S(1)}, f32[256,384]{1,0:T(8,128)S(1)}) custom-call(bf16[256,256]{1,0:T(8,128)(2,1)} %f.1, bf16[3,1024,256]{2,1,0:T(8,128)(2,1)} %bitcast.1), custom_call_target="tpu_custom_call" | custom-call | flops 100663296 | bytes 2097152 | tf_op jit(solution)/shard_map/begin/pallas_call | solution.py:351
  6.6 2.9 %collective-permute-done.sy = bf16[256,256]{1,0:T(8,128)(2,1)S(1)} collective-permute-done((bf16[256,256]{1,0:T(8,128)(2,1)}, bf16[256,256]{1,0:T(8,128)(2,1)S(1)}, u32[]{:S(2)}, u32[]{:S(2)}) %collective-permute-start) | collective-permute-done | bytes 131104 | tf_op jit(solution)/shard_map/ppermute | solution.py:326
  9.5 1.6 %collective-permute-done.2.sd = bf16[256,256]{1,0:T(8,128)(2,1)S(1)} collective-permute-done((bf16[256,256]{1,0:T(8,128)(2,1)}, bf16[256,256]{1,0:T(8,128)(2,1)S(1)}, u32[]{:S(2)}, u32[]{:S(2)}) %collective-permute-start.2) | collective-permute-done | bytes 131104 | tf_op jit(solution)/shard_map/ppermute | solution.py:326
  11.2 0.3 collective-permute-done.1.sx
  11.6 0.4 project_across.1.before
  12.0 1.5 %collective-permute-done.4.other = bf16[1024,256]{1,0:T(8,128)(2,1)S(1)} collective-permute-done((bf16[1024,256]{1,0:T(8,128)(2,1)S(1)}, bf16[1024,256]{1,0:T(8,128)(2,1)S(1)}, u32[]{:S(2)}, u32[]{:S(2)}) %collective-permute-start.4) | collective-permute-done | bytes 524320 | tf_op jit(solution)/shard_map/ppermute | solution.py:326
  14.1 3.1 %collective-permute-start.6 = (bf16[256,256]{1,0:T(8,128)(2,1)S(1)}, bf16[256,256]{1,0:T(8,128)(2,1)S(1)}, u32[]{:S(2)}, u32[]{:S(2)}) collective-permute-start(bf16[256,256]{1,0:T(8,128)(2,1)S(1)} %get-tuple-element.28.own_half.first_kv), channel_id=1, source_target_pairs={{0,8},{1,9},{2,10},{3,11},{4,12},{5,13},{6,14},{7,15},{8,0},{9,1},... | collective-permute-start | bytes 393224 | tf_op jit(solution)/shard_map/ppermute | solution.py:338
  17.3 1.6 %collective-permute-start.3 = (bf16[272,128]{1,0:T(8,128)(2,1)S(1)}, bf16[272,128]{1,0:T(8,128)(2,1)S(1)}, u32[]{:S(2)}, u32[]{:S(2)}) collective-permute-start(bf16[272,128]{1,0:T(8,128)(2,1)S(1)} %payload.1), channel_id=1, source_target_pairs={{0,4},{1,5},{2,6},{3,7},{4,0},{5,1},{6,2},{7,3},{8,12},{9,13},{10,... | collective-permute-start | bytes 208904 | tf_op jit(solution)/shard_map/ppermute | solution.py:326
  18.9 2.4 %collective-permute-start.7 = (bf16[512,256]{1,0:T(8,128)(2,1)S(1)}, bf16[512,256]{1,0:T(8,128)(2,1)S(1)}, u32[]{:S(2)}, u32[]{:S(2)}) collective-permute-start(bf16[512,256]{1,0:T(8,128)(2,1)S(1)} %join_a.1.to_a), channel_id=1, source_target_pairs={{0,8},{1,9},{2,10},{3,11},{4,12},{5,13},{6,14},{7,15},{8,0},{9,1},... | collective-permute-start | bytes 786440 | tf_op jit(solution)/shard_map/ppermute | solution.py:338
  21.9 0.7 %links.1 = s32[5,9]{1,0:T(8,128)S(4)} custom-call(s32[2,9]{1,0:T(2,128)S(1)} %copy-done.1, s32[2,9]{1,0:T(2,128)S(1)} %slice_convert_fusion.other, bf16[512,128]{1,0:T(8,128)(2,1)S(1)} %project_q.1.q), custom_call_target="tpu_custom_call" | custom-call | bytes 2097152 | tf_op jit(solution)/shard_map/links/pallas_call | solution.py:351
  22.7 4.4 %collective-permute-done.7.a2 = bf16[512,256]{1,0:T(8,128)(2,1)S(1)} collective-permute-done((bf16[512,256]{1,0:T(8,128)(2,1)S(1)}, bf16[512,256]{1,0:T(8,128)(2,1)S(1)}, u32[]{:S(2)}, u32[]{:S(2)}) %collective-permute-start.7) | collective-permute-done | bytes 262176 | tf_op jit(solution)/shard_map/ppermute | solution.py:338
  27.0 2.9 %attend.1 = (bf16[4608,256]{1,0:T(8,128)(2,1)S(1)}, bf16[1024,256]{1,0:T(8,128)(2,1)S(1)}, bf16[2048,256]{1,0:T(8,128)(2,1)S(1)}, f32[1024,256]{1,0:T(8,128)S(1)...) custom-call(s32[5,9]{1,0:T(8,128)S(4)} %links.1, bf16[512,128]{1,0:T(8,128)(2,1)S(1)} %project_q.1.q, ...), custom_call_target="tpu_custom_call" | custom-call | flops 603979776 | bytes 2097152 | tf_op jit(solution)/shard_map/attend/pallas_call | solution.py:351
  29.9 2.8 %collective-permute-start.11 = (bf16[256,256]{1,0:T(8,128)(2,1)S(1)}, bf16[256,256]{1,0:T(8,128)(2,1)S(1)}, u32[]{:S(2)}, u32[]{:S(2)}) collective-permute-start(bf16[256,256]{1,0:T(8,128)(2,1)S(1)} %get-tuple-element.37), channel_id=1, source_target_pairs={{0,8},{1,9},{2,10},{3,11},{4,12},{5,13},{6,14},{7,15},{8,0},{9,1},... | collective-permute-start | bytes 393224 | tf_op jit(solution)/shard_map/ppermute | solution.py:338
  32.7 0.8 %near_grads.1 = (f32[512,256]{1,0:T(8,128)S(1)}, bf16[512,256]{1,0:T(8,128)(2,1)S(1)}, bf16[512,256]{1,0:T(8,128)(2,1)S(1)}) custom-call(s32[5,9]{1,0:T(8,128)S(4)} %links.1, bf16[4608,256]{1,0:T(8,128)(2,1)S(1)} %get-tuple-element.29.mixed, bf16[1024,256]{1,0:T(8,128)(2,1)S(1)} %get-tuple-element.32.pairs, f32[1024,256]{1,0:T(8,128)S(1)} %get-tuple-element.33.near_acc), custom_call_target="tpu_custom_call" | custom-call | flops 301989888 | bytes 2097152 | tf_op jit(solution)/shard_map/near_grads/pallas_call | solution.py:351
  33.5 2.1 %collective-permute-done.11.part = bf16[256,256]{1,0:T(8,128)(2,1)S(1)} collective-permute-done((bf16[256,256]{1,0:T(8,128)(2,1)S(1)}, bf16[256,256]{1,0:T(8,128)(2,1)S(1)}, u32[]{:S(2)}, u32[]{:S(2)}) %collective-permute-start.11) | collective-permute-done | bytes 131104 | tf_op jit(solution)/shard_map/ppermute | solution.py:338
  35.9 2.8 %collective-permute-start.10 = (bf16[512,256]{1,0:T(8,128)(2,1)S(1)}, bf16[512,256]{1,0:T(8,128)(2,1)S(1)}, u32[]{:S(2)}, u32[]{:S(2)}) collective-permute-start(bf16[512,256]{1,0:T(8,128)(2,1)S(1)} %merge_a.1), channel_id=1, source_target_pairs={{0,8},{1,9},{2,10},{3,11},{4,12},{5,13},{6,14},{7,15},{8,0},{9,1},... | collective-permute-start | bytes 786440 | tf_op jit(solution)/shard_map/ppermute | solution.py:338
  38.6 1.0 %outputs.1 = (bf16[256,128]{1,0:T(8,128)(2,1)S(1)}, bf16[256,128]{1,0:T(8,128)(2,1)S(1)}, bf16[512,128]{1,0:T(8,128)(2,1)S(1)}) custom-call(s32[5,9]{1,0:T(8,128)S(4)} %links.1, bf16[4608,256]{1,0:T(8,128)(2,1)S(1)} %get-tuple-element.29.mixed, bf16[2048,256]{1,0:T(8,128)(2,1)S(1)} %get-tuple-element.30.win), custom_call_target="tpu_custom_call" | custom-call | flops 301989888 | bytes 2097152 | tf_op jit(solution)/shard_map/outputs/pallas_call | solution.py:351
  39.7 1.6 %collective-permute-start.13 = (bf16[256,128]{1,0:T(8,128)(2,1)S(1)}, bf16[256,128]{1,0:T(8,128)(2,1)S(1)}, u32[]{:S(2)}, u32[]{:S(2)}) collective-permute-start(bf16[256,128]{1,0:T(8,128)(2,1)S(1)} %get-tuple-element.38), channel_id=1, source_target_pairs={{0,4},{1,5},{2,6},{3,7},{4,0},{5,1},{6,2},{7,3},{8,12},{9,13},{10,... | collective-permute-start | bytes 196616 | tf_op jit(solution)/shard_map/ppermute | solution.py:326
  41.3 2.7 %collective-permute-done.13.other = bf16[256,128]{1,0:T(8,128)(2,1)S(1)} collective-permute-done((bf16[256,128]{1,0:T(8,128)(2,1)S(1)}, bf16[256,128]{1,0:T(8,128)(2,1)S(1)}, u32[]{:S(2)}, u32[]{:S(2)}) %collective-permute-start.13) | collective-permute-done | bytes 65568 | tf_op jit(solution)/shard_map/ppermute | solution.py:326
  44.0 0.6 %collective-permute-done.10.from_a = bf16[512,256]{1,0:T(8,128)(2,1)S(1)} collective-permute-done((bf16[512,256]{1,0:T(8,128)(2,1)S(1)}, bf16[512,256]{1,0:T(8,128)(2,1)S(1)}, u32[]{:S(2)}, u32[]{:S(2)}) %collective-permute-start.10) | collective-permute-done | bytes 262176 | tf_op jit(solution)/shard_map/ppermute | solution.py:338
  44.6 0.5 spread_send.1
  45.2 0.5 spread_keep.1
  45.7 1.4 %collective-permute-done.14 = bf16[1024,256]{1,0:T(8,128)(2,1)S(1)} collective-permute-done((bf16[1024,256]{1,0:T(8,128)(2,1)S(1)}, bf16[1024,256]{1,0:T(8,128)(2,1)S(1)}, u32[]{:S(2)}, u32[]{:S(2)}) %collective-permute-start.14) | collective-permute-done | bytes 524320 | tf_op jit(solution)/shard_map/ppermute | solution.py:326
  47.3 2.5 %collective-permute-start.15 = (bf16[256,256]{1,0:T(8,128)(2,1)S(1)}, bf16[256,256]{1,0:T(8,128)(2,1)S(1)}, u32[]{:S(2)}, u32[]{:S(2)}) collective-permute-start(bf16[256,256]{1,0:T(8,128)(2,1)S(1)} %get-tuple-element.46), channel_id=1, source_target_pairs={{0,6},{1,7},{2,4},{3,5},{4,2},{5,3},{6,0},{7,1},{8,14},{9,15},{10,... | collective-permute-start | bytes 393224 | tf_op jit(solution)/shard_map/ppermute | solution.py:326
  49.8 0.5 collective-permute-start.17
  50.3 0.5 collective-permute-start.16
  50.9 0.7 %lay_out.1 = bf16[256,256]{1,0:T(8,128)(2,1)} custom-call(bf16[256,128]{1,0:T(8,128)(2,1)S(1)} %get-tuple-element.31.own, bf16[256,128]{1,0:T(8,128)(2,1)S(1)} %collective-permute-done.13.other), custom_call_target="tpu_custom_call" | custom-call | bytes 2097152 | tf_op jit(solution)/shard_map/lay_out/pallas_call | solution.py:351
  51.5 3.1 %collective-permute-done.15 = bf16[256,256]{1,0:T(8,128)(2,1)S(1)} collective-permute-done((bf16[256,256]{1,0:T(8,128)(2,1)S(1)}, bf16[256,256]{1,0:T(8,128)(2,1)S(1)}, u32[]{:S(2)}, u32[]{:S(2)}) %collective-permute-start.15) | collective-permute-done | bytes 131104 | tf_op jit(solution)/shard_map/ppermute | solution.py:326
  54.6 2.1 %collective-permute-done.17 = bf16[256,256]{1,0:T(8,128)(2,1)S(1)} collective-permute-done((bf16[256,256]{1,0:T(8,128)(2,1)S(1)}, bf16[256,256]{1,0:T(8,128)(2,1)S(1)}, u32[]{:S(2)}, u32[]{:S(2)}) %collective-permute-start.17) | collective-permute-done | bytes 131104 | tf_op jit(solution)/shard_map/ppermute | solution.py:326
  56.7 0.7 %add_convert_fusion.1 = bf16[256,256]{1,0:T(8,128)(2,1)} fusion(bf16[256,256]{1,0:T(8,128)(2,1)S(1)} %collective-permute-done.17, bf16[256,256]{1,0:T(8,128)(2,1)S(1)} %collective-permute-done.16, bf16[256,256]{1,0:T(8,128)(2,1)S(1)} %collective-permute-done.15, bf16[1024,256]{1,0:T(8,128)(2,1)S(1)} %add_convert_fusion), kind=kLoop, calls=%fused_computation.1 | loop fusion | flops 524288 | bytes 655360 | tf_op jit(solution)/shard_map/convert_element_type | solution.py:466
  (31 shorter events, 1.9 us)
Async XLA Ops:
  0.6 8.9 %collective-permute-start = (bf16[256,256]{1,0:T(8,128)(2,1)}, bf16[256,256]{1,0:T(8,128)(2,1)S(1)}, u32[]{:S(2)}, u32[]{:S(2)}) collective-permute-start(bf16[256,256]{1,0:T(8,128)(2,1)} %f.1), channel_id=1, source_target_pairs={{0,4},{1,5},{2,6},{3,7},{4,0},{5,1},{6,2},{7,3},{8,12},{9,13},{10,... | collective-permute-start | bytes 393224 | tf_op jit(solution)/shard_map/ppermute | solution.py:326
  3.7 7.5 %collective-permute-start.2 = (bf16[256,256]{1,0:T(8,128)(2,1)}, bf16[256,256]{1,0:T(8,128)(2,1)S(1)}, u32[]{:S(2)}, u32[]{:S(2)}) collective-permute-start(bf16[256,256]{1,0:T(8,128)(2,1)} %f.1), channel_id=1, source_target_pairs={{0,6},{1,7},{2,4},{3,5},{4,2},{5,3},{6,0},{7,1},{8,14},{9,15},{10,... | collective-permute-start | bytes 393224 | tf_op jit(solution)/shard_map/ppermute | solution.py:326
  5.1 6.4 %collective-permute-start.1 = (bf16[256,256]{1,0:T(8,128)(2,1)}, bf16[256,256]{1,0:T(8,128)(2,1)S(1)}, u32[]{:S(2)}, u32[]{:S(2)}) collective-permute-start(bf16[256,256]{1,0:T(8,128)(2,1)} %f.1), channel_id=1, source_target_pairs={{0,2},{1,3},{2,0},{3,1},{4,6},{5,7},{6,4},{7,5},{8,10},{9,11},{10,... | collective-permute-start | bytes 393224 | tf_op jit(solution)/shard_map/ppermute | solution.py:326
  11.5 5.7 %copy-start.1 = (s32[2,9]{1,0:T(2,128)S(1)}, s32[2,9]{1,0:T(2,128)}, u32[]{:S(2)}) copy-start(s32[2,9]{1,0:T(2,128)} %own.1) | copy-start | bytes 220
  11.6 5.7 %copy-start = (bf16[256,256]{1,0:T(8,128)(2,1)S(1)}, bf16[256,256]{1,0:T(8,128)(2,1)}, u32[]{:S(2)}) copy-start(bf16[256,256]{1,0:T(8,128)(2,1)} %d_own.3) | copy-start | bytes 393220
  11.6 2.0 %collective-permute-start.4 = (bf16[1024,256]{1,0:T(8,128)(2,1)S(1)}, bf16[1024,256]{1,0:T(8,128)(2,1)S(1)}, u32[]{:S(2)}, u32[]{:S(2)}) collective-permute-start(bf16[1024,256]{1,0:T(8,128)(2,1)S(1)} %pack.1), channel_id=1, source_target_pairs={{0,1},{1,0},{2,3},{3,2},{4,5},{5,4},{6,7},{7,6},{8,9},{9,8},{10,11... | collective-permute-start | bytes 1572872 | tf_op jit(solution)/shard_map/ppermute | solution.py:326
  13.8 5.0 %collective-permute-start.5 = (bf16[256,256]{1,0:T(8,128)(2,1)S(1)}, bf16[256,256]{1,0:T(8,128)(2,1)S(1)}, u32[]{:S(2)}, u32[]{:S(2)}) collective-permute-start(bf16[256,256]{1,0:T(8,128)(2,1)S(1)} %get-tuple-element.27.own_half.second_kv), channel_id=1, source_target_pairs={{0,1},{1,0},{2,3},{3,2},{4,5},{5,4},{6,7},{7,6},{8,16},{9,17},{10,... | collective-permute-start | bytes 393224 | tf_op jit(solution)/shard_map/ppermute | solution.py:338
  14.1 7.2 %collective-permute-start.6 = (bf16[256,256]{1,0:T(8,128)(2,1)S(1)}, bf16[256,256]{1,0:T(8,128)(2,1)S(1)}, u32[]{:S(2)}, u32[]{:S(2)}) collective-permute-start(bf16[256,256]{1,0:T(8,128)(2,1)S(1)} %get-tuple-element.28.own_half.first_kv), channel_id=1, source_target_pairs={{0,8},{1,9},{2,10},{3,11},{4,12},{5,13},{6,14},{7,15},{8,0},{9,1},... | collective-permute-start | bytes 393224 | tf_op jit(solution)/shard_map/ppermute | solution.py:338
  17.3 4.4 %collective-permute-start.3 = (bf16[272,128]{1,0:T(8,128)(2,1)S(1)}, bf16[272,128]{1,0:T(8,128)(2,1)S(1)}, u32[]{:S(2)}, u32[]{:S(2)}) collective-permute-start(bf16[272,128]{1,0:T(8,128)(2,1)S(1)} %payload.1), channel_id=1, source_target_pairs={{0,4},{1,5},{2,6},{3,7},{4,0},{5,1},{6,2},{7,3},{8,12},{9,13},{10,... | collective-permute-start | bytes 208904 | tf_op jit(solution)/shard_map/ppermute | solution.py:326
  18.9 8.2 %collective-permute-start.7 = (bf16[512,256]{1,0:T(8,128)(2,1)S(1)}, bf16[512,256]{1,0:T(8,128)(2,1)S(1)}, u32[]{:S(2)}, u32[]{:S(2)}) collective-permute-start(bf16[512,256]{1,0:T(8,128)(2,1)S(1)} %join_a.1.to_a), channel_id=1, source_target_pairs={{0,8},{1,9},{2,10},{3,11},{4,12},{5,13},{6,14},{7,15},{8,0},{9,1},... | collective-permute-start | bytes 786440 | tf_op jit(solution)/shard_map/ppermute | solution.py:338
  21.3 5.8 %collective-permute-start.8 = (bf16[512,256]{1,0:T(8,128)(2,1)S(1)}, bf16[512,256]{1,0:T(8,128)(2,1)S(1)}, u32[]{:S(2)}, u32[]{:S(2)}) collective-permute-start(bf16[512,256]{1,0:T(8,128)(2,1)S(1)} %join_b.1.to_b), channel_id=1, source_target_pairs={{0,1},{1,0},{2,3},{3,2},{4,5},{5,4},{6,7},{7,6},{8,16},{9,17},{10,... | collective-permute-start | bytes 786440 | tf_op jit(solution)/shard_map/ppermute | solution.py:338
  29.9 5.7 %collective-permute-start.11 = (bf16[256,256]{1,0:T(8,128)(2,1)S(1)}, bf16[256,256]{1,0:T(8,128)(2,1)S(1)}, u32[]{:S(2)}, u32[]{:S(2)}) collective-permute-start(bf16[256,256]{1,0:T(8,128)(2,1)S(1)} %get-tuple-element.37), channel_id=1, source_target_pairs={{0,8},{1,9},{2,10},{3,11},{4,12},{5,13},{6,14},{7,15},{8,0},{9,1},... | collective-permute-start | bytes 393224 | tf_op jit(solution)/shard_map/ppermute | solution.py:338
  32.7 3.1 %collective-permute-start.9 = (bf16[256,256]{1,0:T(8,128)(2,1)S(1)}, bf16[256,256]{1,0:T(8,128)(2,1)S(1)}, u32[]{:S(2)}, u32[]{:S(2)}) collective-permute-start(bf16[256,256]{1,0:T(8,128)(2,1)S(1)} %get-tuple-element.35), channel_id=1, source_target_pairs={{0,1},{1,0},{2,3},{3,2},{4,5},{5,4},{6,7},{7,6},{8,16},{9,17},{10,... | collective-permute-start | bytes 393224 | tf_op jit(solution)/shard_map/ppermute | solution.py:338
  35.7 8.3 %collective-permute-start.12 = (bf16[512,256]{1,0:T(8,128)(2,1)S(1)}, bf16[512,256]{1,0:T(8,128)(2,1)S(1)}, u32[]{:S(2)}, u32[]{:S(2)}) collective-permute-start(bf16[512,256]{1,0:T(8,128)(2,1)S(1)} %merge_b.1), channel_id=1, source_target_pairs={{0,1},{1,0},{2,3},{3,2},{4,5},{5,4},{6,7},{7,6},{8,16},{9,17},{10,... | collective-permute-start | bytes 786440 | tf_op jit(solution)/shard_map/ppermute | solution.py:338
  35.9 8.8 %collective-permute-start.10 = (bf16[512,256]{1,0:T(8,128)(2,1)S(1)}, bf16[512,256]{1,0:T(8,128)(2,1)S(1)}, u32[]{:S(2)}, u32[]{:S(2)}) collective-permute-start(bf16[512,256]{1,0:T(8,128)(2,1)S(1)} %merge_a.1), channel_id=1, source_target_pairs={{0,8},{1,9},{2,10},{3,11},{4,12},{5,13},{6,14},{7,15},{8,0},{9,1},... | collective-permute-start | bytes 786440 | tf_op jit(solution)/shard_map/ppermute | solution.py:338
  39.7 4.3 %collective-permute-start.13 = (bf16[256,128]{1,0:T(8,128)(2,1)S(1)}, bf16[256,128]{1,0:T(8,128)(2,1)S(1)}, u32[]{:S(2)}, u32[]{:S(2)}) collective-permute-start(bf16[256,128]{1,0:T(8,128)(2,1)S(1)} %get-tuple-element.38), channel_id=1, source_target_pairs={{0,4},{1,5},{2,6},{3,7},{4,0},{5,1},{6,2},{7,3},{8,12},{9,13},{10,... | collective-permute-start | bytes 196616 | tf_op jit(solution)/shard_map/ppermute | solution.py:326
  45.1 2.0 %collective-permute-start.14 = (bf16[1024,256]{1,0:T(8,128)(2,1)S(1)}, bf16[1024,256]{1,0:T(8,128)(2,1)S(1)}, u32[]{:S(2)}, u32[]{:S(2)}) collective-permute-start(bf16[1024,256]{1,0:T(8,128)(2,1)S(1)} %get-tuple-element.45), channel_id=1, source_target_pairs={{0,1},{1,0},{2,3},{3,2},{4,5},{5,4},{6,7},{7,6},{8,9},{9,8},{10,11... | collective-permute-start | bytes 1572872 | tf_op jit(solution)/shard_map/ppermute | solution.py:326
  47.3 7.3 %collective-permute-start.15 = (bf16[256,256]{1,0:T(8,128)(2,1)S(1)}, bf16[256,256]{1,0:T(8,128)(2,1)S(1)}, u32[]{:S(2)}, u32[]{:S(2)}) collective-permute-start(bf16[256,256]{1,0:T(8,128)(2,1)S(1)} %get-tuple-element.46), channel_id=1, source_target_pairs={{0,6},{1,7},{2,4},{3,5},{4,2},{5,3},{6,0},{7,1},{8,14},{9,15},{10,... | collective-permute-start | bytes 393224 | tf_op jit(solution)/shard_map/ppermute | solution.py:326
  49.8 6.9 %collective-permute-start.17 = (bf16[256,256]{1,0:T(8,128)(2,1)S(1)}, bf16[256,256]{1,0:T(8,128)(2,1)S(1)}, u32[]{:S(2)}, u32[]{:S(2)}) collective-permute-start(bf16[256,256]{1,0:T(8,128)(2,1)S(1)} %get-tuple-element.47), channel_id=1, source_target_pairs={{0,2},{1,3},{2,0},{3,1},{4,6},{5,7},{6,4},{7,5},{8,10},{9,11},{10,... | collective-permute-start | bytes 393224 | tf_op jit(solution)/shard_map/ppermute | solution.py:326
  50.3 6.3 %collective-permute-start.16 = (bf16[256,256]{1,0:T(8,128)(2,1)S(1)}, bf16[256,256]{1,0:T(8,128)(2,1)S(1)}, u32[]{:S(2)}, u32[]{:S(2)}) collective-permute-start(bf16[256,256]{1,0:T(8,128)(2,1)S(1)} %get-tuple-element.48), channel_id=1, source_target_pairs={{0,4},{1,5},{2,6},{3,7},{4,0},{5,1},{6,2},{7,3},{8,12},{9,13},{10,... | collective-permute-start | bytes 393224 | tf_op jit(solution)/shard_map/ppermute | solution.py:326

commit v7 on v6

--- a/solution.py
+++ b/solution.py
@@ -42,9 +42,8 @@
 
 
 def position():
-    ctx = lax.axis_index("ctx")
-    group = ctx // 2
-    return ctx % 2, group % 2, group * GROUP, lax.axis_index("head")
+    ctx, head = lax.axis_index("ctx"), lax.axis_index("head")
+    return ctx % 2, head % 2, ctx // 2 * GROUP, head
 
 
 def begin_kernel(f, w, w_mine, fm, total, sems):
@@ -94,17 +93,17 @@
 
 
 def project_kv_kernel(other, before, w_mine, first_out, second_out):
-    side, odd, _, head = position()
+    side, flip, _, head = position()
     total = (before[:, HD:] + sibling_product(head, other, w_mine, slice(HD, 3 * HD))).astype(BF)
-    near_first = side ^ (1 - odd) == 0
+    near_first = side ^ (1 - flip) == 0
     first_out[...] = jnp.where(near_first, total[:HALF], total[HALF:])
     second_out[...] = jnp.where(near_first, total[HALF:], total[:HALF])
 
 
-def merge_kernel(whole, part, out, which):
-    at = pl.ds(pl.multiple_of((position()[1] ^ which) * HALF, HALF), HALF)
-    out[...] = whole[...]
-    out[at, :] = (whole[at, :].astype(F32) + part[...].astype(F32)).astype(BF)
+def merge_kernel(whole, part, dq, out):
+    del dq
+    out[:HALF, :] = (whole[:HALF, :].astype(F32) + part[...].astype(F32)).astype(BF)
+    out[HALF:, :] = whole[HALF:, :]
 
 
 def lay_out_kernel(own, other, out):
@@ -114,13 +113,8 @@
         out[:, cols] = jnp.where(side == half, own[...], other[...])
 
 
-def join_kernel(own_half, arrived, out):
-    out[:HALF, :] = own_half[...]
-    out[HALF:, :] = arrived[...]
-
-
-def project_q_kernel(other, before, w_mine, to_a, to_b, q_out):
-    del to_a, to_b
+def project_q_kernel(other, before, w_mine, u1, d1, q_out):
+    del u1, d1
     side, _, _, head = position()
     total = before[:, :HD] + sibling_product(head, other, w_mine, slice(0, HD))
     store_groups(side, total.astype(BF), q_out)
@@ -148,27 +142,20 @@
             links[GROUP, 2 * i + t - 1] = jnp.clip(base, 0, WINDOW - SPAN) * BLK
 
 
-def regions(odd):
-    even = 1 - odd
+def regions(flip):
     left_lo, left_hi = NEAR_LEFT, NEAR_LEFT + HALF
     right_lo, right_hi = NEAR_RIGHT, NEAR_RIGHT + HALF
-    pick = lambda at_even, at_odd: pl.multiple_of(even * at_even + odd * at_odd, HALF)
+    pick = lambda plain, flipped: pl.multiple_of((1 - flip) * plain + flip * flipped, HALF)
     return (
         pick(OWN + HALF, OWN),
         pick(OWN, OWN + HALF),
+        pick(left_hi, right_lo),
         pick(right_lo, left_hi),
-        pick(left_hi, right_lo),
+        pick(left_lo, right_hi),
+        pick(0, FAR_RIGHT),
         pick(right_hi, left_lo),
         pick(FAR_RIGHT, 0),
-        pick(left_lo, right_hi),
-        pick(0, FAR_RIGHT),
-    )
-
-
-def near_regions(odd):
-    even = 1 - odd
-    pick = lambda at_even, at_odd: pl.multiple_of(even * at_even + odd * at_odd, HALF)
-    return pick(NEAR_RIGHT, NEAR_LEFT), pick(NEAR_LEFT, NEAR_RIGHT)
+    )
 
 
 def start_of(links, i, t):
@@ -191,18 +178,16 @@
 
 
 def attend_kernel(
-    links, q, first_kv, second_kv, a1, b1, a2, b2, d_own, d_other,
-    mixed, pairs, win, near_acc, far_a_out, far_b_out, acc,
+    links, q, first_kv, second_kv, u1, d1, u2, u3, d2, d3, d_own, d_other,
+    mixed, pairs, win, near_acc, far_u_out, far_d_out, acc,
 ):
-    side, odd, _, _ = position()
+    side, flip, _, _ = position()
     scale = HD ** -0.5
-    places = regions(odd)
-    halves = (
-        first_kv[...], second_kv[...], a1[...], b1[...], a2[:HALF, :], a2[HALF:, :], b2[:HALF, :], b2[HALF:, :],
-    )
+    places = regions(flip)
+    halves = (first_kv, second_kv, u1, d1, u2, u3, d2, d3)
     for at, half in zip(places, halves):
-        win[pl.ds(at, HALF), :] = half
-    at_far_a, at_far_b = places[5], places[7]
+        win[pl.ds(at, HALF), :] = half[...]
+    at_far_u, at_far_d = places[7], places[5]
     acc[...] = jnp.zeros_like(acc)
     zeros = jnp.zeros((BLK, HD), BF)
     own_cols = pl.ds(pl.multiple_of(side * HD, HD), HD)
@@ -253,14 +238,13 @@
             if is_far(i, t):
                 acc[pl.ds(start_of(links, i, t), SPAN * BLK), :] += dot(part, pair, ((1,), (0,)))
     factor = side_factor()
-    far_a_out[...] = (acc[pl.ds(at_far_a, HALF), :] * factor).astype(BF)
-    far_b_out[...] = (acc[pl.ds(at_far_b, HALF), :] * factor).astype(BF)
+    far_u_out[...] = (acc[pl.ds(at_far_u, HALF), :] * factor).astype(BF)
+    far_d_out[...] = (acc[pl.ds(at_far_d, HALF), :] * factor).astype(BF)
     near_acc[:ROWS, :] = acc[NEAR_LEFT:OWN, :]
     near_acc[ROWS:, :] = acc[NEAR_RIGHT:FAR_RIGHT, :]
 
 
-def near_grads_kernel(links, mixed, pairs, near_acc, own_out, a_out, b_out, acc):
-    odd = position()[1]
+def near_grads_kernel(links, mixed, pairs, near_acc, first_own, second_own, u_out, d_out, acc):
     acc[NEAR_LEFT:OWN, :] = near_acc[:ROWS, :]
     acc[OWN:NEAR_RIGHT, :] = jnp.zeros((ROWS, 2 * HD), F32)
     acc[NEAR_RIGHT:FAR_RIGHT, :] = near_acc[ROWS:, :]
@@ -271,10 +255,12 @@
                 at = pl.ds(start_of(links, i, t), SPAN * BLK)
                 acc[at, :] += dot(mixed[run_rows(i, t), :], pair, ((1,), (0,)))
     factor = side_factor()
-    at_a, at_b = near_regions(odd)
-    own_out[...] = acc[OWN : OWN + ROWS, :] * factor
-    a_out[...] = (acc[pl.ds(at_a, ROWS), :] * factor).astype(BF)
-    b_out[...] = (acc[pl.ds(at_b, ROWS), :] * factor).astype(BF)
+    first, second, u1, d1, u2, _, d2, _ = regions(position()[1])
+    first_own[...] = acc[pl.ds(first, HALF), :] * factor
+    second_own[...] = acc[pl.ds(second, HALF), :] * factor
+    for target, at_first, at_second in ((u_out, d1, d2), (d_out, u1, u2)):
+        target[:HALF, :] = (acc[pl.ds(at_first, HALF), :] * factor).astype(BF)
+        target[HALF:, :] = (acc[pl.ds(at_second, HALF), :] * factor).astype(BF)
 
 
 def outputs_kernel(links, mixed, win, att_own, att_other, dq_out, att):
@@ -301,11 +287,13 @@
             target[index * HALF : (index + 1) * HALF, :] = part
 
 
-def spread_send_kernel(own, from_a, from_b, dq, w_mine, send, grads):
-    dkv = (own[...] + from_a[...].astype(F32) + from_b[...].astype(F32)).astype(BF)
+def spread_send_kernel(first_own, second_own, from_u, from_d, dq, w_mine, send, grads):
+    side, flip, _, head = position()
+    first = first_own[...] + from_u[HALF:, :].astype(F32) + from_d[:HALF, :].astype(F32)
+    second = second_own[...] + from_u[:HALF, :].astype(F32) + from_d[HALF:, :].astype(F32)
     grads[:, :HD] = dq[...]
-    grads[:, HD:] = dkv
-    side, _, _, head = position()
+    grads[:HALF, HD:] = jnp.where(flip == 1, first, second).astype(BF)
+    grads[HALF:, HD:] = jnp.where(flip == 1, second, first).astype(BF)
     spread(grads[...], w_mine, side, head ^ 1, send)
 
 
@@ -325,16 +313,15 @@
         ]
         return lax.ppermute(value, ("ctx", "head"), pairs)
 
-    def group_swap(value, offset):
-        partner = list(range(n_group))
-        for low in range(offset, n_group - 1, 2):
-            partner[low], partner[low + 1] = low + 1, low
+    def chain(value, back):
         pairs = []
         for ctx in range(n_ctx):
             group, side = divmod(ctx, 2)
             for h in range(n_head):
-                alone = 1 if partner[group] == group else 0
-                pairs.append((ctx * n_head + h, (2 * partner[group] + side) * n_head + (h ^ alone)))
+                to = group + (1 if h % 2 == back else -1)
+                inside = 0 <= to < n_group
+                target = (2 * to + side) * n_head + h if inside else ctx * n_head + (h ^ 1)
+                pairs.append((ctx * n_head + h, target))
         return lax.ppermute(value, ("ctx", "head"), pairs)
 
     f = features
@@ -384,23 +371,23 @@
         project_kv_kernel, "project_kv", [out(HALF, 2 * HD)] * 2, (other, total, w_mine), 4, product
     )
 
-    a1 = group_swap(first, 0)
-    b1 = group_swap(second, 1)
-    (to_b,) = call(join_kernel, "join_b", [out(ROWS, 2 * HD)], (first, a1), 4, 0)
-    (to_a,) = call(join_kernel, "join_a", [out(ROWS, 2 * HD)], (second, b1), 4, 0)
-    b2 = group_swap(to_b, 1)
-    a2 = group_swap(to_a, 0)
+    u1 = chain(first, 0)
+    d1 = chain(second, 1)
+    u2 = chain(second, 0)
+    d2 = chain(first, 1)
+    u3 = chain(u1, 0)
+    d3 = chain(d1, 1)
     rows, slots = block_links.shape
     link_rows = jnp.pad(block_links.astype(BF), ((0, 16 - rows), (0, HD - slots)))
     (payload,) = call(payload_kernel, "payload", [out(HALF + 16, HD)], (d_out, link_rows, pack), 4, 0)
     d_other = across(payload, 1, 0)
-    (q,) = call(project_q_kernel, "project_q", [held(ROWS, HD)], (other, total, w_mine, to_a, to_b), 4, product)
+    (q,) = call(project_q_kernel, "project_q", [held(ROWS, HD)], (other, total, w_mine, u1, d1), 4, product)
     other_links = d_other[HALF : HALF + rows, :slots].astype(jnp.int32)
     (links,) = call(
         links_kernel, "links", [pltpu.SMEM((GROUP + 1, slots), jnp.int32)], (block_links, other_links, q), 4, 0
     )
     links = pltpu.with_memory_space_constraint(links, pltpu.SMEM)
-    mixed, pairs, win, near_acc, far_a_grad, far_b_grad = call(
+    mixed, pairs, win, near_acc, far_u_grad, far_d_grad = call(
         attend_kernel,
         "attend",
         [
@@ -411,15 +398,15 @@
             out(HALF, 2 * HD),
             out(HALF, 2 * HD),
         ],
-        (links, q, first, second, a1, b1, a2, b2, d_out, d_other),
+        (links, q, first, second, u1, d1, u2, u3, d2, d3, d_out, d_other),
         8,
         2 * attention,
         [pltpu.VMEM((WINDOW * BLK, 2 * HD), F32)],
     )
-    own, near_a_grad, near_b_grad = call(
+    first_own, second_own, u_grad, d_grad = call(
         near_grads_kernel,
         "near_grads",
-        [held(ROWS, 2 * HD, F32), out(ROWS, 2 * HD), out(ROWS, 2 * HD)],
+        [held(HALF, 2 * HD, F32)] * 2 + [out(ROWS, 2 * HD)] * 2,
         (links, mixed, pairs, near_acc),
         4,
         attention,
@@ -435,23 +422,22 @@
         [pltpu.VMEM((ROWS, HD), BF)],
     )
 
-    back_a = group_swap(far_a_grad, 0)
-    back_b = group_swap(far_b_grad, 1)
-
-    def merge(whole, part, which, name):
-        kernel = functools.partial(merge_kernel, which=which)
-        return call(kernel, name, [out(ROWS, 2 * HD)], (whole, part), 4, 0)[0]
-
-    from_b = group_swap(merge(near_b_grad, back_a, 1, "merge_b"), 1)
-    from_a = group_swap(merge(near_a_grad, back_b, 0, "merge_a"), 0)
+    back_u = chain(far_u_grad, 0)
+    back_d = chain(far_d_grad, 1)
+
+    def merge(whole, part, name):
+        return call(merge_kernel, name, [out(ROWS, 2 * HD)], (whole, part, dq), 4, 0)[0]
+
+    from_u = chain(merge(u_grad, back_u, "merge_u"), 0)
+    from_d = chain(merge(d_grad, back_d, "merge_d"), 1)
     att_back = across(att_other, 1, 0)
-    from_a, from_b, att_back = lax.optimization_barrier((from_a, from_b, att_back))
+    from_u, from_d, att_back = lax.optimization_barrier((from_u, from_d, att_back))
     (attended,) = call(lay_out_kernel, "lay_out", [out(HALF, 2 * HD)], (att_own, att_back), 4, 0)
     send, grads = call(
         spread_send_kernel,
         "spread_send",
         [out(4 * HALF, 2 * HD), held(ROWS, 3 * HD)],
-        (own, from_a, from_b, dq, w_mine),
+        (first_own, second_own, from_u, from_d, dq, w_mine),
         4,
         product,
     )

time: 57.6 us -> 55.1 us (0.957)
  waiting for transfers between devices: 23.1 us -> 21.5 us
  starting transfers between devices: 22.8 us -> 22.1 us
    ppermute x8 -> x10, starting transfers between devices: 11.4 us -> 9.84 us  [chain(): return lax.ppermute(value, ('ctx', 'head'), pairs)]
    ppermute x10, starting transfers between devices: 11.4 us -> 12.3 us  [across(): return lax.ppermute(value, ('ctx', 'head'), pairs)]
    ppermute x10, waiting for transfers between devices: 15.9 us -> 15.1 us  [across(): return lax.ppermute(value, ('ctx', 'head'), pairs)]
    ppermute x8 -> x10, waiting for transfers between devices: 7.12 us -> 6.36 us  [chain(): return lax.ppermute(value, ('ctx', 'head'), pairs)]
    pallas_call x17 -> x15, Pallas kernels: 9.74 us -> 9.65 us  [call(): pl.pallas_call(kernel, name=name, out_shape=outs, in_specs=specs, out_spe...]
  transfers between devices with their start and end apart: 18 -> 20, of which waited for: 12 -> 14; matrix products, arithmetic and copies ran while one was open for 0% -> 0% of each run, Pallas kernels for 10% -> 11%
where the time goes in v7:
time: 55.1 us; the launch traced here: 55 us
  starting transfers between devices  22.1 us (40%)
  waiting for transfers between devices  21.5 us (39%)
  Pallas kernels  9.65 us (18%)
  other arithmetic  0.88 us (2%)
  between operations  0.83 us (2%)
    ppermute x10, waiting for transfers between devices, across(): return lax.ppermute(value, ('ctx', 'head'), pairs)  15.1 us
    ppermute x10, starting transfers between devices, across(): return lax.ppermute(value, ('ctx', 'head'), pairs)  12.3 us
    ppermute x10, starting transfers between devices, chain(): return lax.ppermute(value, ('ctx', 'head'), pairs)  9.84 us
    pallas_call x15, Pallas kernels, call(): pl.pallas_call(kernel, name=name, out_shape=outs, in_specs=specs, out_spe...  9.65 us
    ppermute x10, waiting for transfers between devices, chain(): return lax.ppermute(value, ('ctx', 'head'), pairs)  6.36 us
  transfers between devices with their start and end apart: 20, of which 14 were waited for; matrix products, arithmetic and copies ran while one was open for 0% of the time, Pallas kernels for 11%

profile of v7, /device:TPU:0, one launch (start us, length us, event | category | flops | bytes accessed | tf_op | source)
XLA Modules:
  0.0 55.0 jit_solution(1836747375033966418)
XLA Ops:
  0.6 3.0 %collective-permute-start = (bf16[256,256]{1,0:T(8,128)(2,1)}, bf16[256,256]{1,0:T(8,128)(2,1)S(1)}, u32[]{:S(2)}, u32[]{:S(2)}) collective-permute-start(bf16[256,256]{1,0:T(8,128)(2,1)} %f.1), channel_id=1, source_target_pairs={{0,4},{1,5},{2,6},{3,7},{4,0},{5,1},{6,2},{7,3},{8,12},{9,13},{10,... | collective-permute-start | bytes 393224 | tf_op jit(solution)/shard_map/ppermute | solution.py:314
  3.7 1.4 %collective-permute-start.2 = (bf16[256,256]{1,0:T(8,128)(2,1)}, bf16[256,256]{1,0:T(8,128)(2,1)S(1)}, u32[]{:S(2)}, u32[]{:S(2)}) collective-permute-start(bf16[256,256]{1,0:T(8,128)(2,1)} %f.1), channel_id=1, source_target_pairs={{0,6},{1,7},{2,4},{3,5},{4,2},{5,3},{6,0},{7,1},{8,14},{9,15},{10,... | collective-permute-start | bytes 393224 | tf_op jit(solution)/shard_map/ppermute | solution.py:314
  5.2 1.4 %begin.1 = (bf16[1024,384]{1,0:T(8,128)(2,1)S(1)}, bf16[256,256]{1,0:T(8,128)(2,1)S(1)}, f32[256,384]{1,0:T(8,128)S(1)}) custom-call(bf16[256,256]{1,0:T(8,128)(2,1)} %f.1, bf16[3,1024,256]{2,1,0:T(8,128)(2,1)} %bitcast.1), custom_call_target="tpu_custom_call" | custom-call | flops 100663296 | bytes 2097152 | tf_op jit(solution)/shard_map/begin/pallas_call | solution.py:338
  6.6 2.9 %collective-permute-done.sy = bf16[256,256]{1,0:T(8,128)(2,1)S(1)} collective-permute-done((bf16[256,256]{1,0:T(8,128)(2,1)}, bf16[256,256]{1,0:T(8,128)(2,1)S(1)}, u32[]{:S(2)}, u32[]{:S(2)}) %collective-permute-start) | collective-permute-done | bytes 131104 | tf_op jit(solution)/shard_map/ppermute | solution.py:314
  9.5 1.6 %collective-permute-done.2.sd = bf16[256,256]{1,0:T(8,128)(2,1)S(1)} collective-permute-done((bf16[256,256]{1,0:T(8,128)(2,1)}, bf16[256,256]{1,0:T(8,128)(2,1)S(1)}, u32[]{:S(2)}, u32[]{:S(2)}) %collective-permute-start.2) | collective-permute-done | bytes 131104 | tf_op jit(solution)/shard_map/ppermute | solution.py:314
  12.0 1.5 %collective-permute-done.4.other = bf16[1024,256]{1,0:T(8,128)(2,1)S(1)} collective-permute-done((bf16[1024,256]{1,0:T(8,128)(2,1)S(1)}, bf16[1024,256]{1,0:T(8,128)(2,1)S(1)}, u32[]{:S(2)}, u32[]{:S(2)}) %collective-permute-start.4) | collective-permute-done | bytes 524320 | tf_op jit(solution)/shard_map/ppermute | solution.py:314
  13.8 1.7 %collective-permute-start.5 = (bf16[256,256]{1,0:T(8,128)(2,1)S(1)}, bf16[256,256]{1,0:T(8,128)(2,1)S(1)}, u32[]{:S(2)}, u32[]{:S(2)}) collective-permute-start(bf16[256,256]{1,0:T(8,128)(2,1)S(1)} %get-tuple-element.28.first_kv), channel_id=1, source_target_pairs={{0,8},{1,0},{2,10},{3,2},{4,12},{5,4},{6,14},{7,6},{8,16},{9,1},{1... | collective-permute-start | bytes 393224 | tf_op jit(solution)/shard_map/ppermute | solution.py:325
  15.6 1.6 %collective-permute-start.3 = (bf16[272,128]{1,0:T(8,128)(2,1)S(1)}, bf16[272,128]{1,0:T(8,128)(2,1)S(1)}, u32[]{:S(2)}, u32[]{:S(2)}) collective-permute-start(bf16[272,128]{1,0:T(8,128)(2,1)S(1)} %payload.1), channel_id=1, source_target_pairs={{0,4},{1,5},{2,6},{3,7},{4,0},{5,1},{6,2},{7,3},{8,12},{9,13},{10,... | collective-permute-start | bytes 208904 | tf_op jit(solution)/shard_map/ppermute | solution.py:314
  17.2 2.0 %collective-permute-start.7 = (bf16[256,256]{1,0:T(8,128)(2,1)S(1)}, bf16[256,256]{1,0:T(8,128)(2,1)S(1)}, u32[]{:S(2)}, u32[]{:S(2)}) collective-permute-start(bf16[256,256]{1,0:T(8,128)(2,1)S(1)} %get-tuple-element.29.second_kv), channel_id=1, source_target_pairs={{0,8},{1,0},{2,10},{3,2},{4,12},{5,4},{6,14},{7,6},{8,16},{9,1},{1... | collective-permute-start | bytes 393224 | tf_op jit(solution)/shard_map/ppermute | solution.py:325
  19.3 2.0 %collective-permute-start.8 = (bf16[256,256]{1,0:T(8,128)(2,1)S(1)}, bf16[256,256]{1,0:T(8,128)(2,1)S(1)}, u32[]{:S(2)}, u32[]{:S(2)}) collective-permute-start(bf16[256,256]{1,0:T(8,128)(2,1)S(1)} %collective-permute-done.5.u1), channel_id=1, source_target_pairs={{0,8},{1,0},{2,10},{3,2},{4,12},{5,4},{6,14},{7,6},{8,16},{9,1},{1... | collective-permute-start | bytes 393224 | tf_op jit(solution)/shard_map/ppermute | solution.py:325
  21.6 0.7 %links.1 = s32[5,9]{1,0:T(8,128)S(4)} custom-call(s32[2,9]{1,0:T(2,128)S(1)} %copy-done.1, s32[2,9]{1,0:T(2,128)S(1)} %slice_convert_fusion.other, bf16[512,128]{1,0:T(8,128)(2,1)S(1)} %project_q.1.q), custom_call_target="tpu_custom_call" | custom-call | bytes 2097152 | tf_op jit(solution)/shard_map/links/pallas_call | solution.py:338
  22.3 1.2 %collective-permute-done.9.d2 = bf16[256,256]{1,0:T(8,128)(2,1)S(1)} collective-permute-done((bf16[256,256]{1,0:T(8,128)(2,1)S(1)}, bf16[256,256]{1,0:T(8,128)(2,1)S(1)}, u32[]{:S(2)}, u32[]{:S(2)}) %collective-permute-start.9) | collective-permute-done | bytes 131104 | tf_op jit(solution)/shard_map/ppermute | solution.py:325
  23.5 1.0 %collective-permute-done.8.u3 = bf16[256,256]{1,0:T(8,128)(2,1)S(1)} collective-permute-done((bf16[256,256]{1,0:T(8,128)(2,1)S(1)}, bf16[256,256]{1,0:T(8,128)(2,1)S(1)}, u32[]{:S(2)}, u32[]{:S(2)}) %collective-permute-start.8) | collective-permute-done | bytes 131104 | tf_op jit(solution)/shard_map/ppermute | solution.py:325
  24.5 1.9 %collective-permute-done.10.d3 = bf16[256,256]{1,0:T(8,128)(2,1)S(1)} collective-permute-done((bf16[256,256]{1,0:T(8,128)(2,1)S(1)}, bf16[256,256]{1,0:T(8,128)(2,1)S(1)}, u32[]{:S(2)}, u32[]{:S(2)}) %collective-permute-start.10) | collective-permute-done | bytes 131104 | tf_op jit(solution)/shard_map/ppermute | solution.py:325
  26.4 2.9 %attend.1 = (bf16[4608,256]{1,0:T(8,128)(2,1)S(1)}, bf16[1024,256]{1,0:T(8,128)(2,1)S(1)}, bf16[2048,256]{1,0:T(8,128)(2,1)S(1)}, f32[1024,256]{1,0:T(8,128)S(1)...) custom-call(s32[5,9]{1,0:T(8,128)S(4)} %links.1, bf16[512,128]{1,0:T(8,128)(2,1)S(1)} %project_q.1.q, ...), custom_call_target="tpu_custom_call" | custom-call | flops 603979776 | bytes 2097152 | tf_op jit(solution)/shard_map/attend/pallas_call | solution.py:338
  29.3 2.0 %collective-permute-start.11 = (bf16[256,256]{1,0:T(8,128)(2,1)S(1)}, bf16[256,256]{1,0:T(8,128)(2,1)S(1)}, u32[]{:S(2)}, u32[]{:S(2)}) collective-permute-start(bf16[256,256]{1,0:T(8,128)(2,1)S(1)} %get-tuple-element.36), channel_id=1, source_target_pairs={{0,8},{1,0},{2,10},{3,2},{4,12},{5,4},{6,14},{7,6},{8,16},{9,1},{1... | collective-permute-start | bytes 393224 | tf_op jit(solution)/shard_map/ppermute | solution.py:325
  31.3 1.0 %outputs.1 = (bf16[256,128]{1,0:T(8,128)(2,1)S(1)}, bf16[256,128]{1,0:T(8,128)(2,1)S(1)}, bf16[512,128]{1,0:T(8,128)(2,1)S(1)}) custom-call(s32[5,9]{1,0:T(8,128)S(4)} %links.1, bf16[4608,256]{1,0:T(8,128)(2,1)S(1)} %get-tuple-element.30.mixed, bf16[2048,256]{1,0:T(8,128)(2,1)S(1)} %get-tuple-element.31.win), custom_call_target="tpu_custom_call" | custom-call | flops 301989888 | bytes 2097152 | tf_op jit(solution)/shard_map/outputs/pallas_call | solution.py:338
  32.4 0.8 %near_grads.1 = (f32[256,256]{1,0:T(8,128)S(1)}, f32[256,256]{1,0:T(8,128)S(1)}, bf16[512,256]{1,0:T(8,128)(2,1)S(1)}, bf16[512,256]{1,0:T(8,128)(2,1)S(1)}) custom-call(s32[5,9]{1,0:T(8,128)S(4)} %links.1, bf16[4608,256]{1,0:T(8,128)(2,1)S(1)} %get-tuple-element.30.mixed, bf16[1024,256]{1,0:T(8,128)(2,1)S(1)} %get-tuple-element.33.pairs, ...), custom_call_target="tpu_custom_call" | custom-call | flops 301989888 | bytes 2097152 | tf_op jit(solution)/shard_map/near_grads/pallas_call | solution.py:338
  33.2 1.6 %collective-permute-done.13.part = bf16[256,256]{1,0:T(8,128)(2,1)S(1)} collective-permute-done((bf16[256,256]{1,0:T(8,128)(2,1)S(1)}, bf16[256,256]{1,0:T(8,128)(2,1)S(1)}, u32[]{:S(2)}, u32[]{:S(2)}) %collective-permute-start.13) | collective-permute-done | bytes 131104 | tf_op jit(solution)/shard_map/ppermute | solution.py:325
  34.9 2.0 %collective-permute-start.12 = (bf16[512,256]{1,0:T(8,128)(2,1)S(1)}, bf16[512,256]{1,0:T(8,128)(2,1)S(1)}, u32[]{:S(2)}, u32[]{:S(2)}) collective-permute-start(bf16[512,256]{1,0:T(8,128)(2,1)S(1)} %merge_u.1), channel_id=1, source_target_pairs={{0,8},{1,0},{2,10},{3,2},{4,12},{5,4},{6,14},{7,6},{8,16},{9,1},{1... | collective-permute-start | bytes 786440 | tf_op jit(solution)/shard_map/ppermute | solution.py:325
  36.9 2.4 %collective-permute-start.15 = (bf16[256,128]{1,0:T(8,128)(2,1)S(1)}, bf16[256,128]{1,0:T(8,128)(2,1)S(1)}, u32[]{:S(2)}, u32[]{:S(2)}) collective-permute-start(bf16[256,128]{1,0:T(8,128)(2,1)S(1)} %get-tuple-element.40), channel_id=1, source_target_pairs={{0,4},{1,5},{2,6},{3,7},{4,0},{5,1},{6,2},{7,3},{8,12},{9,13},{10,... | collective-permute-start | bytes 196616 | tf_op jit(solution)/shard_map/ppermute | solution.py:314
  39.4 2.2 %collective-permute-done.15.other = bf16[256,128]{1,0:T(8,128)(2,1)S(1)} collective-permute-done((bf16[256,128]{1,0:T(8,128)(2,1)S(1)}, bf16[256,128]{1,0:T(8,128)(2,1)S(1)}, u32[]{:S(2)}, u32[]{:S(2)}) %collective-permute-start.15) | collective-permute-done | bytes 65568 | tf_op jit(solution)/shard_map/ppermute | solution.py:314
  41.6 0.7 %collective-permute-done.14.from_d = bf16[512,256]{1,0:T(8,128)(2,1)S(1)} collective-permute-done((bf16[512,256]{1,0:T(8,128)(2,1)S(1)}, bf16[512,256]{1,0:T(8,128)(2,1)S(1)}, u32[]{:S(2)}, u32[]{:S(2)}) %collective-permute-start.14) | collective-permute-done | bytes 262176 | tf_op jit(solution)/shard_map/ppermute | solution.py:325
  42.3 0.5 spread_send.1
  43.4 1.4 %collective-permute-done.16 = bf16[1024,256]{1,0:T(8,128)(2,1)S(1)} collective-permute-done((bf16[1024,256]{1,0:T(8,128)(2,1)S(1)}, bf16[1024,256]{1,0:T(8,128)(2,1)S(1)}, u32[]{:S(2)}, u32[]{:S(2)}) %collective-permute-start.16) | collective-permute-done | bytes 524320 | tf_op jit(solution)/shard_map/ppermute | solution.py:314
  45.0 2.3 %collective-permute-start.17 = (bf16[256,256]{1,0:T(8,128)(2,1)S(1)}, bf16[256,256]{1,0:T(8,128)(2,1)S(1)}, u32[]{:S(2)}, u32[]{:S(2)}) collective-permute-start(bf16[256,256]{1,0:T(8,128)(2,1)S(1)} %get-tuple-element.48), channel_id=1, source_target_pairs={{0,6},{1,7},{2,4},{3,5},{4,2},{5,3},{6,0},{7,1},{8,14},{9,15},{10,... | collective-permute-start | bytes 393224 | tf_op jit(solution)/shard_map/ppermute | solution.py:314
  47.3 0.5 collective-permute-start.19
  47.8 0.7 %collective-permute-start.18 = (bf16[256,256]{1,0:T(8,128)(2,1)S(1)}, bf16[256,256]{1,0:T(8,128)(2,1)S(1)}, u32[]{:S(2)}, u32[]{:S(2)}) collective-permute-start(bf16[256,256]{1,0:T(8,128)(2,1)S(1)} %get-tuple-element.50), channel_id=1, source_target_pairs={{0,4},{1,5},{2,6},{3,7},{4,0},{5,1},{6,2},{7,3},{8,12},{9,13},{10,... | collective-permute-start | bytes 393224 | tf_op jit(solution)/shard_map/ppermute | solution.py:314
  48.5 0.7 %lay_out.1 = bf16[256,256]{1,0:T(8,128)(2,1)} custom-call(bf16[256,128]{1,0:T(8,128)(2,1)S(1)} %get-tuple-element.32.own, bf16[256,128]{1,0:T(8,128)(2,1)S(1)} %collective-permute-done.15.other), custom_call_target="tpu_custom_call" | custom-call | bytes 2097152 | tf_op jit(solution)/shard_map/lay_out/pallas_call | solution.py:338
  49.2 3.1 %collective-permute-done.17 = bf16[256,256]{1,0:T(8,128)(2,1)S(1)} collective-permute-done((bf16[256,256]{1,0:T(8,128)(2,1)S(1)}, bf16[256,256]{1,0:T(8,128)(2,1)S(1)}, u32[]{:S(2)}, u32[]{:S(2)}) %collective-permute-start.17) | collective-permute-done | bytes 131104 | tf_op jit(solution)/shard_map/ppermute | solution.py:314
  52.3 1.9 %collective-permute-done.19 = bf16[256,256]{1,0:T(8,128)(2,1)S(1)} collective-permute-done((bf16[256,256]{1,0:T(8,128)(2,1)S(1)}, bf16[256,256]{1,0:T(8,128)(2,1)S(1)}, u32[]{:S(2)}, u32[]{:S(2)}) %collective-permute-start.19) | collective-permute-done | bytes 131104 | tf_op jit(solution)/shard_map/ppermute | solution.py:314
  54.3 0.7 %add_convert_fusion.1 = bf16[256,256]{1,0:T(8,128)(2,1)} fusion(bf16[256,256]{1,0:T(8,128)(2,1)S(1)} %collective-permute-done.19, bf16[256,256]{1,0:T(8,128)(2,1)S(1)} %collective-permute-done.18, bf16[256,256]{1,0:T(8,128)(2,1)S(1)} %collective-permute-done.17, bf16[1024,256]{1,0:T(8,128)(2,1)S(1)} %add_convert_fusion), kind=kLoop, calls=%fused_computation.1 | loop fusion | flops 524288 | bytes 655360 | tf_op jit(solution)/shard_map/convert_element_type | solution.py:452
  (33 shorter events, 2.6 us)
Async XLA Ops:
  0.6 8.9 %collective-permute-start = (bf16[256,256]{1,0:T(8,128)(2,1)}, bf16[256,256]{1,0:T(8,128)(2,1)S(1)}, u32[]{:S(2)}, u32[]{:S(2)}) collective-permute-start(bf16[256,256]{1,0:T(8,128)(2,1)} %f.1), channel_id=1, source_target_pairs={{0,4},{1,5},{2,6},{3,7},{4,0},{5,1},{6,2},{7,3},{8,12},{9,13},{10,... | collective-permute-start | bytes 393224 | tf_op jit(solution)/shard_map/ppermute | solution.py:314
  3.7 7.5 %collective-permute-start.2 = (bf16[256,256]{1,0:T(8,128)(2,1)}, bf16[256,256]{1,0:T(8,128)(2,1)S(1)}, u32[]{:S(2)}, u32[]{:S(2)}) collective-permute-start(bf16[256,256]{1,0:T(8,128)(2,1)} %f.1), channel_id=1, source_target_pairs={{0,6},{1,7},{2,4},{3,5},{4,2},{5,3},{6,0},{7,1},{8,14},{9,15},{10,... | collective-permute-start | bytes 393224 | tf_op jit(solution)/shard_map/ppermute | solution.py:314
  5.1 6.4 %collective-permute-start.1 = (bf16[256,256]{1,0:T(8,128)(2,1)}, bf16[256,256]{1,0:T(8,128)(2,1)S(1)}, u32[]{:S(2)}, u32[]{:S(2)}) collective-permute-start(bf16[256,256]{1,0:T(8,128)(2,1)} %f.1), channel_id=1, source_target_pairs={{0,2},{1,3},{2,0},{3,1},{4,6},{5,7},{6,4},{7,5},{8,10},{9,11},{10,... | collective-permute-start | bytes 393224 | tf_op jit(solution)/shard_map/ppermute | solution.py:314
  11.5 4.0 %copy-start.1 = (s32[2,9]{1,0:T(2,128)S(1)}, s32[2,9]{1,0:T(2,128)}, u32[]{:S(2)}) copy-start(s32[2,9]{1,0:T(2,128)} %own.1) | copy-start | bytes 220
  11.6 4.0 %copy-start = (bf16[256,256]{1,0:T(8,128)(2,1)S(1)}, bf16[256,256]{1,0:T(8,128)(2,1)}, u32[]{:S(2)}) copy-start(bf16[256,256]{1,0:T(8,128)(2,1)} %d_own.3) | copy-start | bytes 393220
  11.6 2.0 %collective-permute-start.4 = (bf16[1024,256]{1,0:T(8,128)(2,1)S(1)}, bf16[1024,256]{1,0:T(8,128)(2,1)S(1)}, u32[]{:S(2)}, u32[]{:S(2)}) collective-permute-start(bf16[1024,256]{1,0:T(8,128)(2,1)S(1)} %pack.1), channel_id=1, source_target_pairs={{0,1},{1,0},{2,3},{3,2},{4,5},{5,4},{6,7},{7,6},{8,9},{9,8},{10,11... | collective-permute-start | bytes 1572872 | tf_op jit(solution)/shard_map/ppermute | solution.py:314
  13.8 5.4 %collective-permute-start.5 = (bf16[256,256]{1,0:T(8,128)(2,1)S(1)}, bf16[256,256]{1,0:T(8,128)(2,1)S(1)}, u32[]{:S(2)}, u32[]{:S(2)}) collective-permute-start(bf16[256,256]{1,0:T(8,128)(2,1)S(1)} %get-tuple-element.28.first_kv), channel_id=1, source_target_pairs={{0,8},{1,0},{2,10},{3,2},{4,12},{5,4},{6,14},{7,6},{8,16},{9,1},{1... | collective-permute-start | bytes 393224 | tf_op jit(solution)/shard_map/ppermute | solution.py:325
  15.6 5.7 %collective-permute-start.6 = (bf16[256,256]{1,0:T(8,128)(2,1)S(1)}, bf16[256,256]{1,0:T(8,128)(2,1)S(1)}, u32[]{:S(2)}, u32[]{:S(2)}) collective-permute-start(bf16[256,256]{1,0:T(8,128)(2,1)S(1)} %get-tuple-element.29.second_kv), channel_id=1, source_target_pairs={{0,1},{1,9},{2,3},{3,11},{4,5},{5,13},{6,7},{7,15},{8,0},{9,17},{1... | collective-permute-start | bytes 393224 | tf_op jit(solution)/shard_map/ppermute | solution.py:325
  15.6 5.6 %collective-permute-start.3 = (bf16[272,128]{1,0:T(8,128)(2,1)S(1)}, bf16[272,128]{1,0:T(8,128)(2,1)S(1)}, u32[]{:S(2)}, u32[]{:S(2)}) collective-permute-start(bf16[272,128]{1,0:T(8,128)(2,1)S(1)} %payload.1), channel_id=1, source_target_pairs={{0,4},{1,5},{2,6},{3,7},{4,0},{5,1},{6,2},{7,3},{8,12},{9,13},{10,... | collective-permute-start | bytes 208904 | tf_op jit(solution)/shard_map/ppermute | solution.py:314
  17.2 6.3 %collective-permute-start.9 = (bf16[256,256]{1,0:T(8,128)(2,1)S(1)}, bf16[256,256]{1,0:T(8,128)(2,1)S(1)}, u32[]{:S(2)}, u32[]{:S(2)}) collective-permute-start(bf16[256,256]{1,0:T(8,128)(2,1)S(1)} %get-tuple-element.28.first_kv), channel_id=1, source_target_pairs={{0,1},{1,9},{2,3},{3,11},{4,5},{5,13},{6,7},{7,15},{8,0},{9,17},{1... | collective-permute-start | bytes 393224 | tf_op jit(solution)/shard_map/ppermute | solution.py:325
  17.2 6.3 %collective-permute-start.7 = (bf16[256,256]{1,0:T(8,128)(2,1)S(1)}, bf16[256,256]{1,0:T(8,128)(2,1)S(1)}, u32[]{:S(2)}, u32[]{:S(2)}) collective-permute-start(bf16[256,256]{1,0:T(8,128)(2,1)S(1)} %get-tuple-element.29.second_kv), channel_id=1, source_target_pairs={{0,8},{1,0},{2,10},{3,2},{4,12},{5,4},{6,14},{7,6},{8,16},{9,1},{1... | collective-permute-start | bytes 393224 | tf_op jit(solution)/shard_map/ppermute | solution.py:325
  19.3 5.3 %collective-permute-start.8 = (bf16[256,256]{1,0:T(8,128)(2,1)S(1)}, bf16[256,256]{1,0:T(8,128)(2,1)S(1)}, u32[]{:S(2)}, u32[]{:S(2)}) collective-permute-start(bf16[256,256]{1,0:T(8,128)(2,1)S(1)} %collective-permute-done.5.u1), channel_id=1, source_target_pairs={{0,8},{1,0},{2,10},{3,2},{4,12},{5,4},{6,14},{7,6},{8,16},{9,1},{1... | collective-permute-start | bytes 393224 | tf_op jit(solution)/shard_map/ppermute | solution.py:325
  21.3 5.1 %collective-permute-start.10 = (bf16[256,256]{1,0:T(8,128)(2,1)S(1)}, bf16[256,256]{1,0:T(8,128)(2,1)S(1)}, u32[]{:S(2)}, u32[]{:S(2)}) collective-permute-start(bf16[256,256]{1,0:T(8,128)(2,1)S(1)} %collective-permute-done.6.d1), channel_id=1, source_target_pairs={{0,1},{1,9},{2,3},{3,11},{4,5},{5,13},{6,7},{7,15},{8,0},{9,17},{1... | collective-permute-start | bytes 393224 | tf_op jit(solution)/shard_map/ppermute | solution.py:325
  29.3 5.5 %collective-permute-start.13 = (bf16[256,256]{1,0:T(8,128)(2,1)S(1)}, bf16[256,256]{1,0:T(8,128)(2,1)S(1)}, u32[]{:S(2)}, u32[]{:S(2)}) collective-permute-start(bf16[256,256]{1,0:T(8,128)(2,1)S(1)} %get-tuple-element.39), channel_id=1, source_target_pairs={{0,1},{1,9},{2,3},{3,11},{4,5},{5,13},{6,7},{7,15},{8,0},{9,17},{1... | collective-permute-start | bytes 393224 | tf_op jit(solution)/shard_map/ppermute | solution.py:325
  29.3 5.5 %collective-permute-start.11 = (bf16[256,256]{1,0:T(8,128)(2,1)S(1)}, bf16[256,256]{1,0:T(8,128)(2,1)S(1)}, u32[]{:S(2)}, u32[]{:S(2)}) collective-permute-start(bf16[256,256]{1,0:T(8,128)(2,1)S(1)} %get-tuple-element.36), channel_id=1, source_target_pairs={{0,8},{1,0},{2,10},{3,2},{4,12},{5,4},{6,14},{7,6},{8,16},{9,1},{1... | collective-permute-start | bytes 393224 | tf_op jit(solution)/shard_map/ppermute | solution.py:325
  34.8 7.5 %collective-permute-start.14 = (bf16[512,256]{1,0:T(8,128)(2,1)S(1)}, bf16[512,256]{1,0:T(8,128)(2,1)S(1)}, u32[]{:S(2)}, u32[]{:S(2)}) collective-permute-start(bf16[512,256]{1,0:T(8,128)(2,1)S(1)} %merge_d.1), channel_id=1, source_target_pairs={{0,1},{1,9},{2,3},{3,11},{4,5},{5,13},{6,7},{7,15},{8,0},{9,17},{1... | collective-permute-start | bytes 786440 | tf_op jit(solution)/shard_map/ppermute | solution.py:325
  34.9 7.4 %collective-permute-start.12 = (bf16[512,256]{1,0:T(8,128)(2,1)S(1)}, bf16[512,256]{1,0:T(8,128)(2,1)S(1)}, u32[]{:S(2)}, u32[]{:S(2)}) collective-permute-start(bf16[512,256]{1,0:T(8,128)(2,1)S(1)} %merge_u.1), channel_id=1, source_target_pairs={{0,8},{1,0},{2,10},{3,2},{4,12},{5,4},{6,14},{7,6},{8,16},{9,1},{1... | collective-permute-start | bytes 786440 | tf_op jit(solution)/shard_map/ppermute | solution.py:325
  36.9 4.7 %collective-permute-start.15 = (bf16[256,128]{1,0:T(8,128)(2,1)S(1)}, bf16[256,128]{1,0:T(8,128)(2,1)S(1)}, u32[]{:S(2)}, u32[]{:S(2)}) collective-permute-start(bf16[256,128]{1,0:T(8,128)(2,1)S(1)} %get-tuple-element.40), channel_id=1, source_target_pairs={{0,4},{1,5},{2,6},{3,7},{4,0},{5,1},{6,2},{7,3},{8,12},{9,13},{10,... | collective-permute-start | bytes 196616 | tf_op jit(solution)/shard_map/ppermute | solution.py:314
  42.8 2.0 %collective-permute-start.16 = (bf16[1024,256]{1,0:T(8,128)(2,1)S(1)}, bf16[1024,256]{1,0:T(8,128)(2,1)S(1)}, u32[]{:S(2)}, u32[]{:S(2)}) collective-permute-start(bf16[1024,256]{1,0:T(8,128)(2,1)S(1)} %get-tuple-element.47), channel_id=1, source_target_pairs={{0,1},{1,0},{2,3},{3,2},{4,5},{5,4},{6,7},{7,6},{8,9},{9,8},{10,11... | collective-permute-start | bytes 1572872 | tf_op jit(solution)/shard_map/ppermute | solution.py:314
  45.0 7.3 %collective-permute-start.17 = (bf16[256,256]{1,0:T(8,128)(2,1)S(1)}, bf16[256,256]{1,0:T(8,128)(2,1)S(1)}, u32[]{:S(2)}, u32[]{:S(2)}) collective-permute-start(bf16[256,256]{1,0:T(8,128)(2,1)S(1)} %get-tuple-element.48), channel_id=1, source_target_pairs={{0,6},{1,7},{2,4},{3,5},{4,2},{5,3},{6,0},{7,1},{8,14},{9,15},{10,... | collective-permute-start | bytes 393224 | tf_op jit(solution)/shard_map/ppermute | solution.py:314
  47.3 6.9 %collective-permute-start.19 = (bf16[256,256]{1,0:T(8,128)(2,1)S(1)}, bf16[256,256]{1,0:T(8,128)(2,1)S(1)}, u32[]{:S(2)}, u32[]{:S(2)}) collective-permute-start(bf16[256,256]{1,0:T(8,128)(2,1)S(1)} %get-tuple-element.49), channel_id=1, source_target_pairs={{0,2},{1,3},{2,0},{3,1},{4,6},{5,7},{6,4},{7,5},{8,10},{9,11},{10,... | collective-permute-start | bytes 393224 | tf_op jit(solution)/shard_map/ppermute | solution.py:314
  47.8 6.4 %collective-permute-start.18 = (bf16[256,256]{1,0:T(8,128)(2,1)S(1)}, bf16[256,256]{1,0:T(8,128)(2,1)S(1)}, u32[]{:S(2)}, u32[]{:S(2)}) collective-permute-start(bf16[256,256]{1,0:T(8,128)(2,1)S(1)} %get-tuple-element.50), channel_id=1, source_target_pairs={{0,4},{1,5},{2,6},{3,7},{4,0},{5,1},{6,2},{7,3},{8,12},{9,13},{10,... | collective-permute-start | bytes 393224 | tf_op jit(solution)/shard_map/ppermute | solution.py:314

commit v8 on v7

--- a/solution.py
+++ b/solution.py
@@ -164,12 +164,60 @@
     return pl.multiple_of(links[GROUP, 2 * i + t - 1], BLK)
 
 
-def is_far(i, t):
-    return t == (1 if i < GROUP // 2 else 2)
-
-
-def run_rows(i, t):
-    return slice((i * 3 + t) * SPAN * BLK, (i * 3 + t + 1) * SPAN * BLK)
+def far_run(i):
+    return 1 if i < GROUP // 2 else 2
+
+
+def near_runs(i):
+    return tuple(t for t in range(3) if t != far_run(i))
+
+
+def near_rows(i, index, j):
+    first = ((2 * i + index) * SPAN + j) * BLK
+    return slice(first, first + BLK)
+
+
+def far_rows(i):
+    return slice(i * SPAN * BLK, (i + 1) * SPAN * BLK)
+
+
+def run_scores(links, rows, pair, i, t):
+    product = dot(rows, pair, ((1,), (1,)))
+    blocks = []
+    for j in range(SPAN):
+        block = product[j * BLK : (j + 1) * BLK]
+        bias = jnp.where(links[i, SPAN * t + j] >= 0, 0.0, DEAD).astype(F32)
+        blocks.append((block[:, :BLK], block[:, BLK:], bias))
+    return blocks
+
+
+def fold(block):
+    return block.reshape(BLK // 8, 8, BLK)
+
+
+def largest_of(blocks):
+    best = None
+    for score, _, bias in blocks:
+        peak = jnp.max(fold(score), axis=0) + bias
+        best = peak if best is None else jnp.maximum(best, peak)
+    return jnp.max(best, axis=0, keepdims=True)
+
+
+def exponentials(blocks, largest):
+    terms = []
+    total = jnp.zeros((8, BLK), F32)
+    weighted = jnp.zeros((8, BLK), F32)
+    for score, prob_grad, bias in blocks:
+        term = jnp.exp2((score - (largest - bias)) * (HD ** -0.5 * LOG2E))
+        terms.append(term)
+        total = total + jnp.sum(fold(term), axis=0)
+        weighted = weighted + jnp.sum(fold(term * prob_grad), axis=0)
+    return terms, jnp.sum(total, axis=0, keepdims=True), jnp.sum(weighted, axis=0, keepdims=True)
+
+
+def mix(share, prob_grad, row_dot):
+    grad = share * (prob_grad - row_dot)
+    return jnp.concatenate([grad.astype(BF), share.astype(BF)], axis=1)
 
 
 def side_factor():
@@ -177,18 +225,14 @@
     return jnp.where(lax.broadcasted_iota(jnp.int32, (1, 2 * HD), 1) < HD, scale, 1.0).astype(F32)
 
 
-def attend_kernel(
-    links, q, first_kv, second_kv, u1, d1, u2, u3, d2, d3, d_own, d_other,
-    mixed, pairs, win, near_acc, far_u_out, far_d_out, acc,
+def near_scores_kernel(
+    links, q, first_kv, second_kv, u1, d1, u2, d2, d_own, d_other,
+    pairs, terms_out, prob_grads_out, stats, win,
 ):
     side, flip, _, _ = position()
-    scale = HD ** -0.5
     places = regions(flip)
-    halves = (first_kv, second_kv, u1, d1, u2, u3, d2, d3)
-    for at, half in zip(places, halves):
+    for at, half in zip(places[:5] + places[6:7], (first_kv, second_kv, u1, d1, u2, d2)):
         win[pl.ds(at, HALF), :] = half[...]
-    at_far_u, at_far_d = places[7], places[5]
-    acc[...] = jnp.zeros_like(acc)
     zeros = jnp.zeros((BLK, HD), BF)
     own_cols = pl.ds(pl.multiple_of(side * HD, HD), HD)
     for i in range(GROUP):
@@ -203,57 +247,68 @@
             axis=0,
         )
         pairs[2 * i * BLK : 2 * (i + 1) * BLK, :] = pair
-        scores, prob_grads, peaks, biases = [], [], [], []
-        for t in range(3):
-            product = dot(win[pl.ds(start_of(links, i, t), SPAN * BLK), :], pair, ((1,), (1,)))
-            for j in range(SPAN):
-                block = product[j * BLK : (j + 1) * BLK]
-                bias = jnp.where(links[i, SPAN * t + j] >= 0, 0.0, DEAD).astype(F32)
-                scores.append(block[:, :BLK])
-                prob_grads.append(block[:, BLK:])
-                biases.append(bias)
-                peaks.append(jnp.max(block[:, :BLK].reshape(BLK // 8, 8, BLK), axis=0) + bias)
-        largest = peaks[0]
-        for peak in peaks[1:]:
-            largest = jnp.maximum(largest, peak)
-        largest = jnp.max(largest, axis=0, keepdims=True)
-        terms = []
-        total = jnp.zeros((8, BLK), F32)
-        weighted = jnp.zeros((8, BLK), F32)
-        for n in range(3 * SPAN):
-            term = jnp.exp2((scores[n] - (largest - biases[n])) * (scale * LOG2E))
-            terms.append(term)
-            total = total + jnp.sum(term.reshape(BLK // 8, 8, BLK), axis=0)
-            weighted = weighted + jnp.sum((term * prob_grads[n]).reshape(BLK // 8, 8, BLK), axis=0)
-        inverse = 1.0 / jnp.sum(total, axis=0, keepdims=True)
-        row_dot = jnp.sum(weighted, axis=0, keepdims=True) * inverse
-        for t in range(3):
-            parts = []
-            for n in range(SPAN * t, SPAN * t + SPAN):
-                share = terms[n] * inverse
-                grad = share * (prob_grads[n] - row_dot)
-                parts.append(jnp.concatenate([grad.astype(BF), share.astype(BF)], axis=1))
-            part = jnp.concatenate(parts, axis=0)
-            mixed[run_rows(i, t), :] = part
-            if is_far(i, t):
-                acc[pl.ds(start_of(links, i, t), SPAN * BLK), :] += dot(part, pair, ((1,), (0,)))
+        blocks = []
+        for t in near_runs(i):
+            blocks += run_scores(links, win[pl.ds(start_of(links, i, t), SPAN * BLK), :], pair, i, t)
+        largest = largest_of(blocks)
+        terms, total, weighted = exponentials(blocks, largest)
+        for n, term in enumerate(terms):
+            terms_out[near_rows(i, 0, n), :] = term
+            prob_grads_out[near_rows(i, 0, n), :] = blocks[n][1]
+        for n, row in enumerate((largest, total, weighted)):
+            stats[8 * (3 * i + n) : 8 * (3 * i + n + 1), :] = jnp.broadcast_to(row, (8, BLK))
+
+
+def far_grads_kernel(
+    links, pairs, stats, u1, d1, u2, u3, d2, d3,
+    mixed, near_acc, far_u_out, far_d_out, scales, win, acc,
+):
+    places = regions(position()[1])
+    for at, half in zip(places[2:], (u1, d1, u2, u3, d2, d3)):
+        win[pl.ds(at, HALF), :] = half[...]
+    acc[:OWN, :] = jnp.zeros((OWN, 2 * HD), F32)
+    acc[NEAR_RIGHT:, :] = jnp.zeros((OWN, 2 * HD), F32)
+    for i in range(GROUP):
+        pair = pairs[2 * i * BLK : 2 * (i + 1) * BLK, :]
+        at = pl.ds(start_of(links, i, far_run(i)), SPAN * BLK)
+        blocks = run_scores(links, win[at, :], pair, i, far_run(i))
+        near_largest, near_total, near_weighted = (stats[8 * (3 * i + n) : 8 * (3 * i + n) + 1, :] for n in range(3))
+        largest = jnp.maximum(near_largest, largest_of(blocks))
+        terms, total, weighted = exponentials(blocks, largest)
+        near_scale = jnp.exp2((near_largest - largest) * (HD ** -0.5 * LOG2E))
+        inverse = 1.0 / (total + near_scale * near_total)
+        row_dot = (weighted + near_scale * near_weighted) * inverse
+        for n, row in enumerate((near_scale * inverse, row_dot)):
+            scales[8 * (2 * i + n) : 8 * (2 * i + n + 1), :] = jnp.broadcast_to(row, (8, BLK))
+        part = jnp.concatenate(
+            [mix(term * inverse, block[1], row_dot) for term, block in zip(terms, blocks)], axis=0
+        )
+        mixed[far_rows(i), :] = part
+        acc[at, :] += dot(part, pair, ((1,), (0,)))
     factor = side_factor()
-    far_u_out[...] = (acc[pl.ds(at_far_u, HALF), :] * factor).astype(BF)
-    far_d_out[...] = (acc[pl.ds(at_far_d, HALF), :] * factor).astype(BF)
+    far_u_out[...] = (acc[pl.ds(places[7], HALF), :] * factor).astype(BF)
+    far_d_out[...] = (acc[pl.ds(places[5], HALF), :] * factor).astype(BF)
     near_acc[:ROWS, :] = acc[NEAR_LEFT:OWN, :]
     near_acc[ROWS:, :] = acc[NEAR_RIGHT:FAR_RIGHT, :]
 
 
-def near_grads_kernel(links, mixed, pairs, near_acc, first_own, second_own, u_out, d_out, acc):
+def near_grads_kernel(
+    links, pairs, terms, prob_grads, scales, near_acc, mixed, first_own, second_own, u_out, d_out, acc
+):
     acc[NEAR_LEFT:OWN, :] = near_acc[:ROWS, :]
     acc[OWN:NEAR_RIGHT, :] = jnp.zeros((ROWS, 2 * HD), F32)
     acc[NEAR_RIGHT:FAR_RIGHT, :] = near_acc[ROWS:, :]
     for i in range(GROUP):
         pair = pairs[2 * i * BLK : 2 * (i + 1) * BLK, :]
-        for t in range(3):
-            if not is_far(i, t):
-                at = pl.ds(start_of(links, i, t), SPAN * BLK)
-                acc[at, :] += dot(mixed[run_rows(i, t), :], pair, ((1,), (0,)))
+        scale, row_dot = (scales[8 * (2 * i + n) : 8 * (2 * i + n) + 1, :] for n in range(2))
+        for index, t in enumerate(near_runs(i)):
+            parts = []
+            for j in range(SPAN):
+                rows = near_rows(i, index, j)
+                parts.append(mix(terms[rows, :] * scale, prob_grads[rows, :], row_dot))
+                mixed[rows, :] = parts[-1]
+            at = pl.ds(start_of(links, i, t), SPAN * BLK)
+            acc[at, :] += dot(jnp.concatenate(parts, axis=0), pair, ((1,), (0,)))
     factor = side_factor()
     first, second, u1, d1, u2, _, d2, _ = regions(position()[1])
     first_own[...] = acc[pl.ds(first, HALF), :] * factor
@@ -263,15 +318,21 @@
         target[HALF:, :] = (acc[pl.ds(at_second, HALF), :] * factor).astype(BF)
 
 
-def outputs_kernel(links, mixed, win, att_own, att_other, dq_out, att):
-    side = position()[0]
+def outputs_kernel(
+    links, near_mixed, far_mixed, first_kv, second_kv, u1, d1, u2, u3, d2, d3,
+    att_own, att_other, dq_out, win, att,
+):
+    side, flip, _, _ = position()
+    for at, half in zip(regions(flip), (first_kv, second_kv, u1, d1, u2, u3, d2, d3)):
+        win[pl.ds(at, HALF), :] = half[...]
     for i in range(GROUP):
         rows = slice(i * BLK, (i + 1) * BLK)
-        out = None
-        for t in range(3):
-            keys = win[pl.ds(start_of(links, i, t), SPAN * BLK), :]
-            term = dot(mixed[run_rows(i, t), :], keys, ((0,), (0,)))
-            out = term if out is None else out + term
+        out = dot(
+            far_mixed[far_rows(i), :], win[pl.ds(start_of(links, i, far_run(i)), SPAN * BLK), :], ((0,), (0,))
+        )
+        for index, t in enumerate(near_runs(i)):
+            part = near_mixed[near_rows(i, index, 0).start : near_rows(i, index, SPAN - 1).stop, :]
+            out = out + dot(part, win[pl.ds(start_of(links, i, t), SPAN * BLK), :], ((0,), (0,)))
         att[rows, :] = out[BLK:, HD:].astype(BF)
         dq_out[rows, :] = (out[:BLK, :HD] * (HD ** -0.5)).astype(BF)
     att_own[...] = att[pl.ds(pl.multiple_of(side * HALF, HALF), HALF), :]
@@ -387,39 +448,55 @@
         links_kernel, "links", [pltpu.SMEM((GROUP + 1, slots), jnp.int32)], (block_links, other_links, q), 4, 0
     )
     links = pltpu.with_memory_space_constraint(links, pltpu.SMEM)
-    mixed, pairs, win, near_acc, far_u_grad, far_d_grad = call(
-        attend_kernel,
-        "attend",
+    window = pltpu.VMEM((WINDOW * BLK, 2 * HD), BF)
+    sums = pltpu.VMEM((WINDOW * BLK, 2 * HD), F32)
+    run = SPAN * BLK
+    pairs, terms, prob_grads, stats = call(
+        near_scores_kernel,
+        "near_scores",
         [
-            held(GROUP * 9 * BLK, 2 * HD),
             held(GROUP * 2 * BLK, 2 * HD),
-            held(WINDOW * BLK, 2 * HD),
+            held(GROUP * 2 * run, BLK, F32),
+            held(GROUP * 2 * run, BLK, F32),
+            held(GROUP * 3 * 8, BLK, F32),
+        ],
+        (links, q, first, second, u1, d1, u2, d2, d_out, d_other),
+        6,
+        attention,
+        [window],
+    )
+    far_mixed, near_acc, far_u_grad, far_d_grad, scales = call(
+        far_grads_kernel,
+        "far_grads",
+        [
+            held(GROUP * run, 2 * HD),
             held(2 * ROWS, 2 * HD, F32),
             out(HALF, 2 * HD),
             out(HALF, 2 * HD),
+            held(GROUP * 2 * 8, BLK, F32),
         ],
-        (links, q, first, second, u1, d1, u2, u3, d2, d3, d_out, d_other),
-        8,
-        2 * attention,
-        [pltpu.VMEM((WINDOW * BLK, 2 * HD), F32)],
-    )
-    first_own, second_own, u_grad, d_grad = call(
+        (links, pairs, stats, u1, d1, u2, u3, d2, d3),
+        6,
+        attention,
+        [window, sums],
+    )
+    near_mixed, first_own, second_own, u_grad, d_grad = call(
         near_grads_kernel,
         "near_grads",
-        [held(HALF, 2 * HD, F32)] * 2 + [out(ROWS, 2 * HD)] * 2,
-        (links, mixed, pairs, near_acc),
+        [held(GROUP * 2 * run, 2 * HD)] + [held(HALF, 2 * HD, F32)] * 2 + [out(ROWS, 2 * HD)] * 2,
+        (links, pairs, terms, prob_grads, scales, near_acc),
         4,
         attention,
-        [pltpu.VMEM((WINDOW * BLK, 2 * HD), F32)],
+        [sums],
     )
     att_own, att_other, dq = call(
         outputs_kernel,
         "outputs",
         [out(HALF, HD), out(HALF, HD), held(ROWS, HD)],
-        (links, mixed, win),
+        (links, near_mixed, far_mixed, first, second, u1, d1, u2, u3, d2, d3),
         4,
         attention,
-        [pltpu.VMEM((ROWS, HD), BF)],
+        [window, pltpu.VMEM((ROWS, HD), BF)],
     )
 
     back_u = chain(far_u_grad, 0)

time: 55.1 us -> 53.5 us (0.971)
  waiting for transfers between devices: 21.5 us -> 20.4 us
  Pallas kernels: 9.65 us -> 9.03 us
    ppermute x10, waiting for transfers between devices: 6.36 us -> 5.36 us  [chain(): return lax.ppermute(value, ('ctx', 'head'), pairs)]
    pallas_call x15 -> x16, Pallas kernels: 9.65 us -> 9.03 us  [call(): pl.pallas_call(kernel, name=name, out_shape=outs, in_specs=specs, out_spe...]
  transfers between devices with their start and end apart: 20 -> 20, of which waited for: 14 -> 14; matrix products, arithmetic and copies ran while one was open for 0% -> 0% of each run, Pallas kernels for 11% -> 13%
where the time goes in v8:
time: 53.5 us; the launch traced here: 53.3 us
  starting transfers between devices  22.1 us (41%)
  waiting for transfers between devices  20.4 us (38%)
  Pallas kernels  9.03 us (17%)
  other arithmetic  0.87 us (2%)
  between operations  0.84 us (2%)
    ppermute x10, waiting for transfers between devices, across(): return lax.ppermute(value, ('ctx', 'head'), pairs)  15.1 us
    ppermute x10, starting transfers between devices, across(): return lax.ppermute(value, ('ctx', 'head'), pairs)  12.3 us
    ppermute x10, starting transfers between devices, chain(): return lax.ppermute(value, ('ctx', 'head'), pairs)  9.84 us
    pallas_call x16, Pallas kernels, call(): pl.pallas_call(kernel, name=name, out_shape=outs, in_specs=specs, out_spe...  9.03 us
    ppermute x10, waiting for transfers between devices, chain(): return lax.ppermute(value, ('ctx', 'head'), pairs)  5.36 us
  transfers between devices with their start and end apart: 20, of which 14 were waited for; matrix products, arithmetic and copies ran while one was open for 0% of the time, Pallas kernels for 13%

profile of v8, /device:TPU:0, one launch (start us, length us, event | category | flops | bytes accessed | tf_op | source)
XLA Modules:
  0.0 53.3 jit_solution(14541307470250738183)
XLA Ops:
  0.6 3.0 %collective-permute-start = (bf16[256,256]{1,0:T(8,128)(2,1)}, bf16[256,256]{1,0:T(8,128)(2,1)S(1)}, u32[]{:S(2)}, u32[]{:S(2)}) collective-permute-start(bf16[256,256]{1,0:T(8,128)(2,1)} %f.1), channel_id=1, source_target_pairs={{0,4},{1,5},{2,6},{3,7},{4,0},{5,1},{6,2},{7,3},{8,12},{9,13},{10,... | collective-permute-start | bytes 393224 | tf_op jit(solution)/shard_map/ppermute | solution.py:375
  3.7 1.4 %collective-permute-start.2 = (bf16[256,256]{1,0:T(8,128)(2,1)}, bf16[256,256]{1,0:T(8,128)(2,1)S(1)}, u32[]{:S(2)}, u32[]{:S(2)}) collective-permute-start(bf16[256,256]{1,0:T(8,128)(2,1)} %f.1), channel_id=1, source_target_pairs={{0,6},{1,7},{2,4},{3,5},{4,2},{5,3},{6,0},{7,1},{8,14},{9,15},{10,... | collective-permute-start | bytes 393224 | tf_op jit(solution)/shard_map/ppermute | solution.py:375
  5.2 1.4 %begin.1 = (bf16[1024,384]{1,0:T(8,128)(2,1)S(1)}, bf16[256,256]{1,0:T(8,128)(2,1)S(1)}, f32[256,384]{1,0:T(8,128)S(1)}) custom-call(bf16[256,256]{1,0:T(8,128)(2,1)} %f.1, bf16[3,1024,256]{2,1,0:T(8,128)(2,1)} %bitcast.1), custom_call_target="tpu_custom_call" | custom-call | flops 100663296 | bytes 2097152 | tf_op jit(solution)/shard_map/begin/pallas_call | solution.py:399
  6.6 2.9 %collective-permute-done.sy = bf16[256,256]{1,0:T(8,128)(2,1)S(1)} collective-permute-done((bf16[256,256]{1,0:T(8,128)(2,1)}, bf16[256,256]{1,0:T(8,128)(2,1)S(1)}, u32[]{:S(2)}, u32[]{:S(2)}) %collective-permute-start) | collective-permute-done | bytes 131104 | tf_op jit(solution)/shard_map/ppermute | solution.py:375
  9.5 1.6 %collective-permute-done.2.sd = bf16[256,256]{1,0:T(8,128)(2,1)S(1)} collective-permute-done((bf16[256,256]{1,0:T(8,128)(2,1)}, bf16[256,256]{1,0:T(8,128)(2,1)S(1)}, u32[]{:S(2)}, u32[]{:S(2)}) %collective-permute-start.2) | collective-permute-done | bytes 131104 | tf_op jit(solution)/shard_map/ppermute | solution.py:375
  12.0 1.5 %collective-permute-done.4.other = bf16[1024,256]{1,0:T(8,128)(2,1)S(1)} collective-permute-done((bf16[1024,256]{1,0:T(8,128)(2,1)S(1)}, bf16[1024,256]{1,0:T(8,128)(2,1)S(1)}, u32[]{:S(2)}, u32[]{:S(2)}) %collective-permute-start.4) | collective-permute-done | bytes 524320 | tf_op jit(solution)/shard_map/ppermute | solution.py:375
  13.8 1.7 %collective-permute-start.5 = (bf16[256,256]{1,0:T(8,128)(2,1)S(1)}, bf16[256,256]{1,0:T(8,128)(2,1)S(1)}, u32[]{:S(2)}, u32[]{:S(2)}) collective-permute-start(bf16[256,256]{1,0:T(8,128)(2,1)S(1)} %get-tuple-element.32.first_kv), channel_id=1, source_target_pairs={{0,8},{1,0},{2,10},{3,2},{4,12},{5,4},{6,14},{7,6},{8,16},{9,1},{1... | collective-permute-start | bytes 393224 | tf_op jit(solution)/shard_map/ppermute | solution.py:386
  15.6 1.6 %collective-permute-start.3 = (bf16[272,128]{1,0:T(8,128)(2,1)S(1)}, bf16[272,128]{1,0:T(8,128)(2,1)S(1)}, u32[]{:S(2)}, u32[]{:S(2)}) collective-permute-start(bf16[272,128]{1,0:T(8,128)(2,1)S(1)} %payload.1), channel_id=1, source_target_pairs={{0,4},{1,5},{2,6},{3,7},{4,0},{5,1},{6,2},{7,3},{8,12},{9,13},{10,... | collective-permute-start | bytes 208904 | tf_op jit(solution)/shard_map/ppermute | solution.py:375
  17.2 2.0 %collective-permute-start.7 = (bf16[256,256]{1,0:T(8,128)(2,1)S(1)}, bf16[256,256]{1,0:T(8,128)(2,1)S(1)}, u32[]{:S(2)}, u32[]{:S(2)}) collective-permute-start(bf16[256,256]{1,0:T(8,128)(2,1)S(1)} %get-tuple-element.33.second_kv), channel_id=1, source_target_pairs={{0,8},{1,0},{2,10},{3,2},{4,12},{5,4},{6,14},{7,6},{8,16},{9,1},{1... | collective-permute-start | bytes 393224 | tf_op jit(solution)/shard_map/ppermute | solution.py:386
  19.2 2.0 %collective-permute-start.9 = (bf16[256,256]{1,0:T(8,128)(2,1)S(1)}, bf16[256,256]{1,0:T(8,128)(2,1)S(1)}, u32[]{:S(2)}, u32[]{:S(2)}) collective-permute-start(bf16[256,256]{1,0:T(8,128)(2,1)S(1)} %collective-permute-done.5.u1), channel_id=1, source_target_pairs={{0,8},{1,0},{2,10},{3,2},{4,12},{5,4},{6,14},{7,6},{8,16},{9,1},{1... | collective-permute-start | bytes 393224 | tf_op jit(solution)/shard_map/ppermute | solution.py:386
  21.6 0.7 %links.1 = s32[5,9]{1,0:T(8,128)S(4)} custom-call(s32[2,9]{1,0:T(2,128)S(1)} %copy-done.1, s32[2,9]{1,0:T(2,128)S(1)} %slice_convert_fusion.other, bf16[512,128]{1,0:T(8,128)(2,1)S(1)} %project_q.1.q), custom_call_target="tpu_custom_call" | custom-call | bytes 2097152 | tf_op jit(solution)/shard_map/links/pallas_call | solution.py:399
  22.3 1.2 %collective-permute-done.8.d2 = bf16[256,256]{1,0:T(8,128)(2,1)S(1)} collective-permute-done((bf16[256,256]{1,0:T(8,128)(2,1)S(1)}, bf16[256,256]{1,0:T(8,128)(2,1)S(1)}, u32[]{:S(2)}, u32[]{:S(2)}) %collective-permute-start.8) | collective-permute-done | bytes 131104 | tf_op jit(solution)/shard_map/ppermute | solution.py:386
  23.5 0.9 %near_scores.1 = (bf16[1024,256]{1,0:T(8,128)(2,1)S(1)}, f32[3072,128]{1,0:T(8,128)S(1)}, f32[3072,128]{1,0:T(8,128)S(1)}, f32[96,128]{1,0:T(8,128)S(1)}) custom-call(s32[5,9]{1,0:T(8,128)S(4)} %links.1, bf16[512,128]{1,0:T(8,128)(2,1)S(1)} %project_q.1.q, bf16[256,256]{1,0:T(8,128)(2,1)S(1)} %get-tuple-element.32.first_kv, ...), custom_call_target="tpu_custom_call" | custom-call | flops 301989888 | bytes 2097152 | tf_op jit(solution)/shard_map/near_scores/pallas_call | solution.py:399
  24.5 1.9 %collective-permute-done.10.d3 = bf16[256,256]{1,0:T(8,128)(2,1)S(1)} collective-permute-done((bf16[256,256]{1,0:T(8,128)(2,1)S(1)}, bf16[256,256]{1,0:T(8,128)(2,1)S(1)}, u32[]{:S(2)}, u32[]{:S(2)}) %collective-permute-start.10) | collective-permute-done | bytes 131104 | tf_op jit(solution)/shard_map/ppermute | solution.py:386
  26.4 1.3 %far_grads.1 = (bf16[1536,256]{1,0:T(8,128)(2,1)S(1)}, f32[1024,256]{1,0:T(8,128)S(1)}, bf16[256,256]{1,0:T(8,128)(2,1)S(1)}, bf16[256,256]{1,0:T(8,128)(2,1)S(1)}, f32[64,128]{1,0:T(8,128)S(1)}) custom-call(s32[5,9]{1,0:T(8,128)S(4)} %links.1, bf16[1024,256]{1,0:T(8,128)(2,1)S(1)} %get-tuple-element.34.pairs, f32[96,128]{1,0:T(8,128)S(1)} %get-tuple-element.37.stats, ...), custom_call_target="tpu_custom_call" | custom-call | flops 301989888 | bytes 2097152 | tf_op jit(solution)/shard_map/far_grads/pallas_call | solution.py:399
  27.7 2.0 %collective-permute-start.11 = (bf16[256,256]{1,0:T(8,128)(2,1)S(1)}, bf16[256,256]{1,0:T(8,128)(2,1)S(1)}, u32[]{:S(2)}, u32[]{:S(2)}) collective-permute-start(bf16[256,256]{1,0:T(8,128)(2,1)S(1)} %get-tuple-element.44), channel_id=1, source_target_pairs={{0,8},{1,0},{2,10},{3,2},{4,12},{5,4},{6,14},{7,6},{8,16},{9,1},{1... | collective-permute-start | bytes 393224 | tf_op jit(solution)/shard_map/ppermute | solution.py:386
  29.7 0.9 %near_grads.1 = (bf16[3072,256]{1,0:T(8,128)(2,1)S(1)}, f32[256,256]{1,0:T(8,128)S(1)}, f32[256,256]{1,0:T(8,128)S(1)}, bf16[512,256]{1,0:T(8,128)(2,1)S(1)}, bf16[512,256]{1,0:T(8,128)(2,1)S(1)}) custom-call(s32[5,9]{1,0:T(8,128)S(4)} %links.1, bf16[1024,256]{1,0:T(8,128)(2,1)S(1)} %get-tuple-element.34.pairs, f32[3072,128]{1,0:T(8,128)S(1)} %get-tuple-element.35.terms, ...), custom_call_target="tpu_custom_call" | custom-call | flops 301989888 | bytes 2097152 | tf_op jit(solution)/shard_map/near_grads/pallas_call | solution.py:399
  30.6 1.1 %outputs.1 = (bf16[256,128]{1,0:T(8,128)(2,1)S(1)}, bf16[256,128]{1,0:T(8,128)(2,1)S(1)}, bf16[512,128]{1,0:T(8,128)(2,1)S(1)}) custom-call(s32[5,9]{1,0:T(8,128)S(4)} %links.1, bf16[3072,256]{1,0:T(8,128)(2,1)S(1)} %get-tuple-element.40.near_mixed, bf16[1536,256]{1,0:T(8,128)(2,1)S(1)} %get-tuple-element.41.far_mixed, ...), custom_call_target="tpu_custom_call" | custom-call | flops 301989888 | bytes 2097152 | tf_op jit(solution)/shard_map/outputs/pallas_call | solution.py:399
  31.7 1.5 %collective-permute-done.13.part = bf16[256,256]{1,0:T(8,128)(2,1)S(1)} collective-permute-done((bf16[256,256]{1,0:T(8,128)(2,1)S(1)}, bf16[256,256]{1,0:T(8,128)(2,1)S(1)}, u32[]{:S(2)}, u32[]{:S(2)}) %collective-permute-start.13) | collective-permute-done | bytes 131104 | tf_op jit(solution)/shard_map/ppermute | solution.py:386
  33.3 2.0 %collective-permute-start.12 = (bf16[512,256]{1,0:T(8,128)(2,1)S(1)}, bf16[512,256]{1,0:T(8,128)(2,1)S(1)}, u32[]{:S(2)}, u32[]{:S(2)}) collective-permute-start(bf16[512,256]{1,0:T(8,128)(2,1)S(1)} %merge_u.1), channel_id=1, source_target_pairs={{0,8},{1,0},{2,10},{3,2},{4,12},{5,4},{6,14},{7,6},{8,16},{9,1},{1... | collective-permute-start | bytes 786440 | tf_op jit(solution)/shard_map/ppermute | solution.py:386
  35.3 2.4 %collective-permute-start.15 = (bf16[256,128]{1,0:T(8,128)(2,1)S(1)}, bf16[256,128]{1,0:T(8,128)(2,1)S(1)}, u32[]{:S(2)}, u32[]{:S(2)}) collective-permute-start(bf16[256,128]{1,0:T(8,128)(2,1)S(1)} %get-tuple-element.48), channel_id=1, source_target_pairs={{0,4},{1,5},{2,6},{3,7},{4,0},{5,1},{6,2},{7,3},{8,12},{9,13},{10,... | collective-permute-start | bytes 196616 | tf_op jit(solution)/shard_map/ppermute | solution.py:375
  37.7 2.2 %collective-permute-done.15.other = bf16[256,128]{1,0:T(8,128)(2,1)S(1)} collective-permute-done((bf16[256,128]{1,0:T(8,128)(2,1)S(1)}, bf16[256,128]{1,0:T(8,128)(2,1)S(1)}, u32[]{:S(2)}, u32[]{:S(2)}) %collective-permute-start.15) | collective-permute-done | bytes 65568 | tf_op jit(solution)/shard_map/ppermute | solution.py:375
  40.0 0.7 %collective-permute-done.14.from_d = bf16[512,256]{1,0:T(8,128)(2,1)S(1)} collective-permute-done((bf16[512,256]{1,0:T(8,128)(2,1)S(1)}, bf16[512,256]{1,0:T(8,128)(2,1)S(1)}, u32[]{:S(2)}, u32[]{:S(2)}) %collective-permute-start.14) | collective-permute-done | bytes 262176 | tf_op jit(solution)/shard_map/ppermute | solution.py:386
  40.7 0.5 spread_send.1
  41.7 1.4 %collective-permute-done.16 = bf16[1024,256]{1,0:T(8,128)(2,1)S(1)} collective-permute-done((bf16[1024,256]{1,0:T(8,128)(2,1)S(1)}, bf16[1024,256]{1,0:T(8,128)(2,1)S(1)}, u32[]{:S(2)}, u32[]{:S(2)}) %collective-permute-start.16) | collective-permute-done | bytes 524320 | tf_op jit(solution)/shard_map/ppermute | solution.py:375
  43.3 2.3 %collective-permute-start.17 = (bf16[256,256]{1,0:T(8,128)(2,1)S(1)}, bf16[256,256]{1,0:T(8,128)(2,1)S(1)}, u32[]{:S(2)}, u32[]{:S(2)}) collective-permute-start(bf16[256,256]{1,0:T(8,128)(2,1)S(1)} %get-tuple-element.56), channel_id=1, source_target_pairs={{0,6},{1,7},{2,4},{3,5},{4,2},{5,3},{6,0},{7,1},{8,14},{9,15},{10,... | collective-permute-start | bytes 393224 | tf_op jit(solution)/shard_map/ppermute | solution.py:375
  45.6 0.5 %collective-permute-start.19 = (bf16[256,256]{1,0:T(8,128)(2,1)S(1)}, bf16[256,256]{1,0:T(8,128)(2,1)S(1)}, u32[]{:S(2)}, u32[]{:S(2)}) collective-permute-start(bf16[256,256]{1,0:T(8,128)(2,1)S(1)} %get-tuple-element.57), channel_id=1, source_target_pairs={{0,2},{1,3},{2,0},{3,1},{4,6},{5,7},{6,4},{7,5},{8,10},{9,11},{10,... | collective-permute-start | bytes 393224 | tf_op jit(solution)/shard_map/ppermute | solution.py:375
  46.2 0.7 %collective-permute-start.18 = (bf16[256,256]{1,0:T(8,128)(2,1)S(1)}, bf16[256,256]{1,0:T(8,128)(2,1)S(1)}, u32[]{:S(2)}, u32[]{:S(2)}) collective-permute-start(bf16[256,256]{1,0:T(8,128)(2,1)S(1)} %get-tuple-element.58), channel_id=1, source_target_pairs={{0,4},{1,5},{2,6},{3,7},{4,0},{5,1},{6,2},{7,3},{8,12},{9,13},{10,... | collective-permute-start | bytes 393224 | tf_op jit(solution)/shard_map/ppermute | solution.py:375
  46.9 0.7 %lay_out.1 = bf16[256,256]{1,0:T(8,128)(2,1)} custom-call(bf16[256,128]{1,0:T(8,128)(2,1)S(1)} %get-tuple-element.42.own, bf16[256,128]{1,0:T(8,128)(2,1)S(1)} %collective-permute-done.15.other), custom_call_target="tpu_custom_call" | custom-call | bytes 2097152 | tf_op jit(solution)/shard_map/lay_out/pallas_call | solution.py:399
  47.5 3.1 %collective-permute-done.17 = bf16[256,256]{1,0:T(8,128)(2,1)S(1)} collective-permute-done((bf16[256,256]{1,0:T(8,128)(2,1)S(1)}, bf16[256,256]{1,0:T(8,128)(2,1)S(1)}, u32[]{:S(2)}, u32[]{:S(2)}) %collective-permute-start.17) | collective-permute-done | bytes 131104 | tf_op jit(solution)/shard_map/ppermute | solution.py:375
  50.6 1.9 %collective-permute-done.19 = bf16[256,256]{1,0:T(8,128)(2,1)S(1)} collective-permute-done((bf16[256,256]{1,0:T(8,128)(2,1)S(1)}, bf16[256,256]{1,0:T(8,128)(2,1)S(1)}, u32[]{:S(2)}, u32[]{:S(2)}) %collective-permute-start.19) | collective-permute-done | bytes 131104 | tf_op jit(solution)/shard_map/ppermute | solution.py:375
  52.6 0.7 %add_convert_fusion.1 = bf16[256,256]{1,0:T(8,128)(2,1)} fusion(bf16[256,256]{1,0:T(8,128)(2,1)S(1)} %collective-permute-done.19, bf16[256,256]{1,0:T(8,128)(2,1)S(1)} %collective-permute-done.18, bf16[256,256]{1,0:T(8,128)(2,1)S(1)} %collective-permute-done.17, bf16[1024,256]{1,0:T(8,128)(2,1)S(1)} %add_convert_fusion), kind=kLoop, calls=%fused_computation.1 | loop fusion | flops 524288 | bytes 655360 | tf_op jit(solution)/shard_map/convert_element_type | solution.py:529
  (34 shorter events, 2.7 us)
Async XLA Ops:
  0.6 8.9 %collective-permute-start = (bf16[256,256]{1,0:T(8,128)(2,1)}, bf16[256,256]{1,0:T(8,128)(2,1)S(1)}, u32[]{:S(2)}, u32[]{:S(2)}) collective-permute-start(bf16[256,256]{1,0:T(8,128)(2,1)} %f.1), channel_id=1, source_target_pairs={{0,4},{1,5},{2,6},{3,7},{4,0},{5,1},{6,2},{7,3},{8,12},{9,13},{10,... | collective-permute-start | bytes 393224 | tf_op jit(solution)/shard_map/ppermute | solution.py:375
  3.7 7.5 %collective-permute-start.2 = (bf16[256,256]{1,0:T(8,128)(2,1)}, bf16[256,256]{1,0:T(8,128)(2,1)S(1)}, u32[]{:S(2)}, u32[]{:S(2)}) collective-permute-start(bf16[256,256]{1,0:T(8,128)(2,1)} %f.1), channel_id=1, source_target_pairs={{0,6},{1,7},{2,4},{3,5},{4,2},{5,3},{6,0},{7,1},{8,14},{9,15},{10,... | collective-permute-start | bytes 393224 | tf_op jit(solution)/shard_map/ppermute | solution.py:375
  5.1 6.4 %collective-permute-start.1 = (bf16[256,256]{1,0:T(8,128)(2,1)}, bf16[256,256]{1,0:T(8,128)(2,1)S(1)}, u32[]{:S(2)}, u32[]{:S(2)}) collective-permute-start(bf16[256,256]{1,0:T(8,128)(2,1)} %f.1), channel_id=1, source_target_pairs={{0,2},{1,3},{2,0},{3,1},{4,6},{5,7},{6,4},{7,5},{8,10},{9,11},{10,... | collective-permute-start | bytes 393224 | tf_op jit(solution)/shard_map/ppermute | solution.py:375
  11.5 2.0 %collective-permute-start.4 = (bf16[1024,256]{1,0:T(8,128)(2,1)S(1)}, bf16[1024,256]{1,0:T(8,128)(2,1)S(1)}, u32[]{:S(2)}, u32[]{:S(2)}) collective-permute-start(bf16[1024,256]{1,0:T(8,128)(2,1)S(1)} %pack.1), channel_id=1, source_target_pairs={{0,1},{1,0},{2,3},{3,2},{4,5},{5,4},{6,7},{7,6},{8,9},{9,8},{10,11... | collective-permute-start | bytes 1572872 | tf_op jit(solution)/shard_map/ppermute | solution.py:375
  12.0 3.5 %copy-start.1 = (s32[2,9]{1,0:T(2,128)S(1)}, s32[2,9]{1,0:T(2,128)}, u32[]{:S(2)}) copy-start(s32[2,9]{1,0:T(2,128)} %own.1) | copy-start | bytes 220
  12.0 3.6 %copy-start = (bf16[256,256]{1,0:T(8,128)(2,1)S(1)}, bf16[256,256]{1,0:T(8,128)(2,1)}, u32[]{:S(2)}) copy-start(bf16[256,256]{1,0:T(8,128)(2,1)} %d_own.3) | copy-start | bytes 393220
  13.8 5.4 %collective-permute-start.5 = (bf16[256,256]{1,0:T(8,128)(2,1)S(1)}, bf16[256,256]{1,0:T(8,128)(2,1)S(1)}, u32[]{:S(2)}, u32[]{:S(2)}) collective-permute-start(bf16[256,256]{1,0:T(8,128)(2,1)S(1)} %get-tuple-element.32.first_kv), channel_id=1, source_target_pairs={{0,8},{1,0},{2,10},{3,2},{4,12},{5,4},{6,14},{7,6},{8,16},{9,1},{1... | collective-permute-start | bytes 393224 | tf_op jit(solution)/shard_map/ppermute | solution.py:386
  15.5 5.7 %collective-permute-start.6 = (bf16[256,256]{1,0:T(8,128)(2,1)S(1)}, bf16[256,256]{1,0:T(8,128)(2,1)S(1)}, u32[]{:S(2)}, u32[]{:S(2)}) collective-permute-start(bf16[256,256]{1,0:T(8,128)(2,1)S(1)} %get-tuple-element.33.second_kv), channel_id=1, source_target_pairs={{0,1},{1,9},{2,3},{3,11},{4,5},{5,13},{6,7},{7,15},{8,0},{9,17},{1... | collective-permute-start | bytes 393224 | tf_op jit(solution)/shard_map/ppermute | solution.py:386
  15.6 5.6 %collective-permute-start.3 = (bf16[272,128]{1,0:T(8,128)(2,1)S(1)}, bf16[272,128]{1,0:T(8,128)(2,1)S(1)}, u32[]{:S(2)}, u32[]{:S(2)}) collective-permute-start(bf16[272,128]{1,0:T(8,128)(2,1)S(1)} %payload.1), channel_id=1, source_target_pairs={{0,4},{1,5},{2,6},{3,7},{4,0},{5,1},{6,2},{7,3},{8,12},{9,13},{10,... | collective-permute-start | bytes 208904 | tf_op jit(solution)/shard_map/ppermute | solution.py:375
  17.2 6.3 %collective-permute-start.8 = (bf16[256,256]{1,0:T(8,128)(2,1)S(1)}, bf16[256,256]{1,0:T(8,128)(2,1)S(1)}, u32[]{:S(2)}, u32[]{:S(2)}) collective-permute-start(bf16[256,256]{1,0:T(8,128)(2,1)S(1)} %get-tuple-element.32.first_kv), channel_id=1, source_target_pairs={{0,1},{1,9},{2,3},{3,11},{4,5},{5,13},{6,7},{7,15},{8,0},{9,17},{1... | collective-permute-start | bytes 393224 | tf_op jit(solution)/shard_map/ppermute | solution.py:386
  17.2 6.3 %collective-permute-start.7 = (bf16[256,256]{1,0:T(8,128)(2,1)S(1)}, bf16[256,256]{1,0:T(8,128)(2,1)S(1)}, u32[]{:S(2)}, u32[]{:S(2)}) collective-permute-start(bf16[256,256]{1,0:T(8,128)(2,1)S(1)} %get-tuple-element.33.second_kv), channel_id=1, source_target_pairs={{0,8},{1,0},{2,10},{3,2},{4,12},{5,4},{6,14},{7,6},{8,16},{9,1},{1... | collective-permute-start | bytes 393224 | tf_op jit(solution)/shard_map/ppermute | solution.py:386
  19.2 5.3 %collective-permute-start.9 = (bf16[256,256]{1,0:T(8,128)(2,1)S(1)}, bf16[256,256]{1,0:T(8,128)(2,1)S(1)}, u32[]{:S(2)}, u32[]{:S(2)}) collective-permute-start(bf16[256,256]{1,0:T(8,128)(2,1)S(1)} %collective-permute-done.5.u1), channel_id=1, source_target_pairs={{0,8},{1,0},{2,10},{3,2},{4,12},{5,4},{6,14},{7,6},{8,16},{9,1},{1... | collective-permute-start | bytes 393224 | tf_op jit(solution)/shard_map/ppermute | solution.py:386
  21.2 5.1 %collective-permute-start.10 = (bf16[256,256]{1,0:T(8,128)(2,1)S(1)}, bf16[256,256]{1,0:T(8,128)(2,1)S(1)}, u32[]{:S(2)}, u32[]{:S(2)}) collective-permute-start(bf16[256,256]{1,0:T(8,128)(2,1)S(1)} %collective-permute-done.6.d1), channel_id=1, source_target_pairs={{0,1},{1,9},{2,3},{3,11},{4,5},{5,13},{6,7},{7,15},{8,0},{9,17},{1... | collective-permute-start | bytes 393224 | tf_op jit(solution)/shard_map/ppermute | solution.py:386
  27.7 5.5 %collective-permute-start.13 = (bf16[256,256]{1,0:T(8,128)(2,1)S(1)}, bf16[256,256]{1,0:T(8,128)(2,1)S(1)}, u32[]{:S(2)}, u32[]{:S(2)}) collective-permute-start(bf16[256,256]{1,0:T(8,128)(2,1)S(1)} %get-tuple-element.47), channel_id=1, source_target_pairs={{0,1},{1,9},{2,3},{3,11},{4,5},{5,13},{6,7},{7,15},{8,0},{9,17},{1... | collective-permute-start | bytes 393224 | tf_op jit(solution)/shard_map/ppermute | solution.py:386
  27.7 5.5 %collective-permute-start.11 = (bf16[256,256]{1,0:T(8,128)(2,1)S(1)}, bf16[256,256]{1,0:T(8,128)(2,1)S(1)}, u32[]{:S(2)}, u32[]{:S(2)}) collective-permute-start(bf16[256,256]{1,0:T(8,128)(2,1)S(1)} %get-tuple-element.44), channel_id=1, source_target_pairs={{0,8},{1,0},{2,10},{3,2},{4,12},{5,4},{6,14},{7,6},{8,16},{9,1},{1... | collective-permute-start | bytes 393224 | tf_op jit(solution)/shard_map/ppermute | solution.py:386
  33.2 7.5 %collective-permute-start.14 = (bf16[512,256]{1,0:T(8,128)(2,1)S(1)}, bf16[512,256]{1,0:T(8,128)(2,1)S(1)}, u32[]{:S(2)}, u32[]{:S(2)}) collective-permute-start(bf16[512,256]{1,0:T(8,128)(2,1)S(1)} %merge_d.1), channel_id=1, source_target_pairs={{0,1},{1,9},{2,3},{3,11},{4,5},{5,13},{6,7},{7,15},{8,0},{9,17},{1... | collective-permute-start | bytes 786440 | tf_op jit(solution)/shard_map/ppermute | solution.py:386
  33.3 7.4 %collective-permute-start.12 = (bf16[512,256]{1,0:T(8,128)(2,1)S(1)}, bf16[512,256]{1,0:T(8,128)(2,1)S(1)}, u32[]{:S(2)}, u32[]{:S(2)}) collective-permute-start(bf16[512,256]{1,0:T(8,128)(2,1)S(1)} %merge_u.1), channel_id=1, source_target_pairs={{0,8},{1,0},{2,10},{3,2},{4,12},{5,4},{6,14},{7,6},{8,16},{9,1},{1... | collective-permute-start | bytes 786440 | tf_op jit(solution)/shard_map/ppermute | solution.py:386
  35.3 4.7 %collective-permute-start.15 = (bf16[256,128]{1,0:T(8,128)(2,1)S(1)}, bf16[256,128]{1,0:T(8,128)(2,1)S(1)}, u32[]{:S(2)}, u32[]{:S(2)}) collective-permute-start(bf16[256,128]{1,0:T(8,128)(2,1)S(1)} %get-tuple-element.48), channel_id=1, source_target_pairs={{0,4},{1,5},{2,6},{3,7},{4,0},{5,1},{6,2},{7,3},{8,12},{9,13},{10,... | collective-permute-start | bytes 196616 | tf_op jit(solution)/shard_map/ppermute | solution.py:375
  41.2 2.0 %collective-permute-start.16 = (bf16[1024,256]{1,0:T(8,128)(2,1)S(1)}, bf16[1024,256]{1,0:T(8,128)(2,1)S(1)}, u32[]{:S(2)}, u32[]{:S(2)}) collective-permute-start(bf16[1024,256]{1,0:T(8,128)(2,1)S(1)} %get-tuple-element.55), channel_id=1, source_target_pairs={{0,1},{1,0},{2,3},{3,2},{4,5},{5,4},{6,7},{7,6},{8,9},{9,8},{10,11... | collective-permute-start | bytes 1572872 | tf_op jit(solution)/shard_map/ppermute | solution.py:375
  43.3 7.3 %collective-permute-start.17 = (bf16[256,256]{1,0:T(8,128)(2,1)S(1)}, bf16[256,256]{1,0:T(8,128)(2,1)S(1)}, u32[]{:S(2)}, u32[]{:S(2)}) collective-permute-start(bf16[256,256]{1,0:T(8,128)(2,1)S(1)} %get-tuple-element.56), channel_id=1, source_target_pairs={{0,6},{1,7},{2,4},{3,5},{4,2},{5,3},{6,0},{7,1},{8,14},{9,15},{10,... | collective-permute-start | bytes 393224 | tf_op jit(solution)/shard_map/ppermute | solution.py:375
  45.6 6.9 %collective-permute-start.19 = (bf16[256,256]{1,0:T(8,128)(2,1)S(1)}, bf16[256,256]{1,0:T(8,128)(2,1)S(1)}, u32[]{:S(2)}, u32[]{:S(2)}) collective-permute-start(bf16[256,256]{1,0:T(8,128)(2,1)S(1)} %get-tuple-element.57), channel_id=1, source_target_pairs={{0,2},{1,3},{2,0},{3,1},{4,6},{5,7},{6,4},{7,5},{8,10},{9,11},{10,... | collective-permute-start | bytes 393224 | tf_op jit(solution)/shard_map/ppermute | solution.py:375
  46.2 6.4 %collective-permute-start.18 = (bf16[256,256]{1,0:T(8,128)(2,1)S(1)}, bf16[256,256]{1,0:T(8,128)(2,1)S(1)}, u32[]{:S(2)}, u32[]{:S(2)}) collective-permute-start(bf16[256,256]{1,0:T(8,128)(2,1)S(1)} %get-tuple-element.58), channel_id=1, source_target_pairs={{0,4},{1,5},{2,6},{3,7},{4,0},{5,1},{6,2},{7,3},{8,12},{9,13},{10,... | collective-permute-start | bytes 393224 | tf_op jit(solution)/shard_map/ppermute | solution.py:375

commit v9 on v8

--- a/solution.py
+++ b/solution.py
@@ -63,7 +63,7 @@
     return w_mine[pl.ds(pl.multiple_of(source * width, width), width), :]
 
 
-def pack_kernel(fm, sy, sx, sd, out):
+def pack_kernel(fm, sd, sx, sy, out):
     for index, piece in enumerate((fm, sy, sx, sd)):
         out[index * HALF : (index + 1) * HALF, :] = piece[...]
 
@@ -138,7 +138,7 @@
             for j in range(SPAN):
                 entry = links[i, SPAN * t + j]
                 base = jnp.maximum(base, jnp.where(entry >= 0, entry - j, -(1 << 20)))
-            base = jnp.where(base > -(1 << 19), base - first + REACH, REACH + i)
+            base = jnp.where(base > -(1 << 19), base - first + REACH, i + 1 if t == 1 else i + REACH + SPAN)
             links[GROUP, 2 * i + t - 1] = jnp.clip(base, 0, WINDOW - SPAN) * BLK
 
 
@@ -261,43 +261,50 @@
 
 def far_grads_kernel(
     links, pairs, stats, u1, d1, u2, u3, d2, d3,
-    mixed, near_acc, far_u_out, far_d_out, scales, win, acc,
+    mixed, edges, far_u_out, far_d_out, scales, win,
 ):
     places = regions(position()[1])
     for at, half in zip(places[2:], (u1, d1, u2, u3, d2, d3)):
         win[pl.ds(at, HALF), :] = half[...]
-    acc[:OWN, :] = jnp.zeros((OWN, 2 * HD), F32)
-    acc[NEAR_RIGHT:, :] = jnp.zeros((OWN, 2 * HD), F32)
-    for i in range(GROUP):
-        pair = pairs[2 * i * BLK : 2 * (i + 1) * BLK, :]
-        at = pl.ds(start_of(links, i, far_run(i)), SPAN * BLK)
-        blocks = run_scores(links, win[at, :], pair, i, far_run(i))
-        near_largest, near_total, near_weighted = (stats[8 * (3 * i + n) : 8 * (3 * i + n) + 1, :] for n in range(3))
-        largest = jnp.maximum(near_largest, largest_of(blocks))
-        terms, total, weighted = exponentials(blocks, largest)
-        near_scale = jnp.exp2((near_largest - largest) * (HD ** -0.5 * LOG2E))
-        inverse = 1.0 / (total + near_scale * near_total)
-        row_dot = (weighted + near_scale * near_weighted) * inverse
+    edges[...] = jnp.zeros_like(edges)
+    scale = HD ** -0.5 * LOG2E
+    span = range(GROUP)
+    starts = [start_of(links, i, far_run(i)) for i in span]
+    pair = [pairs[2 * i * BLK : 2 * (i + 1) * BLK, :] for i in span]
+    near = [[stats[8 * (3 * i + n) : 8 * (3 * i + n) + 1, :] for n in range(3)] for i in span]
+    blocks = [
+        run_scores(links, win[pl.ds(starts[i], SPAN * BLK), :], pair[i], i, far_run(i)) for i in span
+    ]
+    largest = [jnp.maximum(near[i][0], largest_of(blocks[i])) for i in span]
+    found = [exponentials(blocks[i], largest[i]) for i in span]
+    parts = []
+    for i in span:
+        terms, total, weighted = found[i]
+        near_scale = jnp.exp2((near[i][0] - largest[i]) * scale)
+        inverse = 1.0 / (total + near_scale * near[i][1])
+        row_dot = (weighted + near_scale * near[i][2]) * inverse
         for n, row in enumerate((near_scale * inverse, row_dot)):
             scales[8 * (2 * i + n) : 8 * (2 * i + n + 1), :] = jnp.broadcast_to(row, (8, BLK))
-        part = jnp.concatenate(
-            [mix(term * inverse, block[1], row_dot) for term, block in zip(terms, blocks)], axis=0
+        parts.append(
+            jnp.concatenate([mix(term * inverse, block[1], row_dot) for term, block in zip(terms, blocks[i])], axis=0)
         )
-        mixed[far_rows(i), :] = part
-        acc[at, :] += dot(part, pair, ((1,), (0,)))
+    for i in span:
+        mixed[far_rows(i), :] = parts[i]
+        at = starts[i] if i < GROUP // 2 else starts[i] - ROWS
+        edges[pl.ds(pl.multiple_of(at, BLK), SPAN * BLK), :] += dot(parts[i], pair[i], ((1,), (0,)))
     factor = side_factor()
-    far_u_out[...] = (acc[pl.ds(places[7], HALF), :] * factor).astype(BF)
-    far_d_out[...] = (acc[pl.ds(places[5], HALF), :] * factor).astype(BF)
-    near_acc[:ROWS, :] = acc[NEAR_LEFT:OWN, :]
-    near_acc[ROWS:, :] = acc[NEAR_RIGHT:FAR_RIGHT, :]
+    flip = position()[1]
+    for target, left in ((far_u_out, flip), (far_d_out, 1 - flip)):
+        at = pl.multiple_of((1 - left) * (2 * OWN - HALF), HALF)
+        target[...] = (edges[pl.ds(at, HALF), :] * factor).astype(BF)
 
 
 def near_grads_kernel(
-    links, pairs, terms, prob_grads, scales, near_acc, mixed, first_own, second_own, u_out, d_out, acc
+    links, pairs, terms, prob_grads, scales, edges, mixed, first_own, second_own, u_out, d_out, acc
 ):
-    acc[NEAR_LEFT:OWN, :] = near_acc[:ROWS, :]
+    acc[NEAR_LEFT:OWN, :] = edges[NEAR_LEFT:OWN, :]
     acc[OWN:NEAR_RIGHT, :] = jnp.zeros((ROWS, 2 * HD), F32)
-    acc[NEAR_RIGHT:FAR_RIGHT, :] = near_acc[ROWS:, :]
+    acc[NEAR_RIGHT:FAR_RIGHT, :] = edges[OWN : OWN + ROWS, :]
     for i in range(GROUP):
         pair = pairs[2 * i * BLK : 2 * (i + 1) * BLK, :]
         scale, row_dot = (scales[8 * (2 * i + n) : 8 * (2 * i + n) + 1, :] for n in range(2))
@@ -423,7 +430,7 @@
         product,
         [pltpu.SemaphoreType.DMA((4,))],
     )
-    (pack,) = call(pack_kernel, "pack", [out(4 * HALF, f.shape[1])], (fm, sy, sx, sd), 4, 0)
+    (pack,) = call(pack_kernel, "pack", [out(4 * HALF, f.shape[1])], (fm, sd, sx, sy), 4, 0)
     other = across(pack, 0, 1)
     (total,) = call(
         project_across_kernel, "project_across", [held(ROWS, 3 * HD, F32)], (pack, total, w_mine), 4, product
@@ -465,12 +472,12 @@
         attention,
         [window],
     )
-    far_mixed, near_acc, far_u_grad, far_d_grad, scales = call(
+    far_mixed, edges, far_u_grad, far_d_grad, scales = call(
         far_grads_kernel,
         "far_grads",
         [
             held(GROUP * run, 2 * HD),
-            held(2 * ROWS, 2 * HD, F32),
+            held(2 * OWN, 2 * HD, F32),
             out(HALF, 2 * HD),
             out(HALF, 2 * HD),
             held(GROUP * 2 * 8, BLK, F32),
@@ -478,13 +485,13 @@
         (links, pairs, stats, u1, d1, u2, u3, d2, d3),
         6,
         attention,
-        [window, sums],
+        [window],
     )
     near_mixed, first_own, second_own, u_grad, d_grad = call(
         near_grads_kernel,
         "near_grads",
         [held(GROUP * 2 * run, 2 * HD)] + [held(HALF, 2 * HD, F32)] * 2 + [out(ROWS, 2 * HD)] * 2,
-        (links, pairs, terms, prob_grads, scales, near_acc),
+        (links, pairs, terms, prob_grads, scales, edges),
         4,
         attention,
         [sums],

time: 53.5 us -> 52.9 us (0.989)
  no operation moved by 1% of the time
where the time goes in v9:
time: 52.9 us; the launch traced here: 52.8 us
  starting transfers between devices  22.1 us (42%)
  waiting for transfers between devices  20.1 us (38%)
  Pallas kernels  8.8 us (17%)
  other arithmetic  0.87 us (2%)
  between operations  0.84 us (2%)
    ppermute x10, waiting for transfers between devices, across(): return lax.ppermute(value, ('ctx', 'head'), pairs)  14.9 us
    ppermute x10, starting transfers between devices, across(): return lax.ppermute(value, ('ctx', 'head'), pairs)  12.2 us
    ppermute x10, starting transfers between devices, chain(): return lax.ppermute(value, ('ctx', 'head'), pairs)  9.9 us
    pallas_call x16, Pallas kernels, call(): pl.pallas_call(kernel, name=name, out_shape=outs, in_specs=specs, out_spe...  8.8 us
    ppermute x10, waiting for transfers between devices, chain(): return lax.ppermute(value, ('ctx', 'head'), pairs)  5.19 us
  transfers between devices with their start and end apart: 20, of which 14 were waited for; matrix products, arithmetic and copies ran while one was open for 0% of the time, Pallas kernels for 13%

profile of v9, /device:TPU:0, one launch (start us, length us, event | category | flops | bytes accessed | tf_op | source)
XLA Modules:
  0.0 52.8 jit_solution(3178040832212931757)
XLA Ops:
  0.6 4.0 %collective-permute-start = (bf16[256,256]{1,0:T(8,128)(2,1)}, bf16[256,256]{1,0:T(8,128)(2,1)S(1)}, u32[]{:S(2)}, u32[]{:S(2)}) collective-permute-start(bf16[256,256]{1,0:T(8,128)(2,1)} %f.1), channel_id=1, source_target_pairs={{0,6},{1,7},{2,4},{3,5},{4,2},{5,3},{6,0},{7,1},{8,14},{9,15},{10,... | collective-permute-start | bytes 393224 | tf_op jit(solution)/shard_map/ppermute | solution.py:382
  4.6 0.5 collective-permute-start.2
  5.2 1.4 %begin.1 = (bf16[1024,384]{1,0:T(8,128)(2,1)S(1)}, bf16[256,256]{1,0:T(8,128)(2,1)S(1)}, f32[256,384]{1,0:T(8,128)S(1)}) custom-call(bf16[256,256]{1,0:T(8,128)(2,1)} %f.1, bf16[3,1024,256]{2,1,0:T(8,128)(2,1)} %bitcast.1), custom_call_target="tpu_custom_call" | custom-call | flops 100663296 | bytes 2097152 | tf_op jit(solution)/shard_map/begin/pallas_call | solution.py:406
  6.7 2.1 %collective-permute-done.sd = bf16[256,256]{1,0:T(8,128)(2,1)S(1)} collective-permute-done((bf16[256,256]{1,0:T(8,128)(2,1)}, bf16[256,256]{1,0:T(8,128)(2,1)S(1)}, u32[]{:S(2)}, u32[]{:S(2)}) %collective-permute-start) | collective-permute-done | bytes 131104 | tf_op jit(solution)/shard_map/ppermute | solution.py:382
  8.8 2.3 %collective-permute-done.2.sy = bf16[256,256]{1,0:T(8,128)(2,1)S(1)} collective-permute-done((bf16[256,256]{1,0:T(8,128)(2,1)}, bf16[256,256]{1,0:T(8,128)(2,1)S(1)}, u32[]{:S(2)}, u32[]{:S(2)}) %collective-permute-start.2) | collective-permute-done | bytes 131104 | tf_op jit(solution)/shard_map/ppermute | solution.py:382
  11.9 1.5 %collective-permute-done.4.other = bf16[1024,256]{1,0:T(8,128)(2,1)S(1)} collective-permute-done((bf16[1024,256]{1,0:T(8,128)(2,1)S(1)}, bf16[1024,256]{1,0:T(8,128)(2,1)S(1)}, u32[]{:S(2)}, u32[]{:S(2)}) %collective-permute-start.4) | collective-permute-done | bytes 524320 | tf_op jit(solution)/shard_map/ppermute | solution.py:382
  13.7 1.6 %collective-permute-start.5 = (bf16[256,256]{1,0:T(8,128)(2,1)S(1)}, bf16[256,256]{1,0:T(8,128)(2,1)S(1)}, u32[]{:S(2)}, u32[]{:S(2)}) collective-permute-start(bf16[256,256]{1,0:T(8,128)(2,1)S(1)} %get-tuple-element.32.first_kv), channel_id=1, source_target_pairs={{0,8},{1,0},{2,10},{3,2},{4,12},{5,4},{6,14},{7,6},{8,16},{9,1},{1... | collective-permute-start | bytes 393224 | tf_op jit(solution)/shard_map/ppermute | solution.py:393
  15.3 1.5 %collective-permute-start.3 = (bf16[272,128]{1,0:T(8,128)(2,1)S(1)}, bf16[272,128]{1,0:T(8,128)(2,1)S(1)}, u32[]{:S(2)}, u32[]{:S(2)}) collective-permute-start(bf16[272,128]{1,0:T(8,128)(2,1)S(1)} %payload.1), channel_id=1, source_target_pairs={{0,4},{1,5},{2,6},{3,7},{4,0},{5,1},{6,2},{7,3},{8,12},{9,13},{10,... | collective-permute-start | bytes 208904 | tf_op jit(solution)/shard_map/ppermute | solution.py:382
  16.9 2.0 %collective-permute-start.7 = (bf16[256,256]{1,0:T(8,128)(2,1)S(1)}, bf16[256,256]{1,0:T(8,128)(2,1)S(1)}, u32[]{:S(2)}, u32[]{:S(2)}) collective-permute-start(bf16[256,256]{1,0:T(8,128)(2,1)S(1)} %get-tuple-element.33.second_kv), channel_id=1, source_target_pairs={{0,8},{1,0},{2,10},{3,2},{4,12},{5,4},{6,14},{7,6},{8,16},{9,1},{1... | collective-permute-start | bytes 393224 | tf_op jit(solution)/shard_map/ppermute | solution.py:393
  18.9 2.2 %collective-permute-start.9 = (bf16[256,256]{1,0:T(8,128)(2,1)S(1)}, bf16[256,256]{1,0:T(8,128)(2,1)S(1)}, u32[]{:S(2)}, u32[]{:S(2)}) collective-permute-start(bf16[256,256]{1,0:T(8,128)(2,1)S(1)} %collective-permute-done.5.u1), channel_id=1, source_target_pairs={{0,8},{1,0},{2,10},{3,2},{4,12},{5,4},{6,14},{7,6},{8,16},{9,1},{1... | collective-permute-start | bytes 393224 | tf_op jit(solution)/shard_map/ppermute | solution.py:393
  21.4 0.7 %links.1 = s32[5,9]{1,0:T(8,128)S(4)} custom-call(s32[2,9]{1,0:T(2,128)S(1)} %copy-done.1, s32[2,9]{1,0:T(2,128)S(1)} %slice_convert_fusion.other, bf16[512,128]{1,0:T(8,128)(2,1)S(1)} %project_q.1.q), custom_call_target="tpu_custom_call" | custom-call | bytes 2097152 | tf_op jit(solution)/shard_map/links/pallas_call | solution.py:406
  22.2 1.0 %collective-permute-done.8.d2 = bf16[256,256]{1,0:T(8,128)(2,1)S(1)} collective-permute-done((bf16[256,256]{1,0:T(8,128)(2,1)S(1)}, bf16[256,256]{1,0:T(8,128)(2,1)S(1)}, u32[]{:S(2)}, u32[]{:S(2)}) %collective-permute-start.8) | collective-permute-done | bytes 131104 | tf_op jit(solution)/shard_map/ppermute | solution.py:393
  23.2 0.9 %near_scores.1 = (bf16[1024,256]{1,0:T(8,128)(2,1)S(1)}, f32[3072,128]{1,0:T(8,128)S(1)}, f32[3072,128]{1,0:T(8,128)S(1)}, f32[96,128]{1,0:T(8,128)S(1)}) custom-call(s32[5,9]{1,0:T(8,128)S(4)} %links.1, bf16[512,128]{1,0:T(8,128)(2,1)S(1)} %project_q.1.q, bf16[256,256]{1,0:T(8,128)(2,1)S(1)} %get-tuple-element.32.first_kv, ...), custom_call_target="tpu_custom_call" | custom-call | flops 301989888 | bytes 2097152 | tf_op jit(solution)/shard_map/near_scores/pallas_call | solution.py:406
  24.2 1.9 %collective-permute-done.10.d3 = bf16[256,256]{1,0:T(8,128)(2,1)S(1)} collective-permute-done((bf16[256,256]{1,0:T(8,128)(2,1)S(1)}, bf16[256,256]{1,0:T(8,128)(2,1)S(1)}, u32[]{:S(2)}, u32[]{:S(2)}) %collective-permute-start.10) | collective-permute-done | bytes 131104 | tf_op jit(solution)/shard_map/ppermute | solution.py:393
  26.1 1.1 %far_grads.1 = (bf16[1536,256]{1,0:T(8,128)(2,1)S(1)}, f32[1536,256]{1,0:T(8,128)S(1)}, bf16[256,256]{1,0:T(8,128)(2,1)S(1)}, bf16[256,256]{1,0:T(8,128)(2,1)S(1)}, f32[64,128]{1,0:T(8,128)S(1)}) custom-call(s32[5,9]{1,0:T(8,128)S(4)} %links.1, bf16[1024,256]{1,0:T(8,128)(2,1)S(1)} %get-tuple-element.34.pairs, f32[96,128]{1,0:T(8,128)S(1)} %get-tuple-element.37.stats, ...), custom_call_target="tpu_custom_call" | custom-call | flops 301989888 | bytes 2097152 | tf_op jit(solution)/shard_map/far_grads/pallas_call | solution.py:406
  27.2 2.0 %collective-permute-start.11 = (bf16[256,256]{1,0:T(8,128)(2,1)S(1)}, bf16[256,256]{1,0:T(8,128)(2,1)S(1)}, u32[]{:S(2)}, u32[]{:S(2)}) collective-permute-start(bf16[256,256]{1,0:T(8,128)(2,1)S(1)} %get-tuple-element.44), channel_id=1, source_target_pairs={{0,8},{1,0},{2,10},{3,2},{4,12},{5,4},{6,14},{7,6},{8,16},{9,1},{1... | collective-permute-start | bytes 393224 | tf_op jit(solution)/shard_map/ppermute | solution.py:393
  29.2 0.9 %near_grads.1 = (bf16[3072,256]{1,0:T(8,128)(2,1)S(1)}, f32[256,256]{1,0:T(8,128)S(1)}, f32[256,256]{1,0:T(8,128)S(1)}, bf16[512,256]{1,0:T(8,128)(2,1)S(1)}, bf16[512,256]{1,0:T(8,128)(2,1)S(1)}) custom-call(s32[5,9]{1,0:T(8,128)S(4)} %links.1, bf16[1024,256]{1,0:T(8,128)(2,1)S(1)} %get-tuple-element.34.pairs, f32[3072,128]{1,0:T(8,128)S(1)} %get-tuple-element.35.terms, ...), custom_call_target="tpu_custom_call" | custom-call | flops 301989888 | bytes 2097152 | tf_op jit(solution)/shard_map/near_grads/pallas_call | solution.py:406
  30.1 1.1 %outputs.1 = (bf16[256,128]{1,0:T(8,128)(2,1)S(1)}, bf16[256,128]{1,0:T(8,128)(2,1)S(1)}, bf16[512,128]{1,0:T(8,128)(2,1)S(1)}) custom-call(s32[5,9]{1,0:T(8,128)S(4)} %links.1, bf16[3072,256]{1,0:T(8,128)(2,1)S(1)} %get-tuple-element.40.near_mixed, bf16[1536,256]{1,0:T(8,128)(2,1)S(1)} %get-tuple-element.41.far_mixed, ...), custom_call_target="tpu_custom_call" | custom-call | flops 301989888 | bytes 2097152 | tf_op jit(solution)/shard_map/outputs/pallas_call | solution.py:406
  31.2 1.5 %collective-permute-done.13.part = bf16[256,256]{1,0:T(8,128)(2,1)S(1)} collective-permute-done((bf16[256,256]{1,0:T(8,128)(2,1)S(1)}, bf16[256,256]{1,0:T(8,128)(2,1)S(1)}, u32[]{:S(2)}, u32[]{:S(2)}) %collective-permute-start.13) | collective-permute-done | bytes 131104 | tf_op jit(solution)/shard_map/ppermute | solution.py:393
  32.7 2.0 %collective-permute-start.12 = (bf16[512,256]{1,0:T(8,128)(2,1)S(1)}, bf16[512,256]{1,0:T(8,128)(2,1)S(1)}, u32[]{:S(2)}, u32[]{:S(2)}) collective-permute-start(bf16[512,256]{1,0:T(8,128)(2,1)S(1)} %merge_u.1), channel_id=1, source_target_pairs={{0,8},{1,0},{2,10},{3,2},{4,12},{5,4},{6,14},{7,6},{8,16},{9,1},{1... | collective-permute-start | bytes 786440 | tf_op jit(solution)/shard_map/ppermute | solution.py:393
  34.8 2.4 %collective-permute-start.15 = (bf16[256,128]{1,0:T(8,128)(2,1)S(1)}, bf16[256,128]{1,0:T(8,128)(2,1)S(1)}, u32[]{:S(2)}, u32[]{:S(2)}) collective-permute-start(bf16[256,128]{1,0:T(8,128)(2,1)S(1)} %get-tuple-element.48), channel_id=1, source_target_pairs={{0,4},{1,5},{2,6},{3,7},{4,0},{5,1},{6,2},{7,3},{8,12},{9,13},{10,... | collective-permute-start | bytes 196616 | tf_op jit(solution)/shard_map/ppermute | solution.py:382
  37.2 2.2 %collective-permute-done.15.other = bf16[256,128]{1,0:T(8,128)(2,1)S(1)} collective-permute-done((bf16[256,128]{1,0:T(8,128)(2,1)S(1)}, bf16[256,128]{1,0:T(8,128)(2,1)S(1)}, u32[]{:S(2)}, u32[]{:S(2)}) %collective-permute-start.15) | collective-permute-done | bytes 65568 | tf_op jit(solution)/shard_map/ppermute | solution.py:382
  39.4 0.7 %collective-permute-done.14.from_d = bf16[512,256]{1,0:T(8,128)(2,1)S(1)} collective-permute-done((bf16[512,256]{1,0:T(8,128)(2,1)S(1)}, bf16[512,256]{1,0:T(8,128)(2,1)S(1)}, u32[]{:S(2)}, u32[]{:S(2)}) %collective-permute-start.14) | collective-permute-done | bytes 262176 | tf_op jit(solution)/shard_map/ppermute | solution.py:393
  40.1 0.5 spread_send.1
  41.2 1.4 %collective-permute-done.16 = bf16[1024,256]{1,0:T(8,128)(2,1)S(1)} collective-permute-done((bf16[1024,256]{1,0:T(8,128)(2,1)S(1)}, bf16[1024,256]{1,0:T(8,128)(2,1)S(1)}, u32[]{:S(2)}, u32[]{:S(2)}) %collective-permute-start.16) | collective-permute-done | bytes 524320 | tf_op jit(solution)/shard_map/ppermute | solution.py:382
  42.7 1.5 %collective-permute-start.17 = (bf16[256,256]{1,0:T(8,128)(2,1)S(1)}, bf16[256,256]{1,0:T(8,128)(2,1)S(1)}, u32[]{:S(2)}, u32[]{:S(2)}) collective-permute-start(bf16[256,256]{1,0:T(8,128)(2,1)S(1)} %get-tuple-element.56), channel_id=1, source_target_pairs={{0,6},{1,7},{2,4},{3,5},{4,2},{5,3},{6,0},{7,1},{8,14},{9,15},{10,... | collective-permute-start | bytes 393224 | tf_op jit(solution)/shard_map/ppermute | solution.py:382
  44.2 1.4 %collective-permute-start.19 = (bf16[256,256]{1,0:T(8,128)(2,1)S(1)}, bf16[256,256]{1,0:T(8,128)(2,1)S(1)}, u32[]{:S(2)}, u32[]{:S(2)}) collective-permute-start(bf16[256,256]{1,0:T(8,128)(2,1)S(1)} %get-tuple-element.57), channel_id=1, source_target_pairs={{0,2},{1,3},{2,0},{3,1},{4,6},{5,7},{6,4},{7,5},{8,10},{9,11},{10,... | collective-permute-start | bytes 393224 | tf_op jit(solution)/shard_map/ppermute | solution.py:382
  45.6 0.7 %collective-permute-start.18 = (bf16[256,256]{1,0:T(8,128)(2,1)S(1)}, bf16[256,256]{1,0:T(8,128)(2,1)S(1)}, u32[]{:S(2)}, u32[]{:S(2)}) collective-permute-start(bf16[256,256]{1,0:T(8,128)(2,1)S(1)} %get-tuple-element.58), channel_id=1, source_target_pairs={{0,4},{1,5},{2,6},{3,7},{4,0},{5,1},{6,2},{7,3},{8,12},{9,13},{10,... | collective-permute-start | bytes 393224 | tf_op jit(solution)/shard_map/ppermute | solution.py:382
  46.3 0.7 %lay_out.1 = bf16[256,256]{1,0:T(8,128)(2,1)} custom-call(bf16[256,128]{1,0:T(8,128)(2,1)S(1)} %get-tuple-element.42.own, bf16[256,128]{1,0:T(8,128)(2,1)S(1)} %collective-permute-done.15.other), custom_call_target="tpu_custom_call" | custom-call | bytes 2097152 | tf_op jit(solution)/shard_map/lay_out/pallas_call | solution.py:406
  47.0 3.1 %collective-permute-done.17 = bf16[256,256]{1,0:T(8,128)(2,1)S(1)} collective-permute-done((bf16[256,256]{1,0:T(8,128)(2,1)S(1)}, bf16[256,256]{1,0:T(8,128)(2,1)S(1)}, u32[]{:S(2)}, u32[]{:S(2)}) %collective-permute-start.17) | collective-permute-done | bytes 131104 | tf_op jit(solution)/shard_map/ppermute | solution.py:382
  50.0 1.9 %collective-permute-done.19 = bf16[256,256]{1,0:T(8,128)(2,1)S(1)} collective-permute-done((bf16[256,256]{1,0:T(8,128)(2,1)S(1)}, bf16[256,256]{1,0:T(8,128)(2,1)S(1)}, u32[]{:S(2)}, u32[]{:S(2)}) %collective-permute-start.19) | collective-permute-done | bytes 131104 | tf_op jit(solution)/shard_map/ppermute | solution.py:382
  52.1 0.7 %add_convert_fusion.1 = bf16[256,256]{1,0:T(8,128)(2,1)} fusion(bf16[256,256]{1,0:T(8,128)(2,1)S(1)} %collective-permute-done.19, bf16[256,256]{1,0:T(8,128)(2,1)S(1)} %collective-permute-done.18, bf16[256,256]{1,0:T(8,128)(2,1)S(1)} %collective-permute-done.17, bf16[1024,256]{1,0:T(8,128)(2,1)S(1)} %add_convert_fusion), kind=kLoop, calls=%fused_computation.1 | loop fusion | flops 524288 | bytes 655360 | tf_op jit(solution)/shard_map/convert_element_type | solution.py:536
  (34 shorter events, 2.6 us)
Async XLA Ops:
  0.6 8.2 %collective-permute-start = (bf16[256,256]{1,0:T(8,128)(2,1)}, bf16[256,256]{1,0:T(8,128)(2,1)S(1)}, u32[]{:S(2)}, u32[]{:S(2)}) collective-permute-start(bf16[256,256]{1,0:T(8,128)(2,1)} %f.1), channel_id=1, source_target_pairs={{0,6},{1,7},{2,4},{3,5},{4,2},{5,3},{6,0},{7,1},{8,14},{9,15},{10,... | collective-permute-start | bytes 393224 | tf_op jit(solution)/shard_map/ppermute | solution.py:382
  4.6 6.5 %collective-permute-start.2 = (bf16[256,256]{1,0:T(8,128)(2,1)}, bf16[256,256]{1,0:T(8,128)(2,1)S(1)}, u32[]{:S(2)}, u32[]{:S(2)}) collective-permute-start(bf16[256,256]{1,0:T(8,128)(2,1)} %f.1), channel_id=1, source_target_pairs={{0,4},{1,5},{2,6},{3,7},{4,0},{5,1},{6,2},{7,3},{8,12},{9,13},{10,... | collective-permute-start | bytes 393224 | tf_op jit(solution)/shard_map/ppermute | solution.py:382
  5.1 6.3 %collective-permute-start.1 = (bf16[256,256]{1,0:T(8,128)(2,1)}, bf16[256,256]{1,0:T(8,128)(2,1)S(1)}, u32[]{:S(2)}, u32[]{:S(2)}) collective-permute-start(bf16[256,256]{1,0:T(8,128)(2,1)} %f.1), channel_id=1, source_target_pairs={{0,2},{1,3},{2,0},{3,1},{4,6},{5,7},{6,4},{7,5},{8,10},{9,11},{10,... | collective-permute-start | bytes 393224 | tf_op jit(solution)/shard_map/ppermute | solution.py:382
  11.4 2.0 %collective-permute-start.4 = (bf16[1024,256]{1,0:T(8,128)(2,1)S(1)}, bf16[1024,256]{1,0:T(8,128)(2,1)S(1)}, u32[]{:S(2)}, u32[]{:S(2)}) collective-permute-start(bf16[1024,256]{1,0:T(8,128)(2,1)S(1)} %pack.1), channel_id=1, source_target_pairs={{0,1},{1,0},{2,3},{3,2},{4,5},{5,4},{6,7},{7,6},{8,9},{9,8},{10,11... | collective-permute-start | bytes 1572872 | tf_op jit(solution)/shard_map/ppermute | solution.py:382
  11.9 3.4 %copy-start.1 = (s32[2,9]{1,0:T(2,128)S(1)}, s32[2,9]{1,0:T(2,128)}, u32[]{:S(2)}) copy-start(s32[2,9]{1,0:T(2,128)} %own.1) | copy-start | bytes 220
  11.9 3.4 %copy-start = (bf16[256,256]{1,0:T(8,128)(2,1)S(1)}, bf16[256,256]{1,0:T(8,128)(2,1)}, u32[]{:S(2)}) copy-start(bf16[256,256]{1,0:T(8,128)(2,1)} %d_own.3) | copy-start | bytes 393220
  13.7 5.2 %collective-permute-start.5 = (bf16[256,256]{1,0:T(8,128)(2,1)S(1)}, bf16[256,256]{1,0:T(8,128)(2,1)S(1)}, u32[]{:S(2)}, u32[]{:S(2)}) collective-permute-start(bf16[256,256]{1,0:T(8,128)(2,1)S(1)} %get-tuple-element.32.first_kv), channel_id=1, source_target_pairs={{0,8},{1,0},{2,10},{3,2},{4,12},{5,4},{6,14},{7,6},{8,16},{9,1},{1... | collective-permute-start | bytes 393224 | tf_op jit(solution)/shard_map/ppermute | solution.py:393
  15.3 5.8 %collective-permute-start.6 = (bf16[256,256]{1,0:T(8,128)(2,1)S(1)}, bf16[256,256]{1,0:T(8,128)(2,1)S(1)}, u32[]{:S(2)}, u32[]{:S(2)}) collective-permute-start(bf16[256,256]{1,0:T(8,128)(2,1)S(1)} %get-tuple-element.33.second_kv), channel_id=1, source_target_pairs={{0,1},{1,9},{2,3},{3,11},{4,5},{5,13},{6,7},{7,15},{8,0},{9,17},{1... | collective-permute-start | bytes 393224 | tf_op jit(solution)/shard_map/ppermute | solution.py:393
  15.3 5.8 %collective-permute-start.3 = (bf16[272,128]{1,0:T(8,128)(2,1)S(1)}, bf16[272,128]{1,0:T(8,128)(2,1)S(1)}, u32[]{:S(2)}, u32[]{:S(2)}) collective-permute-start(bf16[272,128]{1,0:T(8,128)(2,1)S(1)} %payload.1), channel_id=1, source_target_pairs={{0,4},{1,5},{2,6},{3,7},{4,0},{5,1},{6,2},{7,3},{8,12},{9,13},{10,... | collective-permute-start | bytes 208904 | tf_op jit(solution)/shard_map/ppermute | solution.py:382
  16.9 6.3 %collective-permute-start.8 = (bf16[256,256]{1,0:T(8,128)(2,1)S(1)}, bf16[256,256]{1,0:T(8,128)(2,1)S(1)}, u32[]{:S(2)}, u32[]{:S(2)}) collective-permute-start(bf16[256,256]{1,0:T(8,128)(2,1)S(1)} %get-tuple-element.32.first_kv), channel_id=1, source_target_pairs={{0,1},{1,9},{2,3},{3,11},{4,5},{5,13},{6,7},{7,15},{8,0},{9,17},{1... | collective-permute-start | bytes 393224 | tf_op jit(solution)/shard_map/ppermute | solution.py:393
  16.9 6.3 %collective-permute-start.7 = (bf16[256,256]{1,0:T(8,128)(2,1)S(1)}, bf16[256,256]{1,0:T(8,128)(2,1)S(1)}, u32[]{:S(2)}, u32[]{:S(2)}) collective-permute-start(bf16[256,256]{1,0:T(8,128)(2,1)S(1)} %get-tuple-element.33.second_kv), channel_id=1, source_target_pairs={{0,8},{1,0},{2,10},{3,2},{4,12},{5,4},{6,14},{7,6},{8,16},{9,1},{1... | collective-permute-start | bytes 393224 | tf_op jit(solution)/shard_map/ppermute | solution.py:393
  18.9 5.3 %collective-permute-start.9 = (bf16[256,256]{1,0:T(8,128)(2,1)S(1)}, bf16[256,256]{1,0:T(8,128)(2,1)S(1)}, u32[]{:S(2)}, u32[]{:S(2)}) collective-permute-start(bf16[256,256]{1,0:T(8,128)(2,1)S(1)} %collective-permute-done.5.u1), channel_id=1, source_target_pairs={{0,8},{1,0},{2,10},{3,2},{4,12},{5,4},{6,14},{7,6},{8,16},{9,1},{1... | collective-permute-start | bytes 393224 | tf_op jit(solution)/shard_map/ppermute | solution.py:393
  21.1 5.0 %collective-permute-start.10 = (bf16[256,256]{1,0:T(8,128)(2,1)S(1)}, bf16[256,256]{1,0:T(8,128)(2,1)S(1)}, u32[]{:S(2)}, u32[]{:S(2)}) collective-permute-start(bf16[256,256]{1,0:T(8,128)(2,1)S(1)} %collective-permute-done.6.d1), channel_id=1, source_target_pairs={{0,1},{1,9},{2,3},{3,11},{4,5},{5,13},{6,7},{7,15},{8,0},{9,17},{1... | collective-permute-start | bytes 393224 | tf_op jit(solution)/shard_map/ppermute | solution.py:393
  27.1 5.5 %collective-permute-start.13 = (bf16[256,256]{1,0:T(8,128)(2,1)S(1)}, bf16[256,256]{1,0:T(8,128)(2,1)S(1)}, u32[]{:S(2)}, u32[]{:S(2)}) collective-permute-start(bf16[256,256]{1,0:T(8,128)(2,1)S(1)} %get-tuple-element.47), channel_id=1, source_target_pairs={{0,1},{1,9},{2,3},{3,11},{4,5},{5,13},{6,7},{7,15},{8,0},{9,17},{1... | collective-permute-start | bytes 393224 | tf_op jit(solution)/shard_map/ppermute | solution.py:393
  27.2 5.5 %collective-permute-start.11 = (bf16[256,256]{1,0:T(8,128)(2,1)S(1)}, bf16[256,256]{1,0:T(8,128)(2,1)S(1)}, u32[]{:S(2)}, u32[]{:S(2)}) collective-permute-start(bf16[256,256]{1,0:T(8,128)(2,1)S(1)} %get-tuple-element.44), channel_id=1, source_target_pairs={{0,8},{1,0},{2,10},{3,2},{4,12},{5,4},{6,14},{7,6},{8,16},{9,1},{1... | collective-permute-start | bytes 393224 | tf_op jit(solution)/shard_map/ppermute | solution.py:393
  32.7 7.4 %collective-permute-start.14 = (bf16[512,256]{1,0:T(8,128)(2,1)S(1)}, bf16[512,256]{1,0:T(8,128)(2,1)S(1)}, u32[]{:S(2)}, u32[]{:S(2)}) collective-permute-start(bf16[512,256]{1,0:T(8,128)(2,1)S(1)} %merge_d.1), channel_id=1, source_target_pairs={{0,1},{1,9},{2,3},{3,11},{4,5},{5,13},{6,7},{7,15},{8,0},{9,17},{1... | collective-permute-start | bytes 786440 | tf_op jit(solution)/shard_map/ppermute | solution.py:393
  32.7 7.4 %collective-permute-start.12 = (bf16[512,256]{1,0:T(8,128)(2,1)S(1)}, bf16[512,256]{1,0:T(8,128)(2,1)S(1)}, u32[]{:S(2)}, u32[]{:S(2)}) collective-permute-start(bf16[512,256]{1,0:T(8,128)(2,1)S(1)} %merge_u.1), channel_id=1, source_target_pairs={{0,8},{1,0},{2,10},{3,2},{4,12},{5,4},{6,14},{7,6},{8,16},{9,1},{1... | collective-permute-start | bytes 786440 | tf_op jit(solution)/shard_map/ppermute | solution.py:393
  34.8 4.7 %collective-permute-start.15 = (bf16[256,128]{1,0:T(8,128)(2,1)S(1)}, bf16[256,128]{1,0:T(8,128)(2,1)S(1)}, u32[]{:S(2)}, u32[]{:S(2)}) collective-permute-start(bf16[256,128]{1,0:T(8,128)(2,1)S(1)} %get-tuple-element.48), channel_id=1, source_target_pairs={{0,4},{1,5},{2,6},{3,7},{4,0},{5,1},{6,2},{7,3},{8,12},{9,13},{10,... | collective-permute-start | bytes 196616 | tf_op jit(solution)/shard_map/ppermute | solution.py:382
  40.6 2.0 %collective-permute-start.16 = (bf16[1024,256]{1,0:T(8,128)(2,1)S(1)}, bf16[1024,256]{1,0:T(8,128)(2,1)S(1)}, u32[]{:S(2)}, u32[]{:S(2)}) collective-permute-start(bf16[1024,256]{1,0:T(8,128)(2,1)S(1)} %get-tuple-element.55), channel_id=1, source_target_pairs={{0,1},{1,0},{2,3},{3,2},{4,5},{5,4},{6,7},{7,6},{8,9},{9,8},{10,11... | collective-permute-start | bytes 1572872 | tf_op jit(solution)/shard_map/ppermute | solution.py:382
  42.7 7.3 %collective-permute-start.17 = (bf16[256,256]{1,0:T(8,128)(2,1)S(1)}, bf16[256,256]{1,0:T(8,128)(2,1)S(1)}, u32[]{:S(2)}, u32[]{:S(2)}) collective-permute-start(bf16[256,256]{1,0:T(8,128)(2,1)S(1)} %get-tuple-element.56), channel_id=1, source_target_pairs={{0,6},{1,7},{2,4},{3,5},{4,2},{5,3},{6,0},{7,1},{8,14},{9,15},{10,... | collective-permute-start | bytes 393224 | tf_op jit(solution)/shard_map/ppermute | solution.py:382
  44.2 7.7 %collective-permute-start.19 = (bf16[256,256]{1,0:T(8,128)(2,1)S(1)}, bf16[256,256]{1,0:T(8,128)(2,1)S(1)}, u32[]{:S(2)}, u32[]{:S(2)}) collective-permute-start(bf16[256,256]{1,0:T(8,128)(2,1)S(1)} %get-tuple-element.57), channel_id=1, source_target_pairs={{0,2},{1,3},{2,0},{3,1},{4,6},{5,7},{6,4},{7,5},{8,10},{9,11},{10,... | collective-permute-start | bytes 393224 | tf_op jit(solution)/shard_map/ppermute | solution.py:382
  45.6 6.4 %collective-permute-start.18 = (bf16[256,256]{1,0:T(8,128)(2,1)S(1)}, bf16[256,256]{1,0:T(8,128)(2,1)S(1)}, u32[]{:S(2)}, u32[]{:S(2)}) collective-permute-start(bf16[256,256]{1,0:T(8,128)(2,1)S(1)} %get-tuple-element.58), channel_id=1, source_target_pairs={{0,4},{1,5},{2,6},{3,7},{4,0},{5,1},{6,2},{7,3},{8,12},{9,13},{10,... | collective-permute-start | bytes 393224 | tf_op jit(solution)/shard_map/ppermute | solution.py:382

commit v10 on v9

--- a/solution.py
+++ b/solution.py
@@ -63,41 +63,37 @@
     return w_mine[pl.ds(pl.multiple_of(source * width, width), width), :]
 
 
-def pack_kernel(fm, sd, sx, sy, out):
-    for index, piece in enumerate((fm, sy, sx, sd)):
-        out[index * HALF : (index + 1) * HALF, :] = piece[...]
-
-
-def project_across_kernel(pack, before, w_mine, total):
+def pack_kernel(one, two, out):
+    out[:HALF, :] = one[...]
+    out[HALF:, :] = two[...]
+
+
+def project_rest_kernel(before, early, late, other_early, w_mine, total):
     head = position()[3]
-    width = pack.shape[1]
-    far = dot(pack[2 * HALF :, :], weight_rows(w_mine, head ^ 2, width), ((1,), (0,)))
-    total[:HALF, :] = before[...] + far[:HALF]
-    total[HALF:, :] = far[HALF:] + dot(pack[HALF : 2 * HALF, :], weight_rows(w_mine, head, width), ((1,), (0,)))
-
-
-def sibling_product(head, other, w_mine, cols):
-    width = other.shape[1]
-    total = None
-    for index in range(2):
-        rows = pl.ds(pl.multiple_of((head ^ (1 + 2 * index)) * width, width), width)
-        term = dot(other[2 * index * HALF : 2 * (index + 1) * HALF, :], w_mine[rows, cols], ((1,), (0,)))
-        total = term if total is None else total + term
-    return total
-
-
-def store_groups(side, total, target):
-    for group in range(2):
-        rows = pl.ds(pl.multiple_of((side ^ group) * HALF, HALF), HALF)
-        target[rows, :] = total[group * HALF : (group + 1) * HALF]
-
-
-def project_kv_kernel(other, before, w_mine, first_out, second_out):
+    width = early.shape[1]
+    mine, across_x, sibling, across_both = (weight_rows(w_mine, head ^ k, width) for k in (0, 2, 1, 3))
+    own = before[...] + dot(late[HALF:, :], across_x, ((1,), (0,)))
+    total[:HALF, :] = own + dot(other_early[:HALF, :], sibling, ((1,), (0,)))
+    partner = dot(late[:HALF, :], mine, ((1,), (0,))) + dot(early[HALF:, :], across_x, ((1,), (0,)))
+    total[HALF:, :] = partner + dot(other_early[HALF:, :], across_both, ((1,), (0,)))
+
+
+def last_product(head, other_late, w_mine, cols, group):
+    width = other_late.shape[1]
+    rows = pl.ds(pl.multiple_of((head ^ (3 if group == 0 else 1)) * width, width), width)
+    piece = other_late[HALF:, :] if group == 0 else other_late[:HALF, :]
+    return dot(piece, w_mine[rows, cols], ((1,), (0,)))
+
+
+def project_kv_kernel(other_late, before, w_mine, first_out, second_out):
     side, flip, _, head = position()
-    total = (before[:, HD:] + sibling_product(head, other, w_mine, slice(HD, 3 * HD))).astype(BF)
+    own, partner = (
+        (before[g * HALF : (g + 1) * HALF, HD:] + last_product(head, other_late, w_mine, slice(HD, 3 * HD), g)).astype(BF)
+        for g in range(2)
+    )
     near_first = side ^ (1 - flip) == 0
-    first_out[...] = jnp.where(near_first, total[:HALF], total[HALF:])
-    second_out[...] = jnp.where(near_first, total[HALF:], total[:HALF])
+    first_out[...] = jnp.where(near_first, own, partner)
+    second_out[...] = jnp.where(near_first, partner, own)
 
 
 def merge_kernel(whole, part, dq, out):
@@ -113,15 +109,16 @@
         out[:, cols] = jnp.where(side == half, own[...], other[...])
 
 
-def project_q_kernel(other, before, w_mine, u1, d1, q_out):
+def project_q_kernel(other_late, before, w_mine, u1, d1, q_out):
     del u1, d1
     side, _, _, head = position()
-    total = before[:, :HD] + sibling_product(head, other, w_mine, slice(0, HD))
-    store_groups(side, total.astype(BF), q_out)
-
-
-def payload_kernel(d_own, link_rows, pack, payload):
-    del pack
+    for g in range(2):
+        part = before[g * HALF : (g + 1) * HALF, :HD] + last_product(head, other_late, w_mine, slice(0, HD), g)
+        q_out[pl.ds(pl.multiple_of((side ^ g) * HALF, HALF), HALF), :] = part.astype(BF)
+
+
+def payload_kernel(d_own, link_rows, late, payload):
+    del late
     side = position()[0]
     payload[:HALF, :] = jnp.where(side == 0, d_own[:, HD:], d_own[:, :HD])
     payload[HALF:, :] = link_rows[...]
@@ -139,7 +136,8 @@
                 entry = links[i, SPAN * t + j]
                 base = jnp.maximum(base, jnp.where(entry >= 0, entry - j, -(1 << 20)))
             base = jnp.where(base > -(1 << 19), base - first + REACH, i + 1 if t == 1 else i + REACH + SPAN)
-            links[GROUP, 2 * i + t - 1] = jnp.clip(base, 0, WINDOW - SPAN) * BLK
+            lowest = i if t == 1 else i + REACH + SPAN - 1
+            links[GROUP, 2 * i + t - 1] = jnp.clip(base, lowest, lowest + 2) * BLK
 
 
 def regions(flip):
@@ -430,13 +428,20 @@
         product,
         [pltpu.SemaphoreType.DMA((4,))],
     )
-    (pack,) = call(pack_kernel, "pack", [out(4 * HALF, f.shape[1])], (fm, sd, sx, sy), 4, 0)
-    other = across(pack, 0, 1)
+    (early,) = call(pack_kernel, "pack_early", [out(ROWS, f.shape[1])], (fm, sd), 4, 0)
+    other_early = across(early, 0, 1)
+    (late,) = call(pack_kernel, "pack_late", [out(ROWS, f.shape[1])], (sy, sx), 4, 0)
+    other_late = across(late, 0, 1)
     (total,) = call(
-        project_across_kernel, "project_across", [held(ROWS, 3 * HD, F32)], (pack, total, w_mine), 4, product
+        project_rest_kernel,
+        "project_rest",
+        [held(ROWS, 3 * HD, F32)],
+        (total, early, late, other_early, w_mine),
+        4,
+        product,
     )
     first, second = call(
-        project_kv_kernel, "project_kv", [out(HALF, 2 * HD)] * 2, (other, total, w_mine), 4, product
+        project_kv_kernel, "project_kv", [out(HALF, 2 * HD)] * 2, (other_late, total, w_mine), 4, product
     )
 
     u1 = chain(first, 0)
@@ -447,9 +452,9 @@
     d3 = chain(d1, 1)
     rows, slots = block_links.shape
     link_rows = jnp.pad(block_links.astype(BF), ((0, 16 - rows), (0, HD - slots)))
-    (payload,) = call(payload_kernel, "payload", [out(HALF + 16, HD)], (d_out, link_rows, pack), 4, 0)
+    (payload,) = call(payload_kernel, "payload", [out(HALF + 16, HD)], (d_out, link_rows, late), 4, 0)
     d_other = across(payload, 1, 0)
-    (q,) = call(project_q_kernel, "project_q", [held(ROWS, HD)], (other, total, w_mine, u1, d1), 4, product)
+    (q,) = call(project_q_kernel, "project_q", [held(ROWS, HD)], (other_late, total, w_mine, u1, d1), 4, product)
     other_links = d_other[HALF : HALF + rows, :slots].astype(jnp.int32)
     (links,) = call(
         links_kernel, "links", [pltpu.SMEM((GROUP + 1, slots), jnp.int32)], (block_links, other_links, q), 4, 0

time: 52.9 us -> 52.5 us (level)
  waiting for transfers between devices: 20.1 us -> 19.5 us
    ppermute x10 -> x11, waiting for transfers between devices: 14.9 us -> 14.3 us  [across(): return lax.ppermute(value, ('ctx', 'head'), pairs)]
    ppermute x10 -> x11, starting transfers between devices: 12.2 us -> 12.3 us  [across(): return lax.ppermute(value, ('ctx', 'head'), pairs)]
    pallas_call x16 -> x17, Pallas kernels: 8.8 us -> 8.78 us  [call(): pl.pallas_call(kernel, name=name, out_shape=outs, in_specs=specs, out_spe...]
  transfers between devices with their start and end apart: 20 -> 21, of which waited for: 14 -> 13; matrix products, arithmetic and copies ran while one was open for 0% -> 0% of each run, Pallas kernels for 13% -> 13%
where the time goes in v10:
time: 52.5 us; the launch traced here: 52.3 us
  starting transfers between devices  22.2 us (42%)
  waiting for transfers between devices  19.5 us (37%)
  Pallas kernels  8.78 us (17%)
  other arithmetic  0.87 us (2%)
  between operations  0.86 us (2%)
    ppermute x11, waiting for transfers between devices, across(): return lax.ppermute(value, ('ctx', 'head'), pairs)  14.3 us
    ppermute x11, starting transfers between devices, across(): return lax.ppermute(value, ('ctx', 'head'), pairs)  12.3 us
    ppermute x10, starting transfers between devices, chain(): return lax.ppermute(value, ('ctx', 'head'), pairs)  9.92 us
    pallas_call x17, Pallas kernels, call(): pl.pallas_call(kernel, name=name, out_shape=outs, in_specs=specs, out_spe...  8.78 us
    ppermute x10, waiting for transfers between devices, chain(): return lax.ppermute(value, ('ctx', 'head'), pairs)  5.22 us
  transfers between devices with their start and end apart: 21, of which 13 were waited for; matrix products, arithmetic and copies ran while one was open for 0% of the time, Pallas kernels for 13%

profile of v10, /device:TPU:0, one launch (start us, length us, event | category | flops | bytes accessed | tf_op | source)
XLA Modules:
  0.0 52.3 jit_solution(5986560613400600477)
XLA Ops:
  0.6 4.0 %collective-permute-start.4 = (bf16[256,256]{1,0:T(8,128)(2,1)}, bf16[256,256]{1,0:T(8,128)(2,1)S(1)}, u32[]{:S(2)}, u32[]{:S(2)}) collective-permute-start(bf16[256,256]{1,0:T(8,128)(2,1)} %f.1), channel_id=1, source_target_pairs={{0,6},{1,7},{2,4},{3,5},{4,2},{5,3},{6,0},{7,1},{8,14},{9,15},{10,... | collective-permute-start | bytes 393224 | tf_op jit(solution)/shard_map/ppermute | solution.py:380
  4.6 0.5 %collective-permute-start.1 = (bf16[256,256]{1,0:T(8,128)(2,1)}, bf16[256,256]{1,0:T(8,128)(2,1)S(1)}, u32[]{:S(2)}, u32[]{:S(2)}) collective-permute-start(bf16[256,256]{1,0:T(8,128)(2,1)} %f.1), channel_id=1, source_target_pairs={{0,2},{1,3},{2,0},{3,1},{4,6},{5,7},{6,4},{7,5},{8,10},{9,11},{10,... | collective-permute-start | bytes 393224 | tf_op jit(solution)/shard_map/ppermute | solution.py:380
  5.2 1.4 %begin.1 = (bf16[1024,384]{1,0:T(8,128)(2,1)S(1)}, bf16[256,256]{1,0:T(8,128)(2,1)S(1)}, f32[256,384]{1,0:T(8,128)S(1)}) custom-call(bf16[256,256]{1,0:T(8,128)(2,1)} %f.1, bf16[3,1024,256]{2,1,0:T(8,128)(2,1)} %bitcast.1), custom_call_target="tpu_custom_call" | custom-call | flops 100663296 | bytes 2097152 | tf_op jit(solution)/shard_map/begin/pallas_call | solution.py:404
  6.7 2.5 %collective-permute-done.4.two = bf16[256,256]{1,0:T(8,128)(2,1)S(1)} collective-permute-done((bf16[256,256]{1,0:T(8,128)(2,1)}, bf16[256,256]{1,0:T(8,128)(2,1)S(1)}, u32[]{:S(2)}, u32[]{:S(2)}) %collective-permute-start.4) | collective-permute-done | bytes 131104 | tf_op jit(solution)/shard_map/ppermute | solution.py:380
  9.2 2.1 %collective-permute-done.1.two = bf16[256,256]{1,0:T(8,128)(2,1)S(1)} collective-permute-done((bf16[256,256]{1,0:T(8,128)(2,1)}, bf16[256,256]{1,0:T(8,128)(2,1)S(1)}, u32[]{:S(2)}, u32[]{:S(2)}) %collective-permute-start.1) | collective-permute-done | bytes 131104 | tf_op jit(solution)/shard_map/ppermute | solution.py:380
  11.5 0.5 project_rest.1.before
  12.0 1.0 %collective-permute-done.3.other_late = bf16[512,256]{1,0:T(8,128)(2,1)S(1)} collective-permute-done((bf16[512,256]{1,0:T(8,128)(2,1)S(1)}, bf16[512,256]{1,0:T(8,128)(2,1)S(1)}, u32[]{:S(2)}, u32[]{:S(2)}) %collective-permute-start.3) | collective-permute-done | bytes 262176 | tf_op jit(solution)/shard_map/ppermute | solution.py:380
  13.2 1.6 %collective-permute-start.6 = (bf16[256,256]{1,0:T(8,128)(2,1)S(1)}, bf16[256,256]{1,0:T(8,128)(2,1)S(1)}, u32[]{:S(2)}, u32[]{:S(2)}) collective-permute-start(bf16[256,256]{1,0:T(8,128)(2,1)S(1)} %get-tuple-element.32.first_kv), channel_id=1, source_target_pairs={{0,8},{1,0},{2,10},{3,2},{4,12},{5,4},{6,14},{7,6},{8,16},{9,1},{1... | collective-permute-start | bytes 393224 | tf_op jit(solution)/shard_map/ppermute | solution.py:391
  14.9 1.5 %collective-permute-start.2 = (bf16[272,128]{1,0:T(8,128)(2,1)S(1)}, bf16[272,128]{1,0:T(8,128)(2,1)S(1)}, u32[]{:S(2)}, u32[]{:S(2)}) collective-permute-start(bf16[272,128]{1,0:T(8,128)(2,1)S(1)} %payload.1), channel_id=1, source_target_pairs={{0,4},{1,5},{2,6},{3,7},{4,0},{5,1},{6,2},{7,3},{8,12},{9,13},{10,... | collective-permute-start | bytes 208904 | tf_op jit(solution)/shard_map/ppermute | solution.py:380
  16.4 2.0 %collective-permute-start.8 = (bf16[256,256]{1,0:T(8,128)(2,1)S(1)}, bf16[256,256]{1,0:T(8,128)(2,1)S(1)}, u32[]{:S(2)}, u32[]{:S(2)}) collective-permute-start(bf16[256,256]{1,0:T(8,128)(2,1)S(1)} %get-tuple-element.33.second_kv), channel_id=1, source_target_pairs={{0,8},{1,0},{2,10},{3,2},{4,12},{5,4},{6,14},{7,6},{8,16},{9,1},{1... | collective-permute-start | bytes 393224 | tf_op jit(solution)/shard_map/ppermute | solution.py:391
  18.4 2.2 %collective-permute-start.10 = (bf16[256,256]{1,0:T(8,128)(2,1)S(1)}, bf16[256,256]{1,0:T(8,128)(2,1)S(1)}, u32[]{:S(2)}, u32[]{:S(2)}) collective-permute-start(bf16[256,256]{1,0:T(8,128)(2,1)S(1)} %collective-permute-done.6.u1), channel_id=1, source_target_pairs={{0,8},{1,0},{2,10},{3,2},{4,12},{5,4},{6,14},{7,6},{8,16},{9,1},{1... | collective-permute-start | bytes 393224 | tf_op jit(solution)/shard_map/ppermute | solution.py:391
  20.9 0.7 %links.1 = s32[5,9]{1,0:T(8,128)S(4)} custom-call(s32[2,9]{1,0:T(2,128)S(1)} %copy-done.1, s32[2,9]{1,0:T(2,128)S(1)} %slice_convert_fusion.other, bf16[512,128]{1,0:T(8,128)(2,1)S(1)} %project_q.1.q), custom_call_target="tpu_custom_call" | custom-call | bytes 2097152 | tf_op jit(solution)/shard_map/links/pallas_call | solution.py:404
  21.6 1.1 %collective-permute-done.9.d2 = bf16[256,256]{1,0:T(8,128)(2,1)S(1)} collective-permute-done((bf16[256,256]{1,0:T(8,128)(2,1)S(1)}, bf16[256,256]{1,0:T(8,128)(2,1)S(1)}, u32[]{:S(2)}, u32[]{:S(2)}) %collective-permute-start.9) | collective-permute-done | bytes 131104 | tf_op jit(solution)/shard_map/ppermute | solution.py:391
  22.7 0.9 %near_scores.1 = (bf16[1024,256]{1,0:T(8,128)(2,1)S(1)}, f32[3072,128]{1,0:T(8,128)S(1)}, f32[3072,128]{1,0:T(8,128)S(1)}, f32[96,128]{1,0:T(8,128)S(1)}) custom-call(s32[5,9]{1,0:T(8,128)S(4)} %links.1, bf16[512,128]{1,0:T(8,128)(2,1)S(1)} %project_q.1.q, bf16[256,256]{1,0:T(8,128)(2,1)S(1)} %get-tuple-element.32.first_kv, ...), custom_call_target="tpu_custom_call" | custom-call | flops 301989888 | bytes 2097152 | tf_op jit(solution)/shard_map/near_scores/pallas_call | solution.py:404
  23.7 1.9 %collective-permute-done.11.d3 = bf16[256,256]{1,0:T(8,128)(2,1)S(1)} collective-permute-done((bf16[256,256]{1,0:T(8,128)(2,1)S(1)}, bf16[256,256]{1,0:T(8,128)(2,1)S(1)}, u32[]{:S(2)}, u32[]{:S(2)}) %collective-permute-start.11) | collective-permute-done | bytes 131104 | tf_op jit(solution)/shard_map/ppermute | solution.py:391
  25.6 1.1 %far_grads.1 = (bf16[1536,256]{1,0:T(8,128)(2,1)S(1)}, f32[1536,256]{1,0:T(8,128)S(1)}, bf16[256,256]{1,0:T(8,128)(2,1)S(1)}, bf16[256,256]{1,0:T(8,128)(2,1)S(1)}, f32[64,128]{1,0:T(8,128)S(1)}) custom-call(s32[5,9]{1,0:T(8,128)S(4)} %links.1, bf16[1024,256]{1,0:T(8,128)(2,1)S(1)} %get-tuple-element.34.pairs, f32[96,128]{1,0:T(8,128)S(1)} %get-tuple-element.37.stats, ...), custom_call_target="tpu_custom_call" | custom-call | flops 301989888 | bytes 2097152 | tf_op jit(solution)/shard_map/far_grads/pallas_call | solution.py:404
  26.7 2.0 %collective-permute-start.12 = (bf16[256,256]{1,0:T(8,128)(2,1)S(1)}, bf16[256,256]{1,0:T(8,128)(2,1)S(1)}, u32[]{:S(2)}, u32[]{:S(2)}) collective-permute-start(bf16[256,256]{1,0:T(8,128)(2,1)S(1)} %get-tuple-element.44), channel_id=1, source_target_pairs={{0,8},{1,0},{2,10},{3,2},{4,12},{5,4},{6,14},{7,6},{8,16},{9,1},{1... | collective-permute-start | bytes 393224 | tf_op jit(solution)/shard_map/ppermute | solution.py:391
  28.7 0.9 %near_grads.1 = (bf16[3072,256]{1,0:T(8,128)(2,1)S(1)}, f32[256,256]{1,0:T(8,128)S(1)}, f32[256,256]{1,0:T(8,128)S(1)}, bf16[512,256]{1,0:T(8,128)(2,1)S(1)}, bf16[512,256]{1,0:T(8,128)(2,1)S(1)}) custom-call(s32[5,9]{1,0:T(8,128)S(4)} %links.1, bf16[1024,256]{1,0:T(8,128)(2,1)S(1)} %get-tuple-element.34.pairs, f32[3072,128]{1,0:T(8,128)S(1)} %get-tuple-element.35.terms, ...), custom_call_target="tpu_custom_call" | custom-call | flops 301989888 | bytes 2097152 | tf_op jit(solution)/shard_map/near_grads/pallas_call | solution.py:404
  29.6 1.1 %outputs.1 = (bf16[256,128]{1,0:T(8,128)(2,1)S(1)}, bf16[256,128]{1,0:T(8,128)(2,1)S(1)}, bf16[512,128]{1,0:T(8,128)(2,1)S(1)}) custom-call(s32[5,9]{1,0:T(8,128)S(4)} %links.1, bf16[3072,256]{1,0:T(8,128)(2,1)S(1)} %get-tuple-element.40.near_mixed, bf16[1536,256]{1,0:T(8,128)(2,1)S(1)} %get-tuple-element.41.far_mixed, ...), custom_call_target="tpu_custom_call" | custom-call | flops 301989888 | bytes 2097152 | tf_op jit(solution)/shard_map/outputs/pallas_call | solution.py:404
  30.7 1.4 %collective-permute-done.14.part = bf16[256,256]{1,0:T(8,128)(2,1)S(1)} collective-permute-done((bf16[256,256]{1,0:T(8,128)(2,1)S(1)}, bf16[256,256]{1,0:T(8,128)(2,1)S(1)}, u32[]{:S(2)}, u32[]{:S(2)}) %collective-permute-start.14) | collective-permute-done | bytes 131104 | tf_op jit(solution)/shard_map/ppermute | solution.py:391
  32.3 2.0 %collective-permute-start.13 = (bf16[512,256]{1,0:T(8,128)(2,1)S(1)}, bf16[512,256]{1,0:T(8,128)(2,1)S(1)}, u32[]{:S(2)}, u32[]{:S(2)}) collective-permute-start(bf16[512,256]{1,0:T(8,128)(2,1)S(1)} %merge_u.1), channel_id=1, source_target_pairs={{0,8},{1,0},{2,10},{3,2},{4,12},{5,4},{6,14},{7,6},{8,16},{9,1},{1... | collective-permute-start | bytes 786440 | tf_op jit(solution)/shard_map/ppermute | solution.py:391
  34.3 2.4 %collective-permute-start.16 = (bf16[256,128]{1,0:T(8,128)(2,1)S(1)}, bf16[256,128]{1,0:T(8,128)(2,1)S(1)}, u32[]{:S(2)}, u32[]{:S(2)}) collective-permute-start(bf16[256,128]{1,0:T(8,128)(2,1)S(1)} %get-tuple-element.48), channel_id=1, source_target_pairs={{0,4},{1,5},{2,6},{3,7},{4,0},{5,1},{6,2},{7,3},{8,12},{9,13},{10,... | collective-permute-start | bytes 196616 | tf_op jit(solution)/shard_map/ppermute | solution.py:380
  36.7 2.2 %collective-permute-done.16.other = bf16[256,128]{1,0:T(8,128)(2,1)S(1)} collective-permute-done((bf16[256,128]{1,0:T(8,128)(2,1)S(1)}, bf16[256,128]{1,0:T(8,128)(2,1)S(1)}, u32[]{:S(2)}, u32[]{:S(2)}) %collective-permute-start.16) | collective-permute-done | bytes 65568 | tf_op jit(solution)/shard_map/ppermute | solution.py:380
  39.0 0.7 %collective-permute-done.15.from_d = bf16[512,256]{1,0:T(8,128)(2,1)S(1)} collective-permute-done((bf16[512,256]{1,0:T(8,128)(2,1)S(1)}, bf16[512,256]{1,0:T(8,128)(2,1)S(1)}, u32[]{:S(2)}, u32[]{:S(2)}) %collective-permute-start.15) | collective-permute-done | bytes 262176 | tf_op jit(solution)/shard_map/ppermute | solution.py:391
  40.7 1.4 %collective-permute-done.17 = bf16[1024,256]{1,0:T(8,128)(2,1)S(1)} collective-permute-done((bf16[1024,256]{1,0:T(8,128)(2,1)S(1)}, bf16[1024,256]{1,0:T(8,128)(2,1)S(1)}, u32[]{:S(2)}, u32[]{:S(2)}) %collective-permute-start.17) | collective-permute-done | bytes 524320 | tf_op jit(solution)/shard_map/ppermute | solution.py:380
  42.3 2.4 %collective-permute-start.18 = (bf16[256,256]{1,0:T(8,128)(2,1)S(1)}, bf16[256,256]{1,0:T(8,128)(2,1)S(1)}, u32[]{:S(2)}, u32[]{:S(2)}) collective-permute-start(bf16[256,256]{1,0:T(8,128)(2,1)S(1)} %get-tuple-element.56), channel_id=1, source_target_pairs={{0,6},{1,7},{2,4},{3,5},{4,2},{5,3},{6,0},{7,1},{8,14},{9,15},{10,... | collective-permute-start | bytes 393224 | tf_op jit(solution)/shard_map/ppermute | solution.py:380
  44.6 0.5 %collective-permute-start.20 = (bf16[256,256]{1,0:T(8,128)(2,1)S(1)}, bf16[256,256]{1,0:T(8,128)(2,1)S(1)}, u32[]{:S(2)}, u32[]{:S(2)}) collective-permute-start(bf16[256,256]{1,0:T(8,128)(2,1)S(1)} %get-tuple-element.57), channel_id=1, source_target_pairs={{0,2},{1,3},{2,0},{3,1},{4,6},{5,7},{6,4},{7,5},{8,10},{9,11},{10,... | collective-permute-start | bytes 393224 | tf_op jit(solution)/shard_map/ppermute | solution.py:380
  45.2 0.6 %collective-permute-start.19 = (bf16[256,256]{1,0:T(8,128)(2,1)S(1)}, bf16[256,256]{1,0:T(8,128)(2,1)S(1)}, u32[]{:S(2)}, u32[]{:S(2)}) collective-permute-start(bf16[256,256]{1,0:T(8,128)(2,1)S(1)} %get-tuple-element.58), channel_id=1, source_target_pairs={{0,4},{1,5},{2,6},{3,7},{4,0},{5,1},{6,2},{7,3},{8,12},{9,13},{10,... | collective-permute-start | bytes 393224 | tf_op jit(solution)/shard_map/ppermute | solution.py:380
  45.8 0.7 %lay_out.1 = bf16[256,256]{1,0:T(8,128)(2,1)} custom-call(bf16[256,128]{1,0:T(8,128)(2,1)S(1)} %get-tuple-element.42.own, bf16[256,128]{1,0:T(8,128)(2,1)S(1)} %collective-permute-done.16.other), custom_call_target="tpu_custom_call" | custom-call | bytes 2097152 | tf_op jit(solution)/shard_map/lay_out/pallas_call | solution.py:404
  46.5 3.1 %collective-permute-done.18 = bf16[256,256]{1,0:T(8,128)(2,1)S(1)} collective-permute-done((bf16[256,256]{1,0:T(8,128)(2,1)S(1)}, bf16[256,256]{1,0:T(8,128)(2,1)S(1)}, u32[]{:S(2)}, u32[]{:S(2)}) %collective-permute-start.18) | collective-permute-done | bytes 131104 | tf_op jit(solution)/shard_map/ppermute | solution.py:380
  49.6 1.9 %collective-permute-done.20 = bf16[256,256]{1,0:T(8,128)(2,1)S(1)} collective-permute-done((bf16[256,256]{1,0:T(8,128)(2,1)S(1)}, bf16[256,256]{1,0:T(8,128)(2,1)S(1)}, u32[]{:S(2)}, u32[]{:S(2)}) %collective-permute-start.20) | collective-permute-done | bytes 131104 | tf_op jit(solution)/shard_map/ppermute | solution.py:380
  51.6 0.7 %add_convert_fusion.1 = bf16[256,256]{1,0:T(8,128)(2,1)} fusion(bf16[256,256]{1,0:T(8,128)(2,1)S(1)} %collective-permute-done.20, bf16[256,256]{1,0:T(8,128)(2,1)S(1)} %collective-permute-done.19, bf16[256,256]{1,0:T(8,128)(2,1)S(1)} %collective-permute-done.18, bf16[1024,256]{1,0:T(8,128)(2,1)S(1)} %add_convert_fusion), kind=kLoop, calls=%fused_computation.1 | loop fusion | flops 524288 | bytes 655360 | tf_op jit(solution)/shard_map/convert_element_type | solution.py:541
  (37 shorter events, 2.4 us)
Async XLA Ops:
  0.6 8.5 %collective-permute-start.4 = (bf16[256,256]{1,0:T(8,128)(2,1)}, bf16[256,256]{1,0:T(8,128)(2,1)S(1)}, u32[]{:S(2)}, u32[]{:S(2)}) collective-permute-start(bf16[256,256]{1,0:T(8,128)(2,1)} %f.1), channel_id=1, source_target_pairs={{0,6},{1,7},{2,4},{3,5},{4,2},{5,3},{6,0},{7,1},{8,14},{9,15},{10,... | collective-permute-start | bytes 393224 | tf_op jit(solution)/shard_map/ppermute | solution.py:380
  4.6 6.8 %collective-permute-start.1 = (bf16[256,256]{1,0:T(8,128)(2,1)}, bf16[256,256]{1,0:T(8,128)(2,1)S(1)}, u32[]{:S(2)}, u32[]{:S(2)}) collective-permute-start(bf16[256,256]{1,0:T(8,128)(2,1)} %f.1), channel_id=1, source_target_pairs={{0,2},{1,3},{2,0},{3,1},{4,6},{5,7},{6,4},{7,5},{8,10},{9,11},{10,... | collective-permute-start | bytes 393224 | tf_op jit(solution)/shard_map/ppermute | solution.py:380
  5.1 6.2 %collective-permute-start = (bf16[256,256]{1,0:T(8,128)(2,1)}, bf16[256,256]{1,0:T(8,128)(2,1)S(1)}, u32[]{:S(2)}, u32[]{:S(2)}) collective-permute-start(bf16[256,256]{1,0:T(8,128)(2,1)} %f.1), channel_id=1, source_target_pairs={{0,4},{1,5},{2,6},{3,7},{4,0},{5,1},{6,2},{7,3},{8,12},{9,13},{10,... | collective-permute-start | bytes 393224 | tf_op jit(solution)/shard_map/ppermute | solution.py:380
  9.1 2.3 %collective-permute-start.5 = (bf16[512,256]{1,0:T(8,128)(2,1)S(1)}, bf16[512,256]{1,0:T(8,128)(2,1)S(1)}, u32[]{:S(2)}, u32[]{:S(2)}) collective-permute-start(bf16[512,256]{1,0:T(8,128)(2,1)S(1)} %pack_early.1.early), channel_id=1, source_target_pairs={{0,1},{1,0},{2,3},{3,2},{4,5},{5,4},{6,7},{7,6},{8,9},{9,8},{10,11... | collective-permute-start | bytes 786440 | tf_op jit(solution)/shard_map/ppermute | solution.py:380
  11.4 1.6 %collective-permute-start.3 = (bf16[512,256]{1,0:T(8,128)(2,1)S(1)}, bf16[512,256]{1,0:T(8,128)(2,1)S(1)}, u32[]{:S(2)}, u32[]{:S(2)}) collective-permute-start(bf16[512,256]{1,0:T(8,128)(2,1)S(1)} %pack_late.1.late), channel_id=1, source_target_pairs={{0,1},{1,0},{2,3},{3,2},{4,5},{5,4},{6,7},{7,6},{8,9},{9,8},{10,11... | collective-permute-start | bytes 786440 | tf_op jit(solution)/shard_map/ppermute | solution.py:380
  12.0 2.8 %copy-start.1 = (s32[2,9]{1,0:T(2,128)S(1)}, s32[2,9]{1,0:T(2,128)}, u32[]{:S(2)}) copy-start(s32[2,9]{1,0:T(2,128)} %own.1) | copy-start | bytes 220
  12.0 2.8 %copy-start = (bf16[256,256]{1,0:T(8,128)(2,1)S(1)}, bf16[256,256]{1,0:T(8,128)(2,1)}, u32[]{:S(2)}) copy-start(bf16[256,256]{1,0:T(8,128)(2,1)} %d_own.3) | copy-start | bytes 393220
  13.2 5.2 %collective-permute-start.6 = (bf16[256,256]{1,0:T(8,128)(2,1)S(1)}, bf16[256,256]{1,0:T(8,128)(2,1)S(1)}, u32[]{:S(2)}, u32[]{:S(2)}) collective-permute-start(bf16[256,256]{1,0:T(8,128)(2,1)S(1)} %get-tuple-element.32.first_kv), channel_id=1, source_target_pairs={{0,8},{1,0},{2,10},{3,2},{4,12},{5,4},{6,14},{7,6},{8,16},{9,1},{1... | collective-permute-start | bytes 393224 | tf_op jit(solution)/shard_map/ppermute | solution.py:391
  14.8 5.8 %collective-permute-start.7 = (bf16[256,256]{1,0:T(8,128)(2,1)S(1)}, bf16[256,256]{1,0:T(8,128)(2,1)S(1)}, u32[]{:S(2)}, u32[]{:S(2)}) collective-permute-start(bf16[256,256]{1,0:T(8,128)(2,1)S(1)} %get-tuple-element.33.second_kv), channel_id=1, source_target_pairs={{0,1},{1,9},{2,3},{3,11},{4,5},{5,13},{6,7},{7,15},{8,0},{9,17},{1... | collective-permute-start | bytes 393224 | tf_op jit(solution)/shard_map/ppermute | solution.py:391
  14.9 5.8 %collective-permute-start.2 = (bf16[272,128]{1,0:T(8,128)(2,1)S(1)}, bf16[272,128]{1,0:T(8,128)(2,1)S(1)}, u32[]{:S(2)}, u32[]{:S(2)}) collective-permute-start(bf16[272,128]{1,0:T(8,128)(2,1)S(1)} %payload.1), channel_id=1, source_target_pairs={{0,4},{1,5},{2,6},{3,7},{4,0},{5,1},{6,2},{7,3},{8,12},{9,13},{10,... | collective-permute-start | bytes 208904 | tf_op jit(solution)/shard_map/ppermute | solution.py:380
  16.4 6.3 %collective-permute-start.9 = (bf16[256,256]{1,0:T(8,128)(2,1)S(1)}, bf16[256,256]{1,0:T(8,128)(2,1)S(1)}, u32[]{:S(2)}, u32[]{:S(2)}) collective-permute-start(bf16[256,256]{1,0:T(8,128)(2,1)S(1)} %get-tuple-element.32.first_kv), channel_id=1, source_target_pairs={{0,1},{1,9},{2,3},{3,11},{4,5},{5,13},{6,7},{7,15},{8,0},{9,17},{1... | collective-permute-start | bytes 393224 | tf_op jit(solution)/shard_map/ppermute | solution.py:391
  16.4 6.3 %collective-permute-start.8 = (bf16[256,256]{1,0:T(8,128)(2,1)S(1)}, bf16[256,256]{1,0:T(8,128)(2,1)S(1)}, u32[]{:S(2)}, u32[]{:S(2)}) collective-permute-start(bf16[256,256]{1,0:T(8,128)(2,1)S(1)} %get-tuple-element.33.second_kv), channel_id=1, source_target_pairs={{0,8},{1,0},{2,10},{3,2},{4,12},{5,4},{6,14},{7,6},{8,16},{9,1},{1... | collective-permute-start | bytes 393224 | tf_op jit(solution)/shard_map/ppermute | solution.py:391
  18.4 5.3 %collective-permute-start.10 = (bf16[256,256]{1,0:T(8,128)(2,1)S(1)}, bf16[256,256]{1,0:T(8,128)(2,1)S(1)}, u32[]{:S(2)}, u32[]{:S(2)}) collective-permute-start(bf16[256,256]{1,0:T(8,128)(2,1)S(1)} %collective-permute-done.6.u1), channel_id=1, source_target_pairs={{0,8},{1,0},{2,10},{3,2},{4,12},{5,4},{6,14},{7,6},{8,16},{9,1},{1... | collective-permute-start | bytes 393224 | tf_op jit(solution)/shard_map/ppermute | solution.py:391
  20.7 5.0 %collective-permute-start.11 = (bf16[256,256]{1,0:T(8,128)(2,1)S(1)}, bf16[256,256]{1,0:T(8,128)(2,1)S(1)}, u32[]{:S(2)}, u32[]{:S(2)}) collective-permute-start(bf16[256,256]{1,0:T(8,128)(2,1)S(1)} %collective-permute-done.7.d1), channel_id=1, source_target_pairs={{0,1},{1,9},{2,3},{3,11},{4,5},{5,13},{6,7},{7,15},{8,0},{9,17},{1... | collective-permute-start | bytes 393224 | tf_op jit(solution)/shard_map/ppermute | solution.py:391
  26.7 5.5 %collective-permute-start.14 = (bf16[256,256]{1,0:T(8,128)(2,1)S(1)}, bf16[256,256]{1,0:T(8,128)(2,1)S(1)}, u32[]{:S(2)}, u32[]{:S(2)}) collective-permute-start(bf16[256,256]{1,0:T(8,128)(2,1)S(1)} %get-tuple-element.47), channel_id=1, source_target_pairs={{0,1},{1,9},{2,3},{3,11},{4,5},{5,13},{6,7},{7,15},{8,0},{9,17},{1... | collective-permute-start | bytes 393224 | tf_op jit(solution)/shard_map/ppermute | solution.py:391
  26.7 5.5 %collective-permute-start.12 = (bf16[256,256]{1,0:T(8,128)(2,1)S(1)}, bf16[256,256]{1,0:T(8,128)(2,1)S(1)}, u32[]{:S(2)}, u32[]{:S(2)}) collective-permute-start(bf16[256,256]{1,0:T(8,128)(2,1)S(1)} %get-tuple-element.44), channel_id=1, source_target_pairs={{0,8},{1,0},{2,10},{3,2},{4,12},{5,4},{6,14},{7,6},{8,16},{9,1},{1... | collective-permute-start | bytes 393224 | tf_op jit(solution)/shard_map/ppermute | solution.py:391
  32.2 7.4 %collective-permute-start.15 = (bf16[512,256]{1,0:T(8,128)(2,1)S(1)}, bf16[512,256]{1,0:T(8,128)(2,1)S(1)}, u32[]{:S(2)}, u32[]{:S(2)}) collective-permute-start(bf16[512,256]{1,0:T(8,128)(2,1)S(1)} %merge_d.1), channel_id=1, source_target_pairs={{0,1},{1,9},{2,3},{3,11},{4,5},{5,13},{6,7},{7,15},{8,0},{9,17},{1... | collective-permute-start | bytes 786440 | tf_op jit(solution)/shard_map/ppermute | solution.py:391
  32.3 7.3 %collective-permute-start.13 = (bf16[512,256]{1,0:T(8,128)(2,1)S(1)}, bf16[512,256]{1,0:T(8,128)(2,1)S(1)}, u32[]{:S(2)}, u32[]{:S(2)}) collective-permute-start(bf16[512,256]{1,0:T(8,128)(2,1)S(1)} %merge_u.1), channel_id=1, source_target_pairs={{0,8},{1,0},{2,10},{3,2},{4,12},{5,4},{6,14},{7,6},{8,16},{9,1},{1... | collective-permute-start | bytes 786440 | tf_op jit(solution)/shard_map/ppermute | solution.py:391
  34.3 4.7 %collective-permute-start.16 = (bf16[256,128]{1,0:T(8,128)(2,1)S(1)}, bf16[256,128]{1,0:T(8,128)(2,1)S(1)}, u32[]{:S(2)}, u32[]{:S(2)}) collective-permute-start(bf16[256,128]{1,0:T(8,128)(2,1)S(1)} %get-tuple-element.48), channel_id=1, source_target_pairs={{0,4},{1,5},{2,6},{3,7},{4,0},{5,1},{6,2},{7,3},{8,12},{9,13},{10,... | collective-permute-start | bytes 196616 | tf_op jit(solution)/shard_map/ppermute | solution.py:380
  40.1 2.0 %collective-permute-start.17 = (bf16[1024,256]{1,0:T(8,128)(2,1)S(1)}, bf16[1024,256]{1,0:T(8,128)(2,1)S(1)}, u32[]{:S(2)}, u32[]{:S(2)}) collective-permute-start(bf16[1024,256]{1,0:T(8,128)(2,1)S(1)} %get-tuple-element.55), channel_id=1, source_target_pairs={{0,1},{1,0},{2,3},{3,2},{4,5},{5,4},{6,7},{7,6},{8,9},{9,8},{10,11... | collective-permute-start | bytes 1572872 | tf_op jit(solution)/shard_map/ppermute | solution.py:380
  42.3 7.3 %collective-permute-start.18 = (bf16[256,256]{1,0:T(8,128)(2,1)S(1)}, bf16[256,256]{1,0:T(8,128)(2,1)S(1)}, u32[]{:S(2)}, u32[]{:S(2)}) collective-permute-start(bf16[256,256]{1,0:T(8,128)(2,1)S(1)} %get-tuple-element.56), channel_id=1, source_target_pairs={{0,6},{1,7},{2,4},{3,5},{4,2},{5,3},{6,0},{7,1},{8,14},{9,15},{10,... | collective-permute-start | bytes 393224 | tf_op jit(solution)/shard_map/ppermute | solution.py:380
  44.6 6.9 %collective-permute-start.20 = (bf16[256,256]{1,0:T(8,128)(2,1)S(1)}, bf16[256,256]{1,0:T(8,128)(2,1)S(1)}, u32[]{:S(2)}, u32[]{:S(2)}) collective-permute-start(bf16[256,256]{1,0:T(8,128)(2,1)S(1)} %get-tuple-element.57), channel_id=1, source_target_pairs={{0,2},{1,3},{2,0},{3,1},{4,6},{5,7},{6,4},{7,5},{8,10},{9,11},{10,... | collective-permute-start | bytes 393224 | tf_op jit(solution)/shard_map/ppermute | solution.py:380
  45.2 6.4 %collective-permute-start.19 = (bf16[256,256]{1,0:T(8,128)(2,1)S(1)}, bf16[256,256]{1,0:T(8,128)(2,1)S(1)}, u32[]{:S(2)}, u32[]{:S(2)}) collective-permute-start(bf16[256,256]{1,0:T(8,128)(2,1)S(1)} %get-tuple-element.58), channel_id=1, source_target_pairs={{0,4},{1,5},{2,6},{3,7},{4,0},{5,1},{6,2},{7,3},{8,12},{9,13},{10,... | collective-permute-start | bytes 393224 | tf_op jit(solution)/shard_map/ppermute | solution.py:380

commit v11 on v10

--- a/solution.py
+++ b/solution.py
@@ -96,17 +96,32 @@
     second_out[...] = jnp.where(near_first, partner, own)
 
 
-def merge_kernel(whole, part, dq, out):
+def merge_kernel(one, two, dq, out):
     del dq
-    out[:HALF, :] = (whole[:HALF, :].astype(F32) + part[...].astype(F32)).astype(BF)
-    out[HALF:, :] = whole[HALF:, :]
-
-
-def lay_out_kernel(own, other, out):
+    out[...] = (one[...].astype(F32) + two[...].astype(F32)).astype(BF)
+
+
+def gather_kernel(first_own, second_own, d, u, first_out, second_out):
+    first_out[...] = first_own[...] + u[...].astype(F32)
+    second_out[...] = second_own[...] + d[...].astype(F32)
+
+
+def chip_sum_kernel(keep, arrived, att_other, mine, to_x, to_y, to_d):
+    for index, target in enumerate((mine, to_x, to_y, to_d)):
+        rows = slice(index * HALF, (index + 1) * HALF)
+        target[:HALF, :] = (keep[rows, :].astype(F32) + arrived[rows, :].astype(F32)).astype(BF)
+    for half in range(2):
+        to_y[HALF:, half * HD : (half + 1) * HD] = att_other[half * BLK : (half + 1) * BLK, :]
+
+
+def finish_kernel(mine, gd, gx, from_y, att_own, attended, grad_features):
+    total = mine[...].astype(F32) + gd[...].astype(F32) + gx[...].astype(F32) + from_y[:HALF, :].astype(F32)
+    grad_features[...] = total.astype(BF)
     side = position()[0]
+    att_other = jnp.concatenate([from_y[HALF:, :HD], from_y[HALF:, HD:]], axis=0)
     for half in range(2):
         cols = slice(half * HD, (half + 1) * HD)
-        out[:, cols] = jnp.where(side == half, own[...], other[...])
+        attended[:, cols] = jnp.where(side == half, att_own[...], att_other)
 
 
 def project_q_kernel(other_late, before, w_mine, u1, d1, q_out):
@@ -298,7 +313,8 @@
 
 
 def near_grads_kernel(
-    links, pairs, terms, prob_grads, scales, edges, mixed, first_own, second_own, u_out, d_out, acc
+    links, pairs, terms, prob_grads, scales, edges, mixed, first_own, second_own,
+    u2_out, d2_out, u3_out, d3_out, acc,
 ):
     acc[NEAR_LEFT:OWN, :] = edges[NEAR_LEFT:OWN, :]
     acc[OWN:NEAR_RIGHT, :] = jnp.zeros((ROWS, 2 * HD), F32)
@@ -318,9 +334,8 @@
     first, second, u1, d1, u2, _, d2, _ = regions(position()[1])
     first_own[...] = acc[pl.ds(first, HALF), :] * factor
     second_own[...] = acc[pl.ds(second, HALF), :] * factor
-    for target, at_first, at_second in ((u_out, d1, d2), (d_out, u1, u2)):
-        target[:HALF, :] = (acc[pl.ds(at_first, HALF), :] * factor).astype(BF)
-        target[HALF:, :] = (acc[pl.ds(at_second, HALF), :] * factor).astype(BF)
+    for target, at in ((u2_out, d2), (d2_out, u2), (u3_out, d1), (d3_out, u1)):
+        target[...] = (acc[pl.ds(at, HALF), :] * factor).astype(BF)
 
 
 def outputs_kernel(
@@ -353,10 +368,10 @@
             target[index * HALF : (index + 1) * HALF, :] = part
 
 
-def spread_send_kernel(first_own, second_own, from_u, from_d, dq, w_mine, send, grads):
+def spread_send_kernel(first_own, second_own, from_d, from_u, dq, w_mine, send, grads):
     side, flip, _, head = position()
-    first = first_own[...] + from_u[HALF:, :].astype(F32) + from_d[:HALF, :].astype(F32)
-    second = second_own[...] + from_u[:HALF, :].astype(F32) + from_d[HALF:, :].astype(F32)
+    first = first_own[...] + from_d[...].astype(F32)
+    second = second_own[...] + from_u[...].astype(F32)
     grads[:, :HD] = dq[...]
     grads[:HALF, HD:] = jnp.where(flip == 1, first, second).astype(BF)
     grads[HALF:, HD:] = jnp.where(flip == 1, second, first).astype(BF)
@@ -492,10 +507,10 @@
         attention,
         [window],
     )
-    near_mixed, first_own, second_own, u_grad, d_grad = call(
+    near_mixed, first_own, second_own, u2_grad, d2_grad, u3_grad, d3_grad = call(
         near_grads_kernel,
         "near_grads",
-        [held(GROUP * 2 * run, 2 * HD)] + [held(HALF, 2 * HD, F32)] * 2 + [out(ROWS, 2 * HD)] * 2,
+        [held(GROUP * 2 * run, 2 * HD)] + [held(HALF, 2 * HD, F32)] * 2 + [out(HALF, 2 * HD)] * 4,
         (links, pairs, terms, prob_grads, scales, edges),
         4,
         attention,
@@ -511,34 +526,43 @@
         [window, pltpu.VMEM((ROWS, HD), BF)],
     )
 
+    back_d = chain(far_d_grad, 1)
     back_u = chain(far_u_grad, 0)
-    back_d = chain(far_d_grad, 1)
-
-    def merge(whole, part, name):
-        return call(merge_kernel, name, [out(ROWS, 2 * HD)], (whole, part, dq), 4, 0)[0]
-
-    from_u = chain(merge(u_grad, back_u, "merge_u"), 0)
-    from_d = chain(merge(d_grad, back_d, "merge_d"), 1)
-    att_back = across(att_other, 1, 0)
-    from_u, from_d, att_back = lax.optimization_barrier((from_u, from_d, att_back))
-    (attended,) = call(lay_out_kernel, "lay_out", [out(HALF, 2 * HD)], (att_own, att_back), 4, 0)
+    d2_back = chain(d2_grad, 1)
+    u2_back = chain(u2_grad, 0)
+
+    def merge(one, two, name):
+        return call(merge_kernel, name, [out(HALF, 2 * HD)], (one, two, dq), 4, 0)[0]
+
+    from_d = chain(merge(d3_grad, back_d, "merge_d"), 1)
+    from_u = chain(merge(u3_grad, back_u, "merge_u"), 0)
+    first_own, second_own = call(
+        gather_kernel, "gather", [held(HALF, 2 * HD, F32)] * 2, (first_own, second_own, d2_back, u2_back), 4, 0
+    )
     send, grads = call(
         spread_send_kernel,
         "spread_send",
         [out(4 * HALF, 2 * HD), held(ROWS, 3 * HD)],
-        (first_own, second_own, from_u, from_d, dq, w_mine),
+        (first_own, second_own, from_d, from_u, dq, w_mine),
         4,
         product,
     )
     (keep,) = call(spread_keep_kernel, "spread_keep", [held(4 * HALF, 2 * HD)], (grads, w_mine), 4, product)
     arrived = across(send, 0, 1)
-    chip = (keep.astype(F32) + arrived.astype(F32)).astype(BF)
-    gd = across(chip[3 * HALF :], 1, 2)
-    gy = across(chip[2 * HALF : 3 * HALF], 1, 0)
-    gx = across(chip[HALF : 2 * HALF], 0, 2)
-    grad_features = (
-        chip[:HALF].astype(F32) + gd.astype(F32) + gy.astype(F32) + gx.astype(F32)
-    ).astype(BF)
+    mine, to_x, to_y, to_d = call(
+        chip_sum_kernel,
+        "chip_sum",
+        [out(HALF, 2 * HD)] * 2 + [out(HALF + BLK, 2 * HD), out(HALF, 2 * HD)],
+        (keep, arrived, att_other),
+        4,
+        0,
+    )
+    gd = across(to_d, 1, 2)
+    gy = across(to_y, 1, 0)
+    gx = across(to_x, 0, 2)
+    attended, grad_features = call(
+        finish_kernel, "finish", [out(HALF, 2 * HD)] * 2, (mine, gd, gx, gy, att_own), 4, 0
+    )
     return attended, grad_features
 
 

time: 52.5 us -> 51.3 us (0.977)
  other arithmetic: 0.87 us -> 0.01 us
    ppermute x11 -> x10, starting transfers between devices: 12.3 us -> 9.89 us  [across(): return lax.ppermute(value, ('ctx', 'head'), pairs)]
    ppermute x10 -> x12, starting transfers between devices: 9.92 us -> 12 us  [chain(): return lax.ppermute(value, ('ctx', 'head'), pairs)]
    convert_element_type x2 -> x0, other arithmetic: 0.86 us -> none  [the longest x1 0.73 us: body(): grad_features = (chip[:HALF].astype(F32) + gd.astype(F32) + gy.astype(F32...]
    ppermute x11 -> x10, waiting for transfers between devices: 14.3 us -> 13.4 us  [across(): return lax.ppermute(value, ('ctx', 'head'), pairs)]
    ppermute x10 -> x12, waiting for transfers between devices: 5.22 us -> 5.89 us  [chain(): return lax.ppermute(value, ('ctx', 'head'), pairs)]
    pallas_call x17 -> x19, Pallas kernels: 8.78 us -> 9.03 us  [call(): pl.pallas_call(kernel, name=name, out_shape=outs, in_specs=specs, out_spe...]
  transfers between devices with their start and end apart: 21 -> 22, of which waited for: 13 -> 12; matrix products, arithmetic and copies ran while one was open for 0% -> 0% of each run, Pallas kernels for 13% -> 12%
where the time goes in v11:
time: 51.3 us; the launch traced here: 51.2 us
  starting transfers between devices  21.9 us (43%)
  waiting for transfers between devices  19.3 us (38%)
  Pallas kernels  9.03 us (18%)
  between operations  0.87 us (2%)
    ppermute x10, waiting for transfers between devices, across(): return lax.ppermute(value, ('ctx', 'head'), pairs)  13.4 us
    ppermute x12, starting transfers between devices, chain(): return lax.ppermute(value, ('ctx', 'head'), pairs)  12 us
    ppermute x10, starting transfers between devices, across(): return lax.ppermute(value, ('ctx', 'head'), pairs)  9.89 us
    pallas_call x19, Pallas kernels, call(): pl.pallas_call(kernel, name=name, out_shape=outs, in_specs=specs, out_spe...  9.03 us
    ppermute x12, waiting for transfers between devices, chain(): return lax.ppermute(value, ('ctx', 'head'), pairs)  5.89 us
  transfers between devices with their start and end apart: 22, of which 12 were waited for; matrix products, arithmetic and copies ran while one was open for 0% of the time, Pallas kernels for 12%

profile of v11, /device:TPU:0, one launch (start us, length us, event | category | flops | bytes accessed | tf_op | source)
XLA Modules:
  0.0 51.2 jit_solution(7500175761722018857)
XLA Ops:
  0.6 4.0 %collective-permute-start.4 = (bf16[256,256]{1,0:T(8,128)(2,1)}, bf16[256,256]{1,0:T(8,128)(2,1)S(1)}, u32[]{:S(2)}, u32[]{:S(2)}) collective-permute-start(bf16[256,256]{1,0:T(8,128)(2,1)} %f.1), channel_id=1, source_target_pairs={{0,6},{1,7},{2,4},{3,5},{4,2},{5,3},{6,0},{7,1},{8,14},{9,15},{10,... | collective-permute-start | bytes 393224 | tf_op jit(solution)/shard_map/ppermute | solution.py:395
  4.6 0.5 %collective-permute-start.1 = (bf16[256,256]{1,0:T(8,128)(2,1)}, bf16[256,256]{1,0:T(8,128)(2,1)S(1)}, u32[]{:S(2)}, u32[]{:S(2)}) collective-permute-start(bf16[256,256]{1,0:T(8,128)(2,1)} %f.1), channel_id=1, source_target_pairs={{0,2},{1,3},{2,0},{3,1},{4,6},{5,7},{6,4},{7,5},{8,10},{9,11},{10,... | collective-permute-start | bytes 393224 | tf_op jit(solution)/shard_map/ppermute | solution.py:395
  5.2 1.4 %begin.1 = (bf16[1024,384]{1,0:T(8,128)(2,1)S(1)}, bf16[256,256]{1,0:T(8,128)(2,1)S(1)}, f32[256,384]{1,0:T(8,128)S(1)}) custom-call(bf16[256,256]{1,0:T(8,128)(2,1)} %f.1, bf16[3,1024,256]{2,1,0:T(8,128)(2,1)} %bitcast.1), custom_call_target="tpu_custom_call" | custom-call | flops 100663296 | bytes 2097152 | tf_op jit(solution)/shard_map/begin/pallas_call | solution.py:419
  6.7 2.5 %collective-permute-done.4.two = bf16[256,256]{1,0:T(8,128)(2,1)S(1)} collective-permute-done((bf16[256,256]{1,0:T(8,128)(2,1)}, bf16[256,256]{1,0:T(8,128)(2,1)S(1)}, u32[]{:S(2)}, u32[]{:S(2)}) %collective-permute-start.4) | collective-permute-done | bytes 131104 | tf_op jit(solution)/shard_map/ppermute | solution.py:395
  9.2 2.1 %collective-permute-done.1.two = bf16[256,256]{1,0:T(8,128)(2,1)S(1)} collective-permute-done((bf16[256,256]{1,0:T(8,128)(2,1)}, bf16[256,256]{1,0:T(8,128)(2,1)S(1)}, u32[]{:S(2)}, u32[]{:S(2)}) %collective-permute-start.1) | collective-permute-done | bytes 131104 | tf_op jit(solution)/shard_map/ppermute | solution.py:395
  11.5 0.5 project_rest.1.before
  12.0 1.0 %collective-permute-done.3.other_late = bf16[512,256]{1,0:T(8,128)(2,1)S(1)} collective-permute-done((bf16[512,256]{1,0:T(8,128)(2,1)S(1)}, bf16[512,256]{1,0:T(8,128)(2,1)S(1)}, u32[]{:S(2)}, u32[]{:S(2)}) %collective-permute-start.3) | collective-permute-done | bytes 262176 | tf_op jit(solution)/shard_map/ppermute | solution.py:395
  13.2 1.6 %collective-permute-start.6 = (bf16[256,256]{1,0:T(8,128)(2,1)S(1)}, bf16[256,256]{1,0:T(8,128)(2,1)S(1)}, u32[]{:S(2)}, u32[]{:S(2)}) collective-permute-start(bf16[256,256]{1,0:T(8,128)(2,1)S(1)} %get-tuple-element.37.first_kv), channel_id=1, source_target_pairs={{0,8},{1,0},{2,10},{3,2},{4,12},{5,4},{6,14},{7,6},{8,16},{9,1},{1... | collective-permute-start | bytes 393224 | tf_op jit(solution)/shard_map/ppermute | solution.py:406
  14.9 1.5 %collective-permute-start.2 = (bf16[272,128]{1,0:T(8,128)(2,1)S(1)}, bf16[272,128]{1,0:T(8,128)(2,1)S(1)}, u32[]{:S(2)}, u32[]{:S(2)}) collective-permute-start(bf16[272,128]{1,0:T(8,128)(2,1)S(1)} %payload.1), channel_id=1, source_target_pairs={{0,4},{1,5},{2,6},{3,7},{4,0},{5,1},{6,2},{7,3},{8,12},{9,13},{10,... | collective-permute-start | bytes 208904 | tf_op jit(solution)/shard_map/ppermute | solution.py:395
  16.4 2.0 %collective-permute-start.8 = (bf16[256,256]{1,0:T(8,128)(2,1)S(1)}, bf16[256,256]{1,0:T(8,128)(2,1)S(1)}, u32[]{:S(2)}, u32[]{:S(2)}) collective-permute-start(bf16[256,256]{1,0:T(8,128)(2,1)S(1)} %get-tuple-element.38.second_kv), channel_id=1, source_target_pairs={{0,8},{1,0},{2,10},{3,2},{4,12},{5,4},{6,14},{7,6},{8,16},{9,1},{1... | collective-permute-start | bytes 393224 | tf_op jit(solution)/shard_map/ppermute | solution.py:406
  18.4 2.2 %collective-permute-start.10 = (bf16[256,256]{1,0:T(8,128)(2,1)S(1)}, bf16[256,256]{1,0:T(8,128)(2,1)S(1)}, u32[]{:S(2)}, u32[]{:S(2)}) collective-permute-start(bf16[256,256]{1,0:T(8,128)(2,1)S(1)} %collective-permute-done.6.u1), channel_id=1, source_target_pairs={{0,8},{1,0},{2,10},{3,2},{4,12},{5,4},{6,14},{7,6},{8,16},{9,1},{1... | collective-permute-start | bytes 393224 | tf_op jit(solution)/shard_map/ppermute | solution.py:406
  20.9 0.7 %links.1 = s32[5,9]{1,0:T(8,128)S(4)} custom-call(s32[2,9]{1,0:T(2,128)S(1)} %copy-done.1, s32[2,9]{1,0:T(2,128)S(1)} %slice_convert_fusion.other, bf16[512,128]{1,0:T(8,128)(2,1)S(1)} %project_q.1.q), custom_call_target="tpu_custom_call" | custom-call | bytes 2097152 | tf_op jit(solution)/shard_map/links/pallas_call | solution.py:419
  21.6 1.1 %collective-permute-done.9.d2 = bf16[256,256]{1,0:T(8,128)(2,1)S(1)} collective-permute-done((bf16[256,256]{1,0:T(8,128)(2,1)S(1)}, bf16[256,256]{1,0:T(8,128)(2,1)S(1)}, u32[]{:S(2)}, u32[]{:S(2)}) %collective-permute-start.9) | collective-permute-done | bytes 131104 | tf_op jit(solution)/shard_map/ppermute | solution.py:406
  22.7 0.9 %near_scores.1 = (bf16[1024,256]{1,0:T(8,128)(2,1)S(1)}, f32[3072,128]{1,0:T(8,128)S(1)}, f32[3072,128]{1,0:T(8,128)S(1)}, f32[96,128]{1,0:T(8,128)S(1)}) custom-call(s32[5,9]{1,0:T(8,128)S(4)} %links.1, bf16[512,128]{1,0:T(8,128)(2,1)S(1)} %project_q.1.q, bf16[256,256]{1,0:T(8,128)(2,1)S(1)} %get-tuple-element.37.first_kv, ...), custom_call_target="tpu_custom_call" | custom-call | flops 301989888 | bytes 2097152 | tf_op jit(solution)/shard_map/near_scores/pallas_call | solution.py:419
  23.7 1.9 %collective-permute-done.11.d3 = bf16[256,256]{1,0:T(8,128)(2,1)S(1)} collective-permute-done((bf16[256,256]{1,0:T(8,128)(2,1)S(1)}, bf16[256,256]{1,0:T(8,128)(2,1)S(1)}, u32[]{:S(2)}, u32[]{:S(2)}) %collective-permute-start.11) | collective-permute-done | bytes 131104 | tf_op jit(solution)/shard_map/ppermute | solution.py:406
  25.6 1.1 %far_grads.1 = (bf16[1536,256]{1,0:T(8,128)(2,1)S(1)}, f32[1536,256]{1,0:T(8,128)S(1)}, bf16[256,256]{1,0:T(8,128)(2,1)S(1)}, bf16[256,256]{1,0:T(8,128)(2,1)S(1)}, f32[64,128]{1,0:T(8,128)S(1)}) custom-call(s32[5,9]{1,0:T(8,128)S(4)} %links.1, bf16[1024,256]{1,0:T(8,128)(2,1)S(1)} %get-tuple-element.39.pairs, f32[96,128]{1,0:T(8,128)S(1)} %get-tuple-element.42.stats, ...), custom_call_target="tpu_custom_call" | custom-call | flops 301989888 | bytes 2097152 | tf_op jit(solution)/shard_map/far_grads/pallas_call | solution.py:419
  26.7 2.0 %collective-permute-start.16 = (bf16[256,256]{1,0:T(8,128)(2,1)S(1)}, bf16[256,256]{1,0:T(8,128)(2,1)S(1)}, u32[]{:S(2)}, u32[]{:S(2)}) collective-permute-start(bf16[256,256]{1,0:T(8,128)(2,1)S(1)} %get-tuple-element.57), channel_id=1, source_target_pairs={{0,8},{1,0},{2,10},{3,2},{4,12},{5,4},{6,14},{7,6},{8,16},{9,1},{1... | collective-permute-start | bytes 393224 | tf_op jit(solution)/shard_map/ppermute | solution.py:406
  28.7 0.9 %near_grads.1 = (bf16[3072,256]{1,0:T(8,128)(2,1)S(1)}, f32[256,256]{1,0:T(8,128)S(1)}, f32[256,256]{1,0:T(8,128)S(1)}, bf16[256,256]{1,0:T(8,128)(2,1)S(1)}, bf...) custom-call(s32[5,9]{1,0:T(8,128)S(4)} %links.1, ...), custom_call_target="tpu_custom_call" | custom-call | flops 301989888 | bytes 2097152 | tf_op jit(solution)/shard_map/near_grads/pallas_call | solution.py:419
  29.7 2.0 %collective-permute-start.13 = (bf16[256,256]{1,0:T(8,128)(2,1)S(1)}, bf16[256,256]{1,0:T(8,128)(2,1)S(1)}, u32[]{:S(2)}, u32[]{:S(2)}) collective-permute-start(bf16[256,256]{1,0:T(8,128)(2,1)S(1)} %get-tuple-element.48), channel_id=1, source_target_pairs={{0,8},{1,0},{2,10},{3,2},{4,12},{5,4},{6,14},{7,6},{8,16},{9,1},{1... | collective-permute-start | bytes 393224 | tf_op jit(solution)/shard_map/ppermute | solution.py:406
  31.7 1.1 %outputs.1 = (bf16[256,128]{1,0:T(8,128)(2,1)S(1)}, bf16[256,128]{1,0:T(8,128)(2,1)S(1)}, bf16[512,128]{1,0:T(8,128)(2,1)S(1)}) custom-call(s32[5,9]{1,0:T(8,128)S(4)} %links.1, bf16[3072,256]{1,0:T(8,128)(2,1)S(1)} %get-tuple-element.53.near_mixed, bf16[1536,256]{1,0:T(8,128)(2,1)S(1)} %get-tuple-element.54.far_mixed, ...), custom_call_target="tpu_custom_call" | custom-call | flops 301989888 | bytes 2097152 | tf_op jit(solution)/shard_map/outputs/pallas_call | solution.py:419
  32.9 2.1 %collective-permute-start.17 = (bf16[256,256]{1,0:T(8,128)(2,1)S(1)}, bf16[256,256]{1,0:T(8,128)(2,1)S(1)}, u32[]{:S(2)}, u32[]{:S(2)}) collective-permute-start(bf16[256,256]{1,0:T(8,128)(2,1)S(1)} %merge_u.1), channel_id=1, source_target_pairs={{0,8},{1,0},{2,10},{3,2},{4,12},{5,4},{6,14},{7,6},{8,16},{9,1},{1... | collective-permute-start | bytes 393224 | tf_op jit(solution)/shard_map/ppermute | solution.py:406
  35.0 0.5 %collective-permute-done.12.d = bf16[256,256]{1,0:T(8,128)(2,1)S(1)} collective-permute-done((bf16[256,256]{1,0:T(8,128)(2,1)S(1)}, bf16[256,256]{1,0:T(8,128)(2,1)S(1)}, u32[]{:S(2)}, u32[]{:S(2)}) %collective-permute-start.12) | collective-permute-done | bytes 131104 | tf_op jit(solution)/shard_map/ppermute | solution.py:406
  35.6 2.2 %collective-permute-done.15.from_d = bf16[256,256]{1,0:T(8,128)(2,1)S(1)} collective-permute-done((bf16[256,256]{1,0:T(8,128)(2,1)S(1)}, bf16[256,256]{1,0:T(8,128)(2,1)S(1)}, u32[]{:S(2)}, u32[]{:S(2)}) %collective-permute-start.15) | collective-permute-done | bytes 131104 | tf_op jit(solution)/shard_map/ppermute | solution.py:406
  37.8 0.5 spread_send.1
  38.4 0.5 spread_keep.1.keep
  38.9 1.4 %collective-permute-done.18.arrived = bf16[1024,256]{1,0:T(8,128)(2,1)S(1)} collective-permute-done((bf16[1024,256]{1,0:T(8,128)(2,1)S(1)}, bf16[1024,256]{1,0:T(8,128)(2,1)S(1)}, u32[]{:S(2)}, u32[]{:S(2)}) %collective-permute-start.18) | collective-permute-done | bytes 524320 | tf_op jit(solution)/shard_map/ppermute | solution.py:395
  40.4 2.0 %collective-permute-start.21 = (bf16[384,256]{1,0:T(8,128)(2,1)S(1)}, bf16[384,256]{1,0:T(8,128)(2,1)S(1)}, u32[]{:S(2)}, u32[]{:S(2)}) collective-permute-start(bf16[384,256]{1,0:T(8,128)(2,1)S(1)} %get-tuple-element.64), channel_id=1, source_target_pairs={{0,4},{1,5},{2,6},{3,7},{4,0},{5,1},{6,2},{7,3},{8,12},{9,13},{10,... | collective-permute-start | bytes 589832 | tf_op jit(solution)/shard_map/ppermute | solution.py:395
  42.4 1.0 %collective-permute-start.19 = (bf16[256,256]{1,0:T(8,128)(2,1)S(1)}, bf16[256,256]{1,0:T(8,128)(2,1)S(1)}, u32[]{:S(2)}, u32[]{:S(2)}) collective-permute-start(bf16[256,256]{1,0:T(8,128)(2,1)S(1)} %get-tuple-element.62), channel_id=1, source_target_pairs={{0,6},{1,7},{2,4},{3,5},{4,2},{5,3},{6,0},{7,1},{8,14},{9,15},{10,... | collective-permute-start | bytes 393224 | tf_op jit(solution)/shard_map/ppermute | solution.py:395
  43.4 0.5 %collective-permute-start.20 = (bf16[256,256]{1,0:T(8,128)(2,1)S(1)}, bf16[256,256]{1,0:T(8,128)(2,1)S(1)}, u32[]{:S(2)}, u32[]{:S(2)}) collective-permute-start(bf16[256,256]{1,0:T(8,128)(2,1)S(1)} %get-tuple-element.63), channel_id=1, source_target_pairs={{0,2},{1,3},{2,0},{3,1},{4,6},{5,7},{6,4},{7,5},{8,10},{9,11},{10,... | collective-permute-start | bytes 393224 | tf_op jit(solution)/shard_map/ppermute | solution.py:395
  43.9 5.7 %collective-permute-done.19.gd = bf16[256,256]{1,0:T(8,128)(2,1)S(1)} collective-permute-done((bf16[256,256]{1,0:T(8,128)(2,1)S(1)}, bf16[256,256]{1,0:T(8,128)(2,1)S(1)}, u32[]{:S(2)}, u32[]{:S(2)}) %collective-permute-start.19) | collective-permute-done | bytes 131104 | tf_op jit(solution)/shard_map/ppermute | solution.py:395
  49.7 0.6 %collective-permute-done.20.gx = bf16[256,256]{1,0:T(8,128)(2,1)S(1)} collective-permute-done((bf16[256,256]{1,0:T(8,128)(2,1)S(1)}, bf16[256,256]{1,0:T(8,128)(2,1)S(1)}, u32[]{:S(2)}, u32[]{:S(2)}) %collective-permute-start.20) | collective-permute-done | bytes 131104 | tf_op jit(solution)/shard_map/ppermute | solution.py:395
  50.4 0.8 %finish.1 = (bf16[256,256]{1,0:T(8,128)(2,1)}, bf16[256,256]{1,0:T(8,128)(2,1)}) custom-call(bf16[256,256]{1,0:T(8,128)(2,1)S(1)} %get-tuple-element.61.mine, bf16[256,256]{1,0:T(8,128)(2,1)S(1)} %collective-permute-done.19.gd, bf16[256,256]{1,0:T(8,128)(2,1)S(1)} %collective-permute-done.20.gx, bf16[384,256]{1,0:T(8,128)(2,1)S(1)} %collective-permute-done.21.from_y, ...), custom_call_target="tpu_custom_call" | custom-call | bytes 2097152 | tf_op jit(solution)/shard_map/finish/pallas_call | solution.py:419
  (38 shorter events, 1.5 us)
Async XLA Ops:
  0.6 8.5 %collective-permute-start.4 = (bf16[256,256]{1,0:T(8,128)(2,1)}, bf16[256,256]{1,0:T(8,128)(2,1)S(1)}, u32[]{:S(2)}, u32[]{:S(2)}) collective-permute-start(bf16[256,256]{1,0:T(8,128)(2,1)} %f.1), channel_id=1, source_target_pairs={{0,6},{1,7},{2,4},{3,5},{4,2},{5,3},{6,0},{7,1},{8,14},{9,15},{10,... | collective-permute-start | bytes 393224 | tf_op jit(solution)/shard_map/ppermute | solution.py:395
  4.6 6.8 %collective-permute-start.1 = (bf16[256,256]{1,0:T(8,128)(2,1)}, bf16[256,256]{1,0:T(8,128)(2,1)S(1)}, u32[]{:S(2)}, u32[]{:S(2)}) collective-permute-start(bf16[256,256]{1,0:T(8,128)(2,1)} %f.1), channel_id=1, source_target_pairs={{0,2},{1,3},{2,0},{3,1},{4,6},{5,7},{6,4},{7,5},{8,10},{9,11},{10,... | collective-permute-start | bytes 393224 | tf_op jit(solution)/shard_map/ppermute | solution.py:395
  5.1 6.2 %collective-permute-start = (bf16[256,256]{1,0:T(8,128)(2,1)}, bf16[256,256]{1,0:T(8,128)(2,1)S(1)}, u32[]{:S(2)}, u32[]{:S(2)}) collective-permute-start(bf16[256,256]{1,0:T(8,128)(2,1)} %f.1), channel_id=1, source_target_pairs={{0,4},{1,5},{2,6},{3,7},{4,0},{5,1},{6,2},{7,3},{8,12},{9,13},{10,... | collective-permute-start | bytes 393224 | tf_op jit(solution)/shard_map/ppermute | solution.py:395
  9.1 2.3 %collective-permute-start.5 = (bf16[512,256]{1,0:T(8,128)(2,1)S(1)}, bf16[512,256]{1,0:T(8,128)(2,1)S(1)}, u32[]{:S(2)}, u32[]{:S(2)}) collective-permute-start(bf16[512,256]{1,0:T(8,128)(2,1)S(1)} %pack_early.1.early), channel_id=1, source_target_pairs={{0,1},{1,0},{2,3},{3,2},{4,5},{5,4},{6,7},{7,6},{8,9},{9,8},{10,11... | collective-permute-start | bytes 786440 | tf_op jit(solution)/shard_map/ppermute | solution.py:395
  11.4 1.6 %collective-permute-start.3 = (bf16[512,256]{1,0:T(8,128)(2,1)S(1)}, bf16[512,256]{1,0:T(8,128)(2,1)S(1)}, u32[]{:S(2)}, u32[]{:S(2)}) collective-permute-start(bf16[512,256]{1,0:T(8,128)(2,1)S(1)} %pack_late.1.late), channel_id=1, source_target_pairs={{0,1},{1,0},{2,3},{3,2},{4,5},{5,4},{6,7},{7,6},{8,9},{9,8},{10,11... | collective-permute-start | bytes 786440 | tf_op jit(solution)/shard_map/ppermute | solution.py:395
  12.0 2.8 %copy-start.1 = (s32[2,9]{1,0:T(2,128)S(1)}, s32[2,9]{1,0:T(2,128)}, u32[]{:S(2)}) copy-start(s32[2,9]{1,0:T(2,128)} %own.1) | copy-start | bytes 220
  12.0 2.8 %copy-start = (bf16[256,256]{1,0:T(8,128)(2,1)S(1)}, bf16[256,256]{1,0:T(8,128)(2,1)}, u32[]{:S(2)}) copy-start(bf16[256,256]{1,0:T(8,128)(2,1)} %d_own.3) | copy-start | bytes 393220
  13.2 5.2 %collective-permute-start.6 = (bf16[256,256]{1,0:T(8,128)(2,1)S(1)}, bf16[256,256]{1,0:T(8,128)(2,1)S(1)}, u32[]{:S(2)}, u32[]{:S(2)}) collective-permute-start(bf16[256,256]{1,0:T(8,128)(2,1)S(1)} %get-tuple-element.37.first_kv), channel_id=1, source_target_pairs={{0,8},{1,0},{2,10},{3,2},{4,12},{5,4},{6,14},{7,6},{8,16},{9,1},{1... | collective-permute-start | bytes 393224 | tf_op jit(solution)/shard_map/ppermute | solution.py:406
  14.8 5.8 %collective-permute-start.7 = (bf16[256,256]{1,0:T(8,128)(2,1)S(1)}, bf16[256,256]{1,0:T(8,128)(2,1)S(1)}, u32[]{:S(2)}, u32[]{:S(2)}) collective-permute-start(bf16[256,256]{1,0:T(8,128)(2,1)S(1)} %get-tuple-element.38.second_kv), channel_id=1, source_target_pairs={{0,1},{1,9},{2,3},{3,11},{4,5},{5,13},{6,7},{7,15},{8,0},{9,17},{1... | collective-permute-start | bytes 393224 | tf_op jit(solution)/shard_map/ppermute | solution.py:406
  14.9 5.8 %collective-permute-start.2 = (bf16[272,128]{1,0:T(8,128)(2,1)S(1)}, bf16[272,128]{1,0:T(8,128)(2,1)S(1)}, u32[]{:S(2)}, u32[]{:S(2)}) collective-permute-start(bf16[272,128]{1,0:T(8,128)(2,1)S(1)} %payload.1), channel_id=1, source_target_pairs={{0,4},{1,5},{2,6},{3,7},{4,0},{5,1},{6,2},{7,3},{8,12},{9,13},{10,... | collective-permute-start | bytes 208904 | tf_op jit(solution)/shard_map/ppermute | solution.py:395
  16.4 6.3 %collective-permute-start.9 = (bf16[256,256]{1,0:T(8,128)(2,1)S(1)}, bf16[256,256]{1,0:T(8,128)(2,1)S(1)}, u32[]{:S(2)}, u32[]{:S(2)}) collective-permute-start(bf16[256,256]{1,0:T(8,128)(2,1)S(1)} %get-tuple-element.37.first_kv), channel_id=1, source_target_pairs={{0,1},{1,9},{2,3},{3,11},{4,5},{5,13},{6,7},{7,15},{8,0},{9,17},{1... | collective-permute-start | bytes 393224 | tf_op jit(solution)/shard_map/ppermute | solution.py:406
  16.4 6.3 %collective-permute-start.8 = (bf16[256,256]{1,0:T(8,128)(2,1)S(1)}, bf16[256,256]{1,0:T(8,128)(2,1)S(1)}, u32[]{:S(2)}, u32[]{:S(2)}) collective-permute-start(bf16[256,256]{1,0:T(8,128)(2,1)S(1)} %get-tuple-element.38.second_kv), channel_id=1, source_target_pairs={{0,8},{1,0},{2,10},{3,2},{4,12},{5,4},{6,14},{7,6},{8,16},{9,1},{1... | collective-permute-start | bytes 393224 | tf_op jit(solution)/shard_map/ppermute | solution.py:406
  18.4 5.3 %collective-permute-start.10 = (bf16[256,256]{1,0:T(8,128)(2,1)S(1)}, bf16[256,256]{1,0:T(8,128)(2,1)S(1)}, u32[]{:S(2)}, u32[]{:S(2)}) collective-permute-start(bf16[256,256]{1,0:T(8,128)(2,1)S(1)} %collective-permute-done.6.u1), channel_id=1, source_target_pairs={{0,8},{1,0},{2,10},{3,2},{4,12},{5,4},{6,14},{7,6},{8,16},{9,1},{1... | collective-permute-start | bytes 393224 | tf_op jit(solution)/shard_map/ppermute | solution.py:406
  20.7 5.0 %collective-permute-start.11 = (bf16[256,256]{1,0:T(8,128)(2,1)S(1)}, bf16[256,256]{1,0:T(8,128)(2,1)S(1)}, u32[]{:S(2)}, u32[]{:S(2)}) collective-permute-start(bf16[256,256]{1,0:T(8,128)(2,1)S(1)} %collective-permute-done.7.d1), channel_id=1, source_target_pairs={{0,1},{1,9},{2,3},{3,11},{4,5},{5,13},{6,7},{7,15},{8,0},{9,17},{1... | collective-permute-start | bytes 393224 | tf_op jit(solution)/shard_map/ppermute | solution.py:406
  26.7 6.1 %collective-permute-start.14 = (bf16[256,256]{1,0:T(8,128)(2,1)S(1)}, bf16[256,256]{1,0:T(8,128)(2,1)S(1)}, u32[]{:S(2)}, u32[]{:S(2)}) collective-permute-start(bf16[256,256]{1,0:T(8,128)(2,1)S(1)} %get-tuple-element.52), channel_id=1, source_target_pairs={{0,1},{1,9},{2,3},{3,11},{4,5},{5,13},{6,7},{7,15},{8,0},{9,17},{1... | collective-permute-start | bytes 393224 | tf_op jit(solution)/shard_map/ppermute | solution.py:406
  26.7 6.1 %collective-permute-start.16 = (bf16[256,256]{1,0:T(8,128)(2,1)S(1)}, bf16[256,256]{1,0:T(8,128)(2,1)S(1)}, u32[]{:S(2)}, u32[]{:S(2)}) collective-permute-start(bf16[256,256]{1,0:T(8,128)(2,1)S(1)} %get-tuple-element.57), channel_id=1, source_target_pairs={{0,8},{1,0},{2,10},{3,2},{4,12},{5,4},{6,14},{7,6},{8,16},{9,1},{1... | collective-permute-start | bytes 393224 | tf_op jit(solution)/shard_map/ppermute | solution.py:406
  29.6 5.9 %collective-permute-start.12 = (bf16[256,256]{1,0:T(8,128)(2,1)S(1)}, bf16[256,256]{1,0:T(8,128)(2,1)S(1)}, u32[]{:S(2)}, u32[]{:S(2)}) collective-permute-start(bf16[256,256]{1,0:T(8,128)(2,1)S(1)} %get-tuple-element.47), channel_id=1, source_target_pairs={{0,1},{1,9},{2,3},{3,11},{4,5},{5,13},{6,7},{7,15},{8,0},{9,17},{1... | collective-permute-start | bytes 393224 | tf_op jit(solution)/shard_map/ppermute | solution.py:406
  29.7 5.8 %collective-permute-start.13 = (bf16[256,256]{1,0:T(8,128)(2,1)S(1)}, bf16[256,256]{1,0:T(8,128)(2,1)S(1)}, u32[]{:S(2)}, u32[]{:S(2)}) collective-permute-start(bf16[256,256]{1,0:T(8,128)(2,1)S(1)} %get-tuple-element.48), channel_id=1, source_target_pairs={{0,8},{1,0},{2,10},{3,2},{4,12},{5,4},{6,14},{7,6},{8,16},{9,1},{1... | collective-permute-start | bytes 393224 | tf_op jit(solution)/shard_map/ppermute | solution.py:406
  32.8 5.0 %collective-permute-start.15 = (bf16[256,256]{1,0:T(8,128)(2,1)S(1)}, bf16[256,256]{1,0:T(8,128)(2,1)S(1)}, u32[]{:S(2)}, u32[]{:S(2)}) collective-permute-start(bf16[256,256]{1,0:T(8,128)(2,1)S(1)} %merge_d.1), channel_id=1, source_target_pairs={{0,1},{1,9},{2,3},{3,11},{4,5},{5,13},{6,7},{7,15},{8,0},{9,17},{1... | collective-permute-start | bytes 393224 | tf_op jit(solution)/shard_map/ppermute | solution.py:406
  32.9 4.9 %collective-permute-start.17 = (bf16[256,256]{1,0:T(8,128)(2,1)S(1)}, bf16[256,256]{1,0:T(8,128)(2,1)S(1)}, u32[]{:S(2)}, u32[]{:S(2)}) collective-permute-start(bf16[256,256]{1,0:T(8,128)(2,1)S(1)} %merge_u.1), channel_id=1, source_target_pairs={{0,8},{1,0},{2,10},{3,2},{4,12},{5,4},{6,14},{7,6},{8,16},{9,1},{1... | collective-permute-start | bytes 393224 | tf_op jit(solution)/shard_map/ppermute | solution.py:406
  38.3 2.0 %collective-permute-start.18 = (bf16[1024,256]{1,0:T(8,128)(2,1)S(1)}, bf16[1024,256]{1,0:T(8,128)(2,1)S(1)}, u32[]{:S(2)}, u32[]{:S(2)}) collective-permute-start(bf16[1024,256]{1,0:T(8,128)(2,1)S(1)} %get-tuple-element.59), channel_id=1, source_target_pairs={{0,1},{1,0},{2,3},{3,2},{4,5},{5,4},{6,7},{7,6},{8,9},{9,8},{10,11... | collective-permute-start | bytes 1572872 | tf_op jit(solution)/shard_map/ppermute | solution.py:395
  40.4 10.0 %collective-permute-start.21 = (bf16[384,256]{1,0:T(8,128)(2,1)S(1)}, bf16[384,256]{1,0:T(8,128)(2,1)S(1)}, u32[]{:S(2)}, u32[]{:S(2)}) collective-permute-start(bf16[384,256]{1,0:T(8,128)(2,1)S(1)} %get-tuple-element.64), channel_id=1, source_target_pairs={{0,4},{1,5},{2,6},{3,7},{4,0},{5,1},{6,2},{7,3},{8,12},{9,13},{10,... | collective-permute-start | bytes 589832 | tf_op jit(solution)/shard_map/ppermute | solution.py:395
  42.4 7.3 %collective-permute-start.19 = (bf16[256,256]{1,0:T(8,128)(2,1)S(1)}, bf16[256,256]{1,0:T(8,128)(2,1)S(1)}, u32[]{:S(2)}, u32[]{:S(2)}) collective-permute-start(bf16[256,256]{1,0:T(8,128)(2,1)S(1)} %get-tuple-element.62), channel_id=1, source_target_pairs={{0,6},{1,7},{2,4},{3,5},{4,2},{5,3},{6,0},{7,1},{8,14},{9,15},{10,... | collective-permute-start | bytes 393224 | tf_op jit(solution)/shard_map/ppermute | solution.py:395
  43.4 6.9 %collective-permute-start.20 = (bf16[256,256]{1,0:T(8,128)(2,1)S(1)}, bf16[256,256]{1,0:T(8,128)(2,1)S(1)}, u32[]{:S(2)}, u32[]{:S(2)}) collective-permute-start(bf16[256,256]{1,0:T(8,128)(2,1)S(1)} %get-tuple-element.63), channel_id=1, source_target_pairs={{0,2},{1,3},{2,0},{3,1},{4,6},{5,7},{6,4},{7,5},{8,10},{9,11},{10,... | collective-permute-start | bytes 393224 | tf_op jit(solution)/shard_map/ppermute | solution.py:395

commit v12 on v11

--- a/solution.py
+++ b/solution.py
@@ -106,12 +106,18 @@
     second_out[...] = second_own[...] + d[...].astype(F32)
 
 
-def chip_sum_kernel(keep, arrived, att_other, mine, to_x, to_y, to_d):
-    for index, target in enumerate((mine, to_x, to_y, to_d)):
-        rows = slice(index * HALF, (index + 1) * HALF)
-        target[:HALF, :] = (keep[rows, :].astype(F32) + arrived[rows, :].astype(F32)).astype(BF)
+def chip_sum_near_kernel(keep, arrived, att_other, mine, to_y):
+    total = (keep[...].astype(F32) + arrived[...].astype(F32)).astype(BF)
+    mine[...] = total[:HALF]
+    to_y[:HALF, :] = total[HALF:]
     for half in range(2):
         to_y[HALF:, half * HD : (half + 1) * HD] = att_other[half * BLK : (half + 1) * BLK, :]
+
+
+def chip_sum_far_kernel(keep, arrived, to_x, to_d):
+    total = (keep[...].astype(F32) + arrived[...].astype(F32)).astype(BF)
+    to_x[...] = total[:HALF]
+    to_d[...] = total[HALF:]
 
 
 def finish_kernel(mine, gd, gx, from_y, att_own, attended, grad_features):
@@ -360,15 +366,12 @@
 
 
 def spread(grads, w_mine, side, head, target):
-    for step in range(2):
-        out = dot(grads, weight_rows(w_mine, head ^ (2 * step), 2 * HD), ((1,), (1,))).astype(BF)
-        for group in range(2):
-            index = 2 * group + step
-            part = jnp.where(side == group, out[:HALF], out[HALF:])
-            target[index * HALF : (index + 1) * HALF, :] = part
-
-
-def spread_send_kernel(first_own, second_own, from_d, from_u, dq, w_mine, send, grads):
+    out = dot(grads, weight_rows(w_mine, head, 2 * HD), ((1,), (1,))).astype(BF)
+    target[:HALF, :] = jnp.where(side == 0, out[:HALF], out[HALF:])
+    target[HALF:, :] = jnp.where(side == 0, out[HALF:], out[:HALF])
+
+
+def spread_near_kernel(first_own, second_own, from_d, from_u, dq, w_mine, send, grads):
     side, flip, _, head = position()
     first = first_own[...] + from_d[...].astype(F32)
     second = second_own[...] + from_u[...].astype(F32)
@@ -378,9 +381,15 @@
     spread(grads[...], w_mine, side, head ^ 1, send)
 
 
-def spread_keep_kernel(grads, w_mine, keep):
+def spread_far_kernel(grads, w_mine, send):
     side, _, _, head = position()
-    spread(grads[...], w_mine, side, head, keep)
+    spread(grads[...], w_mine, side, head ^ 3, send)
+
+
+def spread_keep_kernel(grads, w_mine, near, far):
+    side, _, _, head = position()
+    spread(grads[...], w_mine, side, head, near)
+    spread(grads[...], w_mine, side, head ^ 2, far)
 
 
 def body(features, w_qkv, block_links, d_out, n_ctx, n_head):
@@ -539,26 +548,29 @@
     first_own, second_own = call(
         gather_kernel, "gather", [held(HALF, 2 * HD, F32)] * 2, (first_own, second_own, d2_back, u2_back), 4, 0
     )
-    send, grads = call(
-        spread_send_kernel,
-        "spread_send",
-        [out(4 * HALF, 2 * HD), held(ROWS, 3 * HD)],
+    near_send, grads = call(
+        spread_near_kernel,
+        "spread_near",
+        [out(ROWS, 2 * HD), held(ROWS, 3 * HD)],
         (first_own, second_own, from_d, from_u, dq, w_mine),
         4,
         product,
     )
-    (keep,) = call(spread_keep_kernel, "spread_keep", [held(4 * HALF, 2 * HD)], (grads, w_mine), 4, product)
-    arrived = across(send, 0, 1)
-    mine, to_x, to_y, to_d = call(
-        chip_sum_kernel,
-        "chip_sum",
-        [out(HALF, 2 * HD)] * 2 + [out(HALF + BLK, 2 * HD), out(HALF, 2 * HD)],
-        (keep, arrived, att_other),
+    near_arrived = across(near_send, 0, 1)
+    (far_send,) = call(spread_far_kernel, "spread_far", [out(ROWS, 2 * HD)], (grads, w_mine), 4, product)
+    far_arrived = across(far_send, 0, 1)
+    near, far = call(spread_keep_kernel, "spread_keep", [held(ROWS, 2 * HD)] * 2, (grads, w_mine), 4, product)
+    mine, to_y = call(
+        chip_sum_near_kernel,
+        "chip_sum_near",
+        [out(HALF, 2 * HD), out(HALF + BLK, 2 * HD)],
+        (near, near_arrived, att_other),
         4,
         0,
     )
+    gy = across(to_y, 1, 0)
+    to_x, to_d = call(chip_sum_far_kernel, "chip_sum_far", [out(HALF, 2 * HD)] * 2, (far, far_arrived), 4, 0)
     gd = across(to_d, 1, 2)
-    gy = across(to_y, 1, 0)
     gx = across(to_x, 0, 2)
     attended, grad_features = call(
         finish_kernel, "finish", [out(HALF, 2 * HD)] * 2, (mine, gd, gx, gy, att_own), 4, 0

time: 51.3 us -> 51.3 us (level)
  waiting for transfers between devices: 19.3 us -> 18.2 us
  starting transfers between devices: 21.9 us -> 22.9 us
    ppermute x10 -> x11, waiting for transfers between devices: 13.4 us -> 12.3 us  [across(): return lax.ppermute(value, ('ctx', 'head'), pairs)]
    ppermute x10 -> x11, starting transfers between devices: 9.89 us -> 10.8 us  [across(): return lax.ppermute(value, ('ctx', 'head'), pairs)]
    pallas_call x19 -> x21, Pallas kernels: 9.03 us -> 9.21 us  [call(): pl.pallas_call(kernel, name=name, out_shape=outs, in_specs=specs, out_spe...]
  transfers between devices with their start and end apart: 22 -> 23, of which waited for: 12 -> 11; matrix products, arithmetic and copies ran while one was open for 0% -> 0% of each run, Pallas kernels for 12% -> 13%
where the time goes in v12:
time: 51.3 us; the launch traced here: 51.2 us
  starting transfers between devices  22.9 us (45%)
  waiting for transfers between devices  18.2 us (35%)
  Pallas kernels  9.21 us (18%)
  between operations  0.88 us (2%)
    ppermute x11, waiting for transfers between devices, across(): return lax.ppermute(value, ('ctx', 'head'), pairs)  12.3 us
    ppermute x12, starting transfers between devices, chain(): return lax.ppermute(value, ('ctx', 'head'), pairs)  12 us
    ppermute x11, starting transfers between devices, across(): return lax.ppermute(value, ('ctx', 'head'), pairs)  10.8 us
    pallas_call x21, Pallas kernels, call(): pl.pallas_call(kernel, name=name, out_shape=outs, in_specs=specs, out_spe...  9.21 us
    ppermute x12, waiting for transfers between devices, chain(): return lax.ppermute(value, ('ctx', 'head'), pairs)  5.89 us
  transfers between devices with their start and end apart: 23, of which 11 were waited for; matrix products, arithmetic and copies ran while one was open for 0% of the time, Pallas kernels for 13%

profile of v12, /device:TPU:0, one launch (start us, length us, event | category | flops | bytes accessed | tf_op | source)
XLA Modules:
  0.0 51.2 jit_solution(6641470781958527551)
XLA Ops:
  0.6 4.0 %collective-permute-start.4 = (bf16[256,256]{1,0:T(8,128)(2,1)}, bf16[256,256]{1,0:T(8,128)(2,1)S(1)}, u32[]{:S(2)}, u32[]{:S(2)}) collective-permute-start(bf16[256,256]{1,0:T(8,128)(2,1)} %f.1), channel_id=1, source_target_pairs={{0,6},{1,7},{2,4},{3,5},{4,2},{5,3},{6,0},{7,1},{8,14},{9,15},{10,... | collective-permute-start | bytes 393224 | tf_op jit(solution)/shard_map/ppermute | solution.py:404
  4.6 0.5 %collective-permute-start.1 = (bf16[256,256]{1,0:T(8,128)(2,1)}, bf16[256,256]{1,0:T(8,128)(2,1)S(1)}, u32[]{:S(2)}, u32[]{:S(2)}) collective-permute-start(bf16[256,256]{1,0:T(8,128)(2,1)} %f.1), channel_id=1, source_target_pairs={{0,2},{1,3},{2,0},{3,1},{4,6},{5,7},{6,4},{7,5},{8,10},{9,11},{10,... | collective-permute-start | bytes 393224 | tf_op jit(solution)/shard_map/ppermute | solution.py:404
  5.2 1.4 %begin.1 = (bf16[1024,384]{1,0:T(8,128)(2,1)S(1)}, bf16[256,256]{1,0:T(8,128)(2,1)S(1)}, f32[256,384]{1,0:T(8,128)S(1)}) custom-call(bf16[256,256]{1,0:T(8,128)(2,1)} %f.1, bf16[3,1024,256]{2,1,0:T(8,128)(2,1)} %bitcast.1), custom_call_target="tpu_custom_call" | custom-call | flops 100663296 | bytes 2097152 | tf_op jit(solution)/shard_map/begin/pallas_call | solution.py:428
  6.7 2.5 %collective-permute-done.4.two = bf16[256,256]{1,0:T(8,128)(2,1)S(1)} collective-permute-done((bf16[256,256]{1,0:T(8,128)(2,1)}, bf16[256,256]{1,0:T(8,128)(2,1)S(1)}, u32[]{:S(2)}, u32[]{:S(2)}) %collective-permute-start.4) | collective-permute-done | bytes 131104 | tf_op jit(solution)/shard_map/ppermute | solution.py:404
  9.2 2.1 %collective-permute-done.1.two = bf16[256,256]{1,0:T(8,128)(2,1)S(1)} collective-permute-done((bf16[256,256]{1,0:T(8,128)(2,1)}, bf16[256,256]{1,0:T(8,128)(2,1)S(1)}, u32[]{:S(2)}, u32[]{:S(2)}) %collective-permute-start.1) | collective-permute-done | bytes 131104 | tf_op jit(solution)/shard_map/ppermute | solution.py:404
  11.5 0.5 project_rest.1.before
  12.0 1.0 %collective-permute-done.3.other_late = bf16[512,256]{1,0:T(8,128)(2,1)S(1)} collective-permute-done((bf16[512,256]{1,0:T(8,128)(2,1)S(1)}, bf16[512,256]{1,0:T(8,128)(2,1)S(1)}, u32[]{:S(2)}, u32[]{:S(2)}) %collective-permute-start.3) | collective-permute-done | bytes 262176 | tf_op jit(solution)/shard_map/ppermute | solution.py:404
  13.2 1.6 %collective-permute-start.6 = (bf16[256,256]{1,0:T(8,128)(2,1)S(1)}, bf16[256,256]{1,0:T(8,128)(2,1)S(1)}, u32[]{:S(2)}, u32[]{:S(2)}) collective-permute-start(bf16[256,256]{1,0:T(8,128)(2,1)S(1)} %get-tuple-element.39.first_kv), channel_id=1, source_target_pairs={{0,8},{1,0},{2,10},{3,2},{4,12},{5,4},{6,14},{7,6},{8,16},{9,1},{1... | collective-permute-start | bytes 393224 | tf_op jit(solution)/shard_map/ppermute | solution.py:415
  14.9 1.5 %collective-permute-start.2 = (bf16[272,128]{1,0:T(8,128)(2,1)S(1)}, bf16[272,128]{1,0:T(8,128)(2,1)S(1)}, u32[]{:S(2)}, u32[]{:S(2)}) collective-permute-start(bf16[272,128]{1,0:T(8,128)(2,1)S(1)} %payload.1), channel_id=1, source_target_pairs={{0,4},{1,5},{2,6},{3,7},{4,0},{5,1},{6,2},{7,3},{8,12},{9,13},{10,... | collective-permute-start | bytes 208904 | tf_op jit(solution)/shard_map/ppermute | solution.py:404
  16.4 2.0 %collective-permute-start.8 = (bf16[256,256]{1,0:T(8,128)(2,1)S(1)}, bf16[256,256]{1,0:T(8,128)(2,1)S(1)}, u32[]{:S(2)}, u32[]{:S(2)}) collective-permute-start(bf16[256,256]{1,0:T(8,128)(2,1)S(1)} %get-tuple-element.40.second_kv), channel_id=1, source_target_pairs={{0,8},{1,0},{2,10},{3,2},{4,12},{5,4},{6,14},{7,6},{8,16},{9,1},{1... | collective-permute-start | bytes 393224 | tf_op jit(solution)/shard_map/ppermute | solution.py:415
  18.4 2.2 %collective-permute-start.10 = (bf16[256,256]{1,0:T(8,128)(2,1)S(1)}, bf16[256,256]{1,0:T(8,128)(2,1)S(1)}, u32[]{:S(2)}, u32[]{:S(2)}) collective-permute-start(bf16[256,256]{1,0:T(8,128)(2,1)S(1)} %collective-permute-done.6.u1), channel_id=1, source_target_pairs={{0,8},{1,0},{2,10},{3,2},{4,12},{5,4},{6,14},{7,6},{8,16},{9,1},{1... | collective-permute-start | bytes 393224 | tf_op jit(solution)/shard_map/ppermute | solution.py:415
  20.9 0.7 %links.1 = s32[5,9]{1,0:T(8,128)S(4)} custom-call(s32[2,9]{1,0:T(2,128)S(1)} %copy-done.1, s32[2,9]{1,0:T(2,128)S(1)} %slice_convert_fusion.other, bf16[512,128]{1,0:T(8,128)(2,1)S(1)} %project_q.1.q), custom_call_target="tpu_custom_call" | custom-call | bytes 2097152 | tf_op jit(solution)/shard_map/links/pallas_call | solution.py:428
  21.6 1.1 %collective-permute-done.9.d2 = bf16[256,256]{1,0:T(8,128)(2,1)S(1)} collective-permute-done((bf16[256,256]{1,0:T(8,128)(2,1)S(1)}, bf16[256,256]{1,0:T(8,128)(2,1)S(1)}, u32[]{:S(2)}, u32[]{:S(2)}) %collective-permute-start.9) | collective-permute-done | bytes 131104 | tf_op jit(solution)/shard_map/ppermute | solution.py:415
  22.7 0.9 %near_scores.1 = (bf16[1024,256]{1,0:T(8,128)(2,1)S(1)}, f32[3072,128]{1,0:T(8,128)S(1)}, f32[3072,128]{1,0:T(8,128)S(1)}, f32[96,128]{1,0:T(8,128)S(1)}) custom-call(s32[5,9]{1,0:T(8,128)S(4)} %links.1, bf16[512,128]{1,0:T(8,128)(2,1)S(1)} %project_q.1.q, bf16[256,256]{1,0:T(8,128)(2,1)S(1)} %get-tuple-element.39.first_kv, ...), custom_call_target="tpu_custom_call" | custom-call | flops 301989888 | bytes 2097152 | tf_op jit(solution)/shard_map/near_scores/pallas_call | solution.py:428
  23.7 1.9 %collective-permute-done.11.d3 = bf16[256,256]{1,0:T(8,128)(2,1)S(1)} collective-permute-done((bf16[256,256]{1,0:T(8,128)(2,1)S(1)}, bf16[256,256]{1,0:T(8,128)(2,1)S(1)}, u32[]{:S(2)}, u32[]{:S(2)}) %collective-permute-start.11) | collective-permute-done | bytes 131104 | tf_op jit(solution)/shard_map/ppermute | solution.py:415
  25.6 1.1 %far_grads.1 = (bf16[1536,256]{1,0:T(8,128)(2,1)S(1)}, f32[1536,256]{1,0:T(8,128)S(1)}, bf16[256,256]{1,0:T(8,128)(2,1)S(1)}, bf16[256,256]{1,0:T(8,128)(2,1)S(1)}, f32[64,128]{1,0:T(8,128)S(1)}) custom-call(s32[5,9]{1,0:T(8,128)S(4)} %links.1, bf16[1024,256]{1,0:T(8,128)(2,1)S(1)} %get-tuple-element.41.pairs, f32[96,128]{1,0:T(8,128)S(1)} %get-tuple-element.44.stats, ...), custom_call_target="tpu_custom_call" | custom-call | flops 301989888 | bytes 2097152 | tf_op jit(solution)/shard_map/far_grads/pallas_call | solution.py:428
  26.7 2.0 %collective-permute-start.16 = (bf16[256,256]{1,0:T(8,128)(2,1)S(1)}, bf16[256,256]{1,0:T(8,128)(2,1)S(1)}, u32[]{:S(2)}, u32[]{:S(2)}) collective-permute-start(bf16[256,256]{1,0:T(8,128)(2,1)S(1)} %get-tuple-element.59), channel_id=1, source_target_pairs={{0,8},{1,0},{2,10},{3,2},{4,12},{5,4},{6,14},{7,6},{8,16},{9,1},{1... | collective-permute-start | bytes 393224 | tf_op jit(solution)/shard_map/ppermute | solution.py:415
  28.7 0.9 %near_grads.1 = (bf16[3072,256]{1,0:T(8,128)(2,1)S(1)}, f32[256,256]{1,0:T(8,128)S(1)}, f32[256,256]{1,0:T(8,128)S(1)}, bf16[256,256]{1,0:T(8,128)(2,1)S(1)}, bf...) custom-call(s32[5,9]{1,0:T(8,128)S(4)} %links.1, ...), custom_call_target="tpu_custom_call" | custom-call | flops 301989888 | bytes 2097152 | tf_op jit(solution)/shard_map/near_grads/pallas_call | solution.py:428
  29.7 2.0 %collective-permute-start.13 = (bf16[256,256]{1,0:T(8,128)(2,1)S(1)}, bf16[256,256]{1,0:T(8,128)(2,1)S(1)}, u32[]{:S(2)}, u32[]{:S(2)}) collective-permute-start(bf16[256,256]{1,0:T(8,128)(2,1)S(1)} %get-tuple-element.50), channel_id=1, source_target_pairs={{0,8},{1,0},{2,10},{3,2},{4,12},{5,4},{6,14},{7,6},{8,16},{9,1},{1... | collective-permute-start | bytes 393224 | tf_op jit(solution)/shard_map/ppermute | solution.py:415
  31.7 1.1 %outputs.1 = (bf16[256,128]{1,0:T(8,128)(2,1)S(1)}, bf16[256,128]{1,0:T(8,128)(2,1)S(1)}, bf16[512,128]{1,0:T(8,128)(2,1)S(1)}) custom-call(s32[5,9]{1,0:T(8,128)S(4)} %links.1, bf16[3072,256]{1,0:T(8,128)(2,1)S(1)} %get-tuple-element.55.near_mixed, bf16[1536,256]{1,0:T(8,128)(2,1)S(1)} %get-tuple-element.56.far_mixed, ...), custom_call_target="tpu_custom_call" | custom-call | flops 301989888 | bytes 2097152 | tf_op jit(solution)/shard_map/outputs/pallas_call | solution.py:428
  32.9 2.1 %collective-permute-start.17 = (bf16[256,256]{1,0:T(8,128)(2,1)S(1)}, bf16[256,256]{1,0:T(8,128)(2,1)S(1)}, u32[]{:S(2)}, u32[]{:S(2)}) collective-permute-start(bf16[256,256]{1,0:T(8,128)(2,1)S(1)} %merge_u.1), channel_id=1, source_target_pairs={{0,8},{1,0},{2,10},{3,2},{4,12},{5,4},{6,14},{7,6},{8,16},{9,1},{1... | collective-permute-start | bytes 393224 | tf_op jit(solution)/shard_map/ppermute | solution.py:415
  35.0 0.5 %collective-permute-done.12.d = bf16[256,256]{1,0:T(8,128)(2,1)S(1)} collective-permute-done((bf16[256,256]{1,0:T(8,128)(2,1)S(1)}, bf16[256,256]{1,0:T(8,128)(2,1)S(1)}, u32[]{:S(2)}, u32[]{:S(2)}) %collective-permute-start.12) | collective-permute-done | bytes 131104 | tf_op jit(solution)/shard_map/ppermute | solution.py:415
  35.6 2.2 %collective-permute-done.15.from_d = bf16[256,256]{1,0:T(8,128)(2,1)S(1)} collective-permute-done((bf16[256,256]{1,0:T(8,128)(2,1)S(1)}, bf16[256,256]{1,0:T(8,128)(2,1)S(1)}, u32[]{:S(2)}, u32[]{:S(2)}) %collective-permute-start.15) | collective-permute-done | bytes 131104 | tf_op jit(solution)/shard_map/ppermute | solution.py:415
  37.8 0.3 spread_near.1
  38.6 0.5 %collective-permute-start.19 = (bf16[512,256]{1,0:T(8,128)(2,1)S(1)}, bf16[512,256]{1,0:T(8,128)(2,1)S(1)}, u32[]{:S(2)}, u32[]{:S(2)}) collective-permute-start(bf16[512,256]{1,0:T(8,128)(2,1)S(1)} %spread_far.1), channel_id=1, source_target_pairs={{0,1},{1,0},{2,3},{3,2},{4,5},{5,4},{6,7},{7,6},{8,9},{9,8},{10,11... | collective-permute-start | bytes 786440 | tf_op jit(solution)/shard_map/ppermute | solution.py:404
  39.1 0.5 spread_keep.1
  39.8 2.0 %collective-permute-start.22 = (bf16[384,256]{1,0:T(8,128)(2,1)S(1)}, bf16[384,256]{1,0:T(8,128)(2,1)S(1)}, u32[]{:S(2)}, u32[]{:S(2)}) collective-permute-start(bf16[384,256]{1,0:T(8,128)(2,1)S(1)} %get-tuple-element.68), channel_id=1, source_target_pairs={{0,4},{1,5},{2,6},{3,7},{4,0},{5,1},{6,2},{7,3},{8,12},{9,13},{10,... | collective-permute-start | bytes 589832 | tf_op jit(solution)/shard_map/ppermute | solution.py:404
  41.9 1.4 %collective-permute-start.20 = (bf16[256,256]{1,0:T(8,128)(2,1)S(1)}, bf16[256,256]{1,0:T(8,128)(2,1)S(1)}, u32[]{:S(2)}, u32[]{:S(2)}) collective-permute-start(bf16[256,256]{1,0:T(8,128)(2,1)S(1)} %get-tuple-element.66), channel_id=1, source_target_pairs={{0,6},{1,7},{2,4},{3,5},{4,2},{5,3},{6,0},{7,1},{8,14},{9,15},{10,... | collective-permute-start | bytes 393224 | tf_op jit(solution)/shard_map/ppermute | solution.py:404
  43.3 0.5 %collective-permute-start.21 = (bf16[256,256]{1,0:T(8,128)(2,1)S(1)}, bf16[256,256]{1,0:T(8,128)(2,1)S(1)}, u32[]{:S(2)}, u32[]{:S(2)}) collective-permute-start(bf16[256,256]{1,0:T(8,128)(2,1)S(1)} %get-tuple-element.67), channel_id=1, source_target_pairs={{0,2},{1,3},{2,0},{3,1},{4,6},{5,7},{6,4},{7,5},{8,10},{9,11},{10,... | collective-permute-start | bytes 393224 | tf_op jit(solution)/shard_map/ppermute | solution.py:404
  43.8 5.4 %collective-permute-done.20.gd = bf16[256,256]{1,0:T(8,128)(2,1)S(1)} collective-permute-done((bf16[256,256]{1,0:T(8,128)(2,1)S(1)}, bf16[256,256]{1,0:T(8,128)(2,1)S(1)}, u32[]{:S(2)}, u32[]{:S(2)}) %collective-permute-start.20) | collective-permute-done | bytes 131104 | tf_op jit(solution)/shard_map/ppermute | solution.py:404
  49.2 1.2 %collective-permute-done.21.gx = bf16[256,256]{1,0:T(8,128)(2,1)S(1)} collective-permute-done((bf16[256,256]{1,0:T(8,128)(2,1)S(1)}, bf16[256,256]{1,0:T(8,128)(2,1)S(1)}, u32[]{:S(2)}, u32[]{:S(2)}) %collective-permute-start.21) | collective-permute-done | bytes 131104 | tf_op jit(solution)/shard_map/ppermute | solution.py:404
  50.4 0.8 %finish.1 = (bf16[256,256]{1,0:T(8,128)(2,1)}, bf16[256,256]{1,0:T(8,128)(2,1)}) custom-call(bf16[256,256]{1,0:T(8,128)(2,1)S(1)} %get-tuple-element.64.mine, bf16[256,256]{1,0:T(8,128)(2,1)S(1)} %collective-permute-done.20.gd, bf16[256,256]{1,0:T(8,128)(2,1)S(1)} %collective-permute-done.21.gx, bf16[384,256]{1,0:T(8,128)(2,1)S(1)} %collective-permute-done.22.from_y, ...), custom_call_target="tpu_custom_call" | custom-call | bytes 2097152 | tf_op jit(solution)/shard_map/finish/pallas_call | solution.py:428
  (42 shorter events, 1.9 us)
Async XLA Ops:
  0.6 8.5 %collective-permute-start.4 = (bf16[256,256]{1,0:T(8,128)(2,1)}, bf16[256,256]{1,0:T(8,128)(2,1)S(1)}, u32[]{:S(2)}, u32[]{:S(2)}) collective-permute-start(bf16[256,256]{1,0:T(8,128)(2,1)} %f.1), channel_id=1, source_target_pairs={{0,6},{1,7},{2,4},{3,5},{4,2},{5,3},{6,0},{7,1},{8,14},{9,15},{10,... | collective-permute-start | bytes 393224 | tf_op jit(solution)/shard_map/ppermute | solution.py:404
  4.6 6.8 %collective-permute-start.1 = (bf16[256,256]{1,0:T(8,128)(2,1)}, bf16[256,256]{1,0:T(8,128)(2,1)S(1)}, u32[]{:S(2)}, u32[]{:S(2)}) collective-permute-start(bf16[256,256]{1,0:T(8,128)(2,1)} %f.1), channel_id=1, source_target_pairs={{0,2},{1,3},{2,0},{3,1},{4,6},{5,7},{6,4},{7,5},{8,10},{9,11},{10,... | collective-permute-start | bytes 393224 | tf_op jit(solution)/shard_map/ppermute | solution.py:404
  5.1 6.2 %collective-permute-start = (bf16[256,256]{1,0:T(8,128)(2,1)}, bf16[256,256]{1,0:T(8,128)(2,1)S(1)}, u32[]{:S(2)}, u32[]{:S(2)}) collective-permute-start(bf16[256,256]{1,0:T(8,128)(2,1)} %f.1), channel_id=1, source_target_pairs={{0,4},{1,5},{2,6},{3,7},{4,0},{5,1},{6,2},{7,3},{8,12},{9,13},{10,... | collective-permute-start | bytes 393224 | tf_op jit(solution)/shard_map/ppermute | solution.py:404
  9.1 2.3 %collective-permute-start.5 = (bf16[512,256]{1,0:T(8,128)(2,1)S(1)}, bf16[512,256]{1,0:T(8,128)(2,1)S(1)}, u32[]{:S(2)}, u32[]{:S(2)}) collective-permute-start(bf16[512,256]{1,0:T(8,128)(2,1)S(1)} %pack_early.1.early), channel_id=1, source_target_pairs={{0,1},{1,0},{2,3},{3,2},{4,5},{5,4},{6,7},{7,6},{8,9},{9,8},{10,11... | collective-permute-start | bytes 786440 | tf_op jit(solution)/shard_map/ppermute | solution.py:404
  11.4 1.6 %collective-permute-start.3 = (bf16[512,256]{1,0:T(8,128)(2,1)S(1)}, bf16[512,256]{1,0:T(8,128)(2,1)S(1)}, u32[]{:S(2)}, u32[]{:S(2)}) collective-permute-start(bf16[512,256]{1,0:T(8,128)(2,1)S(1)} %pack_late.1.late), channel_id=1, source_target_pairs={{0,1},{1,0},{2,3},{3,2},{4,5},{5,4},{6,7},{7,6},{8,9},{9,8},{10,11... | collective-permute-start | bytes 786440 | tf_op jit(solution)/shard_map/ppermute | solution.py:404
  12.0 2.8 %copy-start.1 = (s32[2,9]{1,0:T(2,128)S(1)}, s32[2,9]{1,0:T(2,128)}, u32[]{:S(2)}) copy-start(s32[2,9]{1,0:T(2,128)} %own.1) | copy-start | bytes 220
  12.0 2.8 %copy-start = (bf16[256,256]{1,0:T(8,128)(2,1)S(1)}, bf16[256,256]{1,0:T(8,128)(2,1)}, u32[]{:S(2)}) copy-start(bf16[256,256]{1,0:T(8,128)(2,1)} %d_own.3) | copy-start | bytes 393220
  13.2 5.2 %collective-permute-start.6 = (bf16[256,256]{1,0:T(8,128)(2,1)S(1)}, bf16[256,256]{1,0:T(8,128)(2,1)S(1)}, u32[]{:S(2)}, u32[]{:S(2)}) collective-permute-start(bf16[256,256]{1,0:T(8,128)(2,1)S(1)} %get-tuple-element.39.first_kv), channel_id=1, source_target_pairs={{0,8},{1,0},{2,10},{3,2},{4,12},{5,4},{6,14},{7,6},{8,16},{9,1},{1... | collective-permute-start | bytes 393224 | tf_op jit(solution)/shard_map/ppermute | solution.py:415
  14.8 5.8 %collective-permute-start.7 = (bf16[256,256]{1,0:T(8,128)(2,1)S(1)}, bf16[256,256]{1,0:T(8,128)(2,1)S(1)}, u32[]{:S(2)}, u32[]{:S(2)}) collective-permute-start(bf16[256,256]{1,0:T(8,128)(2,1)S(1)} %get-tuple-element.40.second_kv), channel_id=1, source_target_pairs={{0,1},{1,9},{2,3},{3,11},{4,5},{5,13},{6,7},{7,15},{8,0},{9,17},{1... | collective-permute-start | bytes 393224 | tf_op jit(solution)/shard_map/ppermute | solution.py:415
  14.9 5.8 %collective-permute-start.2 = (bf16[272,128]{1,0:T(8,128)(2,1)S(1)}, bf16[272,128]{1,0:T(8,128)(2,1)S(1)}, u32[]{:S(2)}, u32[]{:S(2)}) collective-permute-start(bf16[272,128]{1,0:T(8,128)(2,1)S(1)} %payload.1), channel_id=1, source_target_pairs={{0,4},{1,5},{2,6},{3,7},{4,0},{5,1},{6,2},{7,3},{8,12},{9,13},{10,... | collective-permute-start | bytes 208904 | tf_op jit(solution)/shard_map/ppermute | solution.py:404
  16.4 6.3 %collective-permute-start.9 = (bf16[256,256]{1,0:T(8,128)(2,1)S(1)}, bf16[256,256]{1,0:T(8,128)(2,1)S(1)}, u32[]{:S(2)}, u32[]{:S(2)}) collective-permute-start(bf16[256,256]{1,0:T(8,128)(2,1)S(1)} %get-tuple-element.39.first_kv), channel_id=1, source_target_pairs={{0,1},{1,9},{2,3},{3,11},{4,5},{5,13},{6,7},{7,15},{8,0},{9,17},{1... | collective-permute-start | bytes 393224 | tf_op jit(solution)/shard_map/ppermute | solution.py:415
  16.4 6.3 %collective-permute-start.8 = (bf16[256,256]{1,0:T(8,128)(2,1)S(1)}, bf16[256,256]{1,0:T(8,128)(2,1)S(1)}, u32[]{:S(2)}, u32[]{:S(2)}) collective-permute-start(bf16[256,256]{1,0:T(8,128)(2,1)S(1)} %get-tuple-element.40.second_kv), channel_id=1, source_target_pairs={{0,8},{1,0},{2,10},{3,2},{4,12},{5,4},{6,14},{7,6},{8,16},{9,1},{1... | collective-permute-start | bytes 393224 | tf_op jit(solution)/shard_map/ppermute | solution.py:415
  18.4 5.3 %collective-permute-start.10 = (bf16[256,256]{1,0:T(8,128)(2,1)S(1)}, bf16[256,256]{1,0:T(8,128)(2,1)S(1)}, u32[]{:S(2)}, u32[]{:S(2)}) collective-permute-start(bf16[256,256]{1,0:T(8,128)(2,1)S(1)} %collective-permute-done.6.u1), channel_id=1, source_target_pairs={{0,8},{1,0},{2,10},{3,2},{4,12},{5,4},{6,14},{7,6},{8,16},{9,1},{1... | collective-permute-start | bytes 393224 | tf_op jit(solution)/shard_map/ppermute | solution.py:415
  20.7 5.0 %collective-permute-start.11 = (bf16[256,256]{1,0:T(8,128)(2,1)S(1)}, bf16[256,256]{1,0:T(8,128)(2,1)S(1)}, u32[]{:S(2)}, u32[]{:S(2)}) collective-permute-start(bf16[256,256]{1,0:T(8,128)(2,1)S(1)} %collective-permute-done.7.d1), channel_id=1, source_target_pairs={{0,1},{1,9},{2,3},{3,11},{4,5},{5,13},{6,7},{7,15},{8,0},{9,17},{1... | collective-permute-start | bytes 393224 | tf_op jit(solution)/shard_map/ppermute | solution.py:415
  26.7 6.1 %collective-permute-start.14 = (bf16[256,256]{1,0:T(8,128)(2,1)S(1)}, bf16[256,256]{1,0:T(8,128)(2,1)S(1)}, u32[]{:S(2)}, u32[]{:S(2)}) collective-permute-start(bf16[256,256]{1,0:T(8,128)(2,1)S(1)} %get-tuple-element.54), channel_id=1, source_target_pairs={{0,1},{1,9},{2,3},{3,11},{4,5},{5,13},{6,7},{7,15},{8,0},{9,17},{1... | collective-permute-start | bytes 393224 | tf_op jit(solution)/shard_map/ppermute | solution.py:415
  26.7 6.1 %collective-permute-start.16 = (bf16[256,256]{1,0:T(8,128)(2,1)S(1)}, bf16[256,256]{1,0:T(8,128)(2,1)S(1)}, u32[]{:S(2)}, u32[]{:S(2)}) collective-permute-start(bf16[256,256]{1,0:T(8,128)(2,1)S(1)} %get-tuple-element.59), channel_id=1, source_target_pairs={{0,8},{1,0},{2,10},{3,2},{4,12},{5,4},{6,14},{7,6},{8,16},{9,1},{1... | collective-permute-start | bytes 393224 | tf_op jit(solution)/shard_map/ppermute | solution.py:415
  29.6 5.9 %collective-permute-start.12 = (bf16[256,256]{1,0:T(8,128)(2,1)S(1)}, bf16[256,256]{1,0:T(8,128)(2,1)S(1)}, u32[]{:S(2)}, u32[]{:S(2)}) collective-permute-start(bf16[256,256]{1,0:T(8,128)(2,1)S(1)} %get-tuple-element.49), channel_id=1, source_target_pairs={{0,1},{1,9},{2,3},{3,11},{4,5},{5,13},{6,7},{7,15},{8,0},{9,17},{1... | collective-permute-start | bytes 393224 | tf_op jit(solution)/shard_map/ppermute | solution.py:415
  29.7 5.8 %collective-permute-start.13 = (bf16[256,256]{1,0:T(8,128)(2,1)S(1)}, bf16[256,256]{1,0:T(8,128)(2,1)S(1)}, u32[]{:S(2)}, u32[]{:S(2)}) collective-permute-start(bf16[256,256]{1,0:T(8,128)(2,1)S(1)} %get-tuple-element.50), channel_id=1, source_target_pairs={{0,8},{1,0},{2,10},{3,2},{4,12},{5,4},{6,14},{7,6},{8,16},{9,1},{1... | collective-permute-start | bytes 393224 | tf_op jit(solution)/shard_map/ppermute | solution.py:415
  32.8 5.0 %collective-permute-start.15 = (bf16[256,256]{1,0:T(8,128)(2,1)S(1)}, bf16[256,256]{1,0:T(8,128)(2,1)S(1)}, u32[]{:S(2)}, u32[]{:S(2)}) collective-permute-start(bf16[256,256]{1,0:T(8,128)(2,1)S(1)} %merge_d.1), channel_id=1, source_target_pairs={{0,1},{1,9},{2,3},{3,11},{4,5},{5,13},{6,7},{7,15},{8,0},{9,17},{1... | collective-permute-start | bytes 393224 | tf_op jit(solution)/shard_map/ppermute | solution.py:415
  32.9 4.9 %collective-permute-start.17 = (bf16[256,256]{1,0:T(8,128)(2,1)S(1)}, bf16[256,256]{1,0:T(8,128)(2,1)S(1)}, u32[]{:S(2)}, u32[]{:S(2)}) collective-permute-start(bf16[256,256]{1,0:T(8,128)(2,1)S(1)} %merge_u.1), channel_id=1, source_target_pairs={{0,8},{1,0},{2,10},{3,2},{4,12},{5,4},{6,14},{7,6},{8,16},{9,1},{1... | collective-permute-start | bytes 393224 | tf_op jit(solution)/shard_map/ppermute | solution.py:415
  38.1 1.6 %collective-permute-start.18 = (bf16[512,256]{1,0:T(8,128)(2,1)S(1)}, bf16[512,256]{1,0:T(8,128)(2,1)S(1)}, u32[]{:S(2)}, u32[]{:S(2)}) collective-permute-start(bf16[512,256]{1,0:T(8,128)(2,1)S(1)} %get-tuple-element.62), channel_id=1, source_target_pairs={{0,1},{1,0},{2,3},{3,2},{4,5},{5,4},{6,7},{7,6},{8,9},{9,8},{10,11... | collective-permute-start | bytes 786440 | tf_op jit(solution)/shard_map/ppermute | solution.py:404
  38.6 3.3 %collective-permute-start.19 = (bf16[512,256]{1,0:T(8,128)(2,1)S(1)}, bf16[512,256]{1,0:T(8,128)(2,1)S(1)}, u32[]{:S(2)}, u32[]{:S(2)}) collective-permute-start(bf16[512,256]{1,0:T(8,128)(2,1)S(1)} %spread_far.1), channel_id=1, source_target_pairs={{0,1},{1,0},{2,3},{3,2},{4,5},{5,4},{6,7},{7,6},{8,9},{9,8},{10,11... | collective-permute-start | bytes 786440 | tf_op jit(solution)/shard_map/ppermute | solution.py:404
  39.8 10.6 %collective-permute-start.22 = (bf16[384,256]{1,0:T(8,128)(2,1)S(1)}, bf16[384,256]{1,0:T(8,128)(2,1)S(1)}, u32[]{:S(2)}, u32[]{:S(2)}) collective-permute-start(bf16[384,256]{1,0:T(8,128)(2,1)S(1)} %get-tuple-element.68), channel_id=1, source_target_pairs={{0,4},{1,5},{2,6},{3,7},{4,0},{5,1},{6,2},{7,3},{8,12},{9,13},{10,... | collective-permute-start | bytes 589832 | tf_op jit(solution)/shard_map/ppermute | solution.py:404
  41.9 7.3 %collective-permute-start.20 = (bf16[256,256]{1,0:T(8,128)(2,1)S(1)}, bf16[256,256]{1,0:T(8,128)(2,1)S(1)}, u32[]{:S(2)}, u32[]{:S(2)}) collective-permute-start(bf16[256,256]{1,0:T(8,128)(2,1)S(1)} %get-tuple-element.66), channel_id=1, source_target_pairs={{0,6},{1,7},{2,4},{3,5},{4,2},{5,3},{6,0},{7,1},{8,14},{9,15},{10,... | collective-permute-start | bytes 393224 | tf_op jit(solution)/shard_map/ppermute | solution.py:404
  43.3 7.1 %collective-permute-start.21 = (bf16[256,256]{1,0:T(8,128)(2,1)S(1)}, bf16[256,256]{1,0:T(8,128)(2,1)S(1)}, u32[]{:S(2)}, u32[]{:S(2)}) collective-permute-start(bf16[256,256]{1,0:T(8,128)(2,1)S(1)} %get-tuple-element.67), channel_id=1, source_target_pairs={{0,2},{1,3},{2,0},{3,1},{4,6},{5,7},{6,4},{7,5},{8,10},{9,11},{10,... | collective-permute-start | bytes 393224 | tf_op jit(solution)/shard_map/ppermute | solution.py:404

commit v13 on v11

--- a/solution.py
+++ b/solution.py
@@ -272,56 +272,63 @@
             stats[8 * (3 * i + n) : 8 * (3 * i + n + 1), :] = jnp.broadcast_to(row, (8, BLK))
 
 
-def far_grads_kernel(
-    links, pairs, stats, u1, d1, u2, u3, d2, d3,
-    mixed, edges, far_u_out, far_d_out, scales, win,
-):
-    places = regions(position()[1])
-    for at, half in zip(places[2:], (u1, d1, u2, u3, d2, d3)):
-        win[pl.ds(at, HALF), :] = half[...]
-    edges[...] = jnp.zeros_like(edges)
+def far_grads_kernel(links, pairs, stats, near, middle, far, after, mixed, edge, far_out, scales, win, chain):
+    del after
+    flip = position()[1]
+    right = flip if chain == 0 else 1 - flip
+    at_far = pl.multiple_of(right * ROWS, HALF)
+    win[pl.ds(at_far, HALF), :] = far[...]
+    win[HALF : 2 * HALF, :] = middle[...]
+    win[pl.ds(pl.multiple_of(ROWS - right * ROWS, HALF), HALF), :] = near[...]
+    edge[...] = jnp.zeros_like(edge)
     scale = HD ** -0.5 * LOG2E
-    span = range(GROUP)
-    starts = [start_of(links, i, far_run(i)) for i in span]
-    pair = [pairs[2 * i * BLK : 2 * (i + 1) * BLK, :] for i in span]
-    near = [[stats[8 * (3 * i + n) : 8 * (3 * i + n) + 1, :] for n in range(3)] for i in span]
+    span = range(GROUP // 2)
+    query = [2 * right + k for k in span]
+    starts = [
+        pl.multiple_of(links[GROUP, 2 * query[k] + right] - right * NEAR_RIGHT, BLK) for k in span
+    ]
+    pair = [pairs[pl.ds(pl.multiple_of(2 * query[k] * BLK, 2 * BLK), 2 * BLK), :] for k in span]
+    known = [
+        [stats[pl.ds(pl.multiple_of(8 * (3 * query[k] + n), 8), 8), :][:1] for n in range(3)] for k in span
+    ]
     blocks = [
-        run_scores(links, win[pl.ds(starts[i], SPAN * BLK), :], pair[i], i, far_run(i)) for i in span
+        run_scores(links, win[pl.ds(starts[k], SPAN * BLK), :], pair[k], query[k], 1 + right) for k in span
     ]
-    largest = [jnp.maximum(near[i][0], largest_of(blocks[i])) for i in span]
-    found = [exponentials(blocks[i], largest[i]) for i in span]
+    largest = [jnp.maximum(known[k][0], largest_of(blocks[k])) for k in span]
+    found = [exponentials(blocks[k], largest[k]) for k in span]
     parts = []
-    for i in span:
-        terms, total, weighted = found[i]
-        near_scale = jnp.exp2((near[i][0] - largest[i]) * scale)
-        inverse = 1.0 / (total + near_scale * near[i][1])
-        row_dot = (weighted + near_scale * near[i][2]) * inverse
+    for k in span:
+        terms, total, weighted = found[k]
+        near_scale = jnp.exp2((known[k][0] - largest[k]) * scale)
+        inverse = 1.0 / (total + near_scale * known[k][1])
+        row_dot = (weighted + near_scale * known[k][2]) * inverse
         for n, row in enumerate((near_scale * inverse, row_dot)):
-            scales[8 * (2 * i + n) : 8 * (2 * i + n + 1), :] = jnp.broadcast_to(row, (8, BLK))
+            scales[8 * (2 * k + n) : 8 * (2 * k + n + 1), :] = jnp.broadcast_to(row, (8, BLK))
         parts.append(
-            jnp.concatenate([mix(term * inverse, block[1], row_dot) for term, block in zip(terms, blocks[i])], axis=0)
+            jnp.concatenate([mix(term * inverse, block[1], row_dot) for term, block in zip(terms, blocks[k])], axis=0)
         )
-    for i in span:
-        mixed[far_rows(i), :] = parts[i]
-        at = starts[i] if i < GROUP // 2 else starts[i] - ROWS
-        edges[pl.ds(pl.multiple_of(at, BLK), SPAN * BLK), :] += dot(parts[i], pair[i], ((1,), (0,)))
-    factor = side_factor()
-    flip = position()[1]
-    for target, left in ((far_u_out, flip), (far_d_out, 1 - flip)):
-        at = pl.multiple_of((1 - left) * (2 * OWN - HALF), HALF)
-        target[...] = (edges[pl.ds(at, HALF), :] * factor).astype(BF)
+    for k in span:
+        mixed[far_rows(k), :] = parts[k]
+        edge[pl.ds(starts[k], SPAN * BLK), :] += dot(parts[k], pair[k], ((1,), (0,)))
+    far_out[...] = (edge[pl.ds(at_far, HALF), :] * side_factor()).astype(BF)
+
+
+def by_side(i, from_u, from_d):
+    left = i < GROUP // 2
+    return jnp.where((position()[1] == 0) == left, from_u, from_d)
 
 
 def near_grads_kernel(
-    links, pairs, terms, prob_grads, scales, edges, mixed, first_own, second_own,
+    links, pairs, terms, prob_grads, u_scales, d_scales, u_edge, d_edge, mixed, first_own, second_own,
     u2_out, d2_out, u3_out, d3_out, acc,
 ):
-    acc[NEAR_LEFT:OWN, :] = edges[NEAR_LEFT:OWN, :]
+    acc[NEAR_LEFT:OWN, :] = by_side(0, u_edge[NEAR_LEFT:OWN, :], d_edge[NEAR_LEFT:OWN, :])
     acc[OWN:NEAR_RIGHT, :] = jnp.zeros((ROWS, 2 * HD), F32)
-    acc[NEAR_RIGHT:FAR_RIGHT, :] = edges[OWN : OWN + ROWS, :]
+    acc[NEAR_RIGHT:FAR_RIGHT, :] = by_side(GROUP - 1, u_edge[:ROWS, :], d_edge[:ROWS, :])
     for i in range(GROUP):
         pair = pairs[2 * i * BLK : 2 * (i + 1) * BLK, :]
-        scale, row_dot = (scales[8 * (2 * i + n) : 8 * (2 * i + n) + 1, :] for n in range(2))
+        at = [8 * (2 * (i % 2) + n) for n in range(2)]
+        scale, row_dot = (by_side(i, u_scales[r : r + 1, :], d_scales[r : r + 1, :]) for r in at)
         for index, t in enumerate(near_runs(i)):
             parts = []
             for j in range(SPAN):
@@ -339,7 +346,7 @@
 
 
 def outputs_kernel(
-    links, near_mixed, far_mixed, first_kv, second_kv, u1, d1, u2, u3, d2, d3,
+    links, near_mixed, u_mixed, d_mixed, first_kv, second_kv, u1, d1, u2, u3, d2, d3,
     att_own, att_other, dq_out, win, att,
 ):
     side, flip, _, _ = position()
@@ -348,7 +355,7 @@
     for i in range(GROUP):
         rows = slice(i * BLK, (i + 1) * BLK)
         out = dot(
-            far_mixed[far_rows(i), :], win[pl.ds(start_of(links, i, far_run(i)), SPAN * BLK), :], ((0,), (0,))
+            by_side(i, u_mixed[far_rows(i % 2), :], d_mixed[far_rows(i % 2), :]), win[pl.ds(start_of(links, i, far_run(i)), SPAN * BLK), :], ((0,), (0,))
         )
         for index, t in enumerate(near_runs(i)):
             part = near_mixed[near_rows(i, index, 0).start : near_rows(i, index, SPAN - 1).stop, :]
@@ -492,26 +499,29 @@
         attention,
         [window],
     )
-    far_mixed, edges, far_u_grad, far_d_grad, scales = call(
-        far_grads_kernel,
-        "far_grads",
-        [
-            held(GROUP * run, 2 * HD),
-            held(2 * OWN, 2 * HD, F32),
-            out(HALF, 2 * HD),
-            out(HALF, 2 * HD),
-            held(GROUP * 2 * 8, BLK, F32),
-        ],
-        (links, pairs, stats, u1, d1, u2, u3, d2, d3),
-        6,
-        attention,
-        [window],
-    )
+    def far_grads(near, middle, far, after, which, name):
+        return call(
+            functools.partial(far_grads_kernel, chain=which),
+            name,
+            [
+                held(GROUP // 2 * run, 2 * HD),
+                held(OWN, 2 * HD, F32),
+                out(HALF, 2 * HD),
+                held(GROUP * 8, BLK, F32),
+            ],
+            (links, pairs, stats, near, middle, far, after),
+            4,
+            attention // 2,
+            [pltpu.VMEM((OWN, 2 * HD), BF)],
+        )
+
+    u_mixed, u_edge, far_d_grad, u_scales = far_grads(u1, u2, u3, stats, 0, "far_grads_u")
+    d_mixed, d_edge, far_u_grad, d_scales = far_grads(d1, d2, d3, far_d_grad, 1, "far_grads_d")
     near_mixed, first_own, second_own, u2_grad, d2_grad, u3_grad, d3_grad = call(
         near_grads_kernel,
         "near_grads",
         [held(GROUP * 2 * run, 2 * HD)] + [held(HALF, 2 * HD, F32)] * 2 + [out(HALF, 2 * HD)] * 4,
-        (links, pairs, terms, prob_grads, scales, edges),
+        (links, pairs, terms, prob_grads, u_scales, d_scales, u_edge, d_edge),
         4,
         attention,
         [sums],
@@ -520,7 +530,7 @@
         outputs_kernel,
         "outputs",
         [out(HALF, HD), out(HALF, HD), held(ROWS, HD)],
-        (links, near_mixed, far_mixed, first, second, u1, d1, u2, u3, d2, d3),
+        (links, near_mixed, u_mixed, d_mixed, first, second, u1, d1, u2, u3, d2, d3),
         4,
         attention,
         [window, pltpu.VMEM((ROWS, HD), BF)],

time: 51.3 us -> 51.2 us (level)
    pallas_call x19 -> x20, Pallas kernels: 9.03 us -> 9.53 us  [call(): pl.pallas_call(kernel, name=name, out_shape=outs, in_specs=specs, out_spe...]
  transfers between devices with their start and end apart: 22 -> 22, of which waited for: 12 -> 12; matrix products, arithmetic and copies ran while one was open for 0% -> 0% of each run, Pallas kernels for 12% -> 15%
where the time goes in v13:
time: 51.2 us; the launch traced here: 51.1 us
  starting transfers between devices  21.7 us (42%)
  waiting for transfers between devices  18.9 us (37%)
  Pallas kernels  9.53 us (19%)
  between operations  0.87 us (2%)
    ppermute x10, waiting for transfers between devices, across(): return lax.ppermute(value, ('ctx', 'head'), pairs)  13.2 us
    ppermute x12, starting transfers between devices, chain(): return lax.ppermute(value, ('ctx', 'head'), pairs)  11.9 us
    ppermute x10, starting transfers between devices, across(): return lax.ppermute(value, ('ctx', 'head'), pairs)  9.89 us
    pallas_call x20, Pallas kernels, call(): pl.pallas_call(kernel, name=name, out_shape=outs, in_specs=specs, out_spe...  9.53 us
    ppermute x12, waiting for transfers between devices, chain(): return lax.ppermute(value, ('ctx', 'head'), pairs)  5.64 us
  transfers between devices with their start and end apart: 22, of which 12 were waited for; matrix products, arithmetic and copies ran while one was open for 0% of the time, Pallas kernels for 15%

profile of v13, /device:TPU:0, one launch (start us, length us, event | category | flops | bytes accessed | tf_op | source)
XLA Modules:
  0.0 51.1 jit_solution(1427138712087992239)
XLA Ops:
  0.6 4.0 %collective-permute-start.4 = (bf16[256,256]{1,0:T(8,128)(2,1)}, bf16[256,256]{1,0:T(8,128)(2,1)S(1)}, u32[]{:S(2)}, u32[]{:S(2)}) collective-permute-start(bf16[256,256]{1,0:T(8,128)(2,1)} %f.1), channel_id=1, source_target_pairs={{0,6},{1,7},{2,4},{3,5},{4,2},{5,3},{6,0},{7,1},{8,14},{9,15},{10,... | collective-permute-start | bytes 393224 | tf_op jit(solution)/shard_map/ppermute | solution.py:402
  4.6 0.5 %collective-permute-start.1 = (bf16[256,256]{1,0:T(8,128)(2,1)}, bf16[256,256]{1,0:T(8,128)(2,1)S(1)}, u32[]{:S(2)}, u32[]{:S(2)}) collective-permute-start(bf16[256,256]{1,0:T(8,128)(2,1)} %f.1), channel_id=1, source_target_pairs={{0,2},{1,3},{2,0},{3,1},{4,6},{5,7},{6,4},{7,5},{8,10},{9,11},{10,... | collective-permute-start | bytes 393224 | tf_op jit(solution)/shard_map/ppermute | solution.py:402
  5.2 1.4 %begin.1 = (bf16[1024,384]{1,0:T(8,128)(2,1)S(1)}, bf16[256,256]{1,0:T(8,128)(2,1)S(1)}, f32[256,384]{1,0:T(8,128)S(1)}) custom-call(bf16[256,256]{1,0:T(8,128)(2,1)} %f.1, bf16[3,1024,256]{2,1,0:T(8,128)(2,1)} %bitcast.1), custom_call_target="tpu_custom_call" | custom-call | flops 100663296 | bytes 2097152 | tf_op jit(solution)/shard_map/begin/pallas_call | solution.py:426
  6.7 2.5 %collective-permute-done.4.two = bf16[256,256]{1,0:T(8,128)(2,1)S(1)} collective-permute-done((bf16[256,256]{1,0:T(8,128)(2,1)}, bf16[256,256]{1,0:T(8,128)(2,1)S(1)}, u32[]{:S(2)}, u32[]{:S(2)}) %collective-permute-start.4) | collective-permute-done | bytes 131104 | tf_op jit(solution)/shard_map/ppermute | solution.py:402
  9.2 2.1 %collective-permute-done.1.two = bf16[256,256]{1,0:T(8,128)(2,1)S(1)} collective-permute-done((bf16[256,256]{1,0:T(8,128)(2,1)}, bf16[256,256]{1,0:T(8,128)(2,1)S(1)}, u32[]{:S(2)}, u32[]{:S(2)}) %collective-permute-start.1) | collective-permute-done | bytes 131104 | tf_op jit(solution)/shard_map/ppermute | solution.py:402
  11.5 0.5 project_rest.1.before
  12.0 1.0 %collective-permute-done.3.other_late = bf16[512,256]{1,0:T(8,128)(2,1)S(1)} collective-permute-done((bf16[512,256]{1,0:T(8,128)(2,1)S(1)}, bf16[512,256]{1,0:T(8,128)(2,1)S(1)}, u32[]{:S(2)}, u32[]{:S(2)}) %collective-permute-start.3) | collective-permute-done | bytes 262176 | tf_op jit(solution)/shard_map/ppermute | solution.py:402
  13.2 1.6 %collective-permute-start.6 = (bf16[256,256]{1,0:T(8,128)(2,1)S(1)}, bf16[256,256]{1,0:T(8,128)(2,1)S(1)}, u32[]{:S(2)}, u32[]{:S(2)}) collective-permute-start(bf16[256,256]{1,0:T(8,128)(2,1)S(1)} %get-tuple-element.40.first_kv), channel_id=1, source_target_pairs={{0,8},{1,0},{2,10},{3,2},{4,12},{5,4},{6,14},{7,6},{8,16},{9,1},{1... | collective-permute-start | bytes 393224 | tf_op jit(solution)/shard_map/ppermute | solution.py:413
  14.9 1.5 %collective-permute-start.2 = (bf16[272,128]{1,0:T(8,128)(2,1)S(1)}, bf16[272,128]{1,0:T(8,128)(2,1)S(1)}, u32[]{:S(2)}, u32[]{:S(2)}) collective-permute-start(bf16[272,128]{1,0:T(8,128)(2,1)S(1)} %payload.1), channel_id=1, source_target_pairs={{0,4},{1,5},{2,6},{3,7},{4,0},{5,1},{6,2},{7,3},{8,12},{9,13},{10,... | collective-permute-start | bytes 208904 | tf_op jit(solution)/shard_map/ppermute | solution.py:402
  16.4 2.0 %collective-permute-start.8 = (bf16[256,256]{1,0:T(8,128)(2,1)S(1)}, bf16[256,256]{1,0:T(8,128)(2,1)S(1)}, u32[]{:S(2)}, u32[]{:S(2)}) collective-permute-start(bf16[256,256]{1,0:T(8,128)(2,1)S(1)} %get-tuple-element.41.second_kv), channel_id=1, source_target_pairs={{0,8},{1,0},{2,10},{3,2},{4,12},{5,4},{6,14},{7,6},{8,16},{9,1},{1... | collective-permute-start | bytes 393224 | tf_op jit(solution)/shard_map/ppermute | solution.py:413
  18.4 2.2 %collective-permute-start.10 = (bf16[256,256]{1,0:T(8,128)(2,1)S(1)}, bf16[256,256]{1,0:T(8,128)(2,1)S(1)}, u32[]{:S(2)}, u32[]{:S(2)}) collective-permute-start(bf16[256,256]{1,0:T(8,128)(2,1)S(1)} %collective-permute-done.6.u1.near), channel_id=1, source_target_pairs={{0,8},{1,0},{2,10},{3,2},{4,12},{5,4},{6,14},{7,6},{8,16},{9,1},{1... | collective-permute-start | bytes 393224 | tf_op jit(solution)/shard_map/ppermute | solution.py:413
  20.9 0.7 %links.1 = s32[5,9]{1,0:T(8,128)S(4)} custom-call(s32[2,9]{1,0:T(2,128)S(1)} %copy-done.1, s32[2,9]{1,0:T(2,128)S(1)} %slice_convert_fusion.other, bf16[512,128]{1,0:T(8,128)(2,1)S(1)} %project_q.1.q), custom_call_target="tpu_custom_call" | custom-call | bytes 2097152 | tf_op jit(solution)/shard_map/links/pallas_call | solution.py:426
  21.6 1.1 %collective-permute-done.9.d2.middle = bf16[256,256]{1,0:T(8,128)(2,1)S(1)} collective-permute-done((bf16[256,256]{1,0:T(8,128)(2,1)S(1)}, bf16[256,256]{1,0:T(8,128)(2,1)S(1)}, u32[]{:S(2)}, u32[]{:S(2)}) %collective-permute-start.9) | collective-permute-done | bytes 131104 | tf_op jit(solution)/shard_map/ppermute | solution.py:413
  22.7 0.9 %near_scores.1 = (bf16[1024,256]{1,0:T(8,128)(2,1)S(1)}, f32[3072,128]{1,0:T(8,128)S(1)}, f32[3072,128]{1,0:T(8,128)S(1)}, f32[96,128]{1,0:T(8,128)S(1)}) custom-call(s32[5,9]{1,0:T(8,128)S(4)} %links.1, bf16[512,128]{1,0:T(8,128)(2,1)S(1)} %project_q.1.q, bf16[256,256]{1,0:T(8,128)(2,1)S(1)} %get-tuple-element.40.first_kv, ...), custom_call_target="tpu_custom_call" | custom-call | flops 301989888 | bytes 2097152 | tf_op jit(solution)/shard_map/near_scores/pallas_call | solution.py:426
  23.7 0.7 %far_grads_u.1 = (bf16[768,256]{1,0:T(8,128)(2,1)S(1)}, f32[768,256]{1,0:T(8,128)S(1)}, bf16[256,256]{1,0:T(8,128)(2,1)S(1)}, f32[32,128]{1,0:T(8,128)S(1)}) custom-call(s32[5,9]{1,0:T(8,128)S(4)} %links.1, bf16[1024,256]{1,0:T(8,128)(2,1)S(1)} %get-tuple-element.42.pairs, f32[96,128]{1,0:T(8,128)S(1)} %get-tuple-element.45.stats.after, ...), custom_call_target="tpu_custom_call" | custom-call | flops 150994944 | bytes 2097152 | tf_op jit(solution)/shard_map/far_grads_u/pallas_call | solution.py:426
  24.8 0.9 %collective-permute-done.11.far.d3 = bf16[256,256]{1,0:T(8,128)(2,1)S(1)} collective-permute-done((bf16[256,256]{1,0:T(8,128)(2,1)S(1)}, bf16[256,256]{1,0:T(8,128)(2,1)S(1)}, u32[]{:S(2)}, u32[]{:S(2)}) %collective-permute-start.11) | collective-permute-done | bytes 131104 | tf_op jit(solution)/shard_map/ppermute | solution.py:413
  25.6 0.8 %far_grads_d.1 = (bf16[768,256]{1,0:T(8,128)(2,1)S(1)}, f32[768,256]{1,0:T(8,128)S(1)}, bf16[256,256]{1,0:T(8,128)(2,1)S(1)}, f32[32,128]{1,0:T(8,128)S(1)}) custom-call(s32[5,9]{1,0:T(8,128)S(4)} %links.1, bf16[1024,256]{1,0:T(8,128)(2,1)S(1)} %get-tuple-element.42.pairs, f32[96,128]{1,0:T(8,128)S(1)} %get-tuple-element.45.stats.after, ...), custom_call_target="tpu_custom_call" | custom-call | flops 150994944 | bytes 2097152 | tf_op jit(solution)/shard_map/far_grads_d/pallas_call | solution.py:426
  26.4 1.6 %collective-permute-start.16 = (bf16[256,256]{1,0:T(8,128)(2,1)S(1)}, bf16[256,256]{1,0:T(8,128)(2,1)S(1)}, u32[]{:S(2)}, u32[]{:S(2)}) collective-permute-start(bf16[256,256]{1,0:T(8,128)(2,1)S(1)} %get-tuple-element.63), channel_id=1, source_target_pairs={{0,8},{1,0},{2,10},{3,2},{4,12},{5,4},{6,14},{7,6},{8,16},{9,1},{1... | collective-permute-start | bytes 393224 | tf_op jit(solution)/shard_map/ppermute | solution.py:413
  28.0 0.9 %near_grads.1 = (bf16[3072,256]{1,0:T(8,128)(2,1)S(1)}, f32[256,256]{1,0:T(8,128)S(1)}, f32[256,256]{1,0:T(8,128)S(1)}, bf16[256,256]{1,0:T(8,128)(2,1)S(1)}, bf...) custom-call(s32[5,9]{1,0:T(8,128)S(4)} %links.1, ...), custom_call_target="tpu_custom_call" | custom-call | flops 301989888 | bytes 2097152 | tf_op jit(solution)/shard_map/near_grads/pallas_call | solution.py:426
  29.0 2.0 %collective-permute-start.13 = (bf16[256,256]{1,0:T(8,128)(2,1)S(1)}, bf16[256,256]{1,0:T(8,128)(2,1)S(1)}, u32[]{:S(2)}, u32[]{:S(2)}) collective-permute-start(bf16[256,256]{1,0:T(8,128)(2,1)S(1)} %get-tuple-element.54), channel_id=1, source_target_pairs={{0,8},{1,0},{2,10},{3,2},{4,12},{5,4},{6,14},{7,6},{8,16},{9,1},{1... | collective-permute-start | bytes 393224 | tf_op jit(solution)/shard_map/ppermute | solution.py:413
  31.0 1.1 %outputs.1 = (bf16[256,128]{1,0:T(8,128)(2,1)S(1)}, bf16[256,128]{1,0:T(8,128)(2,1)S(1)}, bf16[512,128]{1,0:T(8,128)(2,1)S(1)}) custom-call(s32[5,9]{1,0:T(8,128)S(4)} %links.1, bf16[3072,256]{1,0:T(8,128)(2,1)S(1)} %get-tuple-element.58.near_mixed, bf16[768,256]{1,0:T(8,128)(2,1)S(1)} %get-tuple-element.59.u_mixed, ...), custom_call_target="tpu_custom_call" | custom-call | flops 301989888 | bytes 2097152 | tf_op jit(solution)/shard_map/outputs/pallas_call | solution.py:426
  32.2 2.0 %collective-permute-start.17 = (bf16[256,256]{1,0:T(8,128)(2,1)S(1)}, bf16[256,256]{1,0:T(8,128)(2,1)S(1)}, u32[]{:S(2)}, u32[]{:S(2)}) collective-permute-start(bf16[256,256]{1,0:T(8,128)(2,1)S(1)} %merge_u.1), channel_id=1, source_target_pairs={{0,8},{1,0},{2,10},{3,2},{4,12},{5,4},{6,14},{7,6},{8,16},{9,1},{1... | collective-permute-start | bytes 393224 | tf_op jit(solution)/shard_map/ppermute | solution.py:413
  34.3 0.9 %collective-permute-done.12.d = bf16[256,256]{1,0:T(8,128)(2,1)S(1)} collective-permute-done((bf16[256,256]{1,0:T(8,128)(2,1)S(1)}, bf16[256,256]{1,0:T(8,128)(2,1)S(1)}, u32[]{:S(2)}, u32[]{:S(2)}) %collective-permute-start.12) | collective-permute-done | bytes 131104 | tf_op jit(solution)/shard_map/ppermute | solution.py:413
  35.2 2.7 %collective-permute-done.15.from_d = bf16[256,256]{1,0:T(8,128)(2,1)S(1)} collective-permute-done((bf16[256,256]{1,0:T(8,128)(2,1)S(1)}, bf16[256,256]{1,0:T(8,128)(2,1)S(1)}, u32[]{:S(2)}, u32[]{:S(2)}) %collective-permute-start.15) | collective-permute-done | bytes 131104 | tf_op jit(solution)/shard_map/ppermute | solution.py:413
  37.9 0.5 spread_send.1
  38.9 1.4 %collective-permute-done.18.arrived = bf16[1024,256]{1,0:T(8,128)(2,1)S(1)} collective-permute-done((bf16[1024,256]{1,0:T(8,128)(2,1)S(1)}, bf16[1024,256]{1,0:T(8,128)(2,1)S(1)}, u32[]{:S(2)}, u32[]{:S(2)}) %collective-permute-start.18) | collective-permute-done | bytes 524320 | tf_op jit(solution)/shard_map/ppermute | solution.py:402
  40.5 1.3 %collective-permute-start.21 = (bf16[384,256]{1,0:T(8,128)(2,1)S(1)}, bf16[384,256]{1,0:T(8,128)(2,1)S(1)}, u32[]{:S(2)}, u32[]{:S(2)}) collective-permute-start(bf16[384,256]{1,0:T(8,128)(2,1)S(1)} %get-tuple-element.70), channel_id=1, source_target_pairs={{0,4},{1,5},{2,6},{3,7},{4,0},{5,1},{6,2},{7,3},{8,12},{9,13},{10,... | collective-permute-start | bytes 589832 | tf_op jit(solution)/shard_map/ppermute | solution.py:402
  41.7 1.8 %collective-permute-start.19 = (bf16[256,256]{1,0:T(8,128)(2,1)S(1)}, bf16[256,256]{1,0:T(8,128)(2,1)S(1)}, u32[]{:S(2)}, u32[]{:S(2)}) collective-permute-start(bf16[256,256]{1,0:T(8,128)(2,1)S(1)} %get-tuple-element.68), channel_id=1, source_target_pairs={{0,6},{1,7},{2,4},{3,5},{4,2},{5,3},{6,0},{7,1},{8,14},{9,15},{10,... | collective-permute-start | bytes 393224 | tf_op jit(solution)/shard_map/ppermute | solution.py:402
  43.5 0.5 %collective-permute-start.20 = (bf16[256,256]{1,0:T(8,128)(2,1)S(1)}, bf16[256,256]{1,0:T(8,128)(2,1)S(1)}, u32[]{:S(2)}, u32[]{:S(2)}) collective-permute-start(bf16[256,256]{1,0:T(8,128)(2,1)S(1)} %get-tuple-element.69), channel_id=1, source_target_pairs={{0,2},{1,3},{2,0},{3,1},{4,6},{5,7},{6,4},{7,5},{8,10},{9,11},{10,... | collective-permute-start | bytes 393224 | tf_op jit(solution)/shard_map/ppermute | solution.py:402
  44.0 5.0 %collective-permute-done.19.gd = bf16[256,256]{1,0:T(8,128)(2,1)S(1)} collective-permute-done((bf16[256,256]{1,0:T(8,128)(2,1)S(1)}, bf16[256,256]{1,0:T(8,128)(2,1)S(1)}, u32[]{:S(2)}, u32[]{:S(2)}) %collective-permute-start.19) | collective-permute-done | bytes 131104 | tf_op jit(solution)/shard_map/ppermute | solution.py:402
  49.0 1.1 %collective-permute-done.20.gx = bf16[256,256]{1,0:T(8,128)(2,1)S(1)} collective-permute-done((bf16[256,256]{1,0:T(8,128)(2,1)S(1)}, bf16[256,256]{1,0:T(8,128)(2,1)S(1)}, u32[]{:S(2)}, u32[]{:S(2)}) %collective-permute-start.20) | collective-permute-done | bytes 131104 | tf_op jit(solution)/shard_map/ppermute | solution.py:402
  50.3 0.8 %finish.1 = (bf16[256,256]{1,0:T(8,128)(2,1)}, bf16[256,256]{1,0:T(8,128)(2,1)}) custom-call(bf16[256,256]{1,0:T(8,128)(2,1)S(1)} %get-tuple-element.67.mine, bf16[256,256]{1,0:T(8,128)(2,1)S(1)} %collective-permute-done.19.gd, bf16[256,256]{1,0:T(8,128)(2,1)S(1)} %collective-permute-done.20.gx, bf16[384,256]{1,0:T(8,128)(2,1)S(1)} %collective-permute-done.21.from_y, ...), custom_call_target="tpu_custom_call" | custom-call | bytes 2097152 | tf_op jit(solution)/shard_map/finish/pallas_call | solution.py:426
  (39 shorter events, 2.3 us)
Async XLA Ops:
  0.6 8.5 %collective-permute-start.4 = (bf16[256,256]{1,0:T(8,128)(2,1)}, bf16[256,256]{1,0:T(8,128)(2,1)S(1)}, u32[]{:S(2)}, u32[]{:S(2)}) collective-permute-start(bf16[256,256]{1,0:T(8,128)(2,1)} %f.1), channel_id=1, source_target_pairs={{0,6},{1,7},{2,4},{3,5},{4,2},{5,3},{6,0},{7,1},{8,14},{9,15},{10,... | collective-permute-start | bytes 393224 | tf_op jit(solution)/shard_map/ppermute | solution.py:402
  4.6 6.8 %collective-permute-start.1 = (bf16[256,256]{1,0:T(8,128)(2,1)}, bf16[256,256]{1,0:T(8,128)(2,1)S(1)}, u32[]{:S(2)}, u32[]{:S(2)}) collective-permute-start(bf16[256,256]{1,0:T(8,128)(2,1)} %f.1), channel_id=1, source_target_pairs={{0,2},{1,3},{2,0},{3,1},{4,6},{5,7},{6,4},{7,5},{8,10},{9,11},{10,... | collective-permute-start | bytes 393224 | tf_op jit(solution)/shard_map/ppermute | solution.py:402
  5.1 6.2 %collective-permute-start = (bf16[256,256]{1,0:T(8,128)(2,1)}, bf16[256,256]{1,0:T(8,128)(2,1)S(1)}, u32[]{:S(2)}, u32[]{:S(2)}) collective-permute-start(bf16[256,256]{1,0:T(8,128)(2,1)} %f.1), channel_id=1, source_target_pairs={{0,4},{1,5},{2,6},{3,7},{4,0},{5,1},{6,2},{7,3},{8,12},{9,13},{10,... | collective-permute-start | bytes 393224 | tf_op jit(solution)/shard_map/ppermute | solution.py:402
  9.1 2.3 %collective-permute-start.5 = (bf16[512,256]{1,0:T(8,128)(2,1)S(1)}, bf16[512,256]{1,0:T(8,128)(2,1)S(1)}, u32[]{:S(2)}, u32[]{:S(2)}) collective-permute-start(bf16[512,256]{1,0:T(8,128)(2,1)S(1)} %pack_early.1.early), channel_id=1, source_target_pairs={{0,1},{1,0},{2,3},{3,2},{4,5},{5,4},{6,7},{7,6},{8,9},{9,8},{10,11... | collective-permute-start | bytes 786440 | tf_op jit(solution)/shard_map/ppermute | solution.py:402
  11.4 1.6 %collective-permute-start.3 = (bf16[512,256]{1,0:T(8,128)(2,1)S(1)}, bf16[512,256]{1,0:T(8,128)(2,1)S(1)}, u32[]{:S(2)}, u32[]{:S(2)}) collective-permute-start(bf16[512,256]{1,0:T(8,128)(2,1)S(1)} %pack_late.1.late), channel_id=1, source_target_pairs={{0,1},{1,0},{2,3},{3,2},{4,5},{5,4},{6,7},{7,6},{8,9},{9,8},{10,11... | collective-permute-start | bytes 786440 | tf_op jit(solution)/shard_map/ppermute | solution.py:402
  12.0 2.8 %copy-start.1 = (s32[2,9]{1,0:T(2,128)S(1)}, s32[2,9]{1,0:T(2,128)}, u32[]{:S(2)}) copy-start(s32[2,9]{1,0:T(2,128)} %own.1) | copy-start | bytes 220
  12.0 2.8 %copy-start = (bf16[256,256]{1,0:T(8,128)(2,1)S(1)}, bf16[256,256]{1,0:T(8,128)(2,1)}, u32[]{:S(2)}) copy-start(bf16[256,256]{1,0:T(8,128)(2,1)} %d_own.3) | copy-start | bytes 393220
  13.2 5.2 %collective-permute-start.6 = (bf16[256,256]{1,0:T(8,128)(2,1)S(1)}, bf16[256,256]{1,0:T(8,128)(2,1)S(1)}, u32[]{:S(2)}, u32[]{:S(2)}) collective-permute-start(bf16[256,256]{1,0:T(8,128)(2,1)S(1)} %get-tuple-element.40.first_kv), channel_id=1, source_target_pairs={{0,8},{1,0},{2,10},{3,2},{4,12},{5,4},{6,14},{7,6},{8,16},{9,1},{1... | collective-permute-start | bytes 393224 | tf_op jit(solution)/shard_map/ppermute | solution.py:413
  14.8 5.8 %collective-permute-start.7 = (bf16[256,256]{1,0:T(8,128)(2,1)S(1)}, bf16[256,256]{1,0:T(8,128)(2,1)S(1)}, u32[]{:S(2)}, u32[]{:S(2)}) collective-permute-start(bf16[256,256]{1,0:T(8,128)(2,1)S(1)} %get-tuple-element.41.second_kv), channel_id=1, source_target_pairs={{0,1},{1,9},{2,3},{3,11},{4,5},{5,13},{6,7},{7,15},{8,0},{9,17},{1... | collective-permute-start | bytes 393224 | tf_op jit(solution)/shard_map/ppermute | solution.py:413
  14.9 5.8 %collective-permute-start.2 = (bf16[272,128]{1,0:T(8,128)(2,1)S(1)}, bf16[272,128]{1,0:T(8,128)(2,1)S(1)}, u32[]{:S(2)}, u32[]{:S(2)}) collective-permute-start(bf16[272,128]{1,0:T(8,128)(2,1)S(1)} %payload.1), channel_id=1, source_target_pairs={{0,4},{1,5},{2,6},{3,7},{4,0},{5,1},{6,2},{7,3},{8,12},{9,13},{10,... | collective-permute-start | bytes 208904 | tf_op jit(solution)/shard_map/ppermute | solution.py:402
  16.4 6.3 %collective-permute-start.9 = (bf16[256,256]{1,0:T(8,128)(2,1)S(1)}, bf16[256,256]{1,0:T(8,128)(2,1)S(1)}, u32[]{:S(2)}, u32[]{:S(2)}) collective-permute-start(bf16[256,256]{1,0:T(8,128)(2,1)S(1)} %get-tuple-element.40.first_kv), channel_id=1, source_target_pairs={{0,1},{1,9},{2,3},{3,11},{4,5},{5,13},{6,7},{7,15},{8,0},{9,17},{1... | collective-permute-start | bytes 393224 | tf_op jit(solution)/shard_map/ppermute | solution.py:413
  16.4 6.3 %collective-permute-start.8 = (bf16[256,256]{1,0:T(8,128)(2,1)S(1)}, bf16[256,256]{1,0:T(8,128)(2,1)S(1)}, u32[]{:S(2)}, u32[]{:S(2)}) collective-permute-start(bf16[256,256]{1,0:T(8,128)(2,1)S(1)} %get-tuple-element.41.second_kv), channel_id=1, source_target_pairs={{0,8},{1,0},{2,10},{3,2},{4,12},{5,4},{6,14},{7,6},{8,16},{9,1},{1... | collective-permute-start | bytes 393224 | tf_op jit(solution)/shard_map/ppermute | solution.py:413
  18.4 5.3 %collective-permute-start.10 = (bf16[256,256]{1,0:T(8,128)(2,1)S(1)}, bf16[256,256]{1,0:T(8,128)(2,1)S(1)}, u32[]{:S(2)}, u32[]{:S(2)}) collective-permute-start(bf16[256,256]{1,0:T(8,128)(2,1)S(1)} %collective-permute-done.6.u1.near), channel_id=1, source_target_pairs={{0,8},{1,0},{2,10},{3,2},{4,12},{5,4},{6,14},{7,6},{8,16},{9,1},{1... | collective-permute-start | bytes 393224 | tf_op jit(solution)/shard_map/ppermute | solution.py:413
  20.7 5.0 %collective-permute-start.11 = (bf16[256,256]{1,0:T(8,128)(2,1)S(1)}, bf16[256,256]{1,0:T(8,128)(2,1)S(1)}, u32[]{:S(2)}, u32[]{:S(2)}) collective-permute-start(bf16[256,256]{1,0:T(8,128)(2,1)S(1)} %collective-permute-done.7.d1.near), channel_id=1, source_target_pairs={{0,1},{1,9},{2,3},{3,11},{4,5},{5,13},{6,7},{7,15},{8,0},{9,17},{1... | collective-permute-start | bytes 393224 | tf_op jit(solution)/shard_map/ppermute | solution.py:413
  24.5 7.6 %collective-permute-start.14 = (bf16[256,256]{1,0:T(8,128)(2,1)S(1)}, bf16[256,256]{1,0:T(8,128)(2,1)S(1)}, u32[]{:S(2)}, u32[]{:S(2)}) collective-permute-start(bf16[256,256]{1,0:T(8,128)(2,1)S(1)} %get-tuple-element.47.after), channel_id=1, source_target_pairs={{0,1},{1,9},{2,3},{3,11},{4,5},{5,13},{6,7},{7,15},{8,0},{9,17},{1... | collective-permute-start | bytes 393224 | tf_op jit(solution)/shard_map/ppermute | solution.py:413
  26.4 5.8 %collective-permute-start.16 = (bf16[256,256]{1,0:T(8,128)(2,1)S(1)}, bf16[256,256]{1,0:T(8,128)(2,1)S(1)}, u32[]{:S(2)}, u32[]{:S(2)}) collective-permute-start(bf16[256,256]{1,0:T(8,128)(2,1)S(1)} %get-tuple-element.63), channel_id=1, source_target_pairs={{0,8},{1,0},{2,10},{3,2},{4,12},{5,4},{6,14},{7,6},{8,16},{9,1},{1... | collective-permute-start | bytes 393224 | tf_op jit(solution)/shard_map/ppermute | solution.py:413
  29.0 6.2 %collective-permute-start.12 = (bf16[256,256]{1,0:T(8,128)(2,1)S(1)}, bf16[256,256]{1,0:T(8,128)(2,1)S(1)}, u32[]{:S(2)}, u32[]{:S(2)}) collective-permute-start(bf16[256,256]{1,0:T(8,128)(2,1)S(1)} %get-tuple-element.53), channel_id=1, source_target_pairs={{0,1},{1,9},{2,3},{3,11},{4,5},{5,13},{6,7},{7,15},{8,0},{9,17},{1... | collective-permute-start | bytes 393224 | tf_op jit(solution)/shard_map/ppermute | solution.py:413
  29.0 6.1 %collective-permute-start.13 = (bf16[256,256]{1,0:T(8,128)(2,1)S(1)}, bf16[256,256]{1,0:T(8,128)(2,1)S(1)}, u32[]{:S(2)}, u32[]{:S(2)}) collective-permute-start(bf16[256,256]{1,0:T(8,128)(2,1)S(1)} %get-tuple-element.54), channel_id=1, source_target_pairs={{0,8},{1,0},{2,10},{3,2},{4,12},{5,4},{6,14},{7,6},{8,16},{9,1},{1... | collective-permute-start | bytes 393224 | tf_op jit(solution)/shard_map/ppermute | solution.py:413
  32.2 5.7 %collective-permute-start.15 = (bf16[256,256]{1,0:T(8,128)(2,1)S(1)}, bf16[256,256]{1,0:T(8,128)(2,1)S(1)}, u32[]{:S(2)}, u32[]{:S(2)}) collective-permute-start(bf16[256,256]{1,0:T(8,128)(2,1)S(1)} %merge_d.1), channel_id=1, source_target_pairs={{0,1},{1,9},{2,3},{3,11},{4,5},{5,13},{6,7},{7,15},{8,0},{9,17},{1... | collective-permute-start | bytes 393224 | tf_op jit(solution)/shard_map/ppermute | solution.py:413
  32.2 5.6 %collective-permute-start.17 = (bf16[256,256]{1,0:T(8,128)(2,1)S(1)}, bf16[256,256]{1,0:T(8,128)(2,1)S(1)}, u32[]{:S(2)}, u32[]{:S(2)}) collective-permute-start(bf16[256,256]{1,0:T(8,128)(2,1)S(1)} %merge_u.1), channel_id=1, source_target_pairs={{0,8},{1,0},{2,10},{3,2},{4,12},{5,4},{6,14},{7,6},{8,16},{9,1},{1... | collective-permute-start | bytes 393224 | tf_op jit(solution)/shard_map/ppermute | solution.py:413
  38.4 2.0 %collective-permute-start.18 = (bf16[1024,256]{1,0:T(8,128)(2,1)S(1)}, bf16[1024,256]{1,0:T(8,128)(2,1)S(1)}, u32[]{:S(2)}, u32[]{:S(2)}) collective-permute-start(bf16[1024,256]{1,0:T(8,128)(2,1)S(1)} %get-tuple-element.65), channel_id=1, source_target_pairs={{0,1},{1,0},{2,3},{3,2},{4,5},{5,4},{6,7},{7,6},{8,9},{9,8},{10,11... | collective-permute-start | bytes 1572872 | tf_op jit(solution)/shard_map/ppermute | solution.py:402
  40.5 9.8 %collective-permute-start.21 = (bf16[384,256]{1,0:T(8,128)(2,1)S(1)}, bf16[384,256]{1,0:T(8,128)(2,1)S(1)}, u32[]{:S(2)}, u32[]{:S(2)}) collective-permute-start(bf16[384,256]{1,0:T(8,128)(2,1)S(1)} %get-tuple-element.70), channel_id=1, source_target_pairs={{0,4},{1,5},{2,6},{3,7},{4,0},{5,1},{6,2},{7,3},{8,12},{9,13},{10,... | collective-permute-start | bytes 589832 | tf_op jit(solution)/shard_map/ppermute | solution.py:402
  41.7 7.3 %collective-permute-start.19 = (bf16[256,256]{1,0:T(8,128)(2,1)S(1)}, bf16[256,256]{1,0:T(8,128)(2,1)S(1)}, u32[]{:S(2)}, u32[]{:S(2)}) collective-permute-start(bf16[256,256]{1,0:T(8,128)(2,1)S(1)} %get-tuple-element.68), channel_id=1, source_target_pairs={{0,6},{1,7},{2,4},{3,5},{4,2},{5,3},{6,0},{7,1},{8,14},{9,15},{10,... | collective-permute-start | bytes 393224 | tf_op jit(solution)/shard_map/ppermute | solution.py:402
  43.5 6.6 %collective-permute-start.20 = (bf16[256,256]{1,0:T(8,128)(2,1)S(1)}, bf16[256,256]{1,0:T(8,128)(2,1)S(1)}, u32[]{:S(2)}, u32[]{:S(2)}) collective-permute-start(bf16[256,256]{1,0:T(8,128)(2,1)S(1)} %get-tuple-element.69), channel_id=1, source_target_pairs={{0,2},{1,3},{2,0},{3,1},{4,6},{5,7},{6,4},{7,5},{8,10},{9,11},{10,... | collective-permute-start | bytes 393224 | tf_op jit(solution)/shard_map/ppermute | solution.py:402

commit v14 on v13

--- a/solution.py
+++ b/solution.py
@@ -96,8 +96,7 @@
     second_out[...] = jnp.where(near_first, partner, own)
 
 
-def merge_kernel(one, two, dq, out):
-    del dq
+def merge_kernel(one, two, out):
     out[...] = (one[...].astype(F32) + two[...].astype(F32)).astype(BF)
 
 
@@ -106,12 +105,18 @@
     second_out[...] = second_own[...] + d[...].astype(F32)
 
 
-def chip_sum_kernel(keep, arrived, att_other, mine, to_x, to_y, to_d):
-    for index, target in enumerate((mine, to_x, to_y, to_d)):
-        rows = slice(index * HALF, (index + 1) * HALF)
-        target[:HALF, :] = (keep[rows, :].astype(F32) + arrived[rows, :].astype(F32)).astype(BF)
+def chip_sum_near_kernel(keep, arrived, att_other, mine, to_y):
+    total = (keep[...].astype(F32) + arrived[...].astype(F32)).astype(BF)
+    mine[...] = total[:HALF]
+    to_y[:HALF, :] = total[HALF:]
     for half in range(2):
         to_y[HALF:, half * HD : (half + 1) * HD] = att_other[half * BLK : (half + 1) * BLK, :]
+
+
+def chip_sum_far_kernel(keep, arrived, to_x, to_d):
+    total = (keep[...].astype(F32) + arrived[...].astype(F32)).astype(BF)
+    to_x[...] = total[:HALF]
+    to_d[...] = total[HALF:]
 
 
 def finish_kernel(mine, gd, gx, from_y, att_own, attended, grad_features):
@@ -367,15 +372,12 @@
 
 
 def spread(grads, w_mine, side, head, target):
-    for step in range(2):
-        out = dot(grads, weight_rows(w_mine, head ^ (2 * step), 2 * HD), ((1,), (1,))).astype(BF)
-        for group in range(2):
-            index = 2 * group + step
-            part = jnp.where(side == group, out[:HALF], out[HALF:])
-            target[index * HALF : (index + 1) * HALF, :] = part
-
-
-def spread_send_kernel(first_own, second_own, from_d, from_u, dq, w_mine, send, grads):
+    out = dot(grads, weight_rows(w_mine, head, 2 * HD), ((1,), (1,))).astype(BF)
+    target[:HALF, :] = jnp.where(side == 0, out[:HALF], out[HALF:])
+    target[HALF:, :] = jnp.where(side == 0, out[HALF:], out[:HALF])
+
+
+def spread_near_kernel(first_own, second_own, from_d, from_u, dq, w_mine, send, grads):
     side, flip, _, head = position()
     first = first_own[...] + from_d[...].astype(F32)
     second = second_own[...] + from_u[...].astype(F32)
@@ -385,9 +387,15 @@
     spread(grads[...], w_mine, side, head ^ 1, send)
 
 
-def spread_keep_kernel(grads, w_mine, keep):
+def spread_far_kernel(grads, w_mine, send):
     side, _, _, head = position()
-    spread(grads[...], w_mine, side, head, keep)
+    spread(grads[...], w_mine, side, head ^ 3, send)
+
+
+def spread_keep_kernel(grads, w_mine, near, far):
+    side, _, _, head = position()
+    spread(grads[...], w_mine, side, head, near)
+    spread(grads[...], w_mine, side, head ^ 2, far)
 
 
 def body(features, w_qkv, block_links, d_out, n_ctx, n_head):
@@ -542,33 +550,36 @@
     u2_back = chain(u2_grad, 0)
 
     def merge(one, two, name):
-        return call(merge_kernel, name, [out(HALF, 2 * HD)], (one, two, dq), 4, 0)[0]
+        return call(merge_kernel, name, [out(HALF, 2 * HD)], (one, two), 4, 0)[0]
 
     from_d = chain(merge(d3_grad, back_d, "merge_d"), 1)
     from_u = chain(merge(u3_grad, back_u, "merge_u"), 0)
     first_own, second_own = call(
         gather_kernel, "gather", [held(HALF, 2 * HD, F32)] * 2, (first_own, second_own, d2_back, u2_back), 4, 0
     )
-    send, grads = call(
-        spread_send_kernel,
-        "spread_send",
-        [out(4 * HALF, 2 * HD), held(ROWS, 3 * HD)],
+    near_send, grads = call(
+        spread_near_kernel,
+        "spread_near",
+        [out(ROWS, 2 * HD), held(ROWS, 3 * HD)],
         (first_own, second_own, from_d, from_u, dq, w_mine),
         4,
         product,
     )
-    (keep,) = call(spread_keep_kernel, "spread_keep", [held(4 * HALF, 2 * HD)], (grads, w_mine), 4, product)
-    arrived = across(send, 0, 1)
-    mine, to_x, to_y, to_d = call(
-        chip_sum_kernel,
-        "chip_sum",
-        [out(HALF, 2 * HD)] * 2 + [out(HALF + BLK, 2 * HD), out(HALF, 2 * HD)],
-        (keep, arrived, att_other),
+    near_arrived = across(near_send, 0, 1)
+    (far_send,) = call(spread_far_kernel, "spread_far", [out(ROWS, 2 * HD)], (grads, w_mine), 4, product)
+    far_arrived = across(far_send, 0, 1)
+    near, far = call(spread_keep_kernel, "spread_keep", [held(ROWS, 2 * HD)] * 2, (grads, w_mine), 4, product)
+    mine, to_y = call(
+        chip_sum_near_kernel,
+        "chip_sum_near",
+        [out(HALF, 2 * HD), out(HALF + BLK, 2 * HD)],
+        (near, near_arrived, att_other),
         4,
         0,
     )
+    gy = across(to_y, 1, 0)
+    to_x, to_d = call(chip_sum_far_kernel, "chip_sum_far", [out(HALF, 2 * HD)] * 2, (far, far_arrived), 4, 0)
     gd = across(to_d, 1, 2)
-    gy = across(to_y, 1, 0)
     gx = across(to_x, 0, 2)
     attended, grad_features = call(
         finish_kernel, "finish", [out(HALF, 2 * HD)] * 2, (mine, gd, gx, gy, att_own), 4, 0

time: 51.2 us -> 50.7 us (level)
  waiting for transfers between devices: 18.9 us -> 17 us
  starting transfers between devices: 21.7 us -> 22.9 us
    ppermute x10 -> x11, waiting for transfers between devices: 13.2 us -> 11.9 us  [across(): return lax.ppermute(value, ('ctx', 'head'), pairs)]
    ppermute x10 -> x11, starting transfers between devices: 9.89 us -> 10.5 us  [across(): return lax.ppermute(value, ('ctx', 'head'), pairs)]
    ppermute x12, starting transfers between devices: 11.9 us -> 12.4 us  [chain(): return lax.ppermute(value, ('ctx', 'head'), pairs)]
    ppermute x12, waiting for transfers between devices: 5.64 us -> 5.11 us  [chain(): return lax.ppermute(value, ('ctx', 'head'), pairs)]
    pallas_call x20 -> x22, Pallas kernels: 9.53 us -> 9.71 us  [call(): pl.pallas_call(kernel, name=name, out_shape=outs, in_specs=specs, out_spe...]
  transfers between devices with their start and end apart: 22 -> 23, of which waited for: 12 -> 11; matrix products, arithmetic and copies ran while one was open for 0% -> 0% of each run, Pallas kernels for 15% -> 17%
where the time goes in v14:
time: 50.7 us; the launch traced here: 50.5 us
  starting transfers between devices  22.9 us (45%)
  waiting for transfers between devices  17 us (34%)
  Pallas kernels  9.71 us (19%)
  between operations  0.88 us (2%)
    ppermute x12, starting transfers between devices, chain(): return lax.ppermute(value, ('ctx', 'head'), pairs)  12.4 us
    ppermute x11, waiting for transfers between devices, across(): return lax.ppermute(value, ('ctx', 'head'), pairs)  11.9 us
    ppermute x11, starting transfers between devices, across(): return lax.ppermute(value, ('ctx', 'head'), pairs)  10.5 us
    pallas_call x22, Pallas kernels, call(): pl.pallas_call(kernel, name=name, out_shape=outs, in_specs=specs, out_spe...  9.71 us
    ppermute x12, waiting for transfers between devices, chain(): return lax.ppermute(value, ('ctx', 'head'), pairs)  5.11 us
  transfers between devices with their start and end apart: 23, of which 11 were waited for; matrix products, arithmetic and copies ran while one was open for 0% of the time, Pallas kernels for 17%

profile of v14, /device:TPU:0, one launch (start us, length us, event | category | flops | bytes accessed | tf_op | source)
XLA Modules:
  0.0 50.5 jit_solution(10301921577589887488)
XLA Ops:
  0.6 4.0 %collective-permute-start.4 = (bf16[256,256]{1,0:T(8,128)(2,1)}, bf16[256,256]{1,0:T(8,128)(2,1)S(1)}, u32[]{:S(2)}, u32[]{:S(2)}) collective-permute-start(bf16[256,256]{1,0:T(8,128)(2,1)} %f.1), channel_id=1, source_target_pairs={{0,6},{1,7},{2,4},{3,5},{4,2},{5,3},{6,0},{7,1},{8,14},{9,15},{10,... | collective-permute-start | bytes 393224 | tf_op jit(solution)/shard_map/ppermute | solution.py:410
  4.6 0.5 %collective-permute-start.1 = (bf16[256,256]{1,0:T(8,128)(2,1)}, bf16[256,256]{1,0:T(8,128)(2,1)S(1)}, u32[]{:S(2)}, u32[]{:S(2)}) collective-permute-start(bf16[256,256]{1,0:T(8,128)(2,1)} %f.1), channel_id=1, source_target_pairs={{0,2},{1,3},{2,0},{3,1},{4,6},{5,7},{6,4},{7,5},{8,10},{9,11},{10,... | collective-permute-start | bytes 393224 | tf_op jit(solution)/shard_map/ppermute | solution.py:410
  5.2 1.4 %begin.1 = (bf16[1024,384]{1,0:T(8,128)(2,1)S(1)}, bf16[256,256]{1,0:T(8,128)(2,1)S(1)}, f32[256,384]{1,0:T(8,128)S(1)}) custom-call(bf16[256,256]{1,0:T(8,128)(2,1)} %f.1, bf16[3,1024,256]{2,1,0:T(8,128)(2,1)} %bitcast.1), custom_call_target="tpu_custom_call" | custom-call | flops 100663296 | bytes 2097152 | tf_op jit(solution)/shard_map/begin/pallas_call | solution.py:434
  6.7 2.5 %collective-permute-done.4.two = bf16[256,256]{1,0:T(8,128)(2,1)S(1)} collective-permute-done((bf16[256,256]{1,0:T(8,128)(2,1)}, bf16[256,256]{1,0:T(8,128)(2,1)S(1)}, u32[]{:S(2)}, u32[]{:S(2)}) %collective-permute-start.4) | collective-permute-done | bytes 131104 | tf_op jit(solution)/shard_map/ppermute | solution.py:410
  9.2 2.1 %collective-permute-done.1.two = bf16[256,256]{1,0:T(8,128)(2,1)S(1)} collective-permute-done((bf16[256,256]{1,0:T(8,128)(2,1)}, bf16[256,256]{1,0:T(8,128)(2,1)S(1)}, u32[]{:S(2)}, u32[]{:S(2)}) %collective-permute-start.1) | collective-permute-done | bytes 131104 | tf_op jit(solution)/shard_map/ppermute | solution.py:410
  11.5 0.5 %project_rest.1.before = f32[512,384]{1,0:T(8,128)S(1)} custom-call(f32[256,384]{1,0:T(8,128)S(1)} %get-tuple-element.39.before, bf16[512,256]{1,0:T(8,128)(2,1)S(1)} %pack_early.1.early, bf16[512,256]{1,0:T(8,128)(2,1)S(1)} %pack_late.1.late, bf16[512,256]{1,0:T(8,128)(2,1)S(1)} %collective-permute-done.5.other_early, ...), custom_call_target="tpu_custom_call" | custom-call | flops 100663296 | bytes 2097152 | tf_op jit(solution)/shard_map/project_rest/pallas_call | solution.py:434
  12.0 1.0 %collective-permute-done.3.other_late = bf16[512,256]{1,0:T(8,128)(2,1)S(1)} collective-permute-done((bf16[512,256]{1,0:T(8,128)(2,1)S(1)}, bf16[512,256]{1,0:T(8,128)(2,1)S(1)}, u32[]{:S(2)}, u32[]{:S(2)}) %collective-permute-start.3) | collective-permute-done | bytes 262176 | tf_op jit(solution)/shard_map/ppermute | solution.py:410
  13.2 1.6 %collective-permute-start.6 = (bf16[256,256]{1,0:T(8,128)(2,1)S(1)}, bf16[256,256]{1,0:T(8,128)(2,1)S(1)}, u32[]{:S(2)}, u32[]{:S(2)}) collective-permute-start(bf16[256,256]{1,0:T(8,128)(2,1)S(1)} %get-tuple-element.42.first_kv), channel_id=1, source_target_pairs={{0,8},{1,0},{2,10},{3,2},{4,12},{5,4},{6,14},{7,6},{8,16},{9,1},{1... | collective-permute-start | bytes 393224 | tf_op jit(solution)/shard_map/ppermute | solution.py:421
  14.9 1.5 %collective-permute-start.2 = (bf16[272,128]{1,0:T(8,128)(2,1)S(1)}, bf16[272,128]{1,0:T(8,128)(2,1)S(1)}, u32[]{:S(2)}, u32[]{:S(2)}) collective-permute-start(bf16[272,128]{1,0:T(8,128)(2,1)S(1)} %payload.1), channel_id=1, source_target_pairs={{0,4},{1,5},{2,6},{3,7},{4,0},{5,1},{6,2},{7,3},{8,12},{9,13},{10,... | collective-permute-start | bytes 208904 | tf_op jit(solution)/shard_map/ppermute | solution.py:410
  16.4 2.0 %collective-permute-start.8 = (bf16[256,256]{1,0:T(8,128)(2,1)S(1)}, bf16[256,256]{1,0:T(8,128)(2,1)S(1)}, u32[]{:S(2)}, u32[]{:S(2)}) collective-permute-start(bf16[256,256]{1,0:T(8,128)(2,1)S(1)} %get-tuple-element.43.second_kv), channel_id=1, source_target_pairs={{0,8},{1,0},{2,10},{3,2},{4,12},{5,4},{6,14},{7,6},{8,16},{9,1},{1... | collective-permute-start | bytes 393224 | tf_op jit(solution)/shard_map/ppermute | solution.py:421
  18.4 2.2 %collective-permute-start.10 = (bf16[256,256]{1,0:T(8,128)(2,1)S(1)}, bf16[256,256]{1,0:T(8,128)(2,1)S(1)}, u32[]{:S(2)}, u32[]{:S(2)}) collective-permute-start(bf16[256,256]{1,0:T(8,128)(2,1)S(1)} %collective-permute-done.6.u1.near), channel_id=1, source_target_pairs={{0,8},{1,0},{2,10},{3,2},{4,12},{5,4},{6,14},{7,6},{8,16},{9,1},{1... | collective-permute-start | bytes 393224 | tf_op jit(solution)/shard_map/ppermute | solution.py:421
  20.9 0.7 %links.1 = s32[5,9]{1,0:T(8,128)S(4)} custom-call(s32[2,9]{1,0:T(2,128)S(1)} %copy-done.1, s32[2,9]{1,0:T(2,128)S(1)} %slice_convert_fusion.other, bf16[512,128]{1,0:T(8,128)(2,1)S(1)} %project_q.1.q), custom_call_target="tpu_custom_call" | custom-call | bytes 2097152 | tf_op jit(solution)/shard_map/links/pallas_call | solution.py:434
  21.6 1.1 %collective-permute-done.9.d2.middle = bf16[256,256]{1,0:T(8,128)(2,1)S(1)} collective-permute-done((bf16[256,256]{1,0:T(8,128)(2,1)S(1)}, bf16[256,256]{1,0:T(8,128)(2,1)S(1)}, u32[]{:S(2)}, u32[]{:S(2)}) %collective-permute-start.9) | collective-permute-done | bytes 131104 | tf_op jit(solution)/shard_map/ppermute | solution.py:421
  22.7 0.9 %near_scores.1 = (bf16[1024,256]{1,0:T(8,128)(2,1)S(1)}, f32[3072,128]{1,0:T(8,128)S(1)}, f32[3072,128]{1,0:T(8,128)S(1)}, f32[96,128]{1,0:T(8,128)S(1)}) custom-call(s32[5,9]{1,0:T(8,128)S(4)} %links.1, bf16[512,128]{1,0:T(8,128)(2,1)S(1)} %project_q.1.q, bf16[256,256]{1,0:T(8,128)(2,1)S(1)} %get-tuple-element.42.first_kv, ...), custom_call_target="tpu_custom_call" | custom-call | flops 301989888 | bytes 2097152 | tf_op jit(solution)/shard_map/near_scores/pallas_call | solution.py:434
  23.7 0.7 %far_grads_u.1 = (bf16[768,256]{1,0:T(8,128)(2,1)S(1)}, f32[768,256]{1,0:T(8,128)S(1)}, bf16[256,256]{1,0:T(8,128)(2,1)S(1)}, f32[32,128]{1,0:T(8,128)S(1)}) custom-call(s32[5,9]{1,0:T(8,128)S(4)} %links.1, bf16[1024,256]{1,0:T(8,128)(2,1)S(1)} %get-tuple-element.44.pairs, f32[96,128]{1,0:T(8,128)S(1)} %get-tuple-element.47.stats.after, ...), custom_call_target="tpu_custom_call" | custom-call | flops 150994944 | bytes 2097152 | tf_op jit(solution)/shard_map/far_grads_u/pallas_call | solution.py:434
  24.8 0.9 %collective-permute-done.11.far.d3 = bf16[256,256]{1,0:T(8,128)(2,1)S(1)} collective-permute-done((bf16[256,256]{1,0:T(8,128)(2,1)S(1)}, bf16[256,256]{1,0:T(8,128)(2,1)S(1)}, u32[]{:S(2)}, u32[]{:S(2)}) %collective-permute-start.11) | collective-permute-done | bytes 131104 | tf_op jit(solution)/shard_map/ppermute | solution.py:421
  25.6 0.8 %far_grads_d.1 = (bf16[768,256]{1,0:T(8,128)(2,1)S(1)}, f32[768,256]{1,0:T(8,128)S(1)}, bf16[256,256]{1,0:T(8,128)(2,1)S(1)}, f32[32,128]{1,0:T(8,128)S(1)}) custom-call(s32[5,9]{1,0:T(8,128)S(4)} %links.1, bf16[1024,256]{1,0:T(8,128)(2,1)S(1)} %get-tuple-element.44.pairs, f32[96,128]{1,0:T(8,128)S(1)} %get-tuple-element.47.stats.after, ...), custom_call_target="tpu_custom_call" | custom-call | flops 150994944 | bytes 2097152 | tf_op jit(solution)/shard_map/far_grads_d/pallas_call | solution.py:434
  26.4 1.6 %collective-permute-start.16 = (bf16[256,256]{1,0:T(8,128)(2,1)S(1)}, bf16[256,256]{1,0:T(8,128)(2,1)S(1)}, u32[]{:S(2)}, u32[]{:S(2)}) collective-permute-start(bf16[256,256]{1,0:T(8,128)(2,1)S(1)} %get-tuple-element.61), channel_id=1, source_target_pairs={{0,8},{1,0},{2,10},{3,2},{4,12},{5,4},{6,14},{7,6},{8,16},{9,1},{1... | collective-permute-start | bytes 393224 | tf_op jit(solution)/shard_map/ppermute | solution.py:421
  28.0 0.9 %near_grads.1 = (bf16[3072,256]{1,0:T(8,128)(2,1)S(1)}, f32[256,256]{1,0:T(8,128)S(1)}, f32[256,256]{1,0:T(8,128)S(1)}, bf16[256,256]{1,0:T(8,128)(2,1)S(1)}, bf...) custom-call(s32[5,9]{1,0:T(8,128)S(4)} %links.1, ...), custom_call_target="tpu_custom_call" | custom-call | flops 301989888 | bytes 2097152 | tf_op jit(solution)/shard_map/near_grads/pallas_call | solution.py:434
  29.0 2.0 %collective-permute-start.13 = (bf16[256,256]{1,0:T(8,128)(2,1)S(1)}, bf16[256,256]{1,0:T(8,128)(2,1)S(1)}, u32[]{:S(2)}, u32[]{:S(2)}) collective-permute-start(bf16[256,256]{1,0:T(8,128)(2,1)S(1)} %get-tuple-element.56), channel_id=1, source_target_pairs={{0,8},{1,0},{2,10},{3,2},{4,12},{5,4},{6,14},{7,6},{8,16},{9,1},{1... | collective-permute-start | bytes 393224 | tf_op jit(solution)/shard_map/ppermute | solution.py:421
  31.2 2.6 %collective-permute-start.17 = (bf16[256,256]{1,0:T(8,128)(2,1)S(1)}, bf16[256,256]{1,0:T(8,128)(2,1)S(1)}, u32[]{:S(2)}, u32[]{:S(2)}) collective-permute-start(bf16[256,256]{1,0:T(8,128)(2,1)S(1)} %merge_u.1), channel_id=1, source_target_pairs={{0,8},{1,0},{2,10},{3,2},{4,12},{5,4},{6,14},{7,6},{8,16},{9,1},{1... | collective-permute-start | bytes 393224 | tf_op jit(solution)/shard_map/ppermute | solution.py:421
  33.7 1.1 %outputs.1 = (bf16[256,128]{1,0:T(8,128)(2,1)S(1)}, bf16[256,128]{1,0:T(8,128)(2,1)S(1)}, bf16[512,128]{1,0:T(8,128)(2,1)S(1)}) custom-call(s32[5,9]{1,0:T(8,128)S(4)} %links.1, bf16[3072,256]{1,0:T(8,128)(2,1)S(1)} %get-tuple-element.62.near_mixed, bf16[768,256]{1,0:T(8,128)(2,1)S(1)} %get-tuple-element.63.u_mixed, ...), custom_call_target="tpu_custom_call" | custom-call | flops 301989888 | bytes 2097152 | tf_op jit(solution)/shard_map/outputs/pallas_call | solution.py:434
  34.8 0.6 %collective-permute-done.12.d = bf16[256,256]{1,0:T(8,128)(2,1)S(1)} collective-permute-done((bf16[256,256]{1,0:T(8,128)(2,1)S(1)}, bf16[256,256]{1,0:T(8,128)(2,1)S(1)}, u32[]{:S(2)}, u32[]{:S(2)}) %collective-permute-start.12) | collective-permute-done | bytes 131104 | tf_op jit(solution)/shard_map/ppermute | solution.py:421
  35.4 2.5 %collective-permute-done.15.from_d = bf16[256,256]{1,0:T(8,128)(2,1)S(1)} collective-permute-done((bf16[256,256]{1,0:T(8,128)(2,1)S(1)}, bf16[256,256]{1,0:T(8,128)(2,1)S(1)}, u32[]{:S(2)}, u32[]{:S(2)}) %collective-permute-start.15) | collective-permute-done | bytes 131104 | tf_op jit(solution)/shard_map/ppermute | solution.py:421
  38.6 0.6 %collective-permute-start.19 = (bf16[512,256]{1,0:T(8,128)(2,1)S(1)}, bf16[512,256]{1,0:T(8,128)(2,1)S(1)}, u32[]{:S(2)}, u32[]{:S(2)}) collective-permute-start(bf16[512,256]{1,0:T(8,128)(2,1)S(1)} %spread_far.1), channel_id=1, source_target_pairs={{0,1},{1,0},{2,3},{3,2},{4,5},{5,4},{6,7},{7,6},{8,9},{9,8},{10,11... | collective-permute-start | bytes 786440 | tf_op jit(solution)/shard_map/ppermute | solution.py:410
  39.2 0.5 spread_keep.1
  39.9 1.3 %collective-permute-start.22 = (bf16[384,256]{1,0:T(8,128)(2,1)S(1)}, bf16[384,256]{1,0:T(8,128)(2,1)S(1)}, u32[]{:S(2)}, u32[]{:S(2)}) collective-permute-start(bf16[384,256]{1,0:T(8,128)(2,1)S(1)} %get-tuple-element.74), channel_id=1, source_target_pairs={{0,4},{1,5},{2,6},{3,7},{4,0},{5,1},{6,2},{7,3},{8,12},{9,13},{10,... | collective-permute-start | bytes 589832 | tf_op jit(solution)/shard_map/ppermute | solution.py:410
  41.2 1.8 %collective-permute-start.20 = (bf16[256,256]{1,0:T(8,128)(2,1)S(1)}, bf16[256,256]{1,0:T(8,128)(2,1)S(1)}, u32[]{:S(2)}, u32[]{:S(2)}) collective-permute-start(bf16[256,256]{1,0:T(8,128)(2,1)S(1)} %get-tuple-element.72), channel_id=1, source_target_pairs={{0,6},{1,7},{2,4},{3,5},{4,2},{5,3},{6,0},{7,1},{8,14},{9,15},{10,... | collective-permute-start | bytes 393224 | tf_op jit(solution)/shard_map/ppermute | solution.py:410
  43.0 0.5 %collective-permute-start.21 = (bf16[256,256]{1,0:T(8,128)(2,1)S(1)}, bf16[256,256]{1,0:T(8,128)(2,1)S(1)}, u32[]{:S(2)}, u32[]{:S(2)}) collective-permute-start(bf16[256,256]{1,0:T(8,128)(2,1)S(1)} %get-tuple-element.73), channel_id=1, source_target_pairs={{0,2},{1,3},{2,0},{3,1},{4,6},{5,7},{6,4},{7,5},{8,10},{9,11},{10,... | collective-permute-start | bytes 393224 | tf_op jit(solution)/shard_map/ppermute | solution.py:410
  43.6 5.0 %collective-permute-done.20.gd = bf16[256,256]{1,0:T(8,128)(2,1)S(1)} collective-permute-done((bf16[256,256]{1,0:T(8,128)(2,1)S(1)}, bf16[256,256]{1,0:T(8,128)(2,1)S(1)}, u32[]{:S(2)}, u32[]{:S(2)}) %collective-permute-start.20) | collective-permute-done | bytes 131104 | tf_op jit(solution)/shard_map/ppermute | solution.py:410
  48.6 1.2 %collective-permute-done.21.gx = bf16[256,256]{1,0:T(8,128)(2,1)S(1)} collective-permute-done((bf16[256,256]{1,0:T(8,128)(2,1)S(1)}, bf16[256,256]{1,0:T(8,128)(2,1)S(1)}, u32[]{:S(2)}, u32[]{:S(2)}) %collective-permute-start.21) | collective-permute-done | bytes 131104 | tf_op jit(solution)/shard_map/ppermute | solution.py:410
  49.7 0.8 %finish.1 = (bf16[256,256]{1,0:T(8,128)(2,1)}, bf16[256,256]{1,0:T(8,128)(2,1)}) custom-call(bf16[256,256]{1,0:T(8,128)(2,1)S(1)} %get-tuple-element.70.mine, bf16[256,256]{1,0:T(8,128)(2,1)S(1)} %collective-permute-done.20.gd, bf16[256,256]{1,0:T(8,128)(2,1)S(1)} %collective-permute-done.21.gx, bf16[384,256]{1,0:T(8,128)(2,1)S(1)} %collective-permute-done.22.from_y, ...), custom_call_target="tpu_custom_call" | custom-call | bytes 2097152 | tf_op jit(solution)/shard_map/finish/pallas_call | solution.py:434
  (43 shorter events, 2.5 us)
Async XLA Ops:
  0.6 8.5 %collective-permute-start.4 = (bf16[256,256]{1,0:T(8,128)(2,1)}, bf16[256,256]{1,0:T(8,128)(2,1)S(1)}, u32[]{:S(2)}, u32[]{:S(2)}) collective-permute-start(bf16[256,256]{1,0:T(8,128)(2,1)} %f.1), channel_id=1, source_target_pairs={{0,6},{1,7},{2,4},{3,5},{4,2},{5,3},{6,0},{7,1},{8,14},{9,15},{10,... | collective-permute-start | bytes 393224 | tf_op jit(solution)/shard_map/ppermute | solution.py:410
  4.6 6.8 %collective-permute-start.1 = (bf16[256,256]{1,0:T(8,128)(2,1)}, bf16[256,256]{1,0:T(8,128)(2,1)S(1)}, u32[]{:S(2)}, u32[]{:S(2)}) collective-permute-start(bf16[256,256]{1,0:T(8,128)(2,1)} %f.1), channel_id=1, source_target_pairs={{0,2},{1,3},{2,0},{3,1},{4,6},{5,7},{6,4},{7,5},{8,10},{9,11},{10,... | collective-permute-start | bytes 393224 | tf_op jit(solution)/shard_map/ppermute | solution.py:410
  5.1 6.2 %collective-permute-start = (bf16[256,256]{1,0:T(8,128)(2,1)}, bf16[256,256]{1,0:T(8,128)(2,1)S(1)}, u32[]{:S(2)}, u32[]{:S(2)}) collective-permute-start(bf16[256,256]{1,0:T(8,128)(2,1)} %f.1), channel_id=1, source_target_pairs={{0,4},{1,5},{2,6},{3,7},{4,0},{5,1},{6,2},{7,3},{8,12},{9,13},{10,... | collective-permute-start | bytes 393224 | tf_op jit(solution)/shard_map/ppermute | solution.py:410
  9.1 2.3 %collective-permute-start.5 = (bf16[512,256]{1,0:T(8,128)(2,1)S(1)}, bf16[512,256]{1,0:T(8,128)(2,1)S(1)}, u32[]{:S(2)}, u32[]{:S(2)}) collective-permute-start(bf16[512,256]{1,0:T(8,128)(2,1)S(1)} %pack_early.1.early), channel_id=1, source_target_pairs={{0,1},{1,0},{2,3},{3,2},{4,5},{5,4},{6,7},{7,6},{8,9},{9,8},{10,11... | collective-permute-start | bytes 786440 | tf_op jit(solution)/shard_map/ppermute | solution.py:410
  11.4 1.6 %collective-permute-start.3 = (bf16[512,256]{1,0:T(8,128)(2,1)S(1)}, bf16[512,256]{1,0:T(8,128)(2,1)S(1)}, u32[]{:S(2)}, u32[]{:S(2)}) collective-permute-start(bf16[512,256]{1,0:T(8,128)(2,1)S(1)} %pack_late.1.late), channel_id=1, source_target_pairs={{0,1},{1,0},{2,3},{3,2},{4,5},{5,4},{6,7},{7,6},{8,9},{9,8},{10,11... | collective-permute-start | bytes 786440 | tf_op jit(solution)/shard_map/ppermute | solution.py:410
  12.0 2.8 %copy-start.1 = (s32[2,9]{1,0:T(2,128)S(1)}, s32[2,9]{1,0:T(2,128)}, u32[]{:S(2)}) copy-start(s32[2,9]{1,0:T(2,128)} %own.1) | copy-start | bytes 220
  12.0 2.8 %copy-start = (bf16[256,256]{1,0:T(8,128)(2,1)S(1)}, bf16[256,256]{1,0:T(8,128)(2,1)}, u32[]{:S(2)}) copy-start(bf16[256,256]{1,0:T(8,128)(2,1)} %d_own.3) | copy-start | bytes 393220
  13.2 5.2 %collective-permute-start.6 = (bf16[256,256]{1,0:T(8,128)(2,1)S(1)}, bf16[256,256]{1,0:T(8,128)(2,1)S(1)}, u32[]{:S(2)}, u32[]{:S(2)}) collective-permute-start(bf16[256,256]{1,0:T(8,128)(2,1)S(1)} %get-tuple-element.42.first_kv), channel_id=1, source_target_pairs={{0,8},{1,0},{2,10},{3,2},{4,12},{5,4},{6,14},{7,6},{8,16},{9,1},{1... | collective-permute-start | bytes 393224 | tf_op jit(solution)/shard_map/ppermute | solution.py:421
  14.8 5.8 %collective-permute-start.7 = (bf16[256,256]{1,0:T(8,128)(2,1)S(1)}, bf16[256,256]{1,0:T(8,128)(2,1)S(1)}, u32[]{:S(2)}, u32[]{:S(2)}) collective-permute-start(bf16[256,256]{1,0:T(8,128)(2,1)S(1)} %get-tuple-element.43.second_kv), channel_id=1, source_target_pairs={{0,1},{1,9},{2,3},{3,11},{4,5},{5,13},{6,7},{7,15},{8,0},{9,17},{1... | collective-permute-start | bytes 393224 | tf_op jit(solution)/shard_map/ppermute | solution.py:421
  14.9 5.8 %collective-permute-start.2 = (bf16[272,128]{1,0:T(8,128)(2,1)S(1)}, bf16[272,128]{1,0:T(8,128)(2,1)S(1)}, u32[]{:S(2)}, u32[]{:S(2)}) collective-permute-start(bf16[272,128]{1,0:T(8,128)(2,1)S(1)} %payload.1), channel_id=1, source_target_pairs={{0,4},{1,5},{2,6},{3,7},{4,0},{5,1},{6,2},{7,3},{8,12},{9,13},{10,... | collective-permute-start | bytes 208904 | tf_op jit(solution)/shard_map/ppermute | solution.py:410
  16.4 6.3 %collective-permute-start.9 = (bf16[256,256]{1,0:T(8,128)(2,1)S(1)}, bf16[256,256]{1,0:T(8,128)(2,1)S(1)}, u32[]{:S(2)}, u32[]{:S(2)}) collective-permute-start(bf16[256,256]{1,0:T(8,128)(2,1)S(1)} %get-tuple-element.42.first_kv), channel_id=1, source_target_pairs={{0,1},{1,9},{2,3},{3,11},{4,5},{5,13},{6,7},{7,15},{8,0},{9,17},{1... | collective-permute-start | bytes 393224 | tf_op jit(solution)/shard_map/ppermute | solution.py:421
  16.4 6.3 %collective-permute-start.8 = (bf16[256,256]{1,0:T(8,128)(2,1)S(1)}, bf16[256,256]{1,0:T(8,128)(2,1)S(1)}, u32[]{:S(2)}, u32[]{:S(2)}) collective-permute-start(bf16[256,256]{1,0:T(8,128)(2,1)S(1)} %get-tuple-element.43.second_kv), channel_id=1, source_target_pairs={{0,8},{1,0},{2,10},{3,2},{4,12},{5,4},{6,14},{7,6},{8,16},{9,1},{1... | collective-permute-start | bytes 393224 | tf_op jit(solution)/shard_map/ppermute | solution.py:421
  18.4 5.3 %collective-permute-start.10 = (bf16[256,256]{1,0:T(8,128)(2,1)S(1)}, bf16[256,256]{1,0:T(8,128)(2,1)S(1)}, u32[]{:S(2)}, u32[]{:S(2)}) collective-permute-start(bf16[256,256]{1,0:T(8,128)(2,1)S(1)} %collective-permute-done.6.u1.near), channel_id=1, source_target_pairs={{0,8},{1,0},{2,10},{3,2},{4,12},{5,4},{6,14},{7,6},{8,16},{9,1},{1... | collective-permute-start | bytes 393224 | tf_op jit(solution)/shard_map/ppermute | solution.py:421
  20.7 5.0 %collective-permute-start.11 = (bf16[256,256]{1,0:T(8,128)(2,1)S(1)}, bf16[256,256]{1,0:T(8,128)(2,1)S(1)}, u32[]{:S(2)}, u32[]{:S(2)}) collective-permute-start(bf16[256,256]{1,0:T(8,128)(2,1)S(1)} %collective-permute-done.7.d1.near), channel_id=1, source_target_pairs={{0,1},{1,9},{2,3},{3,11},{4,5},{5,13},{6,7},{7,15},{8,0},{9,17},{1... | collective-permute-start | bytes 393224 | tf_op jit(solution)/shard_map/ppermute | solution.py:421
  24.5 6.6 %collective-permute-start.14 = (bf16[256,256]{1,0:T(8,128)(2,1)S(1)}, bf16[256,256]{1,0:T(8,128)(2,1)S(1)}, u32[]{:S(2)}, u32[]{:S(2)}) collective-permute-start(bf16[256,256]{1,0:T(8,128)(2,1)S(1)} %get-tuple-element.49.after), channel_id=1, source_target_pairs={{0,1},{1,9},{2,3},{3,11},{4,5},{5,13},{6,7},{7,15},{8,0},{9,17},{1... | collective-permute-start | bytes 393224 | tf_op jit(solution)/shard_map/ppermute | solution.py:421
  26.4 4.7 %collective-permute-start.16 = (bf16[256,256]{1,0:T(8,128)(2,1)S(1)}, bf16[256,256]{1,0:T(8,128)(2,1)S(1)}, u32[]{:S(2)}, u32[]{:S(2)}) collective-permute-start(bf16[256,256]{1,0:T(8,128)(2,1)S(1)} %get-tuple-element.61), channel_id=1, source_target_pairs={{0,8},{1,0},{2,10},{3,2},{4,12},{5,4},{6,14},{7,6},{8,16},{9,1},{1... | collective-permute-start | bytes 393224 | tf_op jit(solution)/shard_map/ppermute | solution.py:421
  29.0 6.4 %collective-permute-start.12 = (bf16[256,256]{1,0:T(8,128)(2,1)S(1)}, bf16[256,256]{1,0:T(8,128)(2,1)S(1)}, u32[]{:S(2)}, u32[]{:S(2)}) collective-permute-start(bf16[256,256]{1,0:T(8,128)(2,1)S(1)} %get-tuple-element.55), channel_id=1, source_target_pairs={{0,1},{1,9},{2,3},{3,11},{4,5},{5,13},{6,7},{7,15},{8,0},{9,17},{1... | collective-permute-start | bytes 393224 | tf_op jit(solution)/shard_map/ppermute | solution.py:421
  29.0 6.4 %collective-permute-start.13 = (bf16[256,256]{1,0:T(8,128)(2,1)S(1)}, bf16[256,256]{1,0:T(8,128)(2,1)S(1)}, u32[]{:S(2)}, u32[]{:S(2)}) collective-permute-start(bf16[256,256]{1,0:T(8,128)(2,1)S(1)} %get-tuple-element.56), channel_id=1, source_target_pairs={{0,8},{1,0},{2,10},{3,2},{4,12},{5,4},{6,14},{7,6},{8,16},{9,1},{1... | collective-permute-start | bytes 393224 | tf_op jit(solution)/shard_map/ppermute | solution.py:421
  31.1 6.8 %collective-permute-start.15 = (bf16[256,256]{1,0:T(8,128)(2,1)S(1)}, bf16[256,256]{1,0:T(8,128)(2,1)S(1)}, u32[]{:S(2)}, u32[]{:S(2)}) collective-permute-start(bf16[256,256]{1,0:T(8,128)(2,1)S(1)} %merge_d.1), channel_id=1, source_target_pairs={{0,1},{1,9},{2,3},{3,11},{4,5},{5,13},{6,7},{7,15},{8,0},{9,17},{1... | collective-permute-start | bytes 393224 | tf_op jit(solution)/shard_map/ppermute | solution.py:421
  31.2 6.7 %collective-permute-start.17 = (bf16[256,256]{1,0:T(8,128)(2,1)S(1)}, bf16[256,256]{1,0:T(8,128)(2,1)S(1)}, u32[]{:S(2)}, u32[]{:S(2)}) collective-permute-start(bf16[256,256]{1,0:T(8,128)(2,1)S(1)} %merge_u.1), channel_id=1, source_target_pairs={{0,8},{1,0},{2,10},{3,2},{4,12},{5,4},{6,14},{7,6},{8,16},{9,1},{1... | collective-permute-start | bytes 393224 | tf_op jit(solution)/shard_map/ppermute | solution.py:421
  38.2 1.6 %collective-permute-start.18 = (bf16[512,256]{1,0:T(8,128)(2,1)S(1)}, bf16[512,256]{1,0:T(8,128)(2,1)S(1)}, u32[]{:S(2)}, u32[]{:S(2)}) collective-permute-start(bf16[512,256]{1,0:T(8,128)(2,1)S(1)} %get-tuple-element.68), channel_id=1, source_target_pairs={{0,1},{1,0},{2,3},{3,2},{4,5},{5,4},{6,7},{7,6},{8,9},{9,8},{10,11... | collective-permute-start | bytes 786440 | tf_op jit(solution)/shard_map/ppermute | solution.py:410
  38.6 2.5 %collective-permute-start.19 = (bf16[512,256]{1,0:T(8,128)(2,1)S(1)}, bf16[512,256]{1,0:T(8,128)(2,1)S(1)}, u32[]{:S(2)}, u32[]{:S(2)}) collective-permute-start(bf16[512,256]{1,0:T(8,128)(2,1)S(1)} %spread_far.1), channel_id=1, source_target_pairs={{0,1},{1,0},{2,3},{3,2},{4,5},{5,4},{6,7},{7,6},{8,9},{9,8},{10,11... | collective-permute-start | bytes 786440 | tf_op jit(solution)/shard_map/ppermute | solution.py:410
  39.9 9.9 %collective-permute-start.22 = (bf16[384,256]{1,0:T(8,128)(2,1)S(1)}, bf16[384,256]{1,0:T(8,128)(2,1)S(1)}, u32[]{:S(2)}, u32[]{:S(2)}) collective-permute-start(bf16[384,256]{1,0:T(8,128)(2,1)S(1)} %get-tuple-element.74), channel_id=1, source_target_pairs={{0,4},{1,5},{2,6},{3,7},{4,0},{5,1},{6,2},{7,3},{8,12},{9,13},{10,... | collective-permute-start | bytes 589832 | tf_op jit(solution)/shard_map/ppermute | solution.py:410
  41.2 7.3 %collective-permute-start.20 = (bf16[256,256]{1,0:T(8,128)(2,1)S(1)}, bf16[256,256]{1,0:T(8,128)(2,1)S(1)}, u32[]{:S(2)}, u32[]{:S(2)}) collective-permute-start(bf16[256,256]{1,0:T(8,128)(2,1)S(1)} %get-tuple-element.72), channel_id=1, source_target_pairs={{0,6},{1,7},{2,4},{3,5},{4,2},{5,3},{6,0},{7,1},{8,14},{9,15},{10,... | collective-permute-start | bytes 393224 | tf_op jit(solution)/shard_map/ppermute | solution.py:410
  43.0 6.7 %collective-permute-start.21 = (bf16[256,256]{1,0:T(8,128)(2,1)S(1)}, bf16[256,256]{1,0:T(8,128)(2,1)S(1)}, u32[]{:S(2)}, u32[]{:S(2)}) collective-permute-start(bf16[256,256]{1,0:T(8,128)(2,1)S(1)} %get-tuple-element.73), channel_id=1, source_target_pairs={{0,2},{1,3},{2,0},{3,1},{4,6},{5,7},{6,4},{7,5},{8,10},{9,11},{10,... | collective-permute-start | bytes 393224 | tf_op jit(solution)/shard_map/ppermute | solution.py:410

commit v15 on v14

--- a/solution.py
+++ b/solution.py
@@ -119,7 +119,7 @@
     to_d[...] = total[HALF:]
 
 
-def finish_kernel(mine, gd, gx, from_y, att_own, attended, grad_features):
+def finish_kernel(mine, gx, gd, from_y, att_own, attended, grad_features):
     total = mine[...].astype(F32) + gd[...].astype(F32) + gx[...].astype(F32) + from_y[:HALF, :].astype(F32)
     grad_features[...] = total.astype(BF)
     side = position()[0]
@@ -582,7 +582,7 @@
     gd = across(to_d, 1, 2)
     gx = across(to_x, 0, 2)
     attended, grad_features = call(
-        finish_kernel, "finish", [out(HALF, 2 * HD)] * 2, (mine, gd, gx, gy, att_own), 4, 0
+        finish_kernel, "finish", [out(HALF, 2 * HD)] * 2, (mine, gx, gd, gy, att_own), 4, 0
     )
     return attended, grad_features
 

time: 50.7 us -> 50.6 us (level)
  no operation moved by 1% of the time
where the time goes in v15:
time: 50.6 us; the launch traced here: 50.5 us
  starting transfers between devices  22.9 us (45%)
  waiting for transfers between devices  17 us (34%)
  Pallas kernels  9.71 us (19%)
  between operations  0.88 us (2%)
    ppermute x12, starting transfers between devices, chain(): return lax.ppermute(value, ('ctx', 'head'), pairs)  12.4 us
    ppermute x11, waiting for transfers between devices, across(): return lax.ppermute(value, ('ctx', 'head'), pairs)  11.9 us
    ppermute x11, starting transfers between devices, across(): return lax.ppermute(value, ('ctx', 'head'), pairs)  10.5 us
    pallas_call x22, Pallas kernels, call(): pl.pallas_call(kernel, name=name, out_shape=outs, in_specs=specs, out_spe...  9.71 us
    ppermute x12, waiting for transfers between devices, chain(): return lax.ppermute(value, ('ctx', 'head'), pairs)  5.11 us
  transfers between devices with their start and end apart: 23, of which 11 were waited for; matrix products, arithmetic and copies ran while one was open for 0% of the time, Pallas kernels for 17%

profile of v15, /device:TPU:0, one launch (start us, length us, event | category | flops | bytes accessed | tf_op | source)
XLA Modules:
  0.0 50.5 jit_solution(4809041160511636185)
XLA Ops:
  0.6 4.0 %collective-permute-start.4 = (bf16[256,256]{1,0:T(8,128)(2,1)}, bf16[256,256]{1,0:T(8,128)(2,1)S(1)}, u32[]{:S(2)}, u32[]{:S(2)}) collective-permute-start(bf16[256,256]{1,0:T(8,128)(2,1)} %f.1), channel_id=1, source_target_pairs={{0,6},{1,7},{2,4},{3,5},{4,2},{5,3},{6,0},{7,1},{8,14},{9,15},{10,... | collective-permute-start | bytes 393224 | tf_op jit(solution)/shard_map/ppermute | solution.py:410
  4.6 0.5 %collective-permute-start.1 = (bf16[256,256]{1,0:T(8,128)(2,1)}, bf16[256,256]{1,0:T(8,128)(2,1)S(1)}, u32[]{:S(2)}, u32[]{:S(2)}) collective-permute-start(bf16[256,256]{1,0:T(8,128)(2,1)} %f.1), channel_id=1, source_target_pairs={{0,2},{1,3},{2,0},{3,1},{4,6},{5,7},{6,4},{7,5},{8,10},{9,11},{10,... | collective-permute-start | bytes 393224 | tf_op jit(solution)/shard_map/ppermute | solution.py:410
  5.2 1.4 %begin.1 = (bf16[1024,384]{1,0:T(8,128)(2,1)S(1)}, bf16[256,256]{1,0:T(8,128)(2,1)S(1)}, f32[256,384]{1,0:T(8,128)S(1)}) custom-call(bf16[256,256]{1,0:T(8,128)(2,1)} %f.1, bf16[3,1024,256]{2,1,0:T(8,128)(2,1)} %bitcast.1), custom_call_target="tpu_custom_call" | custom-call | flops 100663296 | bytes 2097152 | tf_op jit(solution)/shard_map/begin/pallas_call | solution.py:434
  6.7 2.5 %collective-permute-done.4.two = bf16[256,256]{1,0:T(8,128)(2,1)S(1)} collective-permute-done((bf16[256,256]{1,0:T(8,128)(2,1)}, bf16[256,256]{1,0:T(8,128)(2,1)S(1)}, u32[]{:S(2)}, u32[]{:S(2)}) %collective-permute-start.4) | collective-permute-done | bytes 131104 | tf_op jit(solution)/shard_map/ppermute | solution.py:410
  9.2 2.1 %collective-permute-done.1.two = bf16[256,256]{1,0:T(8,128)(2,1)S(1)} collective-permute-done((bf16[256,256]{1,0:T(8,128)(2,1)}, bf16[256,256]{1,0:T(8,128)(2,1)S(1)}, u32[]{:S(2)}, u32[]{:S(2)}) %collective-permute-start.1) | collective-permute-done | bytes 131104 | tf_op jit(solution)/shard_map/ppermute | solution.py:410
  11.5 0.5 %project_rest.1.before = f32[512,384]{1,0:T(8,128)S(1)} custom-call(f32[256,384]{1,0:T(8,128)S(1)} %get-tuple-element.39.before, bf16[512,256]{1,0:T(8,128)(2,1)S(1)} %pack_early.1.early, bf16[512,256]{1,0:T(8,128)(2,1)S(1)} %pack_late.1.late, bf16[512,256]{1,0:T(8,128)(2,1)S(1)} %collective-permute-done.5.other_early, ...), custom_call_target="tpu_custom_call" | custom-call | flops 100663296 | bytes 2097152 | tf_op jit(solution)/shard_map/project_rest/pallas_call | solution.py:434
  12.0 1.0 %collective-permute-done.3.other_late = bf16[512,256]{1,0:T(8,128)(2,1)S(1)} collective-permute-done((bf16[512,256]{1,0:T(8,128)(2,1)S(1)}, bf16[512,256]{1,0:T(8,128)(2,1)S(1)}, u32[]{:S(2)}, u32[]{:S(2)}) %collective-permute-start.3) | collective-permute-done | bytes 262176 | tf_op jit(solution)/shard_map/ppermute | solution.py:410
  13.2 1.6 %collective-permute-start.6 = (bf16[256,256]{1,0:T(8,128)(2,1)S(1)}, bf16[256,256]{1,0:T(8,128)(2,1)S(1)}, u32[]{:S(2)}, u32[]{:S(2)}) collective-permute-start(bf16[256,256]{1,0:T(8,128)(2,1)S(1)} %get-tuple-element.42.first_kv), channel_id=1, source_target_pairs={{0,8},{1,0},{2,10},{3,2},{4,12},{5,4},{6,14},{7,6},{8,16},{9,1},{1... | collective-permute-start | bytes 393224 | tf_op jit(solution)/shard_map/ppermute | solution.py:421
  14.9 1.5 %collective-permute-start.2 = (bf16[272,128]{1,0:T(8,128)(2,1)S(1)}, bf16[272,128]{1,0:T(8,128)(2,1)S(1)}, u32[]{:S(2)}, u32[]{:S(2)}) collective-permute-start(bf16[272,128]{1,0:T(8,128)(2,1)S(1)} %payload.1), channel_id=1, source_target_pairs={{0,4},{1,5},{2,6},{3,7},{4,0},{5,1},{6,2},{7,3},{8,12},{9,13},{10,... | collective-permute-start | bytes 208904 | tf_op jit(solution)/shard_map/ppermute | solution.py:410
  16.4 2.0 %collective-permute-start.8 = (bf16[256,256]{1,0:T(8,128)(2,1)S(1)}, bf16[256,256]{1,0:T(8,128)(2,1)S(1)}, u32[]{:S(2)}, u32[]{:S(2)}) collective-permute-start(bf16[256,256]{1,0:T(8,128)(2,1)S(1)} %get-tuple-element.43.second_kv), channel_id=1, source_target_pairs={{0,8},{1,0},{2,10},{3,2},{4,12},{5,4},{6,14},{7,6},{8,16},{9,1},{1... | collective-permute-start | bytes 393224 | tf_op jit(solution)/shard_map/ppermute | solution.py:421
  18.4 2.2 %collective-permute-start.10 = (bf16[256,256]{1,0:T(8,128)(2,1)S(1)}, bf16[256,256]{1,0:T(8,128)(2,1)S(1)}, u32[]{:S(2)}, u32[]{:S(2)}) collective-permute-start(bf16[256,256]{1,0:T(8,128)(2,1)S(1)} %collective-permute-done.6.u1.near), channel_id=1, source_target_pairs={{0,8},{1,0},{2,10},{3,2},{4,12},{5,4},{6,14},{7,6},{8,16},{9,1},{1... | collective-permute-start | bytes 393224 | tf_op jit(solution)/shard_map/ppermute | solution.py:421
  20.9 0.7 %links.1 = s32[5,9]{1,0:T(8,128)S(4)} custom-call(s32[2,9]{1,0:T(2,128)S(1)} %copy-done.1, s32[2,9]{1,0:T(2,128)S(1)} %slice_convert_fusion.other, bf16[512,128]{1,0:T(8,128)(2,1)S(1)} %project_q.1.q), custom_call_target="tpu_custom_call" | custom-call | bytes 2097152 | tf_op jit(solution)/shard_map/links/pallas_call | solution.py:434
  21.6 1.1 %collective-permute-done.9.d2.middle = bf16[256,256]{1,0:T(8,128)(2,1)S(1)} collective-permute-done((bf16[256,256]{1,0:T(8,128)(2,1)S(1)}, bf16[256,256]{1,0:T(8,128)(2,1)S(1)}, u32[]{:S(2)}, u32[]{:S(2)}) %collective-permute-start.9) | collective-permute-done | bytes 131104 | tf_op jit(solution)/shard_map/ppermute | solution.py:421
  22.7 0.9 %near_scores.1 = (bf16[1024,256]{1,0:T(8,128)(2,1)S(1)}, f32[3072,128]{1,0:T(8,128)S(1)}, f32[3072,128]{1,0:T(8,128)S(1)}, f32[96,128]{1,0:T(8,128)S(1)}) custom-call(s32[5,9]{1,0:T(8,128)S(4)} %links.1, bf16[512,128]{1,0:T(8,128)(2,1)S(1)} %project_q.1.q, bf16[256,256]{1,0:T(8,128)(2,1)S(1)} %get-tuple-element.42.first_kv, ...), custom_call_target="tpu_custom_call" | custom-call | flops 301989888 | bytes 2097152 | tf_op jit(solution)/shard_map/near_scores/pallas_call | solution.py:434
  23.7 0.7 %far_grads_u.1 = (bf16[768,256]{1,0:T(8,128)(2,1)S(1)}, f32[768,256]{1,0:T(8,128)S(1)}, bf16[256,256]{1,0:T(8,128)(2,1)S(1)}, f32[32,128]{1,0:T(8,128)S(1)}) custom-call(s32[5,9]{1,0:T(8,128)S(4)} %links.1, bf16[1024,256]{1,0:T(8,128)(2,1)S(1)} %get-tuple-element.44.pairs, f32[96,128]{1,0:T(8,128)S(1)} %get-tuple-element.47.stats.after, ...), custom_call_target="tpu_custom_call" | custom-call | flops 150994944 | bytes 2097152 | tf_op jit(solution)/shard_map/far_grads_u/pallas_call | solution.py:434
  24.8 0.9 %collective-permute-done.11.far.d3 = bf16[256,256]{1,0:T(8,128)(2,1)S(1)} collective-permute-done((bf16[256,256]{1,0:T(8,128)(2,1)S(1)}, bf16[256,256]{1,0:T(8,128)(2,1)S(1)}, u32[]{:S(2)}, u32[]{:S(2)}) %collective-permute-start.11) | collective-permute-done | bytes 131104 | tf_op jit(solution)/shard_map/ppermute | solution.py:421
  25.6 0.8 %far_grads_d.1 = (bf16[768,256]{1,0:T(8,128)(2,1)S(1)}, f32[768,256]{1,0:T(8,128)S(1)}, bf16[256,256]{1,0:T(8,128)(2,1)S(1)}, f32[32,128]{1,0:T(8,128)S(1)}) custom-call(s32[5,9]{1,0:T(8,128)S(4)} %links.1, bf16[1024,256]{1,0:T(8,128)(2,1)S(1)} %get-tuple-element.44.pairs, f32[96,128]{1,0:T(8,128)S(1)} %get-tuple-element.47.stats.after, ...), custom_call_target="tpu_custom_call" | custom-call | flops 150994944 | bytes 2097152 | tf_op jit(solution)/shard_map/far_grads_d/pallas_call | solution.py:434
  26.4 1.6 %collective-permute-start.16 = (bf16[256,256]{1,0:T(8,128)(2,1)S(1)}, bf16[256,256]{1,0:T(8,128)(2,1)S(1)}, u32[]{:S(2)}, u32[]{:S(2)}) collective-permute-start(bf16[256,256]{1,0:T(8,128)(2,1)S(1)} %get-tuple-element.61), channel_id=1, source_target_pairs={{0,8},{1,0},{2,10},{3,2},{4,12},{5,4},{6,14},{7,6},{8,16},{9,1},{1... | collective-permute-start | bytes 393224 | tf_op jit(solution)/shard_map/ppermute | solution.py:421
  28.0 0.9 %near_grads.1 = (bf16[3072,256]{1,0:T(8,128)(2,1)S(1)}, f32[256,256]{1,0:T(8,128)S(1)}, f32[256,256]{1,0:T(8,128)S(1)}, bf16[256,256]{1,0:T(8,128)(2,1)S(1)}, bf...) custom-call(s32[5,9]{1,0:T(8,128)S(4)} %links.1, ...), custom_call_target="tpu_custom_call" | custom-call | flops 301989888 | bytes 2097152 | tf_op jit(solution)/shard_map/near_grads/pallas_call | solution.py:434
  29.0 2.0 %collective-permute-start.13 = (bf16[256,256]{1,0:T(8,128)(2,1)S(1)}, bf16[256,256]{1,0:T(8,128)(2,1)S(1)}, u32[]{:S(2)}, u32[]{:S(2)}) collective-permute-start(bf16[256,256]{1,0:T(8,128)(2,1)S(1)} %get-tuple-element.56), channel_id=1, source_target_pairs={{0,8},{1,0},{2,10},{3,2},{4,12},{5,4},{6,14},{7,6},{8,16},{9,1},{1... | collective-permute-start | bytes 393224 | tf_op jit(solution)/shard_map/ppermute | solution.py:421
  31.2 2.6 %collective-permute-start.17 = (bf16[256,256]{1,0:T(8,128)(2,1)S(1)}, bf16[256,256]{1,0:T(8,128)(2,1)S(1)}, u32[]{:S(2)}, u32[]{:S(2)}) collective-permute-start(bf16[256,256]{1,0:T(8,128)(2,1)S(1)} %merge_u.1), channel_id=1, source_target_pairs={{0,8},{1,0},{2,10},{3,2},{4,12},{5,4},{6,14},{7,6},{8,16},{9,1},{1... | collective-permute-start | bytes 393224 | tf_op jit(solution)/shard_map/ppermute | solution.py:421
  33.7 1.1 %outputs.1 = (bf16[256,128]{1,0:T(8,128)(2,1)S(1)}, bf16[256,128]{1,0:T(8,128)(2,1)S(1)}, bf16[512,128]{1,0:T(8,128)(2,1)S(1)}) custom-call(s32[5,9]{1,0:T(8,128)S(4)} %links.1, bf16[3072,256]{1,0:T(8,128)(2,1)S(1)} %get-tuple-element.62.near_mixed, bf16[768,256]{1,0:T(8,128)(2,1)S(1)} %get-tuple-element.63.u_mixed, ...), custom_call_target="tpu_custom_call" | custom-call | flops 301989888 | bytes 2097152 | tf_op jit(solution)/shard_map/outputs/pallas_call | solution.py:434
  34.8 0.6 %collective-permute-done.12.d = bf16[256,256]{1,0:T(8,128)(2,1)S(1)} collective-permute-done((bf16[256,256]{1,0:T(8,128)(2,1)S(1)}, bf16[256,256]{1,0:T(8,128)(2,1)S(1)}, u32[]{:S(2)}, u32[]{:S(2)}) %collective-permute-start.12) | collective-permute-done | bytes 131104 | tf_op jit(solution)/shard_map/ppermute | solution.py:421
  35.4 2.5 %collective-permute-done.15.from_d = bf16[256,256]{1,0:T(8,128)(2,1)S(1)} collective-permute-done((bf16[256,256]{1,0:T(8,128)(2,1)S(1)}, bf16[256,256]{1,0:T(8,128)(2,1)S(1)}, u32[]{:S(2)}, u32[]{:S(2)}) %collective-permute-start.15) | collective-permute-done | bytes 131104 | tf_op jit(solution)/shard_map/ppermute | solution.py:421
  38.6 0.6 %collective-permute-start.19 = (bf16[512,256]{1,0:T(8,128)(2,1)S(1)}, bf16[512,256]{1,0:T(8,128)(2,1)S(1)}, u32[]{:S(2)}, u32[]{:S(2)}) collective-permute-start(bf16[512,256]{1,0:T(8,128)(2,1)S(1)} %spread_far.1), channel_id=1, source_target_pairs={{0,1},{1,0},{2,3},{3,2},{4,5},{5,4},{6,7},{7,6},{8,9},{9,8},{10,11... | collective-permute-start | bytes 786440 | tf_op jit(solution)/shard_map/ppermute | solution.py:410
  39.2 0.5 spread_keep.1
  39.9 1.3 %collective-permute-start.22 = (bf16[384,256]{1,0:T(8,128)(2,1)S(1)}, bf16[384,256]{1,0:T(8,128)(2,1)S(1)}, u32[]{:S(2)}, u32[]{:S(2)}) collective-permute-start(bf16[384,256]{1,0:T(8,128)(2,1)S(1)} %get-tuple-element.74), channel_id=1, source_target_pairs={{0,4},{1,5},{2,6},{3,7},{4,0},{5,1},{6,2},{7,3},{8,12},{9,13},{10,... | collective-permute-start | bytes 589832 | tf_op jit(solution)/shard_map/ppermute | solution.py:410
  41.2 1.6 %collective-permute-start.20 = (bf16[256,256]{1,0:T(8,128)(2,1)S(1)}, bf16[256,256]{1,0:T(8,128)(2,1)S(1)}, u32[]{:S(2)}, u32[]{:S(2)}) collective-permute-start(bf16[256,256]{1,0:T(8,128)(2,1)S(1)} %get-tuple-element.72), channel_id=1, source_target_pairs={{0,2},{1,3},{2,0},{3,1},{4,6},{5,7},{6,4},{7,5},{8,10},{9,11},{10,... | collective-permute-start | bytes 393224 | tf_op jit(solution)/shard_map/ppermute | solution.py:410
  42.8 0.8 %collective-permute-start.21 = (bf16[256,256]{1,0:T(8,128)(2,1)S(1)}, bf16[256,256]{1,0:T(8,128)(2,1)S(1)}, u32[]{:S(2)}, u32[]{:S(2)}) collective-permute-start(bf16[256,256]{1,0:T(8,128)(2,1)S(1)} %get-tuple-element.73), channel_id=1, source_target_pairs={{0,6},{1,7},{2,4},{3,5},{4,2},{5,3},{6,0},{7,1},{8,14},{9,15},{10,... | collective-permute-start | bytes 393224 | tf_op jit(solution)/shard_map/ppermute | solution.py:410
  43.6 4.1 %collective-permute-done.20.gx = bf16[256,256]{1,0:T(8,128)(2,1)S(1)} collective-permute-done((bf16[256,256]{1,0:T(8,128)(2,1)S(1)}, bf16[256,256]{1,0:T(8,128)(2,1)S(1)}, u32[]{:S(2)}, u32[]{:S(2)}) %collective-permute-start.20) | collective-permute-done | bytes 131104 | tf_op jit(solution)/shard_map/ppermute | solution.py:410
  47.7 2.0 %collective-permute-done.21.gd = bf16[256,256]{1,0:T(8,128)(2,1)S(1)} collective-permute-done((bf16[256,256]{1,0:T(8,128)(2,1)S(1)}, bf16[256,256]{1,0:T(8,128)(2,1)S(1)}, u32[]{:S(2)}, u32[]{:S(2)}) %collective-permute-start.21) | collective-permute-done | bytes 131104 | tf_op jit(solution)/shard_map/ppermute | solution.py:410
  49.7 0.8 %finish.1 = (bf16[256,256]{1,0:T(8,128)(2,1)}, bf16[256,256]{1,0:T(8,128)(2,1)}) custom-call(bf16[256,256]{1,0:T(8,128)(2,1)S(1)} %get-tuple-element.70.mine, bf16[256,256]{1,0:T(8,128)(2,1)S(1)} %collective-permute-done.20.gx, bf16[256,256]{1,0:T(8,128)(2,1)S(1)} %collective-permute-done.21.gd, bf16[384,256]{1,0:T(8,128)(2,1)S(1)} %collective-permute-done.22.from_y, ...), custom_call_target="tpu_custom_call" | custom-call | bytes 2097152 | tf_op jit(solution)/shard_map/finish/pallas_call | solution.py:434
  (43 shorter events, 2.5 us)
Async XLA Ops:
  0.6 8.5 %collective-permute-start.4 = (bf16[256,256]{1,0:T(8,128)(2,1)}, bf16[256,256]{1,0:T(8,128)(2,1)S(1)}, u32[]{:S(2)}, u32[]{:S(2)}) collective-permute-start(bf16[256,256]{1,0:T(8,128)(2,1)} %f.1), channel_id=1, source_target_pairs={{0,6},{1,7},{2,4},{3,5},{4,2},{5,3},{6,0},{7,1},{8,14},{9,15},{10,... | collective-permute-start | bytes 393224 | tf_op jit(solution)/shard_map/ppermute | solution.py:410
  4.6 6.8 %collective-permute-start.1 = (bf16[256,256]{1,0:T(8,128)(2,1)}, bf16[256,256]{1,0:T(8,128)(2,1)S(1)}, u32[]{:S(2)}, u32[]{:S(2)}) collective-permute-start(bf16[256,256]{1,0:T(8,128)(2,1)} %f.1), channel_id=1, source_target_pairs={{0,2},{1,3},{2,0},{3,1},{4,6},{5,7},{6,4},{7,5},{8,10},{9,11},{10,... | collective-permute-start | bytes 393224 | tf_op jit(solution)/shard_map/ppermute | solution.py:410
  5.1 6.2 %collective-permute-start = (bf16[256,256]{1,0:T(8,128)(2,1)}, bf16[256,256]{1,0:T(8,128)(2,1)S(1)}, u32[]{:S(2)}, u32[]{:S(2)}) collective-permute-start(bf16[256,256]{1,0:T(8,128)(2,1)} %f.1), channel_id=1, source_target_pairs={{0,4},{1,5},{2,6},{3,7},{4,0},{5,1},{6,2},{7,3},{8,12},{9,13},{10,... | collective-permute-start | bytes 393224 | tf_op jit(solution)/shard_map/ppermute | solution.py:410
  9.1 2.3 %collective-permute-start.5 = (bf16[512,256]{1,0:T(8,128)(2,1)S(1)}, bf16[512,256]{1,0:T(8,128)(2,1)S(1)}, u32[]{:S(2)}, u32[]{:S(2)}) collective-permute-start(bf16[512,256]{1,0:T(8,128)(2,1)S(1)} %pack_early.1.early), channel_id=1, source_target_pairs={{0,1},{1,0},{2,3},{3,2},{4,5},{5,4},{6,7},{7,6},{8,9},{9,8},{10,11... | collective-permute-start | bytes 786440 | tf_op jit(solution)/shard_map/ppermute | solution.py:410
  11.4 1.6 %collective-permute-start.3 = (bf16[512,256]{1,0:T(8,128)(2,1)S(1)}, bf16[512,256]{1,0:T(8,128)(2,1)S(1)}, u32[]{:S(2)}, u32[]{:S(2)}) collective-permute-start(bf16[512,256]{1,0:T(8,128)(2,1)S(1)} %pack_late.1.late), channel_id=1, source_target_pairs={{0,1},{1,0},{2,3},{3,2},{4,5},{5,4},{6,7},{7,6},{8,9},{9,8},{10,11... | collective-permute-start | bytes 786440 | tf_op jit(solution)/shard_map/ppermute | solution.py:410
  12.0 2.8 %copy-start.1 = (s32[2,9]{1,0:T(2,128)S(1)}, s32[2,9]{1,0:T(2,128)}, u32[]{:S(2)}) copy-start(s32[2,9]{1,0:T(2,128)} %own.1) | copy-start | bytes 220
  12.0 2.8 %copy-start = (bf16[256,256]{1,0:T(8,128)(2,1)S(1)}, bf16[256,256]{1,0:T(8,128)(2,1)}, u32[]{:S(2)}) copy-start(bf16[256,256]{1,0:T(8,128)(2,1)} %d_own.3) | copy-start | bytes 393220
  13.2 5.2 %collective-permute-start.6 = (bf16[256,256]{1,0:T(8,128)(2,1)S(1)}, bf16[256,256]{1,0:T(8,128)(2,1)S(1)}, u32[]{:S(2)}, u32[]{:S(2)}) collective-permute-start(bf16[256,256]{1,0:T(8,128)(2,1)S(1)} %get-tuple-element.42.first_kv), channel_id=1, source_target_pairs={{0,8},{1,0},{2,10},{3,2},{4,12},{5,4},{6,14},{7,6},{8,16},{9,1},{1... | collective-permute-start | bytes 393224 | tf_op jit(solution)/shard_map/ppermute | solution.py:421
  14.8 5.8 %collective-permute-start.7 = (bf16[256,256]{1,0:T(8,128)(2,1)S(1)}, bf16[256,256]{1,0:T(8,128)(2,1)S(1)}, u32[]{:S(2)}, u32[]{:S(2)}) collective-permute-start(bf16[256,256]{1,0:T(8,128)(2,1)S(1)} %get-tuple-element.43.second_kv), channel_id=1, source_target_pairs={{0,1},{1,9},{2,3},{3,11},{4,5},{5,13},{6,7},{7,15},{8,0},{9,17},{1... | collective-permute-start | bytes 393224 | tf_op jit(solution)/shard_map/ppermute | solution.py:421
  14.9 5.8 %collective-permute-start.2 = (bf16[272,128]{1,0:T(8,128)(2,1)S(1)}, bf16[272,128]{1,0:T(8,128)(2,1)S(1)}, u32[]{:S(2)}, u32[]{:S(2)}) collective-permute-start(bf16[272,128]{1,0:T(8,128)(2,1)S(1)} %payload.1), channel_id=1, source_target_pairs={{0,4},{1,5},{2,6},{3,7},{4,0},{5,1},{6,2},{7,3},{8,12},{9,13},{10,... | collective-permute-start | bytes 208904 | tf_op jit(solution)/shard_map/ppermute | solution.py:410
  16.4 6.3 %collective-permute-start.9 = (bf16[256,256]{1,0:T(8,128)(2,1)S(1)}, bf16[256,256]{1,0:T(8,128)(2,1)S(1)}, u32[]{:S(2)}, u32[]{:S(2)}) collective-permute-start(bf16[256,256]{1,0:T(8,128)(2,1)S(1)} %get-tuple-element.42.first_kv), channel_id=1, source_target_pairs={{0,1},{1,9},{2,3},{3,11},{4,5},{5,13},{6,7},{7,15},{8,0},{9,17},{1... | collective-permute-start | bytes 393224 | tf_op jit(solution)/shard_map/ppermute | solution.py:421
  16.4 6.3 %collective-permute-start.8 = (bf16[256,256]{1,0:T(8,128)(2,1)S(1)}, bf16[256,256]{1,0:T(8,128)(2,1)S(1)}, u32[]{:S(2)}, u32[]{:S(2)}) collective-permute-start(bf16[256,256]{1,0:T(8,128)(2,1)S(1)} %get-tuple-element.43.second_kv), channel_id=1, source_target_pairs={{0,8},{1,0},{2,10},{3,2},{4,12},{5,4},{6,14},{7,6},{8,16},{9,1},{1... | collective-permute-start | bytes 393224 | tf_op jit(solution)/shard_map/ppermute | solution.py:421
  18.4 5.3 %collective-permute-start.10 = (bf16[256,256]{1,0:T(8,128)(2,1)S(1)}, bf16[256,256]{1,0:T(8,128)(2,1)S(1)}, u32[]{:S(2)}, u32[]{:S(2)}) collective-permute-start(bf16[256,256]{1,0:T(8,128)(2,1)S(1)} %collective-permute-done.6.u1.near), channel_id=1, source_target_pairs={{0,8},{1,0},{2,10},{3,2},{4,12},{5,4},{6,14},{7,6},{8,16},{9,1},{1... | collective-permute-start | bytes 393224 | tf_op jit(solution)/shard_map/ppermute | solution.py:421
  20.7 5.0 %collective-permute-start.11 = (bf16[256,256]{1,0:T(8,128)(2,1)S(1)}, bf16[256,256]{1,0:T(8,128)(2,1)S(1)}, u32[]{:S(2)}, u32[]{:S(2)}) collective-permute-start(bf16[256,256]{1,0:T(8,128)(2,1)S(1)} %collective-permute-done.7.d1.near), channel_id=1, source_target_pairs={{0,1},{1,9},{2,3},{3,11},{4,5},{5,13},{6,7},{7,15},{8,0},{9,17},{1... | collective-permute-start | bytes 393224 | tf_op jit(solution)/shard_map/ppermute | solution.py:421
  24.5 6.6 %collective-permute-start.14 = (bf16[256,256]{1,0:T(8,128)(2,1)S(1)}, bf16[256,256]{1,0:T(8,128)(2,1)S(1)}, u32[]{:S(2)}, u32[]{:S(2)}) collective-permute-start(bf16[256,256]{1,0:T(8,128)(2,1)S(1)} %get-tuple-element.49.after), channel_id=1, source_target_pairs={{0,1},{1,9},{2,3},{3,11},{4,5},{5,13},{6,7},{7,15},{8,0},{9,17},{1... | collective-permute-start | bytes 393224 | tf_op jit(solution)/shard_map/ppermute | solution.py:421
  26.4 4.7 %collective-permute-start.16 = (bf16[256,256]{1,0:T(8,128)(2,1)S(1)}, bf16[256,256]{1,0:T(8,128)(2,1)S(1)}, u32[]{:S(2)}, u32[]{:S(2)}) collective-permute-start(bf16[256,256]{1,0:T(8,128)(2,1)S(1)} %get-tuple-element.61), channel_id=1, source_target_pairs={{0,8},{1,0},{2,10},{3,2},{4,12},{5,4},{6,14},{7,6},{8,16},{9,1},{1... | collective-permute-start | bytes 393224 | tf_op jit(solution)/shard_map/ppermute | solution.py:421
  29.0 6.4 %collective-permute-start.12 = (bf16[256,256]{1,0:T(8,128)(2,1)S(1)}, bf16[256,256]{1,0:T(8,128)(2,1)S(1)}, u32[]{:S(2)}, u32[]{:S(2)}) collective-permute-start(bf16[256,256]{1,0:T(8,128)(2,1)S(1)} %get-tuple-element.55), channel_id=1, source_target_pairs={{0,1},{1,9},{2,3},{3,11},{4,5},{5,13},{6,7},{7,15},{8,0},{9,17},{1... | collective-permute-start | bytes 393224 | tf_op jit(solution)/shard_map/ppermute | solution.py:421
  29.0 6.4 %collective-permute-start.13 = (bf16[256,256]{1,0:T(8,128)(2,1)S(1)}, bf16[256,256]{1,0:T(8,128)(2,1)S(1)}, u32[]{:S(2)}, u32[]{:S(2)}) collective-permute-start(bf16[256,256]{1,0:T(8,128)(2,1)S(1)} %get-tuple-element.56), channel_id=1, source_target_pairs={{0,8},{1,0},{2,10},{3,2},{4,12},{5,4},{6,14},{7,6},{8,16},{9,1},{1... | collective-permute-start | bytes 393224 | tf_op jit(solution)/shard_map/ppermute | solution.py:421
  31.1 6.8 %collective-permute-start.15 = (bf16[256,256]{1,0:T(8,128)(2,1)S(1)}, bf16[256,256]{1,0:T(8,128)(2,1)S(1)}, u32[]{:S(2)}, u32[]{:S(2)}) collective-permute-start(bf16[256,256]{1,0:T(8,128)(2,1)S(1)} %merge_d.1), channel_id=1, source_target_pairs={{0,1},{1,9},{2,3},{3,11},{4,5},{5,13},{6,7},{7,15},{8,0},{9,17},{1... | collective-permute-start | bytes 393224 | tf_op jit(solution)/shard_map/ppermute | solution.py:421
  31.2 6.7 %collective-permute-start.17 = (bf16[256,256]{1,0:T(8,128)(2,1)S(1)}, bf16[256,256]{1,0:T(8,128)(2,1)S(1)}, u32[]{:S(2)}, u32[]{:S(2)}) collective-permute-start(bf16[256,256]{1,0:T(8,128)(2,1)S(1)} %merge_u.1), channel_id=1, source_target_pairs={{0,8},{1,0},{2,10},{3,2},{4,12},{5,4},{6,14},{7,6},{8,16},{9,1},{1... | collective-permute-start | bytes 393224 | tf_op jit(solution)/shard_map/ppermute | solution.py:421
  38.2 1.6 %collective-permute-start.18 = (bf16[512,256]{1,0:T(8,128)(2,1)S(1)}, bf16[512,256]{1,0:T(8,128)(2,1)S(1)}, u32[]{:S(2)}, u32[]{:S(2)}) collective-permute-start(bf16[512,256]{1,0:T(8,128)(2,1)S(1)} %get-tuple-element.68), channel_id=1, source_target_pairs={{0,1},{1,0},{2,3},{3,2},{4,5},{5,4},{6,7},{7,6},{8,9},{9,8},{10,11... | collective-permute-start | bytes 786440 | tf_op jit(solution)/shard_map/ppermute | solution.py:410
  38.6 2.5 %collective-permute-start.19 = (bf16[512,256]{1,0:T(8,128)(2,1)S(1)}, bf16[512,256]{1,0:T(8,128)(2,1)S(1)}, u32[]{:S(2)}, u32[]{:S(2)}) collective-permute-start(bf16[512,256]{1,0:T(8,128)(2,1)S(1)} %spread_far.1), channel_id=1, source_target_pairs={{0,1},{1,0},{2,3},{3,2},{4,5},{5,4},{6,7},{7,6},{8,9},{9,8},{10,11... | collective-permute-start | bytes 786440 | tf_op jit(solution)/shard_map/ppermute | solution.py:410
  39.9 9.8 %collective-permute-start.22 = (bf16[384,256]{1,0:T(8,128)(2,1)S(1)}, bf16[384,256]{1,0:T(8,128)(2,1)S(1)}, u32[]{:S(2)}, u32[]{:S(2)}) collective-permute-start(bf16[384,256]{1,0:T(8,128)(2,1)S(1)} %get-tuple-element.74), channel_id=1, source_target_pairs={{0,4},{1,5},{2,6},{3,7},{4,0},{5,1},{6,2},{7,3},{8,12},{9,13},{10,... | collective-permute-start | bytes 589832 | tf_op jit(solution)/shard_map/ppermute | solution.py:410
  41.2 6.4 %collective-permute-start.20 = (bf16[256,256]{1,0:T(8,128)(2,1)S(1)}, bf16[256,256]{1,0:T(8,128)(2,1)S(1)}, u32[]{:S(2)}, u32[]{:S(2)}) collective-permute-start(bf16[256,256]{1,0:T(8,128)(2,1)S(1)} %get-tuple-element.72), channel_id=1, source_target_pairs={{0,2},{1,3},{2,0},{3,1},{4,6},{5,7},{6,4},{7,5},{8,10},{9,11},{10,... | collective-permute-start | bytes 393224 | tf_op jit(solution)/shard_map/ppermute | solution.py:410
  42.8 6.9 %collective-permute-start.21 = (bf16[256,256]{1,0:T(8,128)(2,1)S(1)}, bf16[256,256]{1,0:T(8,128)(2,1)S(1)}, u32[]{:S(2)}, u32[]{:S(2)}) collective-permute-start(bf16[256,256]{1,0:T(8,128)(2,1)S(1)} %get-tuple-element.73), channel_id=1, source_target_pairs={{0,6},{1,7},{2,4},{3,5},{4,2},{5,3},{6,0},{7,1},{8,14},{9,15},{10,... | collective-permute-start | bytes 393224 | tf_op jit(solution)/shard_map/ppermute | solution.py:410

commit v16 on v14

--- a/solution.py
+++ b/solution.py
@@ -330,8 +330,8 @@
     acc[NEAR_LEFT:OWN, :] = by_side(0, u_edge[NEAR_LEFT:OWN, :], d_edge[NEAR_LEFT:OWN, :])
     acc[OWN:NEAR_RIGHT, :] = jnp.zeros((ROWS, 2 * HD), F32)
     acc[NEAR_RIGHT:FAR_RIGHT, :] = by_side(GROUP - 1, u_edge[:ROWS, :], d_edge[:ROWS, :])
+    runs = []
     for i in range(GROUP):
-        pair = pairs[2 * i * BLK : 2 * (i + 1) * BLK, :]
         at = [8 * (2 * (i % 2) + n) for n in range(2)]
         scale, row_dot = (by_side(i, u_scales[r : r + 1, :], d_scales[r : r + 1, :]) for r in at)
         for index, t in enumerate(near_runs(i)):
@@ -340,8 +340,10 @@
                 rows = near_rows(i, index, j)
                 parts.append(mix(terms[rows, :] * scale, prob_grads[rows, :], row_dot))
                 mixed[rows, :] = parts[-1]
-            at = pl.ds(start_of(links, i, t), SPAN * BLK)
-            acc[at, :] += dot(jnp.concatenate(parts, axis=0), pair, ((1,), (0,)))
+            runs.append((i, t, jnp.concatenate(parts, axis=0)))
+    for i, t, part in runs:
+        at = pl.ds(start_of(links, i, t), SPAN * BLK)
+        acc[at, :] += dot(part, pairs[2 * i * BLK : 2 * (i + 1) * BLK, :], ((1,), (0,)))
     factor = side_factor()
     first, second, u1, d1, u2, _, d2, _ = regions(position()[1])
     first_own[...] = acc[pl.ds(first, HALF), :] * factor
@@ -530,7 +532,7 @@
         "near_grads",
         [held(GROUP * 2 * run, 2 * HD)] + [held(HALF, 2 * HD, F32)] * 2 + [out(HALF, 2 * HD)] * 4,
         (links, pairs, terms, prob_grads, u_scales, d_scales, u_edge, d_edge),
-        4,
+        8,
         attention,
         [sums],
     )

time: 50.7 us -> 50.7 us (level)
  no operation moved by 1% of the time
where the time goes in v16:
time: 50.7 us; the launch traced here: 50.6 us
  starting transfers between devices  22.9 us (45%)
  waiting for transfers between devices  17 us (34%)
  Pallas kernels  9.74 us (19%)
  between operations  0.88 us (2%)
    ppermute x12, starting transfers between devices, chain(): return lax.ppermute(value, ('ctx', 'head'), pairs)  12.4 us
    ppermute x11, waiting for transfers between devices, across(): return lax.ppermute(value, ('ctx', 'head'), pairs)  11.9 us
    ppermute x11, starting transfers between devices, across(): return lax.ppermute(value, ('ctx', 'head'), pairs)  10.5 us
    pallas_call x22, Pallas kernels, call(): pl.pallas_call(kernel, name=name, out_shape=outs, in_specs=specs, out_spe...  9.74 us
    ppermute x12, waiting for transfers between devices, chain(): return lax.ppermute(value, ('ctx', 'head'), pairs)  5.12 us
  transfers between devices with their start and end apart: 23, of which 11 were waited for; matrix products, arithmetic and copies ran while one was open for 0% of the time, Pallas kernels for 17%

profile of v16, /device:TPU:0, one launch (start us, length us, event | category | flops | bytes accessed | tf_op | source)
XLA Modules:
  0.0 50.6 jit_solution(16587423379250008121)
XLA Ops:
  0.6 4.0 %collective-permute-start.4 = (bf16[256,256]{1,0:T(8,128)(2,1)}, bf16[256,256]{1,0:T(8,128)(2,1)S(1)}, u32[]{:S(2)}, u32[]{:S(2)}) collective-permute-start(bf16[256,256]{1,0:T(8,128)(2,1)} %f.1), channel_id=1, source_target_pairs={{0,6},{1,7},{2,4},{3,5},{4,2},{5,3},{6,0},{7,1},{8,14},{9,15},{10,... | collective-permute-start | bytes 393224 | tf_op jit(solution)/shard_map/ppermute | solution.py:412
  4.6 0.5 %collective-permute-start.1 = (bf16[256,256]{1,0:T(8,128)(2,1)}, bf16[256,256]{1,0:T(8,128)(2,1)S(1)}, u32[]{:S(2)}, u32[]{:S(2)}) collective-permute-start(bf16[256,256]{1,0:T(8,128)(2,1)} %f.1), channel_id=1, source_target_pairs={{0,2},{1,3},{2,0},{3,1},{4,6},{5,7},{6,4},{7,5},{8,10},{9,11},{10,... | collective-permute-start | bytes 393224 | tf_op jit(solution)/shard_map/ppermute | solution.py:412
  5.2 1.4 %begin.1 = (bf16[1024,384]{1,0:T(8,128)(2,1)S(1)}, bf16[256,256]{1,0:T(8,128)(2,1)S(1)}, f32[256,384]{1,0:T(8,128)S(1)}) custom-call(bf16[256,256]{1,0:T(8,128)(2,1)} %f.1, bf16[3,1024,256]{2,1,0:T(8,128)(2,1)} %bitcast.1), custom_call_target="tpu_custom_call" | custom-call | flops 100663296 | bytes 2097152 | tf_op jit(solution)/shard_map/begin/pallas_call | solution.py:436
  6.7 2.5 %collective-permute-done.4.two = bf16[256,256]{1,0:T(8,128)(2,1)S(1)} collective-permute-done((bf16[256,256]{1,0:T(8,128)(2,1)}, bf16[256,256]{1,0:T(8,128)(2,1)S(1)}, u32[]{:S(2)}, u32[]{:S(2)}) %collective-permute-start.4) | collective-permute-done | bytes 131104 | tf_op jit(solution)/shard_map/ppermute | solution.py:412
  9.2 2.1 %collective-permute-done.1.two = bf16[256,256]{1,0:T(8,128)(2,1)S(1)} collective-permute-done((bf16[256,256]{1,0:T(8,128)(2,1)}, bf16[256,256]{1,0:T(8,128)(2,1)S(1)}, u32[]{:S(2)}, u32[]{:S(2)}) %collective-permute-start.1) | collective-permute-done | bytes 131104 | tf_op jit(solution)/shard_map/ppermute | solution.py:412
  11.5 0.5 %project_rest.1.before = f32[512,384]{1,0:T(8,128)S(1)} custom-call(f32[256,384]{1,0:T(8,128)S(1)} %get-tuple-element.39.before, bf16[512,256]{1,0:T(8,128)(2,1)S(1)} %pack_early.1.early, bf16[512,256]{1,0:T(8,128)(2,1)S(1)} %pack_late.1.late, bf16[512,256]{1,0:T(8,128)(2,1)S(1)} %collective-permute-done.5.other_early, ...), custom_call_target="tpu_custom_call" | custom-call | flops 100663296 | bytes 2097152 | tf_op jit(solution)/shard_map/project_rest/pallas_call | solution.py:436
  12.0 1.0 %collective-permute-done.3.other_late = bf16[512,256]{1,0:T(8,128)(2,1)S(1)} collective-permute-done((bf16[512,256]{1,0:T(8,128)(2,1)S(1)}, bf16[512,256]{1,0:T(8,128)(2,1)S(1)}, u32[]{:S(2)}, u32[]{:S(2)}) %collective-permute-start.3) | collective-permute-done | bytes 262176 | tf_op jit(solution)/shard_map/ppermute | solution.py:412
  13.2 1.6 %collective-permute-start.6 = (bf16[256,256]{1,0:T(8,128)(2,1)S(1)}, bf16[256,256]{1,0:T(8,128)(2,1)S(1)}, u32[]{:S(2)}, u32[]{:S(2)}) collective-permute-start(bf16[256,256]{1,0:T(8,128)(2,1)S(1)} %get-tuple-element.42.first_kv), channel_id=1, source_target_pairs={{0,8},{1,0},{2,10},{3,2},{4,12},{5,4},{6,14},{7,6},{8,16},{9,1},{1... | collective-permute-start | bytes 393224 | tf_op jit(solution)/shard_map/ppermute | solution.py:423
  14.9 1.5 %collective-permute-start.2 = (bf16[272,128]{1,0:T(8,128)(2,1)S(1)}, bf16[272,128]{1,0:T(8,128)(2,1)S(1)}, u32[]{:S(2)}, u32[]{:S(2)}) collective-permute-start(bf16[272,128]{1,0:T(8,128)(2,1)S(1)} %payload.1), channel_id=1, source_target_pairs={{0,4},{1,5},{2,6},{3,7},{4,0},{5,1},{6,2},{7,3},{8,12},{9,13},{10,... | collective-permute-start | bytes 208904 | tf_op jit(solution)/shard_map/ppermute | solution.py:412
  16.4 2.0 %collective-permute-start.8 = (bf16[256,256]{1,0:T(8,128)(2,1)S(1)}, bf16[256,256]{1,0:T(8,128)(2,1)S(1)}, u32[]{:S(2)}, u32[]{:S(2)}) collective-permute-start(bf16[256,256]{1,0:T(8,128)(2,1)S(1)} %get-tuple-element.43.second_kv), channel_id=1, source_target_pairs={{0,8},{1,0},{2,10},{3,2},{4,12},{5,4},{6,14},{7,6},{8,16},{9,1},{1... | collective-permute-start | bytes 393224 | tf_op jit(solution)/shard_map/ppermute | solution.py:423
  18.4 2.2 %collective-permute-start.10 = (bf16[256,256]{1,0:T(8,128)(2,1)S(1)}, bf16[256,256]{1,0:T(8,128)(2,1)S(1)}, u32[]{:S(2)}, u32[]{:S(2)}) collective-permute-start(bf16[256,256]{1,0:T(8,128)(2,1)S(1)} %collective-permute-done.6.u1.near), channel_id=1, source_target_pairs={{0,8},{1,0},{2,10},{3,2},{4,12},{5,4},{6,14},{7,6},{8,16},{9,1},{1... | collective-permute-start | bytes 393224 | tf_op jit(solution)/shard_map/ppermute | solution.py:423
  20.9 0.7 %links.1 = s32[5,9]{1,0:T(8,128)S(4)} custom-call(s32[2,9]{1,0:T(2,128)S(1)} %copy-done.1, s32[2,9]{1,0:T(2,128)S(1)} %slice_convert_fusion.other, bf16[512,128]{1,0:T(8,128)(2,1)S(1)} %project_q.1.q), custom_call_target="tpu_custom_call" | custom-call | bytes 2097152 | tf_op jit(solution)/shard_map/links/pallas_call | solution.py:436
  21.6 1.1 %collective-permute-done.9.d2.middle = bf16[256,256]{1,0:T(8,128)(2,1)S(1)} collective-permute-done((bf16[256,256]{1,0:T(8,128)(2,1)S(1)}, bf16[256,256]{1,0:T(8,128)(2,1)S(1)}, u32[]{:S(2)}, u32[]{:S(2)}) %collective-permute-start.9) | collective-permute-done | bytes 131104 | tf_op jit(solution)/shard_map/ppermute | solution.py:423
  22.7 0.9 %near_scores.1 = (bf16[1024,256]{1,0:T(8,128)(2,1)S(1)}, f32[3072,128]{1,0:T(8,128)S(1)}, f32[3072,128]{1,0:T(8,128)S(1)}, f32[96,128]{1,0:T(8,128)S(1)}) custom-call(s32[5,9]{1,0:T(8,128)S(4)} %links.1, bf16[512,128]{1,0:T(8,128)(2,1)S(1)} %project_q.1.q, bf16[256,256]{1,0:T(8,128)(2,1)S(1)} %get-tuple-element.42.first_kv, ...), custom_call_target="tpu_custom_call" | custom-call | flops 301989888 | bytes 2097152 | tf_op jit(solution)/shard_map/near_scores/pallas_call | solution.py:436
  23.7 0.7 %far_grads_u.1 = (bf16[768,256]{1,0:T(8,128)(2,1)S(1)}, f32[768,256]{1,0:T(8,128)S(1)}, bf16[256,256]{1,0:T(8,128)(2,1)S(1)}, f32[32,128]{1,0:T(8,128)S(1)}) custom-call(s32[5,9]{1,0:T(8,128)S(4)} %links.1, bf16[1024,256]{1,0:T(8,128)(2,1)S(1)} %get-tuple-element.44.pairs, f32[96,128]{1,0:T(8,128)S(1)} %get-tuple-element.47.stats.after, ...), custom_call_target="tpu_custom_call" | custom-call | flops 150994944 | bytes 2097152 | tf_op jit(solution)/shard_map/far_grads_u/pallas_call | solution.py:436
  24.8 0.8 %collective-permute-done.11.far.d3 = bf16[256,256]{1,0:T(8,128)(2,1)S(1)} collective-permute-done((bf16[256,256]{1,0:T(8,128)(2,1)S(1)}, bf16[256,256]{1,0:T(8,128)(2,1)S(1)}, u32[]{:S(2)}, u32[]{:S(2)}) %collective-permute-start.11) | collective-permute-done | bytes 131104 | tf_op jit(solution)/shard_map/ppermute | solution.py:423
  25.6 0.8 %far_grads_d.1 = (bf16[768,256]{1,0:T(8,128)(2,1)S(1)}, f32[768,256]{1,0:T(8,128)S(1)}, bf16[256,256]{1,0:T(8,128)(2,1)S(1)}, f32[32,128]{1,0:T(8,128)S(1)}) custom-call(s32[5,9]{1,0:T(8,128)S(4)} %links.1, bf16[1024,256]{1,0:T(8,128)(2,1)S(1)} %get-tuple-element.44.pairs, f32[96,128]{1,0:T(8,128)S(1)} %get-tuple-element.47.stats.after, ...), custom_call_target="tpu_custom_call" | custom-call | flops 150994944 | bytes 2097152 | tf_op jit(solution)/shard_map/far_grads_d/pallas_call | solution.py:436
  26.4 1.6 %collective-permute-start.16 = (bf16[256,256]{1,0:T(8,128)(2,1)S(1)}, bf16[256,256]{1,0:T(8,128)(2,1)S(1)}, u32[]{:S(2)}, u32[]{:S(2)}) collective-permute-start(bf16[256,256]{1,0:T(8,128)(2,1)S(1)} %get-tuple-element.61), channel_id=1, source_target_pairs={{0,8},{1,0},{2,10},{3,2},{4,12},{5,4},{6,14},{7,6},{8,16},{9,1},{1... | collective-permute-start | bytes 393224 | tf_op jit(solution)/shard_map/ppermute | solution.py:423
  28.0 1.0 %near_grads.1 = (bf16[3072,256]{1,0:T(8,128)(2,1)S(1)}, f32[256,256]{1,0:T(8,128)S(1)}, f32[256,256]{1,0:T(8,128)S(1)}, bf16[256,256]{1,0:T(8,128)(2,1)S(1)}, bf...) custom-call(s32[5,9]{1,0:T(8,128)S(4)} %links.1, ...), custom_call_target="tpu_custom_call" | custom-call | flops 301989888 | bytes 2097152 | tf_op jit(solution)/shard_map/near_grads/pallas_call | solution.py:436
  29.0 2.0 %collective-permute-start.13 = (bf16[256,256]{1,0:T(8,128)(2,1)S(1)}, bf16[256,256]{1,0:T(8,128)(2,1)S(1)}, u32[]{:S(2)}, u32[]{:S(2)}) collective-permute-start(bf16[256,256]{1,0:T(8,128)(2,1)S(1)} %get-tuple-element.56), channel_id=1, source_target_pairs={{0,8},{1,0},{2,10},{3,2},{4,12},{5,4},{6,14},{7,6},{8,16},{9,1},{1... | collective-permute-start | bytes 393224 | tf_op jit(solution)/shard_map/ppermute | solution.py:423
  31.2 2.5 %collective-permute-start.17 = (bf16[256,256]{1,0:T(8,128)(2,1)S(1)}, bf16[256,256]{1,0:T(8,128)(2,1)S(1)}, u32[]{:S(2)}, u32[]{:S(2)}) collective-permute-start(bf16[256,256]{1,0:T(8,128)(2,1)S(1)} %merge_u.1), channel_id=1, source_target_pairs={{0,8},{1,0},{2,10},{3,2},{4,12},{5,4},{6,14},{7,6},{8,16},{9,1},{1... | collective-permute-start | bytes 393224 | tf_op jit(solution)/shard_map/ppermute | solution.py:423
  33.7 1.1 %outputs.1 = (bf16[256,128]{1,0:T(8,128)(2,1)S(1)}, bf16[256,128]{1,0:T(8,128)(2,1)S(1)}, bf16[512,128]{1,0:T(8,128)(2,1)S(1)}) custom-call(s32[5,9]{1,0:T(8,128)S(4)} %links.1, bf16[3072,256]{1,0:T(8,128)(2,1)S(1)} %get-tuple-element.62.near_mixed, bf16[768,256]{1,0:T(8,128)(2,1)S(1)} %get-tuple-element.63.u_mixed, ...), custom_call_target="tpu_custom_call" | custom-call | flops 301989888 | bytes 2097152 | tf_op jit(solution)/shard_map/outputs/pallas_call | solution.py:436
  34.8 0.6 %collective-permute-done.12.d = bf16[256,256]{1,0:T(8,128)(2,1)S(1)} collective-permute-done((bf16[256,256]{1,0:T(8,128)(2,1)S(1)}, bf16[256,256]{1,0:T(8,128)(2,1)S(1)}, u32[]{:S(2)}, u32[]{:S(2)}) %collective-permute-start.12) | collective-permute-done | bytes 131104 | tf_op jit(solution)/shard_map/ppermute | solution.py:423
  35.4 2.5 %collective-permute-done.15.from_d = bf16[256,256]{1,0:T(8,128)(2,1)S(1)} collective-permute-done((bf16[256,256]{1,0:T(8,128)(2,1)S(1)}, bf16[256,256]{1,0:T(8,128)(2,1)S(1)}, u32[]{:S(2)}, u32[]{:S(2)}) %collective-permute-start.15) | collective-permute-done | bytes 131104 | tf_op jit(solution)/shard_map/ppermute | solution.py:423
  38.7 0.5 %collective-permute-start.19 = (bf16[512,256]{1,0:T(8,128)(2,1)S(1)}, bf16[512,256]{1,0:T(8,128)(2,1)S(1)}, u32[]{:S(2)}, u32[]{:S(2)}) collective-permute-start(bf16[512,256]{1,0:T(8,128)(2,1)S(1)} %spread_far.1), channel_id=1, source_target_pairs={{0,1},{1,0},{2,3},{3,2},{4,5},{5,4},{6,7},{7,6},{8,9},{9,8},{10,11... | collective-permute-start | bytes 786440 | tf_op jit(solution)/shard_map/ppermute | solution.py:412
  39.2 0.5 spread_keep.1
  39.9 1.3 %collective-permute-start.22 = (bf16[384,256]{1,0:T(8,128)(2,1)S(1)}, bf16[384,256]{1,0:T(8,128)(2,1)S(1)}, u32[]{:S(2)}, u32[]{:S(2)}) collective-permute-start(bf16[384,256]{1,0:T(8,128)(2,1)S(1)} %get-tuple-element.74), channel_id=1, source_target_pairs={{0,4},{1,5},{2,6},{3,7},{4,0},{5,1},{6,2},{7,3},{8,12},{9,13},{10,... | collective-permute-start | bytes 589832 | tf_op jit(solution)/shard_map/ppermute | solution.py:412
  41.2 1.8 %collective-permute-start.20 = (bf16[256,256]{1,0:T(8,128)(2,1)S(1)}, bf16[256,256]{1,0:T(8,128)(2,1)S(1)}, u32[]{:S(2)}, u32[]{:S(2)}) collective-permute-start(bf16[256,256]{1,0:T(8,128)(2,1)S(1)} %get-tuple-element.72), channel_id=1, source_target_pairs={{0,6},{1,7},{2,4},{3,5},{4,2},{5,3},{6,0},{7,1},{8,14},{9,15},{10,... | collective-permute-start | bytes 393224 | tf_op jit(solution)/shard_map/ppermute | solution.py:412
  43.1 0.5 %collective-permute-start.21 = (bf16[256,256]{1,0:T(8,128)(2,1)S(1)}, bf16[256,256]{1,0:T(8,128)(2,1)S(1)}, u32[]{:S(2)}, u32[]{:S(2)}) collective-permute-start(bf16[256,256]{1,0:T(8,128)(2,1)S(1)} %get-tuple-element.73), channel_id=1, source_target_pairs={{0,2},{1,3},{2,0},{3,1},{4,6},{5,7},{6,4},{7,5},{8,10},{9,11},{10,... | collective-permute-start | bytes 393224 | tf_op jit(solution)/shard_map/ppermute | solution.py:412
  43.6 5.0 %collective-permute-done.20.gd = bf16[256,256]{1,0:T(8,128)(2,1)S(1)} collective-permute-done((bf16[256,256]{1,0:T(8,128)(2,1)S(1)}, bf16[256,256]{1,0:T(8,128)(2,1)S(1)}, u32[]{:S(2)}, u32[]{:S(2)}) %collective-permute-start.20) | collective-permute-done | bytes 131104 | tf_op jit(solution)/shard_map/ppermute | solution.py:412
  48.6 1.2 %collective-permute-done.21.gx = bf16[256,256]{1,0:T(8,128)(2,1)S(1)} collective-permute-done((bf16[256,256]{1,0:T(8,128)(2,1)S(1)}, bf16[256,256]{1,0:T(8,128)(2,1)S(1)}, u32[]{:S(2)}, u32[]{:S(2)}) %collective-permute-start.21) | collective-permute-done | bytes 131104 | tf_op jit(solution)/shard_map/ppermute | solution.py:412
  49.8 0.8 %finish.1 = (bf16[256,256]{1,0:T(8,128)(2,1)}, bf16[256,256]{1,0:T(8,128)(2,1)}) custom-call(bf16[256,256]{1,0:T(8,128)(2,1)S(1)} %get-tuple-element.70.mine, bf16[256,256]{1,0:T(8,128)(2,1)S(1)} %collective-permute-done.20.gd, bf16[256,256]{1,0:T(8,128)(2,1)S(1)} %collective-permute-done.21.gx, bf16[384,256]{1,0:T(8,128)(2,1)S(1)} %collective-permute-done.22.from_y, ...), custom_call_target="tpu_custom_call" | custom-call | bytes 2097152 | tf_op jit(solution)/shard_map/finish/pallas_call | solution.py:436
  (43 shorter events, 2.5 us)
Async XLA Ops:
  0.6 8.5 %collective-permute-start.4 = (bf16[256,256]{1,0:T(8,128)(2,1)}, bf16[256,256]{1,0:T(8,128)(2,1)S(1)}, u32[]{:S(2)}, u32[]{:S(2)}) collective-permute-start(bf16[256,256]{1,0:T(8,128)(2,1)} %f.1), channel_id=1, source_target_pairs={{0,6},{1,7},{2,4},{3,5},{4,2},{5,3},{6,0},{7,1},{8,14},{9,15},{10,... | collective-permute-start | bytes 393224 | tf_op jit(solution)/shard_map/ppermute | solution.py:412
  4.6 6.8 %collective-permute-start.1 = (bf16[256,256]{1,0:T(8,128)(2,1)}, bf16[256,256]{1,0:T(8,128)(2,1)S(1)}, u32[]{:S(2)}, u32[]{:S(2)}) collective-permute-start(bf16[256,256]{1,0:T(8,128)(2,1)} %f.1), channel_id=1, source_target_pairs={{0,2},{1,3},{2,0},{3,1},{4,6},{5,7},{6,4},{7,5},{8,10},{9,11},{10,... | collective-permute-start | bytes 393224 | tf_op jit(solution)/shard_map/ppermute | solution.py:412
  5.1 6.2 %collective-permute-start = (bf16[256,256]{1,0:T(8,128)(2,1)}, bf16[256,256]{1,0:T(8,128)(2,1)S(1)}, u32[]{:S(2)}, u32[]{:S(2)}) collective-permute-start(bf16[256,256]{1,0:T(8,128)(2,1)} %f.1), channel_id=1, source_target_pairs={{0,4},{1,5},{2,6},{3,7},{4,0},{5,1},{6,2},{7,3},{8,12},{9,13},{10,... | collective-permute-start | bytes 393224 | tf_op jit(solution)/shard_map/ppermute | solution.py:412
  9.1 2.3 %collective-permute-start.5 = (bf16[512,256]{1,0:T(8,128)(2,1)S(1)}, bf16[512,256]{1,0:T(8,128)(2,1)S(1)}, u32[]{:S(2)}, u32[]{:S(2)}) collective-permute-start(bf16[512,256]{1,0:T(8,128)(2,1)S(1)} %pack_early.1.early), channel_id=1, source_target_pairs={{0,1},{1,0},{2,3},{3,2},{4,5},{5,4},{6,7},{7,6},{8,9},{9,8},{10,11... | collective-permute-start | bytes 786440 | tf_op jit(solution)/shard_map/ppermute | solution.py:412
  11.4 1.6 %collective-permute-start.3 = (bf16[512,256]{1,0:T(8,128)(2,1)S(1)}, bf16[512,256]{1,0:T(8,128)(2,1)S(1)}, u32[]{:S(2)}, u32[]{:S(2)}) collective-permute-start(bf16[512,256]{1,0:T(8,128)(2,1)S(1)} %pack_late.1.late), channel_id=1, source_target_pairs={{0,1},{1,0},{2,3},{3,2},{4,5},{5,4},{6,7},{7,6},{8,9},{9,8},{10,11... | collective-permute-start | bytes 786440 | tf_op jit(solution)/shard_map/ppermute | solution.py:412
  12.0 2.8 %copy-start.1 = (s32[2,9]{1,0:T(2,128)S(1)}, s32[2,9]{1,0:T(2,128)}, u32[]{:S(2)}) copy-start(s32[2,9]{1,0:T(2,128)} %own.1) | copy-start | bytes 220
  12.0 2.8 %copy-start = (bf16[256,256]{1,0:T(8,128)(2,1)S(1)}, bf16[256,256]{1,0:T(8,128)(2,1)}, u32[]{:S(2)}) copy-start(bf16[256,256]{1,0:T(8,128)(2,1)} %d_own.3) | copy-start | bytes 393220
  13.2 5.2 %collective-permute-start.6 = (bf16[256,256]{1,0:T(8,128)(2,1)S(1)}, bf16[256,256]{1,0:T(8,128)(2,1)S(1)}, u32[]{:S(2)}, u32[]{:S(2)}) collective-permute-start(bf16[256,256]{1,0:T(8,128)(2,1)S(1)} %get-tuple-element.42.first_kv), channel_id=1, source_target_pairs={{0,8},{1,0},{2,10},{3,2},{4,12},{5,4},{6,14},{7,6},{8,16},{9,1},{1... | collective-permute-start | bytes 393224 | tf_op jit(solution)/shard_map/ppermute | solution.py:423
  14.8 5.8 %collective-permute-start.7 = (bf16[256,256]{1,0:T(8,128)(2,1)S(1)}, bf16[256,256]{1,0:T(8,128)(2,1)S(1)}, u32[]{:S(2)}, u32[]{:S(2)}) collective-permute-start(bf16[256,256]{1,0:T(8,128)(2,1)S(1)} %get-tuple-element.43.second_kv), channel_id=1, source_target_pairs={{0,1},{1,9},{2,3},{3,11},{4,5},{5,13},{6,7},{7,15},{8,0},{9,17},{1... | collective-permute-start | bytes 393224 | tf_op jit(solution)/shard_map/ppermute | solution.py:423
  14.9 5.8 %collective-permute-start.2 = (bf16[272,128]{1,0:T(8,128)(2,1)S(1)}, bf16[272,128]{1,0:T(8,128)(2,1)S(1)}, u32[]{:S(2)}, u32[]{:S(2)}) collective-permute-start(bf16[272,128]{1,0:T(8,128)(2,1)S(1)} %payload.1), channel_id=1, source_target_pairs={{0,4},{1,5},{2,6},{3,7},{4,0},{5,1},{6,2},{7,3},{8,12},{9,13},{10,... | collective-permute-start | bytes 208904 | tf_op jit(solution)/shard_map/ppermute | solution.py:412
  16.4 6.3 %collective-permute-start.9 = (bf16[256,256]{1,0:T(8,128)(2,1)S(1)}, bf16[256,256]{1,0:T(8,128)(2,1)S(1)}, u32[]{:S(2)}, u32[]{:S(2)}) collective-permute-start(bf16[256,256]{1,0:T(8,128)(2,1)S(1)} %get-tuple-element.42.first_kv), channel_id=1, source_target_pairs={{0,1},{1,9},{2,3},{3,11},{4,5},{5,13},{6,7},{7,15},{8,0},{9,17},{1... | collective-permute-start | bytes 393224 | tf_op jit(solution)/shard_map/ppermute | solution.py:423
  16.4 6.3 %collective-permute-start.8 = (bf16[256,256]{1,0:T(8,128)(2,1)S(1)}, bf16[256,256]{1,0:T(8,128)(2,1)S(1)}, u32[]{:S(2)}, u32[]{:S(2)}) collective-permute-start(bf16[256,256]{1,0:T(8,128)(2,1)S(1)} %get-tuple-element.43.second_kv), channel_id=1, source_target_pairs={{0,8},{1,0},{2,10},{3,2},{4,12},{5,4},{6,14},{7,6},{8,16},{9,1},{1... | collective-permute-start | bytes 393224 | tf_op jit(solution)/shard_map/ppermute | solution.py:423
  18.4 5.3 %collective-permute-start.10 = (bf16[256,256]{1,0:T(8,128)(2,1)S(1)}, bf16[256,256]{1,0:T(8,128)(2,1)S(1)}, u32[]{:S(2)}, u32[]{:S(2)}) collective-permute-start(bf16[256,256]{1,0:T(8,128)(2,1)S(1)} %collective-permute-done.6.u1.near), channel_id=1, source_target_pairs={{0,8},{1,0},{2,10},{3,2},{4,12},{5,4},{6,14},{7,6},{8,16},{9,1},{1... | collective-permute-start | bytes 393224 | tf_op jit(solution)/shard_map/ppermute | solution.py:423
  20.7 5.0 %collective-permute-start.11 = (bf16[256,256]{1,0:T(8,128)(2,1)S(1)}, bf16[256,256]{1,0:T(8,128)(2,1)S(1)}, u32[]{:S(2)}, u32[]{:S(2)}) collective-permute-start(bf16[256,256]{1,0:T(8,128)(2,1)S(1)} %collective-permute-done.7.d1.near), channel_id=1, source_target_pairs={{0,1},{1,9},{2,3},{3,11},{4,5},{5,13},{6,7},{7,15},{8,0},{9,17},{1... | collective-permute-start | bytes 393224 | tf_op jit(solution)/shard_map/ppermute | solution.py:423
  24.5 6.6 %collective-permute-start.14 = (bf16[256,256]{1,0:T(8,128)(2,1)S(1)}, bf16[256,256]{1,0:T(8,128)(2,1)S(1)}, u32[]{:S(2)}, u32[]{:S(2)}) collective-permute-start(bf16[256,256]{1,0:T(8,128)(2,1)S(1)} %get-tuple-element.49.after), channel_id=1, source_target_pairs={{0,1},{1,9},{2,3},{3,11},{4,5},{5,13},{6,7},{7,15},{8,0},{9,17},{1... | collective-permute-start | bytes 393224 | tf_op jit(solution)/shard_map/ppermute | solution.py:423
  26.4 4.7 %collective-permute-start.16 = (bf16[256,256]{1,0:T(8,128)(2,1)S(1)}, bf16[256,256]{1,0:T(8,128)(2,1)S(1)}, u32[]{:S(2)}, u32[]{:S(2)}) collective-permute-start(bf16[256,256]{1,0:T(8,128)(2,1)S(1)} %get-tuple-element.61), channel_id=1, source_target_pairs={{0,8},{1,0},{2,10},{3,2},{4,12},{5,4},{6,14},{7,6},{8,16},{9,1},{1... | collective-permute-start | bytes 393224 | tf_op jit(solution)/shard_map/ppermute | solution.py:423
  29.0 6.4 %collective-permute-start.12 = (bf16[256,256]{1,0:T(8,128)(2,1)S(1)}, bf16[256,256]{1,0:T(8,128)(2,1)S(1)}, u32[]{:S(2)}, u32[]{:S(2)}) collective-permute-start(bf16[256,256]{1,0:T(8,128)(2,1)S(1)} %get-tuple-element.55), channel_id=1, source_target_pairs={{0,1},{1,9},{2,3},{3,11},{4,5},{5,13},{6,7},{7,15},{8,0},{9,17},{1... | collective-permute-start | bytes 393224 | tf_op jit(solution)/shard_map/ppermute | solution.py:423
  29.0 6.4 %collective-permute-start.13 = (bf16[256,256]{1,0:T(8,128)(2,1)S(1)}, bf16[256,256]{1,0:T(8,128)(2,1)S(1)}, u32[]{:S(2)}, u32[]{:S(2)}) collective-permute-start(bf16[256,256]{1,0:T(8,128)(2,1)S(1)} %get-tuple-element.56), channel_id=1, source_target_pairs={{0,8},{1,0},{2,10},{3,2},{4,12},{5,4},{6,14},{7,6},{8,16},{9,1},{1... | collective-permute-start | bytes 393224 | tf_op jit(solution)/shard_map/ppermute | solution.py:423
  31.1 6.8 %collective-permute-start.15 = (bf16[256,256]{1,0:T(8,128)(2,1)S(1)}, bf16[256,256]{1,0:T(8,128)(2,1)S(1)}, u32[]{:S(2)}, u32[]{:S(2)}) collective-permute-start(bf16[256,256]{1,0:T(8,128)(2,1)S(1)} %merge_d.1), channel_id=1, source_target_pairs={{0,1},{1,9},{2,3},{3,11},{4,5},{5,13},{6,7},{7,15},{8,0},{9,17},{1... | collective-permute-start | bytes 393224 | tf_op jit(solution)/shard_map/ppermute | solution.py:423
  31.2 6.7 %collective-permute-start.17 = (bf16[256,256]{1,0:T(8,128)(2,1)S(1)}, bf16[256,256]{1,0:T(8,128)(2,1)S(1)}, u32[]{:S(2)}, u32[]{:S(2)}) collective-permute-start(bf16[256,256]{1,0:T(8,128)(2,1)S(1)} %merge_u.1), channel_id=1, source_target_pairs={{0,8},{1,0},{2,10},{3,2},{4,12},{5,4},{6,14},{7,6},{8,16},{9,1},{1... | collective-permute-start | bytes 393224 | tf_op jit(solution)/shard_map/ppermute | solution.py:423
  38.2 1.6 %collective-permute-start.18 = (bf16[512,256]{1,0:T(8,128)(2,1)S(1)}, bf16[512,256]{1,0:T(8,128)(2,1)S(1)}, u32[]{:S(2)}, u32[]{:S(2)}) collective-permute-start(bf16[512,256]{1,0:T(8,128)(2,1)S(1)} %get-tuple-element.68), channel_id=1, source_target_pairs={{0,1},{1,0},{2,3},{3,2},{4,5},{5,4},{6,7},{7,6},{8,9},{9,8},{10,11... | collective-permute-start | bytes 786440 | tf_op jit(solution)/shard_map/ppermute | solution.py:412
  38.7 2.5 %collective-permute-start.19 = (bf16[512,256]{1,0:T(8,128)(2,1)S(1)}, bf16[512,256]{1,0:T(8,128)(2,1)S(1)}, u32[]{:S(2)}, u32[]{:S(2)}) collective-permute-start(bf16[512,256]{1,0:T(8,128)(2,1)S(1)} %spread_far.1), channel_id=1, source_target_pairs={{0,1},{1,0},{2,3},{3,2},{4,5},{5,4},{6,7},{7,6},{8,9},{9,8},{10,11... | collective-permute-start | bytes 786440 | tf_op jit(solution)/shard_map/ppermute | solution.py:412
  39.9 9.9 %collective-permute-start.22 = (bf16[384,256]{1,0:T(8,128)(2,1)S(1)}, bf16[384,256]{1,0:T(8,128)(2,1)S(1)}, u32[]{:S(2)}, u32[]{:S(2)}) collective-permute-start(bf16[384,256]{1,0:T(8,128)(2,1)S(1)} %get-tuple-element.74), channel_id=1, source_target_pairs={{0,4},{1,5},{2,6},{3,7},{4,0},{5,1},{6,2},{7,3},{8,12},{9,13},{10,... | collective-permute-start | bytes 589832 | tf_op jit(solution)/shard_map/ppermute | solution.py:412
  41.2 7.3 %collective-permute-start.20 = (bf16[256,256]{1,0:T(8,128)(2,1)S(1)}, bf16[256,256]{1,0:T(8,128)(2,1)S(1)}, u32[]{:S(2)}, u32[]{:S(2)}) collective-permute-start(bf16[256,256]{1,0:T(8,128)(2,1)S(1)} %get-tuple-element.72), channel_id=1, source_target_pairs={{0,6},{1,7},{2,4},{3,5},{4,2},{5,3},{6,0},{7,1},{8,14},{9,15},{10,... | collective-permute-start | bytes 393224 | tf_op jit(solution)/shard_map/ppermute | solution.py:412
  43.1 6.7 %collective-permute-start.21 = (bf16[256,256]{1,0:T(8,128)(2,1)S(1)}, bf16[256,256]{1,0:T(8,128)(2,1)S(1)}, u32[]{:S(2)}, u32[]{:S(2)}) collective-permute-start(bf16[256,256]{1,0:T(8,128)(2,1)S(1)} %get-tuple-element.73), channel_id=1, source_target_pairs={{0,2},{1,3},{2,0},{3,1},{4,6},{5,7},{6,4},{7,5},{8,10},{9,11},{10,... | collective-permute-start | bytes 393224 | tf_op jit(solution)/shard_map/ppermute | solution.py:412
